TPU v7x, 32 devices: a whole 2x2x4 slice. The times are simulated.
32 devices in a mesh: seq: 16 (over z, x, core), head: 2 (over y).
Axes of the slice: x: 2, y: 2, z: 4, core: 2. Of those that a mesh axis runs over, the one named last changes fastest.
Arguments:
- queries: bfloat16 [8192, 3072], P('seq', 'head'), may hold values from -6 to 6
- key_vectors: bfloat16 [8192, 3072], P('seq', 'head'), may hold values from -6 to 6
- value_vectors: bfloat16 [8192, 3072], P('seq', 'head'), may hold values from -6 to 6
- doc_lengths: int32 [16], replicated, may hold values from 1 to 5120, 8192 in all
- norm_gain: float32 [3072], P('head'), may hold values from 0.1 to 1.9
- out_weight: bfloat16 [3072, 4096], P('head'), may hold values from -0.15625 to 0.15625
Outputs:
- layer_out: bfloat16 [8192, 4096], P('seq', 'head')
Inputs may be any that keep to these rules, and one draw needn't show every extreme that they name: doc_lengths sum to 8192; the longest document has exactly 5120 tokens.
All inputs are finite; a program needn't handle non-finite values.
Results may differ from a plain program's by a relative error of at most 0.014.
Values may be sent and summed in bfloat16 or wider, within the bound.
No kernel may reach another device: no remote copies, remote signals or barrier semaphores. Data moves between devices by JAX's collectives and lax.ppermute only.
A program may use at most 64 MiB of HBM per device.

v0:
```python
import jax
import jax.numpy as jnp
from jax import lax
from jax.sharding import PartitionSpec as P

DH = 128


def attend_block(query_h, key_h, value_h, segment):
    row_count = query_h.shape[0]
    row_ids = jnp.arange(row_count, dtype=jnp.int32)
    allowed = (row_ids[None, :] <= row_ids[:, None]) & (segment[None, :] == segment[:, None])
    scores = jnp.einsum("thd,shd->hts", query_h, key_h, preferred_element_type=jnp.float32)
    scores = jnp.where(allowed[None], scores, 0.0).astype(jnp.bfloat16)
    within = jnp.einsum("hts,shd->thd", scores, value_h, preferred_element_type=jnp.float32)
    last_rows = segment == segment[-1]
    key_last = jnp.where(last_rows[:, None, None], key_h, jnp.zeros_like(key_h))
    block_state = jnp.einsum("thd,the->hde", key_last, value_h, preferred_element_type=jnp.float32)
    return (within, block_state)


def body(queries, key_vectors, value_vectors, doc_lengths, norm_gain, out_weight):
    row_count = queries.shape[0]
    head_count = queries.shape[1] // DH
    group_width = head_count * DH
    my_block = lax.axis_index("seq")
    offset = my_block * row_count
    doc_bounds = jnp.cumsum(doc_lengths)
    positions = offset + jnp.arange(row_count, dtype=jnp.int32)
    before = doc_bounds[None, :] <= positions[:, None]
    segment = jnp.sum(before.astype(jnp.int32), axis=1)
    starts = jnp.sum(jnp.where(before, doc_lengths[None, :], 0), axis=1)
    query_h = queries.reshape(row_count, head_count, DH)
    key_h = key_vectors.reshape(row_count, head_count, DH)
    value_h = value_vectors.reshape(row_count, head_count, DH)
    within, block_state = attend_block(query_h, key_h, value_h, segment)
    first_block = starts[0] // row_count
    shards = lax.all_gather(block_state[None], "seq", axis=0, tiled=True)
    shard_ids = jnp.arange(shards.shape[0], dtype=jnp.int32)
    weights = ((shard_ids >= first_block) & (shard_ids < my_block)).astype(jnp.float32)
    carried = jnp.sum(weights[:, None, None, None] * shards, axis=0)
    carried = carried.astype(jnp.bfloat16)
    cross_rows = (segment == segment[0]) & (starts[0] < offset)
    query_cross = jnp.where(cross_rows[:, None, None], query_h, jnp.zeros_like(query_h))
    carried_term = jnp.einsum(
        "thd,hde->the", query_cross, carried, preferred_element_type=jnp.float32
    )
    mixture = within + carried_term
    square_mean = jnp.mean(mixture * mixture, axis=-1, keepdims=True)
    gain_heads = norm_gain.reshape(head_count, DH)
    normed = (mixture * lax.rsqrt(square_mean + 1e-06) * gain_heads).astype(jnp.bfloat16)
    normed = normed.reshape(row_count, group_width)
    partial_sum = jnp.dot(normed, out_weight, preferred_element_type=jnp.float32)
    layer_out = lax.psum_scatter(
        partial_sum.astype(jnp.bfloat16), "head", scatter_dimension=1, tiled=True
    )
    return layer_out


def solution(mesh):
    return jax.shard_map(
        body,
        mesh=mesh,
        in_specs=(
            P("seq", "head"),
            P("seq", "head"),
            P("seq", "head"),
            P(),
            P("head"),
            P("head", None),
        ),
        out_specs=P("seq", "head"),
        check_vma=False,
    )
```

profile of v0, /device:TPU:0, one launch (start us, length us, event | category | flops | bytes accessed | tf_op | source)
XLA Modules:
  0.0 212.6 jit_solution(12752009923045508519)
XLA Ops:
  6.5 0.0 all-gather.3.cloned.1.call-start
  6.5 0.7 copy.28
  7.3 0.1 reduce
  7.4 0.7 fusion.16
  8.2 0.6 slice.10
  9.5 0.6 fusion.20
  10.1 1.8 copy.30
  11.9 0.0 copy-done
  12.0 1.7 copy.33
  13.6 1.3 broadcast_compare_fusion
  14.9 0.0 copy-start.1
  14.9 3.0 %fusion.7 = f32[12,128,128]{2,1,0:T(8,128)} fusion(bf16[512,12,128]{0,2,1:T(8,128)(2,1)} %bitcast.26, bf16[512,12,128]{0,2,1:T(8,128)(2,1)S(1)} %bitcast.24, pred[512]{0:T(512)(128)(4,1)S(1)} %get-tuple-element.7), kind=kOutput, calls=%fused_computation.12 | convolution fusion | flops 202113024 | bytes 3932672 | tf_op jit(solution)/shard_map/thd,the->hde/dot_general | solution.py:18
  17.9 0.0 all-gather.3.cloned.1.call-update
  17.9 0.0 reduce-scatter.2.cloned.1.call-start
  20.7 0.7 copy.29
  21.4 0.2 fusion.11
  21.7 99.8 %all-gather.3.cloned.1.call-done = f32[192,128,128]{2,1,0:T(8,128)} async-done(((f32[12,128,128]{2,1,0:T(8,128)}), f32[192,128,128]{2,1,0:T(8,128)}) %all-gather.3.cloned.1.call-update) | async-done | bytes 12582928 | tf_op jit(solution)/shard_map/all_gather | solution.py:38
  121.5 6.1 %multiply_reduce_fusion = bf16[12,128,128]{2,1,0:T(8,128)(2,1)S(1)} fusion(f32[16,12,128,128]{3,2,1,0:T(8,128)} %bitcast.21, f32[16]{0:T(128)S(1)} %and_convert_fusion), kind=kLoop, calls=%fused_computation | loop fusion | flops 6094848 | bytes 12976192 | tf_op jit(solution)/shard_map/reduce_sum | solution.py:41
  127.6 2.3 %fusion.5 = f32[12,128,512]{2,1,0:T(8,128)} fusion(bf16[512,12,128]{0,2,1:T(8,128)(2,1)S(1)} %bitcast.22, pred[512]{0:T(512)(128)(4,1)S(1)} %get-tuple-element.8, bf16[12,128,128]{2,1,0:T(8,128)(2,1)S(1)} %multiply_reduce_fusion), kind=kOutput, calls=%fused_computation.10 | convolution fusion | flops 202113024 | bytes 5112320 | tf_op jit(solution)/shard_map/thd,hde->the/dot_general | solution.py:45
  129.9 7.9 %multiply_reduce_fusion.1 = (f32[512,12]{0,1:T(8,128)S(1)}, f32[512,12,128]{0,2,1:T(8,128)}) fusion(f32[12,128,512]{2,1,0:T(8,128)} %fusion.5, bf16[512,12,128]{0,2,1:T(8,128)(2,1)} %bitcast.27, pred[512,512]{1,0:T(8,128)(4,1)S(1)} %fusion.11, bf16[512,12,128]{0,2,1:T(8,128)(2,1)S(1)} %bitcast.23, bf16[512,12,128]{0,2,1:T(8,128)(2,1)S(1)} %bitcast.25), kind=kOutput, calls=%fused_computation.9 | convolution fusion | flops 1619257344 | bytes 11296768 | tf_op jit(solution)/shard_map/hts,shd->thd/dot_general | solution.py:15
  137.9 2.3 %multiply_convert_fusion = bf16[512,12,128]{0,2,1:T(8,128)(2,1)S(1)} fusion(f32[512,12,128]{0,2,1:T(8,128)} %get-tuple-element.12, f32[12,128]{1,0:T(8,128)S(1)} %bitcast.29, f32[512,12]{0,1:T(8,128)S(1)} %add_rsqrt_fusion), kind=kLoop, calls=%fused_computation.8 | loop fusion | flops 2359296 | bytes 4749312 | tf_op jit(solution)/shard_map/convert_element_type | solution.py:51
  140.2 12.9 %convolution_convert_fusion = bf16[512,4096]{1,0:T(8,128)(2,1)} fusion(bf16[512,1536]{0,1:T(8,128)(2,1)S(1)} %bitcast.28, bf16[1536,4096]{1,0:T(8,128)(2,1)} %param.11), kind=kOutput, calls=%fused_computation.5 | convolution fusion | flops 6444548096 | bytes 18350080 | tf_op jit(solution)/shard_map/dot_general | solution.py:53
  153.1 0.0 reduce-scatter.2.cloned.1.call-update
  153.1 52.6 %reduce-scatter.2.cloned.1.call-done = bf16[512,2048]{1,0:T(8,128)(2,1)} async-done(((bf16[512,4096]{1,0:T(8,128)(2,1)}), bf16[512,2048]{1,0:T(8,128)(2,1)}) %reduce-scatter.2.cloned.1.call-update) | async-done | bytes 2097168 | tf_op jit(solution)/shard_map/reduce_scatter | solution.py:54
  (12 shorter events, 0.1 us)
Async XLA Ops:
  6.5 115.0 %all-gather.3.cloned.1.call-start = ((), (), s32[]{:S(2)}) async-start(), calls=%async_computation.2 | async-start | bytes 13369344 | tf_op jit(solution)/shard_map/all_gather | solution.py:38
  10.1 1.9 copy-start
  12.0 2.9 %copy-start.2 = (bf16[512,1536]{0,1:T(8,128)(2,1)}, bf16[512,1536]{0,1:T(8,128)(2,1)S(1)}, u32[]{:S(2)}) copy-start(bf16[512,1536]{0,1:T(8,128)(2,1)S(1)} %copy.30) | copy-start | bytes 4718596
  14.9 5.8 %copy-start.1 = (bf16[512,1536]{1,0:T(8,128)(2,1)S(1)}, bf16[512,1536]{1,0:T(8,128)(2,1)}, u32[]{:S(2)}) copy-start(bf16[512,1536]{1,0:T(8,128)(2,1)} %param.6) | copy-start | bytes 4718596
  17.9 187.9 %reduce-scatter.2.cloned.1.call-start = ((), (), s32[]{:S(2)}) async-start(), calls=%async_computation.1 | async-start | bytes 6291456 | tf_op jit(solution)/shard_map/reduce_scatter | solution.py:54
  127.6 2.3 %copy-start.3 = (bf16[512,1536]{0,1:T(8,128)(2,1)S(1)}, bf16[512,1536]{0,1:T(8,128)(2,1)}, u32[]{:S(2)}) copy-start(bf16[512,1536]{0,1:T(8,128)(2,1)} %copy-done.2) | copy-start | bytes 4718596
  129.9 7.9 %copy-start.4 = (f32[1536]{0:T(1024)S(1)}, f32[1536]{0:T(1024)}, u32[]{:S(2)}) copy-start(f32[1536]{0:T(1024)} %param.10) | copy-start | bytes 18436
Sparse Core Ops, SparseCore 0:
  18.0 103.4 all-gather.2
  153.3 52.4 reduce-scatter.1
where the time goes:
time: 213 us
  waiting for transfers between devices  152 us (71%)
  matrix products  26.1 us (12%)
  between operations  17 us (8%)
  other arithmetic  10.8 us (5%)
  local copies, waits for them, and re-layouts  6.18 us (3%)
    all_gather x1, waiting for transfers between devices, body(): shards = lax.all_gather(block_state[None], 'seq', axis=0, tiled=True)  99.8 us
    reduce_scatter x1, waiting for transfers between devices, body(): lax.psum_scatter(partial_sum.astype(jnp.bfloat16), 'head', scatter_dimens...  52.6 us
    dot_general x1, matrix products, body(): jnp.dot(normed, out_weight, preferred_element_type=jnp.float32)  12.9 us
    dot_general x1, matrix products, attend_block(): jnp.einsum('hts,shd->thd', scores, value_h, preferred_element_type=jnp.fl...  7.92 us
    reduce_sum x1, other arithmetic, body(): carried = jnp.sum(weights[:, None, None, None] * shards, axis=0)  6.11 us
  transfers between devices with their start and end apart: 2, of which 2 were waited for; matrix products, arithmetic and copies ran while one was open for 0% of the time, Pallas kernels for 0%

commit v1 on v0

v1 whole, which is shorter than its diff:
```python
import functools

import jax
import jax.numpy as jnp
from jax import lax
from jax.experimental import pallas as pl
from jax.experimental.pallas import tpu as pltpu
from jax.sharding import PartitionSpec as P

DH = 128
PLANES = 4
F32, BF16 = jnp.float32, jnp.bfloat16
LENS = 8
VMEM_LIMIT = 48 * 1024 * 1024


def doc_start(meta, doc_count, token):
    bound = jnp.int32(0)
    start = jnp.int32(0)
    for d in range(doc_count):
        bound = bound + meta[LENS + d]
        start = jnp.where(bound <= token, bound, start)
    return start


def call(kernel, grid, in_specs, out_specs, out_shape, flops, bytes_accessed, scratch=()):
    return pl.pallas_call(
        kernel,
        grid_spec=pltpu.PrefetchScalarGridSpec(
            num_scalar_prefetch=1,
            grid=grid,
            in_specs=in_specs,
            out_specs=out_specs,
            scratch_shapes=scratch,
        ),
        out_shape=out_shape,
        compiler_params=pltpu.CompilerParams(vmem_limit_bytes=VMEM_LIMIT),
        cost_estimate=pl.CostEstimate(flops=flops, bytes_accessed=bytes_accessed, transcendentals=0),
    )


def block_states(meta, key, value, doc_count, steps):
    rows, width = key.shape
    part = width // steps

    def kernel(meta_ref, k_ref, v_ref, o_ref):
        offset = meta_ref[0] * rows
        first = doc_start(meta_ref, doc_count, offset + rows - 1) - offset
        live = lax.broadcasted_iota(jnp.int32, (rows, DH), 0) >= first
        for h in range(part // DH):
            cols = slice(h * DH, (h + 1) * DH)
            k = jnp.where(live, k_ref[:, cols], jnp.zeros((), BF16))
            s = lax.dot_general(k, v_ref[:, cols], (((0,), (0,)), ((), ())), preferred_element_type=F32)
            o_ref[0, cols, :] = s.astype(BF16)

    def slot(g, m):
        return (g ^ m[1], 0, 0) if steps > 1 else (0, 0, 0)

    return call(
        kernel,
        (steps,),
        [pl.BlockSpec((rows, part), lambda g, m: (0, g))] * 2,
        pl.BlockSpec((1, part, DH), slot),
        jax.ShapeDtypeStruct((steps, part, DH), BF16),
        2 * rows * width * DH,
        2 * 2 * rows * width,
    )(meta, key, value)


def within_block(meta, query, key, value, doc_count):
    rows, width = query.shape
    part = DH
    for heads in (4, 3, 2):
        if width % (heads * DH) == 0:
            part = heads * DH
            break
    tile = rows // 2

    def kernel(meta_ref, q_ref, k_ref, v_ref, o_ref, mask_ref):
        @pl.when(pl.program_id(0) == 0)
        def _():
            offset = meta_ref[0] * rows
            t = lax.broadcasted_iota(jnp.int32, (rows, rows), 0)
            s = lax.broadcasted_iota(jnp.int32, (rows, rows), 1)
            pos = lax.broadcasted_iota(jnp.int32, (rows, 1), 0)
            first = jnp.zeros((rows, 1), jnp.int32)
            bound = -offset
            for d in range(doc_count):
                bound = bound + meta_ref[LENS + d]
                first = jnp.where(bound <= pos, bound, first)
            mask_ref[...] = jnp.where((s <= t) & (s >= first), 1.0, 0.0).astype(BF16)

        for h in range(part // DH):
            cols = slice(h * DH, (h + 1) * DH)
            for i in range(2):
                r = slice(i * tile, (i + 1) * tile)
                seen = (i + 1) * tile
                scores = lax.dot_general(
                    q_ref[r, cols], k_ref[:seen, cols], (((1,), (1,)), ((), ())), preferred_element_type=F32
                )
                scores = scores.astype(BF16) * mask_ref[r, :seen]
                o_ref[r, cols] = jnp.dot(scores, v_ref[:seen, cols], preferred_element_type=F32)

    spec = pl.BlockSpec((rows, part), lambda g, m: (0, g))
    return call(
        kernel,
        (width // part,),
        [spec] * 3,
        spec,
        jax.ShapeDtypeStruct((rows, width), F32),
        3 * rows * rows * width,
        10 * rows * width,
        [pltpu.VMEM((rows, rows), BF16)],
    )(meta, query, key, value)


def norm_heads(meta, query, within, carry, gain, doc_count, slot):
    rows, width = query.shape
    part = carry.shape[0]

    def kernel(meta_ref, q_ref, w_ref, c_ref, g_ref, o_ref):
        offset = meta_ref[0] * rows
        begins = doc_start(meta_ref, doc_count, offset)
        bound = jnp.int32(0)
        end = jnp.int32(0)
        for d in range(doc_count):
            previous = bound
            bound = bound + meta_ref[LENS + d]
            end = jnp.where(previous <= offset, bound, end)
        stop = jnp.where(begins < offset, end - offset, 0)
        cross = lax.broadcasted_iota(jnp.int32, (rows, DH), 0) < stop
        for h in range(part // DH):
            cols = slice(h * DH, (h + 1) * DH)
            term = jnp.dot(q_ref[:, cols], c_ref[cols, :], preferred_element_type=F32)
            mixture = w_ref[:, cols] + jnp.where(cross, term, 0.0)
            mean = jnp.mean(mixture * mixture, axis=-1, keepdims=True)
            o_ref[:, cols] = (mixture * lax.rsqrt(mean + 1e-06) * g_ref[:, cols]).astype(BF16)

    def block(i, m):
        return (0, 0) if slot is None else (0, m[1] ^ slot)

    spec = pl.BlockSpec((rows, part), block)
    return call(
        kernel,
        (1,),
        [spec, spec, pl.BlockSpec((part, DH), lambda i, m: (0, 0)), pl.BlockSpec((1, part), block)],
        pl.BlockSpec((rows, part), lambda i, m: (0, 0)),
        jax.ShapeDtypeStruct((rows, part), BF16),
        2 * rows * part * DH,
        8 * rows * part,
    )(meta, query, within, carry, gain.reshape(1, width))


def project_own(meta, pieces, weight, columns):
    rows, part = pieces[0].shape
    tile = columns // 4
    count = len(pieces)

    def kernel(meta_ref, *refs):
        ns, ws, o_ref = refs[:count], refs[count : 2 * count], refs[-1]
        total = jnp.dot(ns[0][...], ws[0][...], preferred_element_type=F32)
        for n, w in zip(ns[1:], ws[1:]):
            total = total + jnp.dot(n[...], w[...], preferred_element_type=F32)
        o_ref[...] = total

    return call(
        kernel,
        (4,),
        [pl.BlockSpec((rows, part), lambda n, m: (0, 0))] * count
        + [pl.BlockSpec((part, tile), lambda n, m, s=s: (m[1] ^ s, m[2] * 4 + n)) for s in range(count)],
        pl.BlockSpec((rows, tile), lambda n, m: (0, n)),
        jax.ShapeDtypeStruct((rows, columns), F32),
        2 * rows * part * count * columns,
        2 * part * count * columns + 4 * rows * columns,
    )(meta, *pieces, *[weight] * count)


def project_more(meta, total, pieces, weights, dtype):
    rows, columns = total.shape
    part = pieces[0].shape[1]
    count, ranges = len(pieces), len(weights[0])
    steps = 2
    tile = columns // (ranges * steps)
    flat = [w for ws in weights for w in ws]

    def kernel(meta_ref, t_ref, *refs):
        ns, ws, o_ref = refs[:count], refs[count:-1], refs[-1]
        for c in range(ranges):

            @pl.when(pl.program_id(0) == c)
            def _():
                out = t_ref[...]
                for s in range(count):
                    out = out + jnp.dot(ns[s][...], ws[s * ranges + c][...], preferred_element_type=F32)
                o_ref[...] = out.astype(dtype)

    def column(c):
        return lambda g, n, m: (0, jnp.where(g < c, 0, jnp.where(g > c, steps - 1, n)))

    out_spec = pl.BlockSpec((rows, tile), lambda g, n, m: (0, g * steps + n))
    return call(
        kernel,
        (ranges, steps),
        [out_spec]
        + [pl.BlockSpec((rows, part), lambda g, n, m: (0, 0))] * count
        + [pl.BlockSpec((part, tile), column(c)) for _ in range(count) for c in range(ranges)],
        out_spec,
        jax.ShapeDtypeStruct((rows, columns), dtype),
        2 * rows * part * count * columns,
        2 * part * count * columns + 6 * rows * columns,
    )(meta, total, *pieces, *flat)


def body(n_seq, n_head, query, key, value, doc_lengths, gain, weight):
    rows, width = query.shape
    doc_count = doc_lengths.shape[0]
    plane = n_seq // PLANES
    columns = weight.shape[1] // n_head
    block = lax.axis_index("seq").astype(jnp.int32)
    group = lax.axis_index("head").astype(jnp.int32)
    member = block % plane
    meta = jnp.concatenate([
        jnp.stack([block, member, group]), jnp.zeros((LENS - 3,), jnp.int32), doc_lengths
    ])

    bounds = jnp.cumsum(doc_lengths)

    def first_block(token):
        starts = jnp.max(jnp.where(bounds <= token, bounds, 0))
        return starts // rows

    def weigh(condition):
        return condition.astype(F32)

    def swap(x, bit):
        return lax.ppermute(x, "seq", [(i, i ^ bit) for i in range(n_seq)])

    def flip(x):
        return lax.ppermute(x, "head", [(0, 1), (1, 0)])

    by_slot = (width // DH) % plane == 0
    steps = plane if by_slot else 1
    states = block_states(meta, key, value, doc_count, steps)
    if not by_slot:
        states = states.reshape(plane, width // plane, DH)[jnp.arange(plane, dtype=jnp.int32) ^ member]
    slots = [states[s] for s in range(plane)]

    pair = n_head == 2 and by_slot and plane == 4
    part = width // plane
    if pair:
        far_weight = lax.dynamic_slice(weight, (member * part, (1 - group) * columns), (part, columns))
        half = columns // 2
        w0 = [flip(far_weight[:, c * half : (c + 1) * half]) for c in range(2)]

    kept = []
    bit = 1
    while bit < plane:
        mine, send = slots[0::2], slots[1::2]
        got = swap(jnp.stack(send), bit)
        got = [got[i] for i in range(len(send))]
        upper = (member & bit) != 0
        unit = block & ~(2 * bit - 1)
        joined = weigh(first_block((unit + 2 * bit) * rows - 1) < unit + bit)
        own_factor = jnp.where(upper, 1.0, joined)
        got_factor = jnp.where(upper, joined, 1.0)
        kept.append((mine, got, bit, upper, unit))
        slots = [
            (own_factor * a.astype(F32) + got_factor * b.astype(F32)).astype(BF16) for a, b in zip(mine, got)
        ]
        bit *= 2
    base = block - member
    begins = first_block(base * rows)
    carry = jnp.zeros(slots[0].shape, F32)
    for d in range(PLANES - 1, 0, -1):
        shift = d * plane
        got = lax.ppermute(slots[0], "seq", [(i, i + shift) for i in range(n_seq - shift)])
        carry = carry + weigh((base - shift + plane - 1 >= begins) & (base >= shift)) * got.astype(F32)
    carries = [carry]

    for mine, got, bit, upper, unit in reversed(kept):
        middle = unit + bit
        begins = first_block(middle * rows)
        through, joined = weigh(begins < unit), weigh(begins < middle)
        ours, theirs = [], []
        for carry, a, b in zip(carries, mine, got):
            lower_state = jnp.where(upper, b, a).astype(F32)
            after = through * carry + joined * lower_state
            ours.append(jnp.where(upper, after, carry))
            theirs.append(jnp.where(upper, carry, after).astype(BF16))
        back = swap(jnp.stack(theirs), bit)
        carries = [x for i, c in enumerate(ours) for x in (c, back[i])]
    carries = [c.astype(BF16) for c in carries]

    within = within_block(meta, query, key, value, doc_count)
    if not pair:
        natural = jnp.stack(carries)[jnp.arange(plane, dtype=jnp.int32) ^ member].reshape(width, DH)
        normed = norm_heads(meta, query, within, natural, gain, doc_count, None)
        partial_sum = jnp.dot(normed, weight, preferred_element_type=F32)
        return lax.psum_scatter(partial_sum.astype(BF16), "head", scatter_dimension=1, tiled=True)

    order = (0, 2, 1, 3)
    normed = {s: norm_heads(meta, query, within, carries[s], gain, doc_count, s) for s in order}
    far = {s: flip(normed[s]) for s in order}
    w0 = list(lax.optimization_barrier((*w0, carries[2])))[:2]
    w2 = [swap(w, 2) for w in w0]
    w1 = [swap(w, 1) for w in w0]
    w3 = [swap(w, 1) for w in w2]
    weights = {0: w0, 1: w1, 2: w2, 3: w3}
    total = project_own(meta, [normed[s] for s in range(plane)], weight, columns)
    total = project_more(meta, total, [far[s] for s in order[:3]], [weights[s] for s in order[:3]], F32)
    return project_more(meta, total, [far[3]], [weights[3]], BF16)


def solution(mesh):
    return jax.shard_map(
        functools.partial(body, mesh.shape["seq"], mesh.shape["head"]),
        mesh=mesh,
        in_specs=(
            P("seq", "head"),
            P("seq", "head"),
            P("seq", "head"),
            P(),
            P("head"),
            P("head", None),
        ),
        out_specs=P("seq", "head"),
        check_vma=False,
    )
```

time: 213 us -> 132 us (0.62)
  waiting for transfers between devices: 152 us -> 35.6 us
  Pallas kernels: 0 us -> 32.2 us
  matrix products: 26.1 us -> 0 us
  starting transfers between devices: 0.04 us -> 26 us
  local copies, waits for them, and re-layouts: 6.18 us -> 14.4 us
  between operations: 17 us -> 13.1 us
    all_gather x1 -> x0, waiting for transfers between devices: 99.8 us -> none  [body(): shards = lax.all_gather(block_state[None], 'seq', axis=0, tiled=True)]
    reduce_scatter x1 -> x0, waiting for transfers between devices: 52.6 us -> none  [body(): lax.psum_scatter(partial_sum.astype(jnp.bfloat16), 'head', scatter_dimens...]
    ppermute x0 -> x19, waiting for transfers between devices: none -> 35.6 us  [the longest x6 18.7 us: flip(): return lax.ppermute(x, 'head', [(0, 1), (1, 0)])]
    pallas_call x0 -> x9, Pallas kernels: none -> 32.2 us  [the longest x2 11.8 us: project_more(): call(kernel, (ranges, steps), [out_spec] + [pl.BlockSpec((rows, part), la...]
    dot_general x4 -> x0, matrix products: 26.1 us -> none  [the longest x1 12.9 us: body(): jnp.dot(normed, out_weight, preferred_element_type=jnp.float32)]
    ppermute x0 -> x19, starting transfers between devices: none -> 26 us  [the longest x3 10.8 us: body(): lax.ppermute(slots[0], 'seq', [(i, i + shift) for i in range(n_seq - shif...]
    reduce_sum x2 -> x0, other arithmetic: 6.85 us -> none  [the longest x1 6.11 us: body(): carried = jnp.sum(weights[:, None, None, None] * shards, axis=0)]
    unnamed x13 -> x20, local copies, waits for them, and re-layouts: 4.25 us -> 10.3 us
  transfers between devices with their start and end apart: 2 -> 19, of which waited for: 2 -> 6; matrix products, arithmetic and copies ran while one was open for 0% -> 7% of each run, Pallas kernels for 0% -> 20%
where the time goes in v1:
time: 132 us; the launch traced here: 131 us
  waiting for transfers between devices  35.6 us (27%)
  Pallas kernels  32.2 us (24%)
  starting transfers between devices  26 us (20%)
  local copies, waits for them, and re-layouts  14.4 us (11%)
  between operations  13.1 us (10%)
  other arithmetic  10.2 us (8%)
    ppermute x6, waiting for transfers between devices, flip(): return lax.ppermute(x, 'head', [(0, 1), (1, 0)])  18.7 us
    ppermute x10, waiting for transfers between devices, swap(): return lax.ppermute(x, 'seq', [(i, i ^ bit) for i in range(n_seq)])  16.9 us
    pallas_call x2, Pallas kernels, project_more(): call(kernel, (ranges, steps), [out_spec] + [pl.BlockSpec((rows, part), la...  11.8 us
    ppermute x3, starting transfers between devices, body(): lax.ppermute(slots[0], 'seq', [(i, i + shift) for i in range(n_seq - shif...  10.8 us
    unnamed x20, local copies, waits for them, and re-layouts  10.3 us
    ppermute x6, starting transfers between devices, flip(): return lax.ppermute(x, 'head', [(0, 1), (1, 0)])  8.32 us
    pallas_call x1, Pallas kernels, project_own(): call(kernel, (4,), [pl.BlockSpec((rows, part), lambda n, m: (0, 0))] * co...  7.35 us
    ppermute x10, starting transfers between devices, swap(): return lax.ppermute(x, 'seq', [(i, i ^ bit) for i in range(n_seq)])  6.87 us
  transfers between devices with their start and end apart: 19, of which 6 were waited for; matrix products, arithmetic and copies ran while one was open for 7% of the time, Pallas kernels for 20%

profile of v1, /device:TPU:0, one launch (start us, length us, event | category | flops | bytes accessed | tf_op | source)
XLA Modules:
  0.0 131.4 jit_solution(10555969789187507894)
XLA Ops:
  3.6 2.3 %shard_map.65 = bf16[4,384,128]{2,1,0:T(8,128)(2,1)S(1)} custom-call(s32[24]{0:T(128)S(1)} %concatenate.3.meta_ref, bf16[512,1536]{1,0:T(8,128)(2,1)S(1)} %copy-done.4, bf16[512,1536]{1,0:T(8,128)(2,1)S(1)} %copy-done.6), custom_call_target="tpu_custom_call" | custom-call | flops 201326592 | bytes 3145728 | tf_op jit(solution)/shard_map/pallas_call | solution.py:59
  12.0 1.6 %add_convert_fusion.1 = bf16[1,384,128]{2,1,0:T(8,128)(2,1)} fusion(f32[]{:T(128)S(6)} %select_n.128, f32[]{:T(128)S(6)} %select_n.127, bf16[2,384,128]{2,1,0:T(8,128)(2,1)} %collective-permute-done, bf16[4,384,128]{2,1,0:T(8,128)(2,1)S(1)} %shard_map.65), kind=kLoop, calls=%fused_computation.20 | loop fusion | flops 294912 | bytes 294920 | tf_op jit(solution)/shard_map/convert_element_type | solution.py:268
  13.6 2.5 %collective-permute-start.1 = (bf16[1,384,128]{2,1,0:T(8,128)(2,1)}, bf16[1,384,128]{2,1,0:T(8,128)(2,1)}, u32[]{:S(2)}, u32[]{:S(2)}) collective-permute-start(bf16[1,384,128]{2,1,0:T(8,128)(2,1)} %add_convert_fusion.1), channel_id=1, source_target_pairs={{0,4},{2,6},{4,0},{6,2},{8,12},{10,14},{12,8},{14,10},{16,20},{18,... | collective-permute-start | bytes 294920 | tf_op jit(solution)/shard_map/ppermute | solution.py:236
  19.9 1.7 %fusion.9 = bf16[384,128]{1,0:T(8,128)(2,1)} fusion(bf16[1,384,128]{2,1,0:T(8,128)(2,1)} %collective-permute-done.1, f32[]{:T(128)S(6)} %select_n.129, f32[]{:T(128)S(6)} %select_n.124, bf16[2,384,128]{2,1,0:T(8,128)(2,1)} %collective-permute-done, f32[]{:T(128)S(6)} %select_n.128, bf16[4,384,128]{2,1,0:T(8,128)(2,1)S(1)} %shard_map.65, f32[]{:T(128)S(6)} %select_n.127), kind=kLoop, calls=%fused_computation.24 | loop fusion | flops 589824 | bytes 393232 | tf_op jit(solution)/shard_map/convert_element_type | solution.py:268
  21.5 6.4 %collective-permute-start.2 = (bf16[384,128]{1,0:T(8,128)(2,1)}, bf16[384,128]{1,0:T(8,128)(2,1)}, u32[]{:S(2)}, u32[]{:S(2)}) collective-permute-start(bf16[384,128]{1,0:T(8,128)(2,1)} %fusion.9), channel_id=1, source_target_pairs={{0,24},{2,26},{4,28},{6,30},{1,25},{3,27},{5,29},{7,31}} | collective-permute-start | bytes 294920 | tf_op jit(solution)/shard_map/ppermute | solution.py:276
  27.9 1.9 %collective-permute-start.3 = (bf16[384,128]{1,0:T(8,128)(2,1)}, bf16[384,128]{1,0:T(8,128)(2,1)}, u32[]{:S(2)}, u32[]{:S(2)}) collective-permute-start(bf16[384,128]{1,0:T(8,128)(2,1)} %fusion.9), channel_id=1, source_target_pairs={{0,16},{2,18},{4,20},{6,22},{8,24},{10,26},{12,28},{14,30},{1,17},... | collective-permute-start | bytes 294920 | tf_op jit(solution)/shard_map/ppermute | solution.py:276
  29.9 2.5 %collective-permute-start.4 = (bf16[384,128]{1,0:T(8,128)(2,1)}, bf16[384,128]{1,0:T(8,128)(2,1)}, u32[]{:S(2)}, u32[]{:S(2)}) collective-permute-start(bf16[384,128]{1,0:T(8,128)(2,1)} %fusion.9), channel_id=1, source_target_pairs={{0,8},{2,10},{4,12},{6,14},{8,16},{10,18},{12,20},{14,22},{16,24},... | collective-permute-start | bytes 294920 | tf_op jit(solution)/shard_map/ppermute | solution.py:276
  32.3 2.6 %fusion.15 = (bf16[384,1024]{1,0:T(8,128)(2,1)}, bf16[384,1024]{1,0:T(8,128)(2,1)}) fusion(bf16[1536,4096]{1,0:T(8,128)(2,1)} %refs_7_.1, s32[]{:T(128)S(6)} %select_n.140, s32[]{:T(128)S(6)} %add.97, s32[]{:T(128)S(6)} %select_n.141), kind=kLoop, calls=%fused_computation.40 | loop fusion | bytes 3145740 | tf_op jit(solution)/shard_map/slice | solution.py:253
  35.0 1.5 %collective-permute-start.10 = (bf16[384,1024]{1,0:T(8,128)(2,1)}, bf16[384,1024]{1,0:T(8,128)(2,1)}, u32[]{:S(2)}, u32[]{:S(2)}) collective-permute-start(bf16[384,1024]{1,0:T(8,128)(2,1)} %get-tuple-element.17), channel_id=1, source_target_pairs={{0,1},{1,0},{2,3},{3,2},{4,5},{5,4},{6,7},{7,6},{8,9},{9,8},{10,11... | collective-permute-start | bytes 2359304 | tf_op jit(solution)/shard_map/ppermute | solution.py:239
  47.2 1.6 %collective-permute-start.5 = (bf16[1,384,128]{2,1,0:T(8,128)(2,1)S(1)}, bf16[1,384,128]{2,1,0:T(8,128)(2,1)S(1)}, u32[]{:S(2)}, u32[]{:S(2)}) collective-permute-start(bf16[1,384,128]{2,1,0:T(8,128)(2,1)S(1)} %fusion.8), channel_id=1, source_target_pairs={{0,4},{2,6},{4,0},{6,2},{8,12},{10,14},{12,8},{14,10},{16,20},{18,... | collective-permute-start | bytes 294920 | tf_op jit(solution)/shard_map/ppermute | solution.py:236
  50.2 6.6 %shard_map.64.w_ref = f32[512,1536]{1,0:T(8,128)} custom-call(s32[24]{0:T(128)S(1)} %concatenate.3.meta_ref, bf16[512,1536]{1,0:T(8,128)(2,1)S(1)} %copy-done.1, bf16[512,1536]{1,0:T(8,128)(2,1)S(1)} %copy-done.5, bf16[512,1536]{1,0:T(8,128)(2,1)S(1)} %copy-done.7), custom_call_target="tpu_custom_call" | custom-call | flops 1207959552 | bytes 7864320 | tf_op jit(solution)/shard_map/pallas_call | solution.py:105
  58.1 1.9 %copy-done = f32[512,1536]{1,0:T(8,128)S(1)} copy-done((f32[512,1536]{1,0:T(8,128)S(1)}, f32[512,1536]{1,0:T(8,128)}, u32[]{:S(2)}) %copy-start) | copy-done | bytes 3145752
  61.1 1.6 %collective-permute-start.8 = (bf16[512,384]{1,0:T(8,128)(2,1)S(1)}, bf16[512,384]{1,0:T(8,128)(2,1)S(1)}, u32[]{:S(2)}, u32[]{:S(2)}) collective-permute-start(bf16[512,384]{1,0:T(8,128)(2,1)S(1)} %shard_map.68.refs_2_), channel_id=1, source_target_pairs={{0,1},{1,0},{2,3},{3,2},{4,5},{5,4},{6,7},{7,6},{8,9},{9,8},{10,11... | collective-permute-start | bytes 1179656 | tf_op jit(solution)/shard_map/ppermute | solution.py:239
  62.6 10.0 %collective-permute-done.11.refs_4_ = bf16[384,1024]{1,0:T(8,128)(2,1)} collective-permute-done((bf16[384,1024]{1,0:T(8,128)(2,1)}, bf16[384,1024]{1,0:T(8,128)(2,1)}, u32[]{:S(2)}, u32[]{:S(2)}) %collective-permute-start.11) | collective-permute-done | bytes 786464 | tf_op jit(solution)/shard_map/ppermute | solution.py:239
  76.7 1.6 %collective-permute-start.7 = (bf16[512,384]{1,0:T(8,128)(2,1)S(1)}, bf16[512,384]{1,0:T(8,128)(2,1)S(1)}, u32[]{:S(2)}, u32[]{:S(2)}) collective-permute-start(bf16[512,384]{1,0:T(8,128)(2,1)S(1)} %shard_map.66.refs_0_), channel_id=1, source_target_pairs={{0,1},{1,0},{2,3},{3,2},{4,5},{5,4},{6,7},{7,6},{8,9},{9,8},{10,11... | collective-permute-start | bytes 1179656 | tf_op jit(solution)/shard_map/ppermute | solution.py:239
  80.1 8.2 %collective-permute-done.7.refs_0_ = bf16[512,384]{1,0:T(8,128)(2,1)S(1)} collective-permute-done((bf16[512,384]{1,0:T(8,128)(2,1)S(1)}, bf16[512,384]{1,0:T(8,128)(2,1)S(1)}, u32[]{:S(2)}, u32[]{:S(2)}) %collective-permute-start.7) | collective-permute-done | bytes 393248 | tf_op jit(solution)/shard_map/ppermute | solution.py:239
  89.8 3.5 %collective-permute-done.12.refs_5_ = bf16[384,1024]{1,0:T(8,128)(2,1)S(1)} collective-permute-done((bf16[384,1024]{1,0:T(8,128)(2,1)}, bf16[384,1024]{1,0:T(8,128)(2,1)S(1)}, u32[]{:S(2)}, u32[]{:S(2)}) %collective-permute-start.12) | collective-permute-done | bytes 786464 | tf_op jit(solution)/shard_map/ppermute | solution.py:236
  93.3 12.2 %collective-permute-done.13.refs_6_ = bf16[384,1024]{1,0:T(8,128)(2,1)S(1)} collective-permute-done((bf16[384,1024]{1,0:T(8,128)(2,1)}, bf16[384,1024]{1,0:T(8,128)(2,1)S(1)}, u32[]{:S(2)}, u32[]{:S(2)}) %collective-permute-start.13) | collective-permute-done | bytes 786464 | tf_op jit(solution)/shard_map/ppermute | solution.py:236
  106.5 1.6 %collective-permute-start.16 = (bf16[512,384]{1,0:T(8,128)(2,1)S(1)}, bf16[512,384]{1,0:T(8,128)(2,1)S(1)}, u32[]{:S(2)}, u32[]{:S(2)}) collective-permute-start(bf16[512,384]{1,0:T(8,128)(2,1)S(1)} %shard_map.69.refs_3_), channel_id=1, source_target_pairs={{0,1},{1,0},{2,3},{3,2},{4,5},{5,4},{6,7},{7,6},{8,9},{9,8},{10,11... | collective-permute-start | bytes 1179656 | tf_op jit(solution)/shard_map/ppermute | solution.py:239
  108.1 7.3 %shard_map.70.t_ref = f32[512,2048]{1,0:T(8,128)S(1)} custom-call(s32[24]{0:T(128)S(1)} %concatenate.3.meta_ref, bf16[512,384]{1,0:T(8,128)(2,1)S(1)} %shard_map.66.refs_0_, bf16[512,384]{1,0:T(8,128)(2,1)S(1)} %shard_map.67.refs_1_, bf16[512,384]{1,0:T(8,128)(2,1)S(1)} %shard_map.68.refs_2_, bf16[512,384]{1,0:T(8,128)(2,1)S(1)} %shard_map.69.refs_3_, ...), custom_call_target="tpu_custom_call" | custom-call | flops 3221225472 | bytes 10485760 | tf_op jit(solution)/shard_map/pallas_call | solution.py:166
  115.5 1.9 %copy-done.2 = f32[512,2048]{1,0:T(8,128)} copy-done((f32[512,2048]{1,0:T(8,128)}, f32[512,2048]{1,0:T(8,128)S(1)}, u32[]{:S(2)}) %copy-start.2) | copy-done | bytes 4194328
  117.4 7.9 %shard_map.71.t_ref = f32[512,2048]{1,0:T(8,128)} custom-call(s32[24]{0:T(128)S(1)} %concatenate.3.meta_ref, f32[512,2048]{1,0:T(8,128)} %copy-done.2, bf16[512,384]{1,0:T(8,128)(2,1)S(1)} %collective-permute-done.7.refs_0_, bf16[512,384]{1,0:T(8,128)(2,1)S(1)} %collective-permute-done.8.refs_1_, bf16[512,384]{1,0:T(8,128)(2,1)S(1)} %collective-permute-done.9.refs_2_, ...), custom_call_target="tpu_custom_call" | custom-call | flops 2415919104 | bytes 11010048 | tf_op jit(solution)/shard_map/pallas_call | solution.py:201
  125.4 2.2 %copy-done.3 = f32[512,2048]{1,0:T(8,128)S(1)} copy-done((f32[512,2048]{1,0:T(8,128)S(1)}, f32[512,2048]{1,0:T(8,128)}, u32[]{:S(2)}) %copy-start.3) | copy-done | bytes 4194328
  127.5 3.9 %shard_map.72 = bf16[512,2048]{1,0:T(8,128)(2,1)} custom-call(s32[24]{0:T(128)S(1)} %concatenate.3.meta_ref, f32[512,2048]{1,0:T(8,128)S(1)} %copy-done.3, bf16[512,384]{1,0:T(8,128)(2,1)S(1)} %collective-permute-done.16.refs_0_, bf16[384,1024]{1,0:T(8,128)(2,1)S(1)} %collective-permute-done.17.refs_1_, bf16[384,1024]{1,0:T(8,128)(2,1)S(1)} %collective-permute-done.18.refs_2_), custom_call_target="tpu_custom_call" | custom-call | flops 805306368 | bytes 7864320 | tf_op jit(solution)/shard_map/pallas_call | solution.py:201
  (61 shorter events, 23.3 us)
Async XLA Ops:
  0.0 7.2 %copy-start.9 = (s32[16]{0:T(128)S(1)}, s32[16]{0:T(128)}, u32[]{:S(2)}) copy-start(s32[16]{0:T(128)} %param.9) | copy-start | bytes 196
  6.0 42.8 %copy-start.1 = (bf16[512,1536]{1,0:T(8,128)(2,1)S(1)}, bf16[512,1536]{1,0:T(8,128)(2,1)}, u32[]{:S(2)}) copy-start(bf16[512,1536]{1,0:T(8,128)(2,1)} %q_ref.9) | copy-start | bytes 4718596
  6.0 42.8 %copy-start.5 = (bf16[512,1536]{1,0:T(8,128)(2,1)S(1)}, bf16[512,1536]{1,0:T(8,128)(2,1)}, u32[]{:S(2)}) copy-start(bf16[512,1536]{1,0:T(8,128)(2,1)} %k_ref.3) | copy-start | bytes 4718596
  6.7 5.3 %collective-permute-start = (bf16[2,384,128]{2,1,0:T(8,128)(2,1)}, bf16[2,384,128]{2,1,0:T(8,128)(2,1)}, u32[]{:S(2)}, u32[]{:S(2)}) collective-permute-start(bf16[2,384,128]{2,1,0:T(8,128)(2,1)} %pad_maximum_fusion), channel_id=1, source_target_pairs={{0,2},{2,0},{4,6},{6,4},{8,10},{10,8},{12,14},{14,12},{16,18},{18,... | collective-permute-start | bytes 589832 | tf_op jit(solution)/shard_map/ppermute | solution.py:236
  8.7 36.1 %copy-start.8 = (f32[1536]{0:T(1024)S(1)}, f32[1536]{0:T(1024)}, u32[]{:S(2)}) copy-start(f32[1536]{0:T(1024)} %param.10) | copy-start | bytes 18436
  13.6 6.3 %collective-permute-start.1 = (bf16[1,384,128]{2,1,0:T(8,128)(2,1)}, bf16[1,384,128]{2,1,0:T(8,128)(2,1)}, u32[]{:S(2)}, u32[]{:S(2)}) collective-permute-start(bf16[1,384,128]{2,1,0:T(8,128)(2,1)} %add_convert_fusion.1), channel_id=1, source_target_pairs={{0,4},{2,6},{4,0},{6,2},{8,12},{10,14},{12,8},{14,10},{16,20},{18,... | collective-permute-start | bytes 294920 | tf_op jit(solution)/shard_map/ppermute | solution.py:236
  21.5 23.3 %collective-permute-start.2 = (bf16[384,128]{1,0:T(8,128)(2,1)}, bf16[384,128]{1,0:T(8,128)(2,1)}, u32[]{:S(2)}, u32[]{:S(2)}) collective-permute-start(bf16[384,128]{1,0:T(8,128)(2,1)} %fusion.9), channel_id=1, source_target_pairs={{0,24},{2,26},{4,28},{6,30},{1,25},{3,27},{5,29},{7,31}} | collective-permute-start | bytes 294920 | tf_op jit(solution)/shard_map/ppermute | solution.py:276
  27.9 16.9 %collective-permute-start.3 = (bf16[384,128]{1,0:T(8,128)(2,1)}, bf16[384,128]{1,0:T(8,128)(2,1)}, u32[]{:S(2)}, u32[]{:S(2)}) collective-permute-start(bf16[384,128]{1,0:T(8,128)(2,1)} %fusion.9), channel_id=1, source_target_pairs={{0,16},{2,18},{4,20},{6,22},{8,24},{10,26},{12,28},{14,30},{1,17},... | collective-permute-start | bytes 294920 | tf_op jit(solution)/shard_map/ppermute | solution.py:276
  29.9 15.0 %collective-permute-start.4 = (bf16[384,128]{1,0:T(8,128)(2,1)}, bf16[384,128]{1,0:T(8,128)(2,1)}, u32[]{:S(2)}, u32[]{:S(2)}) collective-permute-start(bf16[384,128]{1,0:T(8,128)(2,1)} %fusion.9), channel_id=1, source_target_pairs={{0,8},{2,10},{4,12},{6,14},{8,16},{10,18},{12,20},{14,22},{16,24},... | collective-permute-start | bytes 294920 | tf_op jit(solution)/shard_map/ppermute | solution.py:276
  35.0 27.7 %collective-permute-start.10 = (bf16[384,1024]{1,0:T(8,128)(2,1)}, bf16[384,1024]{1,0:T(8,128)(2,1)}, u32[]{:S(2)}, u32[]{:S(2)}) collective-permute-start(bf16[384,1024]{1,0:T(8,128)(2,1)} %get-tuple-element.17), channel_id=1, source_target_pairs={{0,1},{1,0},{2,3},{3,2},{4,5},{5,4},{6,7},{7,6},{8,9},{9,8},{10,11... | collective-permute-start | bytes 2359304 | tf_op jit(solution)/shard_map/ppermute | solution.py:239
  36.5 36.1 %collective-permute-start.11 = (bf16[384,1024]{1,0:T(8,128)(2,1)}, bf16[384,1024]{1,0:T(8,128)(2,1)}, u32[]{:S(2)}, u32[]{:S(2)}) collective-permute-start(bf16[384,1024]{1,0:T(8,128)(2,1)} %get-tuple-element.16), channel_id=1, source_target_pairs={{0,1},{1,0},{2,3},{3,2},{4,5},{5,4},{6,7},{7,6},{8,9},{9,8},{10,11... | collective-permute-start | bytes 2359304 | tf_op jit(solution)/shard_map/ppermute | solution.py:239
  47.2 9.7 %collective-permute-start.5 = (bf16[1,384,128]{2,1,0:T(8,128)(2,1)S(1)}, bf16[1,384,128]{2,1,0:T(8,128)(2,1)S(1)}, u32[]{:S(2)}, u32[]{:S(2)}) collective-permute-start(bf16[1,384,128]{2,1,0:T(8,128)(2,1)S(1)} %fusion.8), channel_id=1, source_target_pairs={{0,4},{2,6},{4,0},{6,2},{8,12},{10,14},{12,8},{14,10},{16,20},{18,... | collective-permute-start | bytes 294920 | tf_op jit(solution)/shard_map/ppermute | solution.py:236
  61.1 18.0 %collective-permute-start.8 = (bf16[512,384]{1,0:T(8,128)(2,1)S(1)}, bf16[512,384]{1,0:T(8,128)(2,1)S(1)}, u32[]{:S(2)}, u32[]{:S(2)}) collective-permute-start(bf16[512,384]{1,0:T(8,128)(2,1)S(1)} %shard_map.68.refs_2_), channel_id=1, source_target_pairs={{0,1},{1,0},{2,3},{3,2},{4,5},{5,4},{6,7},{7,6},{8,9},{9,8},{10,11... | collective-permute-start | bytes 1179656 | tf_op jit(solution)/shard_map/ppermute | solution.py:239
  72.6 20.7 %collective-permute-start.12 = (bf16[384,1024]{1,0:T(8,128)(2,1)}, bf16[384,1024]{1,0:T(8,128)(2,1)S(1)}, u32[]{:S(2)}, u32[]{:S(2)}) collective-permute-start(bf16[384,1024]{1,0:T(8,128)(2,1)} %collective-permute-done.10.refs_3_), channel_id=1, source_target_pairs={{0,4},{2,6},{4,0},{6,2},{8,12},{10,14},{12,8},{14,10},{16,20},{18,... | collective-permute-start | bytes 2359304 | tf_op jit(solution)/shard_map/ppermute | solution.py:236
  74.1 31.4 %collective-permute-start.13 = (bf16[384,1024]{1,0:T(8,128)(2,1)}, bf16[384,1024]{1,0:T(8,128)(2,1)S(1)}, u32[]{:S(2)}, u32[]{:S(2)}) collective-permute-start(bf16[384,1024]{1,0:T(8,128)(2,1)} %collective-permute-done.11.refs_4_), channel_id=1, source_target_pairs={{0,4},{2,6},{4,0},{6,2},{8,12},{10,14},{12,8},{14,10},{16,20},{18,... | collective-permute-start | bytes 2359304 | tf_op jit(solution)/shard_map/ppermute | solution.py:236
  75.6 2.7 %collective-permute-start.6 = (bf16[2,384,128]{2,1,0:T(8,128)(2,1)S(1)}, bf16[2,384,128]{2,1,0:T(8,128)(2,1)S(1)}, u32[]{:S(2)}, u32[]{:S(2)}) collective-permute-start(bf16[2,384,128]{2,1,0:T(8,128)(2,1)S(1)} %pad_maximum_fusion.1), channel_id=1, source_target_pairs={{0,2},{2,0},{4,6},{6,4},{8,10},{10,8},{12,14},{14,12},{16,18},{18,... | collective-permute-start | bytes 589832 | tf_op jit(solution)/shard_map/ppermute | solution.py:236
  76.7 11.6 %collective-permute-start.7 = (bf16[512,384]{1,0:T(8,128)(2,1)S(1)}, bf16[512,384]{1,0:T(8,128)(2,1)S(1)}, u32[]{:S(2)}, u32[]{:S(2)}) collective-permute-start(bf16[512,384]{1,0:T(8,128)(2,1)S(1)} %shard_map.66.refs_0_), channel_id=1, source_target_pairs={{0,1},{1,0},{2,3},{3,2},{4,5},{5,4},{6,7},{7,6},{8,9},{9,8},{10,11... | collective-permute-start | bytes 1179656 | tf_op jit(solution)/shard_map/ppermute | solution.py:239
  78.3 39.1 %collective-permute-start.14 = (bf16[384,1024]{1,0:T(8,128)(2,1)}, bf16[384,1024]{1,0:T(8,128)(2,1)S(1)}, u32[]{:S(2)}, u32[]{:S(2)}) collective-permute-start(bf16[384,1024]{1,0:T(8,128)(2,1)} %collective-permute-done.10.refs_3_), channel_id=1, source_target_pairs={{0,2},{2,0},{4,6},{6,4},{8,10},{10,8},{12,14},{14,12},{16,18},{18,... | collective-permute-start | bytes 2359304 | tf_op jit(solution)/shard_map/ppermute | solution.py:236
  79.1 38.4 %collective-permute-start.15 = (bf16[384,1024]{1,0:T(8,128)(2,1)}, bf16[384,1024]{1,0:T(8,128)(2,1)S(1)}, u32[]{:S(2)}, u32[]{:S(2)}) collective-permute-start(bf16[384,1024]{1,0:T(8,128)(2,1)} %collective-permute-done.11.refs_4_), channel_id=1, source_target_pairs={{0,2},{2,0},{4,6},{6,4},{8,10},{10,8},{12,14},{14,12},{16,18},{18,... | collective-permute-start | bytes 2359304 | tf_op jit(solution)/shard_map/ppermute | solution.py:236
  88.3 18.2 %collective-permute-start.9 = (bf16[512,384]{1,0:T(8,128)(2,1)S(1)}, bf16[512,384]{1,0:T(8,128)(2,1)S(1)}, u32[]{:S(2)}, u32[]{:S(2)}) collective-permute-start(bf16[512,384]{1,0:T(8,128)(2,1)S(1)} %shard_map.67.refs_1_), channel_id=1, source_target_pairs={{0,1},{1,0},{2,3},{3,2},{4,5},{5,4},{6,7},{7,6},{8,9},{9,8},{10,11... | collective-permute-start | bytes 1179656 | tf_op jit(solution)/shard_map/ppermute | solution.py:239
  93.3 32.0 %collective-permute-start.17 = (bf16[384,1024]{1,0:T(8,128)(2,1)S(1)}, bf16[384,1024]{1,0:T(8,128)(2,1)S(1)}, u32[]{:S(2)}, u32[]{:S(2)}) collective-permute-start(bf16[384,1024]{1,0:T(8,128)(2,1)S(1)} %collective-permute-done.12.refs_5_), channel_id=1, source_target_pairs={{0,2},{2,0},{4,6},{6,4},{8,10},{10,8},{12,14},{14,12},{16,18},{18,... | collective-permute-start | bytes 2359304 | tf_op jit(solution)/shard_map/ppermute | solution.py:236
  105.5 19.8 %collective-permute-start.18 = (bf16[384,1024]{1,0:T(8,128)(2,1)S(1)}, bf16[384,1024]{1,0:T(8,128)(2,1)S(1)}, u32[]{:S(2)}, u32[]{:S(2)}) collective-permute-start(bf16[384,1024]{1,0:T(8,128)(2,1)S(1)} %collective-permute-done.13.refs_6_), channel_id=1, source_target_pairs={{0,2},{2,0},{4,6},{6,4},{8,10},{10,8},{12,14},{14,12},{16,18},{18,... | collective-permute-start | bytes 2359304 | tf_op jit(solution)/shard_map/ppermute | solution.py:236
  106.5 18.8 %collective-permute-start.16 = (bf16[512,384]{1,0:T(8,128)(2,1)S(1)}, bf16[512,384]{1,0:T(8,128)(2,1)S(1)}, u32[]{:S(2)}, u32[]{:S(2)}) collective-permute-start(bf16[512,384]{1,0:T(8,128)(2,1)S(1)} %shard_map.69.refs_3_), channel_id=1, source_target_pairs={{0,1},{1,0},{2,3},{3,2},{4,5},{5,4},{6,7},{7,6},{8,9},{9,8},{10,11... | collective-permute-start | bytes 1179656 | tf_op jit(solution)/shard_map/ppermute | solution.py:239
  125.4 2.2 %copy-start.3 = (f32[512,2048]{1,0:T(8,128)S(1)}, f32[512,2048]{1,0:T(8,128)}, u32[]{:S(2)}) copy-start(f32[512,2048]{1,0:T(8,128)} %shard_map.71.t_ref) | copy-start | bytes 12582916
  (5 other events, 8.1 us)

commit v2 on v1

--- a/solution.py
+++ b/solution.py
@@ -11,7 +11,7 @@
 PLANES = 4
 F32, BF16 = jnp.float32, jnp.bfloat16
 LENS = 8
-VMEM_LIMIT = 48 * 1024 * 1024
+VMEM_LIMIT = 60 * 1024 * 1024
 
 
 def doc_start(meta, doc_count, token):
@@ -114,8 +114,192 @@
     )(meta, query, key, value)
 
 
-def norm_heads(meta, query, within, carry, gain, doc_count, slot):
+def whole(shape):
+    return pl.BlockSpec(shape, lambda *_: (0,) * len(shape))
+
+
+def after(meta, *arrays):
+    return lax.optimization_barrier((meta, *arrays))[0]
+
+
+def factor(condition):
+    return jnp.where(condition, 1.0, 0.0)
+
+
+def split_states(meta, key, value, doc_count):
+    rows, width = key.shape
+    part = width // 4
+
+    def slot(g):
+        return jnp.where(g < 2, 2 * g + 1, 2 * g - 4)
+
+    def kernel(meta_ref, k_ref, v_ref, send_ref, keep_ref):
+        offset = meta_ref[0] * rows
+        first = doc_start(meta_ref, doc_count, offset + rows - 1) - offset
+        live = lax.broadcasted_iota(jnp.int32, (rows, DH), 0) >= first
+        for h in range(part // DH):
+            cols = slice(h * DH, (h + 1) * DH)
+            k = jnp.where(live, k_ref[:, cols], jnp.zeros((), BF16))
+            s = lax.dot_general(k, v_ref[:, cols], (((0,), (0,)), ((), ())), preferred_element_type=F32)
+            s = s.astype(BF16)
+
+            @pl.when(pl.program_id(0) < 2)
+            def _():
+                send_ref[0, cols, :] = s
+
+            @pl.when(pl.program_id(0) >= 2)
+            def _():
+                keep_ref[0, cols, :] = s
+
+    return call(
+        kernel,
+        (4,),
+        [pl.BlockSpec((rows, part), lambda g, m: (0, slot(g) ^ m[1]))] * 2,
+        [
+            pl.BlockSpec((1, part, DH), lambda g, m: (jnp.minimum(g, 1), 0, 0)),
+            pl.BlockSpec((1, part, DH), lambda g, m: (jnp.maximum(g - 2, 0), 0, 0)),
+        ],
+        [jax.ShapeDtypeStruct((2, part, DH), BF16)] * 2,
+        2 * rows * width * DH,
+        2 * 2 * rows * width,
+    )(meta, key, value)
+
+
+def within_slots(meta, query, key, value, doc_count, slots, dtype, with_query):
     rows, width = query.shape
+    part = width // 4
+    tile = rows // 2
+
+    def kernel(meta_ref, q_ref, k_ref, v_ref, o_ref, *rest):
+        mask_ref = rest[-1]
+
+        @pl.when(pl.program_id(0) == 0)
+        def _():
+            offset = meta_ref[0] * rows
+            t = lax.broadcasted_iota(jnp.int32, (rows, rows), 0)
+            s = lax.broadcasted_iota(jnp.int32, (rows, rows), 1)
+            pos = lax.broadcasted_iota(jnp.int32, (rows, 1), 0)
+            first = jnp.zeros((rows, 1), jnp.int32)
+            bound = -offset
+            for d in range(doc_count):
+                bound = bound + meta_ref[LENS + d]
+                first = jnp.where(bound <= pos, bound, first)
+            mask_ref[...] = jnp.where((s <= t) & (s >= first), 1.0, 0.0).astype(BF16)
+
+        for h in range(part // DH):
+            cols = slice(h * DH, (h + 1) * DH)
+            for i in range(2):
+                r = slice(i * tile, (i + 1) * tile)
+                seen = (i + 1) * tile
+                scores = lax.dot_general(
+                    q_ref[r, cols], k_ref[:seen, cols], (((1,), (1,)), ((), ())), preferred_element_type=F32
+                )
+                scores = scores.astype(BF16) * mask_ref[r, :seen]
+                o_ref[r, cols] = jnp.dot(scores, v_ref[:seen, cols], preferred_element_type=F32).astype(dtype)
+        if with_query:
+            rest[0][...] = q_ref[...]
+
+    count = len(slots)
+    spec = pl.BlockSpec((rows, part), lambda g, m: (0, (g + slots[0]) ^ m[1]))
+    out = pl.BlockSpec((rows, part), lambda g, m: (0, g))
+    shape = (rows, part * count)
+    return call(
+        kernel,
+        (count,),
+        [spec] * 3,
+        [out] * (1 + with_query),
+        [jax.ShapeDtypeStruct(shape, dtype)] + [jax.ShapeDtypeStruct(shape, BF16)] * with_query,
+        3 * rows * rows * part * count,
+        10 * rows * part * count,
+        [pltpu.VMEM((rows, rows), BF16)],
+    )(meta, query, key, value)
+
+
+def small(kernel, meta, arrays, shape, count):
+    return call(
+        kernel,
+        (1,),
+        [whole(a.shape) for a in arrays],
+        [whole(shape)] * count,
+        [jax.ShapeDtypeStruct(shape, BF16)] * count,
+        shape[0] * shape[1],
+        2 * shape[0] * shape[1] * (len(arrays) + count),
+    )(meta, *arrays)
+
+
+def join_core(meta, keep, got, rows, doc_count):
+    def kernel(meta_ref, keep_ref, got_ref, a_ref, b_ref):
+        low = meta_ref[0] & -2
+        joined = factor(doc_start(meta_ref, doc_count, (low + 2) * rows - 1) < (low + 1) * rows)
+        upper = (meta_ref[1] & 1) != 0
+        own, other = jnp.where(upper, 1.0, joined), jnp.where(upper, joined, 1.0)
+        for i, o_ref in enumerate((a_ref, b_ref)):
+            o_ref[...] = (own * keep_ref[i].astype(F32) + other * got_ref[i].astype(F32)).astype(BF16)
+
+    return small(kernel, meta, (keep, got), keep.shape[1:], 2)
+
+
+def join_chips(meta, mine, got, rows, doc_count):
+    def kernel(meta_ref, a_ref, b_ref, o_ref):
+        low = meta_ref[0] & -4
+        joined = factor(doc_start(meta_ref, doc_count, (low + 4) * rows - 1) < (low + 2) * rows)
+        upper = (meta_ref[1] & 2) != 0
+        own, other = jnp.where(upper, 1.0, joined), jnp.where(upper, joined, 1.0)
+        o_ref[...] = (own * a_ref[...].astype(F32) + other * b_ref[...].astype(F32)).astype(BF16)
+
+    return small(kernel, meta, (mine, got), mine.shape, 1)[0]
+
+
+def join_planes(meta, plane_sum, previous, rows, doc_count):
+    def kernel(meta_ref, a_ref, b_ref, o_ref):
+        low = meta_ref[0] & -4
+        joined = factor(doc_start(meta_ref, doc_count, (low + 4) * rows - 1) < low * rows)
+        o_ref[...] = (a_ref[...].astype(F32) + joined * b_ref[...].astype(F32)).astype(BF16)
+
+    return small(kernel, meta, (plane_sum, previous), plane_sum.shape, 1)[0]
+
+
+def carry_in_chip(meta_ref, chip, keep, got, rows, doc_count):
+    low = meta_ref[0] & -2
+    begins = doc_start(meta_ref, doc_count, (low + 1) * rows)
+    through, joined = factor(begins < low * rows), factor(begins < (low + 1) * rows)
+    upper = (meta_ref[1] & 1) != 0
+    later = through * chip + joined * jnp.where(upper, got, keep).astype(F32)
+    return jnp.where(upper, later, chip), jnp.where(upper, chip, later)
+
+
+def carry_first(meta, near, far, mine, got, keep, core_got, rows, doc_count):
+    def kernel(meta_ref, near_ref, far_ref, a_ref, b_ref, keep_ref, got_ref, o_ref, core_ref, chip_ref):
+        low = meta_ref[0] & -4
+        begins = doc_start(meta_ref, doc_count, low * rows)
+        first = factor(begins < low * rows) * near_ref[...].astype(F32)
+        first = first + factor(begins < (low - 4) * rows) * far_ref[...].astype(F32)
+        begins = doc_start(meta_ref, doc_count, (low + 2) * rows)
+        through, joined = factor(begins < low * rows), factor(begins < (low + 2) * rows)
+        upper = (meta_ref[1] & 2) != 0
+        later = through * first + joined * jnp.where(upper, b_ref[...], a_ref[...]).astype(F32)
+        chip_ref[...] = jnp.where(upper, first, later).astype(BF16)
+        chip = jnp.where(upper, later, first)
+        ours, theirs = carry_in_chip(meta_ref, chip, keep_ref[0], got_ref[0], rows, doc_count)
+        o_ref[...] = ours.astype(BF16)
+        core_ref[...] = theirs.astype(BF16)
+
+    return small(kernel, meta, (near, far, mine, got, keep, core_got), mine.shape, 3)
+
+
+def carry_second(meta, chip, keep, core_got, rows, doc_count):
+    def kernel(meta_ref, chip_ref, keep_ref, got_ref, o_ref, core_ref):
+        ours, theirs = carry_in_chip(
+            meta_ref, chip_ref[...].astype(F32), keep_ref[1], got_ref[1], rows, doc_count
+        )
+        o_ref[...] = ours.astype(BF16)
+        core_ref[...] = theirs.astype(BF16)
+
+    return small(kernel, meta, (chip, keep, core_got), chip.shape, 2)
+
+
+def norm_heads(meta, query, within, carry, gain, doc_count, slots=(None, None, None)):
+    rows = query.shape[0]
     part = carry.shape[0]
 
     def kernel(meta_ref, q_ref, w_ref, c_ref, g_ref, o_ref):
@@ -132,42 +316,52 @@
         for h in range(part // DH):
             cols = slice(h * DH, (h + 1) * DH)
             term = jnp.dot(q_ref[:, cols], c_ref[cols, :], preferred_element_type=F32)
-            mixture = w_ref[:, cols] + jnp.where(cross, term, 0.0)
+            mixture = w_ref[:, cols].astype(F32) + jnp.where(cross, term, 0.0)
             mean = jnp.mean(mixture * mixture, axis=-1, keepdims=True)
             o_ref[:, cols] = (mixture * lax.rsqrt(mean + 1e-06) * g_ref[:, cols]).astype(BF16)
 
-    def block(i, m):
-        return (0, 0) if slot is None else (0, m[1] ^ slot)
-
-    spec = pl.BlockSpec((rows, part), block)
+    def block(place):
+        if place is None:
+            return lambda i, m: (0, 0)
+        if isinstance(place, int):
+            return lambda i, m: (0, place)
+        return lambda i, m: (0, m[1] ^ place[1])
+
     return call(
         kernel,
         (1,),
-        [spec, spec, pl.BlockSpec((part, DH), lambda i, m: (0, 0)), pl.BlockSpec((1, part), block)],
-        pl.BlockSpec((rows, part), lambda i, m: (0, 0)),
+        [
+            pl.BlockSpec((rows, part), block(slots[0])),
+            pl.BlockSpec((rows, part), block(slots[1])),
+            whole((part, DH)),
+            pl.BlockSpec((1, part), block(slots[2])),
+        ],
+        whole((rows, part)),
         jax.ShapeDtypeStruct((rows, part), BF16),
         2 * rows * part * DH,
         8 * rows * part,
-    )(meta, query, within, carry, gain.reshape(1, width))
+    )(meta, query, within, carry, gain.reshape(1, -1))
+
+
+TILES = 4
 
 
 def project_own(meta, pieces, weight, columns):
     rows, part = pieces[0].shape
-    tile = columns // 4
+    tile = columns // TILES
     count = len(pieces)
 
     def kernel(meta_ref, *refs):
         ns, ws, o_ref = refs[:count], refs[count : 2 * count], refs[-1]
-        total = jnp.dot(ns[0][...], ws[0][...], preferred_element_type=F32)
-        for n, w in zip(ns[1:], ws[1:]):
-            total = total + jnp.dot(n[...], w[...], preferred_element_type=F32)
-        o_ref[...] = total
-
-    return call(
-        kernel,
-        (4,),
-        [pl.BlockSpec((rows, part), lambda n, m: (0, 0))] * count
-        + [pl.BlockSpec((part, tile), lambda n, m, s=s: (m[1] ^ s, m[2] * 4 + n)) for s in range(count)],
+        n = jnp.concatenate([r[...] for r in ns], axis=1)
+        w = jnp.concatenate([r[...] for r in ws], axis=0)
+        o_ref[...] = jnp.dot(n, w, preferred_element_type=F32)
+
+    return call(
+        kernel,
+        (TILES,),
+        [whole((rows, part))] * count
+        + [pl.BlockSpec((part, tile), lambda n, m, s=s: (m[1] ^ s, m[2] * TILES + n)) for s in range(count)],
         pl.BlockSpec((rows, tile), lambda n, m: (0, n)),
         jax.ShapeDtypeStruct((rows, columns), F32),
         2 * rows * part * count * columns,
@@ -178,44 +372,135 @@
 def project_more(meta, total, pieces, weights, dtype):
     rows, columns = total.shape
     part = pieces[0].shape[1]
-    count, ranges = len(pieces), len(weights[0])
-    steps = 2
-    tile = columns // (ranges * steps)
-    flat = [w for ws in weights for w in ws]
+    tile = columns // TILES
+    count = len(pieces)
+    flat = []
+    for ws in weights:
+        start = 0
+        for w in ws:
+            tiles = w.shape[1] // tile
+            flat.append((w, start, tiles))
+            start += tiles
 
     def kernel(meta_ref, t_ref, *refs):
         ns, ws, o_ref = refs[:count], refs[count:-1], refs[-1]
-        for c in range(ranges):
+        n = jnp.concatenate([r[...] for r in ns], axis=1)
+        for c in range(TILES):
 
             @pl.when(pl.program_id(0) == c)
             def _():
-                out = t_ref[...]
-                for s in range(count):
-                    out = out + jnp.dot(ns[s][...], ws[s * ranges + c][...], preferred_element_type=F32)
-                o_ref[...] = out.astype(dtype)
-
-    def column(c):
-        return lambda g, n, m: (0, jnp.where(g < c, 0, jnp.where(g > c, steps - 1, n)))
-
-    out_spec = pl.BlockSpec((rows, tile), lambda g, n, m: (0, g * steps + n))
-    return call(
-        kernel,
-        (ranges, steps),
+                held = [r[...] for r, (_, start, tiles) in zip(ws, flat) if start <= c < start + tiles]
+                w = jnp.concatenate(held, axis=0)
+                o_ref[...] = (t_ref[...] + jnp.dot(n, w, preferred_element_type=F32)).astype(dtype)
+
+    def column(start, tiles):
+        return lambda n, m: (0, jnp.clip(n - start, 0, tiles - 1))
+
+    out_spec = pl.BlockSpec((rows, tile), lambda n, m: (0, n ^ (m[3] * (TILES // 2))))
+    return call(
+        kernel,
+        (TILES,),
         [out_spec]
-        + [pl.BlockSpec((rows, part), lambda g, n, m: (0, 0))] * count
-        + [pl.BlockSpec((part, tile), column(c)) for _ in range(count) for c in range(ranges)],
+        + [whole((rows, part))] * count
+        + [pl.BlockSpec((part, tile), column(start, tiles)) for _, start, tiles in flat],
         out_spec,
         jax.ShapeDtypeStruct((rows, columns), dtype),
         2 * rows * part * count * columns,
         2 * part * count * columns + 6 * rows * columns,
-    )(meta, total, *pieces, *flat)
+    )(meta, total, *pieces, *[w for w, _, _ in flat])
+
+
+def pair_body(n_seq, query, key, value, doc_lengths, gain, weight):
+    rows, width = query.shape
+    docs = doc_lengths.shape[0]
+    plane, part = 4, width // 4
+    columns = weight.shape[1] // 2
+    half = columns // 2
+    block = lax.axis_index("seq").astype(jnp.int32)
+    group = lax.axis_index("head").astype(jnp.int32)
+    member = block % plane
+    side = (block // plane) % 2
+    meta = jnp.concatenate([
+        jnp.stack([block, member, group, side]), jnp.zeros((LENS - 4,), jnp.int32), doc_lengths
+    ])
+
+    def swap(x, bit):
+        return lax.ppermute(x, "seq", [(i, i ^ bit) for i in range(n_seq)])
+
+    def shift(x, count):
+        return lax.ppermute(x, "seq", [(i, i + count) for i in range(n_seq - count)])
+
+    def flip(x):
+        return lax.ppermute(x, "head", [(0, 1), (1, 0)])
+
+    def behind(x, *arrays):
+        return lax.optimization_barrier((x, *arrays))[0]
+
+    sent_weight = lax.dynamic_slice(
+        weight, (member * part, (1 - group) * columns + side * half), (part, half)
+    )
+    far_gain = flip(lax.dynamic_slice(gain, ((member ^ 3) * part,), (part,)))
+    w0 = [flip(sent_weight), None]
+
+    send, keep = split_states(after(meta, sent_weight), key, value, docs)
+    core_got = swap(send, 1)
+    within3, query3 = within_slots(after(meta, send), query, key, value, docs, (3,), BF16, True)
+    far_query, far_within = flip(query3), flip(within3)
+    chip0, chip2 = join_core(after(meta, within3), keep, core_got, rows, docs)
+    chip_got = swap(chip2, 2)
+    (within,) = within_slots(after(meta, chip0), query, key, value, docs, (0, 1, 2), F32, False)
+    plane_sum = join_chips(after(meta, within), chip0, chip_got, rows, docs)
+    near = shift(plane_sum, plane)
+    both = join_planes(after(meta, w0[0]), plane_sum, near, rows, docs)
+    far = shift(both, 2 * plane)
+    carry0, core_carry0, chip_carry = carry_first(
+        meta, near, far, chip0, chip_got, keep, core_got, rows, docs
+    )
+    carry1 = swap(core_carry0, 1)
+    chip_carry2 = swap(chip_carry, 2)
+
+    def norm(slot, carry):
+        return norm_heads(
+            meta,
+            query,
+            within3 if slot == 3 else within,
+            carry,
+            gain,
+            docs,
+            (("slot", slot), None if slot == 3 else slot, ("slot", slot)),
+        )
+
+    normed0 = norm(0, carry0)
+    far0 = flip(normed0)
+    normed1 = norm(1, carry1)
+    far1 = flip(normed1)
+    carry2, core_carry2 = carry_second(meta, chip_carry2, keep, core_got, rows, docs)
+    carry3 = swap(core_carry2, 1)
+    far_carry3 = flip(carry3)
+    normed2 = norm(2, carry2)
+    far2 = flip(behind(normed2, carry3))
+    normed3 = norm(3, carry3)
+
+    w0[1] = swap(behind(w0[0], far), plane)
+    quarter = half // 2
+    w2 = [swap(w0[0], 2)]
+    w2.append(swap(w0[1][:, :quarter], 2))
+    w2.append(swap(w2[0][:, quarter:], plane))
+    w1 = [swap(w, 1) for w in w0]
+    w3 = [swap(w, 1) for w in w2]
+
+    total = project_own(meta, [normed0, normed1, normed2, normed3], weight, columns)
+    total = project_more(meta, total, [far0, far1], [w0, w1], F32)
+    far3 = norm_heads(meta, far_query, far_within, far_carry3, far_gain, docs)
+    return project_more(meta, total, [far2, far3], [w2, w3], BF16)
 
 
 def body(n_seq, n_head, query, key, value, doc_lengths, gain, weight):
     rows, width = query.shape
     doc_count = doc_lengths.shape[0]
     plane = n_seq // PLANES
-    columns = weight.shape[1] // n_head
+    if n_head == 2 and plane == 4 and width % (4 * DH) == 0:
+        return pair_body(n_seq, query, key, value, doc_lengths, gain, weight)
     block = lax.axis_index("seq").astype(jnp.int32)
     group = lax.axis_index("head").astype(jnp.int32)
     member = block % plane
@@ -235,22 +520,12 @@
     def swap(x, bit):
         return lax.ppermute(x, "seq", [(i, i ^ bit) for i in range(n_seq)])
 
-    def flip(x):
-        return lax.ppermute(x, "head", [(0, 1), (1, 0)])
-
     by_slot = (width // DH) % plane == 0
     steps = plane if by_slot else 1
     states = block_states(meta, key, value, doc_count, steps)
     if not by_slot:
         states = states.reshape(plane, width // plane, DH)[jnp.arange(plane, dtype=jnp.int32) ^ member]
     slots = [states[s] for s in range(plane)]
-
-    pair = n_head == 2 and by_slot and plane == 4
-    part = width // plane
-    if pair:
-        far_weight = lax.dynamic_slice(weight, (member * part, (1 - group) * columns), (part, columns))
-        half = columns // 2
-        w0 = [flip(far_weight[:, c * half : (c + 1) * half]) for c in range(2)]
 
     kept = []
     bit = 1
@@ -292,23 +567,10 @@
     carries = [c.astype(BF16) for c in carries]
 
     within = within_block(meta, query, key, value, doc_count)
-    if not pair:
-        natural = jnp.stack(carries)[jnp.arange(plane, dtype=jnp.int32) ^ member].reshape(width, DH)
-        normed = norm_heads(meta, query, within, natural, gain, doc_count, None)
-        partial_sum = jnp.dot(normed, weight, preferred_element_type=F32)
-        return lax.psum_scatter(partial_sum.astype(BF16), "head", scatter_dimension=1, tiled=True)
-
-    order = (0, 2, 1, 3)
-    normed = {s: norm_heads(meta, query, within, carries[s], gain, doc_count, s) for s in order}
-    far = {s: flip(normed[s]) for s in order}
-    w0 = list(lax.optimization_barrier((*w0, carries[2])))[:2]
-    w2 = [swap(w, 2) for w in w0]
-    w1 = [swap(w, 1) for w in w0]
-    w3 = [swap(w, 1) for w in w2]
-    weights = {0: w0, 1: w1, 2: w2, 3: w3}
-    total = project_own(meta, [normed[s] for s in range(plane)], weight, columns)
-    total = project_more(meta, total, [far[s] for s in order[:3]], [weights[s] for s in order[:3]], F32)
-    return project_more(meta, total, [far[3]], [weights[3]], BF16)
+    natural = jnp.stack(carries)[jnp.arange(plane, dtype=jnp.int32) ^ member].reshape(width, DH)
+    normed = norm_heads(meta, query, within, natural, gain, doc_count)
+    partial_sum = jnp.dot(normed, weight, preferred_element_type=F32)
+    return lax.psum_scatter(partial_sum.astype(BF16), "head", scatter_dimension=1, tiled=True)
 
 
 def solution(mesh):

time: 132 us -> 143 us (1.083)
  Pallas kernels: 32.2 us -> 68.6 us
  between operations: 13.1 us -> 0.15 us
  other arithmetic: 10.2 us -> 0 us
  local copies, waits for them, and re-layouts: 14.4 us -> 8.9 us
  waiting for transfers between devices: 35.6 us -> 39.8 us
    pallas_call x9 -> x16, Pallas kernels: 32.2 us -> 68.6 us  [the longest x5 15.5 us: norm_heads(): call(kernel, (1,), [pl.BlockSpec((rows, part), block(slots[0])), pl.Block...]
    ppermute x10 -> x14, waiting for transfers between devices: 16.9 us -> 6.79 us  [swap(): return lax.ppermute(x, 'seq', [(i, i ^ bit) for i in range(n_seq)])]
    ppermute x6 -> x8, waiting for transfers between devices: 18.7 us -> 28.4 us  [flip(): return lax.ppermute(x, 'head', [(0, 1), (1, 0)])]
    unnamed x20 -> x38, local copies, waits for them, and re-layouts: 10.3 us -> 3.59 us
    convert_element_type x4 -> x0, other arithmetic: 5.5 us -> none  [the longest x2 3.24 us: body(): (own_factor * a.astype(F32) + got_factor * b.astype(F32)).astype(BF16)]
    ppermute x3 -> x2, waiting for transfers between devices: 0.01 us -> 4.63 us  [shift(): lax.ppermute(x, 'seq', [(i, i + count) for i in range(n_seq - count)])]
    another operation x6 -> x0, other arithmetic: 3.87 us -> none  [the longest x3 2.33 us: body(): back = swap(jnp.stack(theirs), bit)]
    ppermute x3 -> x2, starting transfers between devices: 10.8 us -> 8.76 us  [shift(): lax.ppermute(x, 'seq', [(i, i + count) for i in range(n_seq - count)])]
  transfers between devices with their start and end apart: 19 -> 24, of which waited for: 6 -> 7; matrix products, arithmetic and copies ran while one was open for 7% -> 3% of each run, Pallas kernels for 20% -> 42%
where the time goes in v2:
time: 143 us; the launch traced here: 142 us
  Pallas kernels  68.6 us (48%)
  waiting for transfers between devices  39.8 us (28%)
  starting transfers between devices  24.7 us (17%)
  local copies, waits for them, and re-layouts  8.9 us (6%)
    ppermute x8, waiting for transfers between devices, flip(): return lax.ppermute(x, 'head', [(0, 1), (1, 0)])  28.4 us
    pallas_call x5, Pallas kernels, norm_heads(): call(kernel, (1,), [pl.BlockSpec((rows, part), block(slots[0])), pl.Block...  15.5 us
    pallas_call x2, Pallas kernels, project_more(): call(kernel, (TILES,), [out_spec] + [whole((rows, part))] * count + [pl.B...  15.1 us
    pallas_call x5, Pallas kernels, small(): call(kernel, (1,), [whole(a.shape) for a in arrays], [whole(shape)] * cou...  12.1 us
    pallas_call x2, Pallas kernels, within_slots(): call(kernel, (count,), [spec] * 3, [out] * (1 + with_query), [jax.ShapeDt...  11.3 us
    ppermute x2, starting transfers between devices, shift(): lax.ppermute(x, 'seq', [(i, i + count) for i in range(n_seq - count)])  8.76 us
    ppermute x8, starting transfers between devices, flip(): return lax.ppermute(x, 'head', [(0, 1), (1, 0)])  8.71 us
    pallas_call x1, Pallas kernels, project_own(): call(kernel, (TILES,), [whole((rows, part))] * count + [pl.BlockSpec((par...  8.56 us
  transfers between devices with their start and end apart: 24, of which 7 were waited for; matrix products, arithmetic and copies ran while one was open for 3% of the time, Pallas kernels for 42%

profile of v2, /device:TPU:0, one launch (start us, length us, event | category | flops | bytes accessed | tf_op | source)
XLA Modules:
  0.0 142.1 jit_solution(10177615770659020094)
XLA Ops:
  1.2 3.0 %collective-permute-start.3 = (bf16[384,1024]{1,0:T(8,128)(2,1)S(1)}, bf16[384,1024]{1,0:T(8,128)(2,1)S(1)}, u32[]{:S(2)}, u32[]{:S(2)}) collective-permute-start(bf16[384,1024]{1,0:T(8,128)(2,1)S(1)} %dynamic_slice.6), channel_id=1, source_target_pairs={{0,1},{1,0},{2,3},{3,2},{4,5},{5,4},{6,7},{7,6},{8,9},{9,8},{10,11... | collective-permute-start | bytes 2359304 | tf_op jit(solution)/shard_map/ppermute | solution.py:434
  5.5 6.0 %shard_map.64 = (bf16[2,384,128]{2,1,0:T(8,128)(2,1)}, bf16[2,384,128]{2,1,0:T(8,128)(2,1)}) custom-call(s32[24]{0:T(128)} %concatenate.3.meta_ref, bf16[512,1536]{1,0:T(8,128)(2,1)} %k_ref.5, bf16[512,1536]{1,0:T(8,128)(2,1)} %v_ref.5), custom_call_target="tpu_custom_call" | custom-call | flops 201326592 | bytes 3145728 | tf_op jit(solution)/shard_map/pallas_call | solution.py:154
  11.4 4.0 %shard_map.65 = (bf16[512,384]{1,0:T(8,128)(2,1)}, bf16[512,384]{1,0:T(8,128)(2,1)}) custom-call(s32[24]{0:T(128)} %concatenate.3.meta_ref, bf16[512,1536]{1,0:T(8,128)(2,1)} %q_ref.11, bf16[512,1536]{1,0:T(8,128)(2,1)} %k_ref.5, bf16[512,1536]{1,0:T(8,128)(2,1)} %v_ref.5), custom_call_target="tpu_custom_call" | custom-call | flops 301989888 | bytes 1966080 | tf_op jit(solution)/shard_map/pallas_call | solution.py:206
  16.1 2.4 %shard_map.66 = (bf16[384,128]{1,0:T(8,128)(2,1)}, bf16[384,128]{1,0:T(8,128)(2,1)}) custom-call(s32[24]{0:T(128)} %concatenate.3.meta_ref, bf16[2,384,128]{2,1,0:T(8,128)(2,1)} %get-tuple-element.29.keep_ref, bf16[2,384,128]{2,1,0:T(8,128)(2,1)} %copy-done.2), custom_call_target="tpu_custom_call" | custom-call | flops 49152 | bytes 393216 | tf_op jit(solution)/shard_map/pallas_call | solution.py:219
  20.1 7.2 %shard_map.67.w_ref = f32[512,1152]{1,0:T(8,128)} custom-call(s32[24]{0:T(128)} %concatenate.3.meta_ref, bf16[512,1536]{1,0:T(8,128)(2,1)} %q_ref.11, bf16[512,1536]{1,0:T(8,128)(2,1)} %k_ref.5, bf16[512,1536]{1,0:T(8,128)(2,1)} %v_ref.5), custom_call_target="tpu_custom_call" | custom-call | flops 905969664 | bytes 5898240 | tf_op jit(solution)/shard_map/pallas_call | solution.py:206
  27.9 2.3 %shard_map.68.a_ref = bf16[384,128]{1,0:T(8,128)(2,1)} custom-call(s32[24]{0:T(128)} %concatenate.3.meta_ref, bf16[384,128]{1,0:T(8,128)(2,1)} %get-tuple-element.30.a_ref, bf16[384,128]{1,0:T(8,128)(2,1)} %copy-done.11), custom_call_target="tpu_custom_call" | custom-call | flops 49152 | bytes 294912 | tf_op jit(solution)/shard_map/pallas_call | solution.py:219
  30.2 3.5 %collective-permute-start.2 = (bf16[384,128]{1,0:T(8,128)(2,1)}, bf16[384,128]{1,0:T(8,128)(2,1)S(1)}, u32[]{:S(2)}, u32[]{:S(2)}) collective-permute-start(bf16[384,128]{1,0:T(8,128)(2,1)} %shard_map.68.a_ref), channel_id=1, source_target_pairs={{0,8},{2,10},{4,12},{6,14},{8,16},{10,18},{12,20},{14,22},{16,24},... | collective-permute-start | bytes 294920 | tf_op jit(solution)/shard_map/ppermute | solution.py:431
  33.7 2.7 %collective-permute-done.2.b_ref.near_ref = bf16[384,128]{1,0:T(8,128)(2,1)S(1)} collective-permute-done((bf16[384,128]{1,0:T(8,128)(2,1)}, bf16[384,128]{1,0:T(8,128)(2,1)S(1)}, u32[]{:S(2)}, u32[]{:S(2)}) %collective-permute-start.2) | collective-permute-done | bytes 98336 | tf_op jit(solution)/shard_map/ppermute | solution.py:431
  39.4 5.3 %collective-permute-start.4 = (bf16[384,128]{1,0:T(8,128)(2,1)}, bf16[384,128]{1,0:T(8,128)(2,1)S(1)}, u32[]{:S(2)}, u32[]{:S(2)}) collective-permute-start(bf16[384,128]{1,0:T(8,128)(2,1)} %shard_map.69), channel_id=1, source_target_pairs={{0,16},{2,18},{4,20},{6,22},{8,24},{10,26},{12,28},{14,30},{1,17},... | collective-permute-start | bytes 294920 | tf_op jit(solution)/shard_map/ppermute | solution.py:431
  47.2 3.0 %collective-permute-start.10 = (bf16[384,1024]{1,0:T(8,128)(2,1)S(1)}, bf16[384,1024]{1,0:T(8,128)(2,1)S(1)}, u32[]{:S(2)}, u32[]{:S(2)}) collective-permute-start(bf16[384,1024]{1,0:T(8,128)(2,1)S(1)} %collective-permute-done.3.refs_2_), channel_id=1, source_target_pairs={{0,8},{2,10},{4,12},{6,14},{8,0},{10,2},{12,4},{14,6},{16,24},{18,... | collective-permute-start | bytes 2359304 | tf_op jit(solution)/shard_map/ppermute | solution.py:428
  52.7 2.7 %shard_map.70 = (bf16[384,128]{1,0:T(8,128)(2,1)}, bf16[384,128]{1,0:T(8,128)(2,1)}, bf16[384,128]{1,0:T(8,128)(2,1)}) custom-call(s32[24]{0:T(128)} %concatenate.3.meta_ref, bf16[384,128]{1,0:T(8,128)(2,1)} %copy-done.12, bf16[384,128]{1,0:T(8,128)(2,1)} %copy-done.16, bf16[384,128]{1,0:T(8,128)(2,1)} %get-tuple-element.30.a_ref, ...), custom_call_target="tpu_custom_call" | custom-call | flops 49152 | bytes 884736 | tf_op jit(solution)/shard_map/pallas_call | solution.py:219
  55.5 13.7 %collective-permute-done.17 = f32[384]{0:T(512)S(1)} collective-permute-done((f32[384]{0:T(512)S(1)}, f32[384]{0:T(512)S(1)}, u32[]{:S(2)}, u32[]{:S(2)}) %collective-permute-start.17) | collective-permute-done | bytes 1568 | tf_op jit(solution)/shard_map/ppermute | solution.py:434
  69.7 4.3 %collective-permute-done.6.chip_ref = bf16[384,128]{1,0:T(8,128)(2,1)S(1)} collective-permute-done((bf16[384,128]{1,0:T(8,128)(2,1)}, bf16[384,128]{1,0:T(8,128)(2,1)S(1)}, u32[]{:S(2)}, u32[]{:S(2)}) %collective-permute-start.6) | collective-permute-done | bytes 98336 | tf_op jit(solution)/shard_map/ppermute | solution.py:428
  74.7 2.5 %shard_map.73 = (bf16[384,128]{1,0:T(8,128)(2,1)}, bf16[384,128]{1,0:T(8,128)(2,1)}) custom-call(s32[24]{0:T(128)} %concatenate.3.meta_ref, bf16[384,128]{1,0:T(8,128)(2,1)} %copy-done.15, bf16[2,384,128]{2,1,0:T(8,128)(2,1)} %get-tuple-element.29.keep_ref, bf16[2,384,128]{2,1,0:T(8,128)(2,1)} %copy-done.2), custom_call_target="tpu_custom_call" | custom-call | flops 49152 | bytes 491520 | tf_op jit(solution)/shard_map/pallas_call | solution.py:219
  78.3 3.1 %shard_map.71.refs_0_ = bf16[512,384]{1,0:T(8,128)(2,1)} custom-call(s32[24]{0:T(128)} %concatenate.3.meta_ref, bf16[512,1536]{1,0:T(8,128)(2,1)} %q_ref.11, f32[512,1152]{1,0:T(8,128)} %shard_map.67.w_ref, bf16[384,128]{1,0:T(8,128)(2,1)} %get-tuple-element.35.c_ref, f32[1,1536]{1,0:T(1,128)} %reshape.4.g_ref), custom_call_target="tpu_custom_call" | custom-call | flops 50331648 | bytes 1572864 | tf_op jit(solution)/shard_map/pallas_call | solution.py:330
  82.0 3.1 %shard_map.72.refs_1_ = bf16[512,384]{1,0:T(8,128)(2,1)} custom-call(s32[24]{0:T(128)} %concatenate.3.meta_ref, bf16[512,1536]{1,0:T(8,128)(2,1)} %q_ref.11, f32[512,1152]{1,0:T(8,128)} %shard_map.67.w_ref, bf16[384,128]{1,0:T(8,128)(2,1)} %copy-done.17, f32[1,1536]{1,0:T(1,128)} %reshape.4.g_ref), custom_call_target="tpu_custom_call" | custom-call | flops 50331648 | bytes 1572864 | tf_op jit(solution)/shard_map/pallas_call | solution.py:330
  88.8 14.6 %collective-permute-done.16.c_ref = bf16[384,128]{1,0:T(8,128)(2,1)S(1)} collective-permute-done((bf16[384,128]{1,0:T(8,128)(2,1)S(1)}, bf16[384,128]{1,0:T(8,128)(2,1)S(1)}, u32[]{:S(2)}, u32[]{:S(2)}) %collective-permute-start.16) | collective-permute-done | bytes 98336 | tf_op jit(solution)/shard_map/ppermute | solution.py:434
  104.8 3.1 %shard_map.74.refs_2_ = bf16[512,384]{1,0:T(8,128)(2,1)} custom-call(s32[24]{0:T(128)} %concatenate.3.meta_ref, bf16[512,1536]{1,0:T(8,128)(2,1)} %q_ref.11, f32[512,1152]{1,0:T(8,128)} %shard_map.67.w_ref, bf16[384,128]{1,0:T(8,128)(2,1)} %get-tuple-element.38.c_ref, f32[1,1536]{1,0:T(1,128)} %reshape.4.g_ref), custom_call_target="tpu_custom_call" | custom-call | flops 50331648 | bytes 1572864 | tf_op jit(solution)/shard_map/pallas_call | solution.py:330
  107.9 3.1 %shard_map.75.refs_3_ = bf16[512,384]{1,0:T(8,128)(2,1)} custom-call(s32[24]{0:T(128)} %concatenate.3.meta_ref, bf16[512,1536]{1,0:T(8,128)(2,1)} %q_ref.11, bf16[512,384]{1,0:T(8,128)(2,1)} %get-tuple-element.27.w_ref, bf16[384,128]{1,0:T(8,128)(2,1)} %copy-done.13, f32[1,1536]{1,0:T(1,128)} %reshape.4.g_ref), custom_call_target="tpu_custom_call" | custom-call | flops 50331648 | bytes 1572864 | tf_op jit(solution)/shard_map/pallas_call | solution.py:330
  111.6 2.4 %collective-permute-done.20.refs_4_ = bf16[384,512]{1,0:T(8,128)(2,1)} collective-permute-done((bf16[384,512]{1,0:T(8,128)(2,1)}, bf16[384,512]{1,0:T(8,128)(2,1)}, u32[]{:S(2)}, u32[]{:S(2)}) %collective-permute-start.20) | collective-permute-done | bytes 393248 | tf_op jit(solution)/shard_map/ppermute | solution.py:428
  114.5 8.6 %shard_map.76.t_ref = f32[512,2048]{1,0:T(8,128)} custom-call(s32[24]{0:T(128)} %concatenate.3.meta_ref, bf16[512,384]{1,0:T(8,128)(2,1)} %shard_map.71.refs_0_, bf16[512,384]{1,0:T(8,128)(2,1)} %shard_map.72.refs_1_, bf16[512,384]{1,0:T(8,128)(2,1)} %shard_map.74.refs_2_, bf16[512,384]{1,0:T(8,128)(2,1)} %shard_map.75.refs_3_, bf16[1536,4096]{1,0:T(8,128)(2,1)} %refs_7_.1, ...), custom_call_target="tpu_custom_call" | custom-call | flops 3221225472 | bytes 10485760 | tf_op jit(solution)/shard_map/pallas_call | solution.py:360
  123.1 3.0 %shard_map.78.refs_1_ = bf16[512,384]{1,0:T(8,128)(2,1)} custom-call(s32[24]{0:T(128)} %concatenate.3.meta_ref, bf16[512,384]{1,0:T(8,128)(2,1)} %copy-done.10, bf16[512,384]{1,0:T(8,128)(2,1)} %collective-permute-done.15.w_ref, bf16[384,128]{1,0:T(8,128)(2,1)} %copy-done.14, f32[1,384]{1,0:T(1,128)} %reshape.10.g_ref), custom_call_target="tpu_custom_call" | custom-call | flops 50331648 | bytes 1572864 | tf_op jit(solution)/shard_map/pallas_call | solution.py:330
  126.1 7.9 %shard_map.77.t_ref = f32[512,2048]{1,0:T(8,128)} custom-call(s32[24]{0:T(128)} %concatenate.3.meta_ref, f32[512,2048]{1,0:T(8,128)} %shard_map.76.t_ref, bf16[512,384]{1,0:T(8,128)(2,1)} %copy-done.6, bf16[512,384]{1,0:T(8,128)(2,1)} %collective-permute-done.9.refs_1_, bf16[384,1024]{1,0:T(8,128)(2,1)} %copy-done.4, bf16[384,1024]{1,0:T(8,128)(2,1)} %copy-done.1, ...), custom_call_target="tpu_custom_call" | custom-call | flops 1610612736 | bytes 9437184 | tf_op jit(solution)/shard_map/pallas_call | solution.py:400
  134.9 7.2 %shard_map.79 = bf16[512,2048]{1,0:T(8,128)(2,1)} custom-call(s32[24]{0:T(128)} %concatenate.3.meta_ref, f32[512,2048]{1,0:T(8,128)} %shard_map.77.t_ref, bf16[512,384]{1,0:T(8,128)(2,1)} %copy-done.7, bf16[512,384]{1,0:T(8,128)(2,1)} %shard_map.78.refs_1_, bf16[384,1024]{1,0:T(8,128)(2,1)} %copy-done, bf16[384,512]{1,0:T(8,128)(2,1)} %collective-permute-done.19.refs_3_, ...), custom_call_target="tpu_custom_call" | custom-call | flops 1610612736 | bytes 9437184 | tf_op jit(solution)/shard_map/pallas_call | solution.py:400
  (86 shorter events, 23.1 us)
Async XLA Ops:
  1.2 32.5 %collective-permute-start.3 = (bf16[384,1024]{1,0:T(8,128)(2,1)S(1)}, bf16[384,1024]{1,0:T(8,128)(2,1)S(1)}, u32[]{:S(2)}, u32[]{:S(2)}) collective-permute-start(bf16[384,1024]{1,0:T(8,128)(2,1)S(1)} %dynamic_slice.6), channel_id=1, source_target_pairs={{0,1},{1,0},{2,3},{3,2},{4,5},{5,4},{6,7},{7,6},{8,9},{9,8},{10,11... | collective-permute-start | bytes 2359304 | tf_op jit(solution)/shard_map/ppermute | solution.py:434
  11.4 4.0 %collective-permute-start = (bf16[2,384,128]{2,1,0:T(8,128)(2,1)}, bf16[2,384,128]{2,1,0:T(8,128)(2,1)S(1)}, u32[]{:S(2)}, u32[]{:S(2)}) collective-permute-start(bf16[2,384,128]{2,1,0:T(8,128)(2,1)} %get-tuple-element.25), channel_id=1, source_target_pairs={{0,2},{2,0},{4,6},{6,4},{8,10},{10,8},{12,14},{14,12},{16,18},{18,... | collective-permute-start | bytes 589832 | tf_op jit(solution)/shard_map/ppermute | solution.py:428
  18.6 8.7 %collective-permute-start.1 = (bf16[384,128]{1,0:T(8,128)(2,1)}, bf16[384,128]{1,0:T(8,128)(2,1)S(1)}, u32[]{:S(2)}, u32[]{:S(2)}) collective-permute-start(bf16[384,128]{1,0:T(8,128)(2,1)} %get-tuple-element.33), channel_id=1, source_target_pairs={{0,4},{2,6},{4,0},{6,2},{8,12},{10,14},{12,8},{14,10},{16,20},{18,... | collective-permute-start | bytes 294920 | tf_op jit(solution)/shard_map/ppermute | solution.py:428
  30.2 6.2 %collective-permute-start.2 = (bf16[384,128]{1,0:T(8,128)(2,1)}, bf16[384,128]{1,0:T(8,128)(2,1)S(1)}, u32[]{:S(2)}, u32[]{:S(2)}) collective-permute-start(bf16[384,128]{1,0:T(8,128)(2,1)} %shard_map.68.a_ref), channel_id=1, source_target_pairs={{0,8},{2,10},{4,12},{6,14},{8,16},{10,18},{12,20},{14,22},{16,24},... | collective-permute-start | bytes 294920 | tf_op jit(solution)/shard_map/ppermute | solution.py:431
  39.4 7.8 %collective-permute-start.4 = (bf16[384,128]{1,0:T(8,128)(2,1)}, bf16[384,128]{1,0:T(8,128)(2,1)S(1)}, u32[]{:S(2)}, u32[]{:S(2)}) collective-permute-start(bf16[384,128]{1,0:T(8,128)(2,1)} %shard_map.69), channel_id=1, source_target_pairs={{0,16},{2,18},{4,20},{6,22},{8,24},{10,26},{12,28},{14,30},{1,17},... | collective-permute-start | bytes 294920 | tf_op jit(solution)/shard_map/ppermute | solution.py:431
  44.6 42.0 %collective-permute-start.18 = (bf16[384,1024]{1,0:T(8,128)(2,1)S(1)}, bf16[384,1024]{1,0:T(8,128)(2,1)S(1)}, u32[]{:S(2)}, u32[]{:S(2)}) collective-permute-start(bf16[384,1024]{1,0:T(8,128)(2,1)S(1)} %collective-permute-done.3.refs_2_), channel_id=1, source_target_pairs={{0,4},{2,6},{4,0},{6,2},{8,12},{10,14},{12,8},{14,10},{16,20},{18,... | collective-permute-start | bytes 2359304 | tf_op jit(solution)/shard_map/ppermute | solution.py:428
  47.2 40.0 %collective-permute-start.10 = (bf16[384,1024]{1,0:T(8,128)(2,1)S(1)}, bf16[384,1024]{1,0:T(8,128)(2,1)S(1)}, u32[]{:S(2)}, u32[]{:S(2)}) collective-permute-start(bf16[384,1024]{1,0:T(8,128)(2,1)S(1)} %collective-permute-done.3.refs_2_), channel_id=1, source_target_pairs={{0,8},{2,10},{4,12},{6,14},{8,0},{10,2},{12,4},{14,6},{16,24},{18,... | collective-permute-start | bytes 2359304 | tf_op jit(solution)/shard_map/ppermute | solution.py:428
  50.1 27.0 %collective-permute-start.14 = (bf16[512,384]{1,0:T(8,128)(2,1)}, bf16[512,384]{1,0:T(8,128)(2,1)S(1)}, u32[]{:S(2)}, u32[]{:S(2)}) collective-permute-start(bf16[512,384]{1,0:T(8,128)(2,1)} %get-tuple-element.42), channel_id=1, source_target_pairs={{0,1},{1,0},{2,3},{3,2},{4,5},{5,4},{6,7},{7,6},{8,9},{9,8},{10,11... | collective-permute-start | bytes 1179656 | tf_op jit(solution)/shard_map/ppermute | solution.py:434
  50.6 27.3 %collective-permute-start.15 = (bf16[512,384]{1,0:T(8,128)(2,1)S(1)}, bf16[512,384]{1,0:T(8,128)(2,1)}, u32[]{:S(2)}, u32[]{:S(2)}) collective-permute-start(bf16[512,384]{1,0:T(8,128)(2,1)S(1)} %copy-done.9), channel_id=1, source_target_pairs={{0,1},{1,0},{2,3},{3,2},{4,5},{5,4},{6,7},{7,6},{8,9},{9,8},{10,11... | collective-permute-start | bytes 1179656 | tf_op jit(solution)/shard_map/ppermute | solution.py:434
  52.3 16.9 %collective-permute-start.17 = (f32[384]{0:T(512)S(1)}, f32[384]{0:T(512)S(1)}, u32[]{:S(2)}, u32[]{:S(2)}) collective-permute-start(f32[384]{0:T(512)S(1)} %dynamic_slice.7), channel_id=1, source_target_pairs={{0,1},{1,0},{2,3},{3,2},{4,5},{5,4},{6,7},{7,6},{8,9},{9,8},{10,11... | collective-permute-start | bytes 4616 | tf_op jit(solution)/shard_map/ppermute | solution.py:434
  69.2 4.8 %collective-permute-start.6 = (bf16[384,128]{1,0:T(8,128)(2,1)}, bf16[384,128]{1,0:T(8,128)(2,1)S(1)}, u32[]{:S(2)}, u32[]{:S(2)}) collective-permute-start(bf16[384,128]{1,0:T(8,128)(2,1)} %get-tuple-element.37), channel_id=1, source_target_pairs={{0,4},{2,6},{4,0},{6,2},{8,12},{10,14},{12,8},{14,10},{16,20},{18,... | collective-permute-start | bytes 294920 | tf_op jit(solution)/shard_map/ppermute | solution.py:428
  74.0 7.4 %collective-permute-start.5 = (bf16[384,128]{1,0:T(8,128)(2,1)}, bf16[384,128]{1,0:T(8,128)(2,1)S(1)}, u32[]{:S(2)}, u32[]{:S(2)}) collective-permute-start(bf16[384,128]{1,0:T(8,128)(2,1)} %get-tuple-element.36), channel_id=1, source_target_pairs={{0,2},{2,0},{4,6},{6,4},{8,10},{10,8},{12,14},{14,12},{16,18},{18,... | collective-permute-start | bytes 294920 | tf_op jit(solution)/shard_map/ppermute | solution.py:428
  77.1 8.0 %collective-permute-start.7 = (bf16[384,128]{1,0:T(8,128)(2,1)}, bf16[384,128]{1,0:T(8,128)(2,1)S(1)}, u32[]{:S(2)}, u32[]{:S(2)}) collective-permute-start(bf16[384,128]{1,0:T(8,128)(2,1)} %get-tuple-element.39), channel_id=1, source_target_pairs={{0,2},{2,0},{4,6},{6,4},{8,10},{10,8},{12,14},{14,12},{16,18},{18,... | collective-permute-start | bytes 294920 | tf_op jit(solution)/shard_map/ppermute | solution.py:428
  77.9 33.2 %collective-permute-start.11 = (bf16[384,1024]{1,0:T(8,128)(2,1)S(1)}, bf16[384,1024]{1,0:T(8,128)(2,1)S(1)}, u32[]{:S(2)}, u32[]{:S(2)}) collective-permute-start(bf16[384,1024]{1,0:T(8,128)(2,1)S(1)} %collective-permute-done.3.refs_2_), channel_id=1, source_target_pairs={{0,2},{2,0},{4,6},{6,4},{8,10},{10,8},{12,14},{14,12},{16,18},{18,... | collective-permute-start | bytes 2359304 | tf_op jit(solution)/shard_map/ppermute | solution.py:428
  81.4 22.2 %collective-permute-start.8 = (bf16[512,384]{1,0:T(8,128)(2,1)}, bf16[512,384]{1,0:T(8,128)(2,1)S(1)}, u32[]{:S(2)}, u32[]{:S(2)}) collective-permute-start(bf16[512,384]{1,0:T(8,128)(2,1)} %shard_map.71.refs_0_), channel_id=1, source_target_pairs={{0,1},{1,0},{2,3},{3,2},{4,5},{5,4},{6,7},{7,6},{8,9},{9,8},{10,11... | collective-permute-start | bytes 1179656 | tf_op jit(solution)/shard_map/ppermute | solution.py:434
  85.2 19.0 %collective-permute-start.9 = (bf16[512,384]{1,0:T(8,128)(2,1)}, bf16[512,384]{1,0:T(8,128)(2,1)}, u32[]{:S(2)}, u32[]{:S(2)}) collective-permute-start(bf16[512,384]{1,0:T(8,128)(2,1)} %shard_map.72.refs_1_), channel_id=1, source_target_pairs={{0,1},{1,0},{2,3},{3,2},{4,5},{5,4},{6,7},{7,6},{8,9},{9,8},{10,11... | collective-permute-start | bytes 1179656 | tf_op jit(solution)/shard_map/ppermute | solution.py:434
  86.6 16.7 %collective-permute-start.16 = (bf16[384,128]{1,0:T(8,128)(2,1)S(1)}, bf16[384,128]{1,0:T(8,128)(2,1)S(1)}, u32[]{:S(2)}, u32[]{:S(2)}) collective-permute-start(bf16[384,128]{1,0:T(8,128)(2,1)S(1)} %collective-permute-done.7.c_ref), channel_id=1, source_target_pairs={{0,1},{1,0},{2,3},{3,2},{4,5},{5,4},{6,7},{7,6},{8,9},{9,8},{10,11... | collective-permute-start | bytes 294920 | tf_op jit(solution)/shard_map/ppermute | solution.py:434
  87.2 38.9 %collective-permute-start.12 = (bf16[384,1024]{1,0:T(8,128)(2,1)S(1)}, bf16[384,1024]{1,0:T(8,128)(2,1)}, u32[]{:S(2)}, u32[]{:S(2)}) collective-permute-start(bf16[384,1024]{1,0:T(8,128)(2,1)S(1)} %collective-permute-done.10.refs_3_), channel_id=1, source_target_pairs={{0,2},{2,0},{4,6},{6,4},{8,10},{10,8},{12,14},{14,12},{16,18},{18,... | collective-permute-start | bytes 2359304 | tf_op jit(solution)/shard_map/ppermute | solution.py:428
  103.4 10.6 %collective-permute-start.20 = (bf16[384,512]{1,0:T(8,128)(2,1)}, bf16[384,512]{1,0:T(8,128)(2,1)}, u32[]{:S(2)}, u32[]{:S(2)}) collective-permute-start(bf16[384,512]{1,0:T(8,128)(2,1)} %slice.9), channel_id=1, source_target_pairs={{0,8},{2,10},{4,12},{6,14},{8,0},{10,2},{12,4},{14,6},{16,24},{18,... | collective-permute-start | bytes 1179656 | tf_op jit(solution)/shard_map/ppermute | solution.py:428
  103.7 10.4 %collective-permute-start.19 = (bf16[384,512]{1,0:T(8,128)(2,1)}, bf16[384,512]{1,0:T(8,128)(2,1)}, u32[]{:S(2)}, u32[]{:S(2)}) collective-permute-start(bf16[384,512]{1,0:T(8,128)(2,1)} %slice.8), channel_id=1, source_target_pairs={{0,4},{2,6},{4,0},{6,2},{8,12},{10,14},{12,8},{14,10},{16,20},{18,... | collective-permute-start | bytes 1179656 | tf_op jit(solution)/shard_map/ppermute | solution.py:428
  104.2 29.8 %collective-permute-start.21 = (bf16[384,1024]{1,0:T(8,128)(2,1)S(1)}, bf16[384,1024]{1,0:T(8,128)(2,1)}, u32[]{:S(2)}, u32[]{:S(2)}) collective-permute-start(bf16[384,1024]{1,0:T(8,128)(2,1)S(1)} %collective-permute-done.18.refs_2_), channel_id=1, source_target_pairs={{0,2},{2,0},{4,6},{6,4},{8,10},{10,8},{12,14},{14,12},{16,18},{18,... | collective-permute-start | bytes 2359304 | tf_op jit(solution)/shard_map/ppermute | solution.py:428
  111.1 22.9 %collective-permute-start.13 = (bf16[512,384]{1,0:T(8,128)(2,1)S(1)}, bf16[512,384]{1,0:T(8,128)(2,1)S(1)}, u32[]{:S(2)}, u32[]{:S(2)}) collective-permute-start(bf16[512,384]{1,0:T(8,128)(2,1)S(1)} %copy-done.3), channel_id=1, source_target_pairs={{0,1},{1,0},{2,3},{3,2},{4,5},{5,4},{6,7},{7,6},{8,9},{9,8},{10,11... | collective-permute-start | bytes 1179656 | tf_op jit(solution)/shard_map/ppermute | solution.py:434
  114.0 20.0 %collective-permute-start.23 = (bf16[384,512]{1,0:T(8,128)(2,1)}, bf16[384,512]{1,0:T(8,128)(2,1)S(1)}, u32[]{:S(2)}, u32[]{:S(2)}) collective-permute-start(bf16[384,512]{1,0:T(8,128)(2,1)} %collective-permute-done.20.refs_4_), channel_id=1, source_target_pairs={{0,2},{2,0},{4,6},{6,4},{8,10},{10,8},{12,14},{14,12},{16,18},{18,... | collective-permute-start | bytes 1179656 | tf_op jit(solution)/shard_map/ppermute | solution.py:428
  114.1 19.9 %collective-permute-start.22 = (bf16[384,512]{1,0:T(8,128)(2,1)}, bf16[384,512]{1,0:T(8,128)(2,1)}, u32[]{:S(2)}, u32[]{:S(2)}) collective-permute-start(bf16[384,512]{1,0:T(8,128)(2,1)} %collective-permute-done.19.refs_3_), channel_id=1, source_target_pairs={{0,2},{2,0},{4,6},{6,4},{8,10},{10,8},{12,14},{14,12},{16,18},{18,... | collective-permute-start | bytes 1179656 | tf_op jit(solution)/shard_map/ppermute | solution.py:428
  (19 other events, 203.4 us)

commit v3 on v2

--- a/solution.py
+++ b/solution.py
@@ -11,7 +11,7 @@
 PLANES = 4
 F32, BF16 = jnp.float32, jnp.bfloat16
 LENS = 8
-VMEM_LIMIT = 60 * 1024 * 1024
+VMEM_LIMIT = 16 * 1024 * 1024
 
 
 def doc_start(meta, doc_count, token):
@@ -446,15 +446,16 @@
     core_got = swap(send, 1)
     within3, query3 = within_slots(after(meta, send), query, key, value, docs, (3,), BF16, True)
     far_query, far_within = flip(query3), flip(within3)
-    chip0, chip2 = join_core(after(meta, within3), keep, core_got, rows, docs)
+    chip0, chip2 = join_core(after(meta, within3, far_gain), keep, core_got, rows, docs)
     chip_got = swap(chip2, 2)
     (within,) = within_slots(after(meta, chip0), query, key, value, docs, (0, 1, 2), F32, False)
-    plane_sum = join_chips(after(meta, within), chip0, chip_got, rows, docs)
+    plane_sum = join_chips(after(meta, within, w0[0]), chip0, chip_got, rows, docs)
     near = shift(plane_sum, plane)
-    both = join_planes(after(meta, w0[0]), plane_sum, near, rows, docs)
+    both = join_planes(after(meta, far_query), plane_sum, near, rows, docs)
+    w2 = [swap(w0[0], 2)]
     far = shift(both, 2 * plane)
     carry0, core_carry0, chip_carry = carry_first(
-        meta, near, far, chip0, chip_got, keep, core_got, rows, docs
+        after(meta, far_within, w2[0]), near, far, chip0, chip_got, keep, core_got, rows, docs
     )
     carry1 = swap(core_carry0, 1)
     chip_carry2 = swap(chip_carry, 2)
@@ -483,7 +484,6 @@
 
     w0[1] = swap(behind(w0[0], far), plane)
     quarter = half // 2
-    w2 = [swap(w0[0], 2)]
     w2.append(swap(w0[1][:, :quarter], 2))
     w2.append(swap(w2[0][:, quarter:], plane))
     w1 = [swap(w, 1) for w in w0]

time: 143 us -> 112 us (0.78)
  Pallas kernels: 68.6 us -> 35.9 us
  starting transfers between devices: 24.7 us -> 28.5 us
  local copies, waits for them, and re-layouts: 8.9 us -> 6.68 us
    pallas_call x5, Pallas kernels: 15.5 us -> 6.09 us  [norm_heads(): call(kernel, (1,), [pl.BlockSpec((rows, part), block(slots[0])), pl.Block...]
    pallas_call x5, Pallas kernels: 12.1 us -> 3.15 us  [small(): call(kernel, (1,), [whole(a.shape) for a in arrays], [whole(shape)] * cou...]
    pallas_call x2, Pallas kernels: 15.1 us -> 9.3 us  [project_more(): call(kernel, (TILES,), [out_spec] + [whole((rows, part))] * count + [pl.B...]
    pallas_call x2, Pallas kernels: 11.3 us -> 7.39 us  [within_slots(): call(kernel, (count,), [spec] * 3, [out] * (1 + with_query), [jax.ShapeDt...]
    pallas_call x1, Pallas kernels: 8.56 us -> 5.36 us  [project_own(): call(kernel, (TILES,), [whole((rows, part))] * count + [pl.BlockSpec((par...]
    ppermute x8, starting transfers between devices: 8.71 us -> 11.7 us  [flip(): return lax.ppermute(x, 'head', [(0, 1), (1, 0)])]
    ppermute x8, waiting for transfers between devices: 28.4 us -> 25.9 us  [flip(): return lax.ppermute(x, 'head', [(0, 1), (1, 0)])]
    ppermute x14, waiting for transfers between devices: 6.79 us -> 9.18 us  [swap(): return lax.ppermute(x, 'seq', [(i, i ^ bit) for i in range(n_seq)])]
  transfers between devices with their start and end apart: 24 -> 24, of which waited for: 7 -> 9; matrix products, arithmetic and copies ran while one was open for 3% -> 1% of each run, Pallas kernels for 42% -> 28%
where the time goes in v3:
time: 112 us; the launch traced here: 111 us
  waiting for transfers between devices  39.8 us (36%)
  Pallas kernels  35.9 us (32%)
  starting transfers between devices  28.5 us (25%)
  local copies, waits for them, and re-layouts  6.68 us (6%)
    ppermute x8, waiting for transfers between devices, flip(): return lax.ppermute(x, 'head', [(0, 1), (1, 0)])  25.9 us
    ppermute x8, starting transfers between devices, flip(): return lax.ppermute(x, 'head', [(0, 1), (1, 0)])  11.7 us
    pallas_call x2, Pallas kernels, project_more(): call(kernel, (TILES,), [out_spec] + [whole((rows, part))] * count + [pl.B...  9.3 us
    ppermute x14, waiting for transfers between devices, swap(): return lax.ppermute(x, 'seq', [(i, i ^ bit) for i in range(n_seq)])  9.18 us
    ppermute x2, starting transfers between devices, shift(): lax.ppermute(x, 'seq', [(i, i + count) for i in range(n_seq - count)])  9.04 us
    ppermute x14, starting transfers between devices, swap(): return lax.ppermute(x, 'seq', [(i, i ^ bit) for i in range(n_seq)])  7.8 us
    pallas_call x2, Pallas kernels, within_slots(): call(kernel, (count,), [spec] * 3, [out] * (1 + with_query), [jax.ShapeDt...  7.39 us
    pallas_call x5, Pallas kernels, norm_heads(): call(kernel, (1,), [pl.BlockSpec((rows, part), block(slots[0])), pl.Block...  6.09 us
  transfers between devices with their start and end apart: 24, of which 9 were waited for; matrix products, arithmetic and copies ran while one was open for 1% of the time, Pallas kernels for 28%

profile of v3, /device:TPU:0, one launch (start us, length us, event | category | flops | bytes accessed | tf_op | source)
XLA Modules:
  0.0 111.3 jit_solution(14109856975516371577)
XLA Ops:
  0.0 2.2 %dynamic_slice.6 = bf16[384,1024]{1,0:T(8,128)(2,1)} dynamic-slice(bf16[1536,4096]{1,0:T(8,128)(2,1)} %refs_7_.1, s32[]{:T(128)S(6)} %select_n.27, s32[]{:T(128)S(6)} %select_n.28), dynamic_slice_sizes={384,1024} | dynamic-slice | bytes 1572868 | tf_op jit(solution)/shard_map/dynamic_slice | solution.py:439
  2.2 3.0 %collective-permute-start.3 = (bf16[384,1024]{1,0:T(8,128)(2,1)}, bf16[384,1024]{1,0:T(8,128)(2,1)}, u32[]{:S(2)}, u32[]{:S(2)}) collective-permute-start(bf16[384,1024]{1,0:T(8,128)(2,1)} %dynamic_slice.6), channel_id=1, source_target_pairs={{0,1},{1,0},{2,3},{3,2},{4,5},{5,4},{6,7},{7,6},{8,9},{9,8},{10,11... | collective-permute-start | bytes 2359304 | tf_op jit(solution)/shard_map/ppermute | solution.py:434
  7.3 4.6 %shard_map.64 = (bf16[2,384,128]{2,1,0:T(8,128)(2,1)}, bf16[2,384,128]{2,1,0:T(8,128)(2,1)S(1)}) custom-call(s32[24]{0:T(128)S(1)} %concatenate.3.meta_ref, bf16[512,1536]{1,0:T(8,128)(2,1)S(1)} %copy-done.1, bf16[512,1536]{1,0:T(8,128)(2,1)S(1)} %copy-done.2), custom_call_target="tpu_custom_call" | custom-call | flops 201326592 | bytes 3145728 | tf_op jit(solution)/shard_map/pallas_call | solution.py:154
  12.0 2.4 %shard_map.65 = (bf16[512,384]{1,0:T(8,128)(2,1)S(1)}, bf16[512,384]{1,0:T(8,128)(2,1)}) custom-call(s32[24]{0:T(128)S(1)} %concatenate.3.meta_ref, bf16[512,1536]{1,0:T(8,128)(2,1)S(1)} %copy-done, bf16[512,1536]{1,0:T(8,128)(2,1)S(1)} %copy-done.1, bf16[512,1536]{1,0:T(8,128)(2,1)S(1)} %copy-done.2), custom_call_target="tpu_custom_call" | custom-call | flops 301989888 | bytes 1966080 | tf_op jit(solution)/shard_map/pallas_call | solution.py:206
  15.1 2.0 %collective-permute-start = (f32[384]{0:T(512)S(1)}, f32[384]{0:T(512)S(1)}, u32[]{:S(2)}, u32[]{:S(2)}) collective-permute-start(f32[384]{0:T(512)S(1)} %dynamic_slice.7), channel_id=1, source_target_pairs={{0,1},{1,0},{2,3},{3,2},{4,5},{5,4},{6,7},{7,6},{8,9},{9,8},{10,11... | collective-permute-start | bytes 4616 | tf_op jit(solution)/shard_map/ppermute | solution.py:434
  17.2 14.3 %collective-permute-done = f32[384]{0:T(512)S(1)} collective-permute-done((f32[384]{0:T(512)S(1)}, f32[384]{0:T(512)S(1)}, u32[]{:S(2)}, u32[]{:S(2)}) %collective-permute-start) | collective-permute-done | bytes 1568 | tf_op jit(solution)/shard_map/ppermute | solution.py:434
  32.1 1.8 %collective-permute-start.5 = (bf16[384,128]{1,0:T(8,128)(2,1)S(1)}, bf16[384,128]{1,0:T(8,128)(2,1)S(1)}, u32[]{:S(2)}, u32[]{:S(2)}) collective-permute-start(bf16[384,128]{1,0:T(8,128)(2,1)S(1)} %get-tuple-element.35), channel_id=1, source_target_pairs={{0,4},{2,6},{4,0},{6,2},{8,12},{10,14},{12,8},{14,10},{16,20},{18,... | collective-permute-start | bytes 294920 | tf_op jit(solution)/shard_map/ppermute | solution.py:428
  35.6 5.0 %shard_map.67.w_ref = f32[512,1152]{1,0:T(8,128)S(1)} custom-call(s32[24]{0:T(128)S(1)} %concatenate.3.meta_ref, bf16[512,1536]{1,0:T(8,128)(2,1)S(1)} %copy-done, bf16[512,1536]{1,0:T(8,128)(2,1)S(1)} %copy-done.1, bf16[512,1536]{1,0:T(8,128)(2,1)S(1)} %copy-done.3), custom_call_target="tpu_custom_call" | custom-call | flops 905969664 | bytes 5898240 | tf_op jit(solution)/shard_map/pallas_call | solution.py:206
  41.3 3.7 %collective-permute-start.6 = (bf16[384,128]{1,0:T(8,128)(2,1)S(1)}, bf16[384,128]{1,0:T(8,128)(2,1)S(1)}, u32[]{:S(2)}, u32[]{:S(2)}) collective-permute-start(bf16[384,128]{1,0:T(8,128)(2,1)S(1)} %shard_map.68.a_ref), channel_id=1, source_target_pairs={{0,8},{2,10},{4,12},{6,14},{8,16},{10,18},{12,20},{14,22},{16,24},... | collective-permute-start | bytes 294920 | tf_op jit(solution)/shard_map/ppermute | solution.py:431
  45.0 2.2 %collective-permute-done.6.b_ref.near_ref = bf16[384,128]{1,0:T(8,128)(2,1)S(1)} collective-permute-done((bf16[384,128]{1,0:T(8,128)(2,1)S(1)}, bf16[384,128]{1,0:T(8,128)(2,1)S(1)}, u32[]{:S(2)}, u32[]{:S(2)}) %collective-permute-start.6) | collective-permute-done | bytes 98336 | tf_op jit(solution)/shard_map/ppermute | solution.py:431
  47.8 5.3 %collective-permute-start.8 = (bf16[384,128]{1,0:T(8,128)(2,1)S(1)}, bf16[384,128]{1,0:T(8,128)(2,1)S(1)}, u32[]{:S(2)}, u32[]{:S(2)}) collective-permute-start(bf16[384,128]{1,0:T(8,128)(2,1)S(1)} %shard_map.69), channel_id=1, source_target_pairs={{0,16},{2,18},{4,20},{6,22},{8,24},{10,26},{12,28},{14,30},{1,17},... | collective-permute-start | bytes 294920 | tf_op jit(solution)/shard_map/ppermute | solution.py:431
  53.1 2.6 %collective-permute-done.8.far_ref = bf16[384,128]{1,0:T(8,128)(2,1)S(1)} collective-permute-done((bf16[384,128]{1,0:T(8,128)(2,1)S(1)}, bf16[384,128]{1,0:T(8,128)(2,1)S(1)}, u32[]{:S(2)}, u32[]{:S(2)}) %collective-permute-start.8) | collective-permute-done | bytes 98336 | tf_op jit(solution)/shard_map/ppermute | solution.py:431
  55.8 2.1 %collective-permute-start.14 = (bf16[384,1024]{1,0:T(8,128)(2,1)}, bf16[384,1024]{1,0:T(8,128)(2,1)S(1)}, u32[]{:S(2)}, u32[]{:S(2)}) collective-permute-start(bf16[384,1024]{1,0:T(8,128)(2,1)} %collective-permute-done.3.refs_2_), channel_id=1, source_target_pairs={{0,8},{2,10},{4,12},{6,14},{8,0},{10,2},{12,4},{14,6},{16,24},{18,... | collective-permute-start | bytes 2359304 | tf_op jit(solution)/shard_map/ppermute | solution.py:428
  57.8 1.5 %collective-permute-start.2 = (bf16[512,384]{1,0:T(8,128)(2,1)S(1)}, bf16[512,384]{1,0:T(8,128)(2,1)S(1)}, u32[]{:S(2)}, u32[]{:S(2)}) collective-permute-start(bf16[512,384]{1,0:T(8,128)(2,1)S(1)} %copy-done.5), channel_id=1, source_target_pairs={{0,1},{1,0},{2,3},{3,2},{4,5},{5,4},{6,7},{7,6},{8,9},{9,8},{10,11... | collective-permute-start | bytes 1179656 | tf_op jit(solution)/shard_map/ppermute | solution.py:434
  59.3 10.0 %collective-permute-done.2.w_ref = bf16[512,384]{1,0:T(8,128)(2,1)S(1)} collective-permute-done((bf16[512,384]{1,0:T(8,128)(2,1)S(1)}, bf16[512,384]{1,0:T(8,128)(2,1)S(1)}, u32[]{:S(2)}, u32[]{:S(2)}) %collective-permute-start.2) | collective-permute-done | bytes 393248 | tf_op jit(solution)/shard_map/ppermute | solution.py:434
  71.1 1.6 %collective-permute-start.12 = (bf16[512,384]{1,0:T(8,128)(2,1)S(1)}, bf16[512,384]{1,0:T(8,128)(2,1)S(1)}, u32[]{:S(2)}, u32[]{:S(2)}) collective-permute-start(bf16[512,384]{1,0:T(8,128)(2,1)S(1)} %shard_map.71.refs_0_), channel_id=1, source_target_pairs={{0,1},{1,0},{2,3},{3,2},{4,5},{5,4},{6,7},{7,6},{8,9},{9,8},{10,11... | collective-permute-start | bytes 1179656 | tf_op jit(solution)/shard_map/ppermute | solution.py:434
  74.2 3.1 %collective-permute-done.10.chip_ref = bf16[384,128]{1,0:T(8,128)(2,1)S(1)} collective-permute-done((bf16[384,128]{1,0:T(8,128)(2,1)S(1)}, bf16[384,128]{1,0:T(8,128)(2,1)S(1)}, u32[]{:S(2)}, u32[]{:S(2)}) %collective-permute-start.10) | collective-permute-done | bytes 98336 | tf_op jit(solution)/shard_map/ppermute | solution.py:428
  81.0 1.6 %collective-permute-start.13 = (bf16[512,384]{1,0:T(8,128)(2,1)S(1)}, bf16[512,384]{1,0:T(8,128)(2,1)S(1)}, u32[]{:S(2)}, u32[]{:S(2)}) collective-permute-start(bf16[512,384]{1,0:T(8,128)(2,1)S(1)} %shard_map.72.refs_1_), channel_id=1, source_target_pairs={{0,1},{1,0},{2,3},{3,2},{4,5},{5,4},{6,7},{7,6},{8,9},{9,8},{10,11... | collective-permute-start | bytes 1179656 | tf_op jit(solution)/shard_map/ppermute | solution.py:434
  82.6 1.5 %collective-permute-done.18.c_ref = bf16[384,128]{1,0:T(8,128)(2,1)S(1)} collective-permute-done((bf16[384,128]{1,0:T(8,128)(2,1)S(1)}, bf16[384,128]{1,0:T(8,128)(2,1)S(1)}, u32[]{:S(2)}, u32[]{:S(2)}) %collective-permute-start.18) | collective-permute-done | bytes 98336 | tf_op jit(solution)/shard_map/ppermute | solution.py:434
  87.7 3.7 %collective-permute-done.20.refs_4_ = bf16[384,512]{1,0:T(8,128)(2,1)S(1)} collective-permute-done((bf16[384,512]{1,0:T(8,128)(2,1)S(1)}, bf16[384,512]{1,0:T(8,128)(2,1)S(1)}, u32[]{:S(2)}, u32[]{:S(2)}) %collective-permute-start.20) | collective-permute-done | bytes 393248 | tf_op jit(solution)/shard_map/ppermute | solution.py:428
  94.5 5.4 %shard_map.76.t_ref = f32[512,2048]{1,0:T(8,128)S(1)} custom-call(s32[24]{0:T(128)S(1)} %concatenate.3.meta_ref, bf16[512,384]{1,0:T(8,128)(2,1)S(1)} %shard_map.71.refs_0_, bf16[512,384]{1,0:T(8,128)(2,1)S(1)} %shard_map.72.refs_1_, bf16[512,384]{1,0:T(8,128)(2,1)S(1)} %shard_map.74.refs_2_, bf16[512,384]{1,0:T(8,128)(2,1)S(1)} %shard_map.75.refs_3_, ...), custom_call_target="tpu_custom_call" | custom-call | flops 3221225472 | bytes 10485760 | tf_op jit(solution)/shard_map/pallas_call | solution.py:360
  99.9 2.0 %shard_map.78.refs_1_ = bf16[512,384]{1,0:T(8,128)(2,1)S(1)} custom-call(s32[24]{0:T(128)S(1)} %concatenate.3.meta_ref, bf16[512,384]{1,0:T(8,128)(2,1)} %collective-permute-done.7.q_ref, bf16[512,384]{1,0:T(8,128)(2,1)S(1)} %collective-permute-done.2.w_ref, bf16[384,128]{1,0:T(8,128)(2,1)S(1)} %collective-permute-done.18.c_ref, f32[1,384]{1,0:T(1,128)S(1)} %reshape.10.g_ref), custom_call_target="tpu_custom_call" | custom-call | flops 50331648 | bytes 1572864 | tf_op jit(solution)/shard_map/pallas_call | solution.py:330
  101.9 4.9 %shard_map.77.t_ref = f32[512,2048]{1,0:T(8,128)S(1)} custom-call(s32[24]{0:T(128)S(1)} %concatenate.3.meta_ref, f32[512,2048]{1,0:T(8,128)S(1)} %shard_map.76.t_ref, bf16[512,384]{1,0:T(8,128)(2,1)S(1)} %collective-permute-done.12.refs_0_, bf16[512,384]{1,0:T(8,128)(2,1)S(1)} %collective-permute-done.13.refs_1_, ...), custom_call_target="tpu_custom_call" | custom-call | flops 1610612736 | bytes 9437184 | tf_op jit(solution)/shard_map/pallas_call | solution.py:400
  106.8 4.4 %shard_map.79 = bf16[512,2048]{1,0:T(8,128)(2,1)} custom-call(s32[24]{0:T(128)S(1)} %concatenate.3.meta_ref, f32[512,2048]{1,0:T(8,128)S(1)} %shard_map.77.t_ref, bf16[512,384]{1,0:T(8,128)(2,1)S(1)} %collective-permute-done.17.refs_0_, bf16[512,384]{1,0:T(8,128)(2,1)S(1)} %shard_map.78.refs_1_, bf16[384,1024]{1,0:T(8,128)(2,1)S(1)} %collective-permute-done.4.refs_2_, ...), custom_call_target="tpu_custom_call" | custom-call | flops 1610612736 | bytes 9437184 | tf_op jit(solution)/shard_map/pallas_call | solution.py:400
  (69 shorter events, 20.0 us)
Async XLA Ops:
  2.2 31.7 %collective-permute-start.3 = (bf16[384,1024]{1,0:T(8,128)(2,1)}, bf16[384,1024]{1,0:T(8,128)(2,1)}, u32[]{:S(2)}, u32[]{:S(2)}) collective-permute-start(bf16[384,1024]{1,0:T(8,128)(2,1)} %dynamic_slice.6), channel_id=1, source_target_pairs={{0,1},{1,0},{2,3},{3,2},{4,5},{5,4},{6,7},{7,6},{8,9},{9,8},{10,11... | collective-permute-start | bytes 2359304 | tf_op jit(solution)/shard_map/ppermute | solution.py:434
  11.9 19.5 %collective-permute-start.1 = (bf16[2,384,128]{2,1,0:T(8,128)(2,1)}, bf16[2,384,128]{2,1,0:T(8,128)(2,1)S(1)}, u32[]{:S(2)}, u32[]{:S(2)}) collective-permute-start(bf16[2,384,128]{2,1,0:T(8,128)(2,1)} %get-tuple-element.26), channel_id=1, source_target_pairs={{0,2},{2,0},{4,6},{6,4},{8,10},{10,8},{12,14},{14,12},{16,18},{18,... | collective-permute-start | bytes 589832 | tf_op jit(solution)/shard_map/ppermute | solution.py:428
  15.1 30.0 %collective-permute-start.7 = (bf16[512,384]{1,0:T(8,128)(2,1)}, bf16[512,384]{1,0:T(8,128)(2,1)}, u32[]{:S(2)}, u32[]{:S(2)}) collective-permute-start(bf16[512,384]{1,0:T(8,128)(2,1)} %get-tuple-element.36), channel_id=1, source_target_pairs={{0,1},{1,0},{2,3},{3,2},{4,5},{5,4},{6,7},{7,6},{8,9},{9,8},{10,11... | collective-permute-start | bytes 1179656 | tf_op jit(solution)/shard_map/ppermute | solution.py:434
  15.1 16.3 %collective-permute-start = (f32[384]{0:T(512)S(1)}, f32[384]{0:T(512)S(1)}, u32[]{:S(2)}, u32[]{:S(2)}) collective-permute-start(f32[384]{0:T(512)S(1)} %dynamic_slice.7), channel_id=1, source_target_pairs={{0,1},{1,0},{2,3},{3,2},{4,5},{5,4},{6,7},{7,6},{8,9},{9,8},{10,11... | collective-permute-start | bytes 4616 | tf_op jit(solution)/shard_map/ppermute | solution.py:434
  32.1 8.6 %collective-permute-start.5 = (bf16[384,128]{1,0:T(8,128)(2,1)S(1)}, bf16[384,128]{1,0:T(8,128)(2,1)S(1)}, u32[]{:S(2)}, u32[]{:S(2)}) collective-permute-start(bf16[384,128]{1,0:T(8,128)(2,1)S(1)} %get-tuple-element.35), channel_id=1, source_target_pairs={{0,4},{2,6},{4,0},{6,2},{8,12},{10,14},{12,8},{14,10},{16,20},{18,... | collective-permute-start | bytes 294920 | tf_op jit(solution)/shard_map/ppermute | solution.py:428
  33.9 35.4 %collective-permute-start.4 = (bf16[384,1024]{1,0:T(8,128)(2,1)}, bf16[384,1024]{1,0:T(8,128)(2,1)S(1)}, u32[]{:S(2)}, u32[]{:S(2)}) collective-permute-start(bf16[384,1024]{1,0:T(8,128)(2,1)} %collective-permute-done.3.refs_2_), channel_id=1, source_target_pairs={{0,4},{2,6},{4,0},{6,2},{8,12},{10,14},{12,8},{14,10},{16,20},{18,... | collective-permute-start | bytes 2359304 | tf_op jit(solution)/shard_map/ppermute | solution.py:428
  41.3 5.9 %collective-permute-start.6 = (bf16[384,128]{1,0:T(8,128)(2,1)S(1)}, bf16[384,128]{1,0:T(8,128)(2,1)S(1)}, u32[]{:S(2)}, u32[]{:S(2)}) collective-permute-start(bf16[384,128]{1,0:T(8,128)(2,1)S(1)} %shard_map.68.a_ref), channel_id=1, source_target_pairs={{0,8},{2,10},{4,12},{6,14},{8,16},{10,18},{12,20},{14,22},{16,24},... | collective-permute-start | bytes 294920 | tf_op jit(solution)/shard_map/ppermute | solution.py:431
  47.8 7.9 %collective-permute-start.8 = (bf16[384,128]{1,0:T(8,128)(2,1)S(1)}, bf16[384,128]{1,0:T(8,128)(2,1)S(1)}, u32[]{:S(2)}, u32[]{:S(2)}) collective-permute-start(bf16[384,128]{1,0:T(8,128)(2,1)S(1)} %shard_map.69), channel_id=1, source_target_pairs={{0,16},{2,18},{4,20},{6,22},{8,24},{10,26},{12,28},{14,30},{1,17},... | collective-permute-start | bytes 294920 | tf_op jit(solution)/shard_map/ppermute | solution.py:431
  55.8 24.1 %collective-permute-start.14 = (bf16[384,1024]{1,0:T(8,128)(2,1)}, bf16[384,1024]{1,0:T(8,128)(2,1)S(1)}, u32[]{:S(2)}, u32[]{:S(2)}) collective-permute-start(bf16[384,1024]{1,0:T(8,128)(2,1)} %collective-permute-done.3.refs_2_), channel_id=1, source_target_pairs={{0,8},{2,10},{4,12},{6,14},{8,0},{10,2},{12,4},{14,6},{16,24},{18,... | collective-permute-start | bytes 2359304 | tf_op jit(solution)/shard_map/ppermute | solution.py:428
  57.8 23.2 %collective-permute-start.15 = (bf16[384,1024]{1,0:T(8,128)(2,1)}, bf16[384,1024]{1,0:T(8,128)(2,1)S(1)}, u32[]{:S(2)}, u32[]{:S(2)}) collective-permute-start(bf16[384,1024]{1,0:T(8,128)(2,1)} %collective-permute-done.3.refs_2_), channel_id=1, source_target_pairs={{0,2},{2,0},{4,6},{6,4},{8,10},{10,8},{12,14},{14,12},{16,18},{18,... | collective-permute-start | bytes 2359304 | tf_op jit(solution)/shard_map/ppermute | solution.py:428
  57.8 11.5 %collective-permute-start.2 = (bf16[512,384]{1,0:T(8,128)(2,1)S(1)}, bf16[512,384]{1,0:T(8,128)(2,1)S(1)}, u32[]{:S(2)}, u32[]{:S(2)}) collective-permute-start(bf16[512,384]{1,0:T(8,128)(2,1)S(1)} %copy-done.5), channel_id=1, source_target_pairs={{0,1},{1,0},{2,3},{3,2},{4,5},{5,4},{6,7},{7,6},{8,9},{9,8},{10,11... | collective-permute-start | bytes 1179656 | tf_op jit(solution)/shard_map/ppermute | solution.py:434
  71.1 14.5 %collective-permute-start.12 = (bf16[512,384]{1,0:T(8,128)(2,1)S(1)}, bf16[512,384]{1,0:T(8,128)(2,1)S(1)}, u32[]{:S(2)}, u32[]{:S(2)}) collective-permute-start(bf16[512,384]{1,0:T(8,128)(2,1)S(1)} %shard_map.71.refs_0_), channel_id=1, source_target_pairs={{0,1},{1,0},{2,3},{3,2},{4,5},{5,4},{6,7},{7,6},{8,9},{9,8},{10,11... | collective-permute-start | bytes 1179656 | tf_op jit(solution)/shard_map/ppermute | solution.py:434
  72.7 4.6 %collective-permute-start.10 = (bf16[384,128]{1,0:T(8,128)(2,1)S(1)}, bf16[384,128]{1,0:T(8,128)(2,1)S(1)}, u32[]{:S(2)}, u32[]{:S(2)}) collective-permute-start(bf16[384,128]{1,0:T(8,128)(2,1)S(1)} %get-tuple-element.40), channel_id=1, source_target_pairs={{0,4},{2,6},{4,0},{6,2},{8,12},{10,14},{12,8},{14,10},{16,20},{18,... | collective-permute-start | bytes 294920 | tf_op jit(solution)/shard_map/ppermute | solution.py:428
  77.9 1.4 %collective-permute-start.11 = (bf16[384,128]{1,0:T(8,128)(2,1)S(1)}, bf16[384,128]{1,0:T(8,128)(2,1)S(1)}, u32[]{:S(2)}, u32[]{:S(2)}) collective-permute-start(bf16[384,128]{1,0:T(8,128)(2,1)S(1)} %get-tuple-element.42), channel_id=1, source_target_pairs={{0,2},{2,0},{4,6},{6,4},{8,10},{10,8},{12,14},{14,12},{16,18},{18,... | collective-permute-start | bytes 294920 | tf_op jit(solution)/shard_map/ppermute | solution.py:428
  78.0 1.9 %collective-permute-start.9 = (bf16[384,128]{1,0:T(8,128)(2,1)S(1)}, bf16[384,128]{1,0:T(8,128)(2,1)S(1)}, u32[]{:S(2)}, u32[]{:S(2)}) collective-permute-start(bf16[384,128]{1,0:T(8,128)(2,1)S(1)} %get-tuple-element.39), channel_id=1, source_target_pairs={{0,2},{2,0},{4,6},{6,4},{8,10},{10,8},{12,14},{14,12},{16,18},{18,... | collective-permute-start | bytes 294920 | tf_op jit(solution)/shard_map/ppermute | solution.py:428
  79.3 4.9 %collective-permute-start.18 = (bf16[384,128]{1,0:T(8,128)(2,1)S(1)}, bf16[384,128]{1,0:T(8,128)(2,1)S(1)}, u32[]{:S(2)}, u32[]{:S(2)}) collective-permute-start(bf16[384,128]{1,0:T(8,128)(2,1)S(1)} %collective-permute-done.11.c_ref), channel_id=1, source_target_pairs={{0,1},{1,0},{2,3},{3,2},{4,5},{5,4},{6,7},{7,6},{8,9},{9,8},{10,11... | collective-permute-start | bytes 294920 | tf_op jit(solution)/shard_map/ppermute | solution.py:434
  79.8 22.1 %collective-permute-start.16 = (bf16[384,1024]{1,0:T(8,128)(2,1)S(1)}, bf16[384,1024]{1,0:T(8,128)(2,1)S(1)}, u32[]{:S(2)}, u32[]{:S(2)}) collective-permute-start(bf16[384,1024]{1,0:T(8,128)(2,1)S(1)} %collective-permute-done.14.refs_3_), channel_id=1, source_target_pairs={{0,2},{2,0},{4,6},{6,4},{8,10},{10,8},{12,14},{14,12},{16,18},{18,... | collective-permute-start | bytes 2359304 | tf_op jit(solution)/shard_map/ppermute | solution.py:428
  79.9 11.6 %collective-permute-start.20 = (bf16[384,512]{1,0:T(8,128)(2,1)S(1)}, bf16[384,512]{1,0:T(8,128)(2,1)S(1)}, u32[]{:S(2)}, u32[]{:S(2)}) collective-permute-start(bf16[384,512]{1,0:T(8,128)(2,1)S(1)} %slice.9), channel_id=1, source_target_pairs={{0,8},{2,10},{4,12},{6,14},{8,0},{10,2},{12,4},{14,6},{16,24},{18,... | collective-permute-start | bytes 1179656 | tf_op jit(solution)/shard_map/ppermute | solution.py:428
  81.0 12.0 %collective-permute-start.13 = (bf16[512,384]{1,0:T(8,128)(2,1)S(1)}, bf16[512,384]{1,0:T(8,128)(2,1)S(1)}, u32[]{:S(2)}, u32[]{:S(2)}) collective-permute-start(bf16[512,384]{1,0:T(8,128)(2,1)S(1)} %shard_map.72.refs_1_), channel_id=1, source_target_pairs={{0,1},{1,0},{2,3},{3,2},{4,5},{5,4},{6,7},{7,6},{8,9},{9,8},{10,11... | collective-permute-start | bytes 1179656 | tf_op jit(solution)/shard_map/ppermute | solution.py:434
  84.1 10.3 %collective-permute-start.19 = (bf16[384,512]{1,0:T(8,128)(2,1)S(1)}, bf16[384,512]{1,0:T(8,128)(2,1)S(1)}, u32[]{:S(2)}, u32[]{:S(2)}) collective-permute-start(bf16[384,512]{1,0:T(8,128)(2,1)S(1)} %slice.8), channel_id=1, source_target_pairs={{0,4},{2,6},{4,0},{6,2},{8,12},{10,14},{12,8},{14,10},{16,20},{18,... | collective-permute-start | bytes 1179656 | tf_op jit(solution)/shard_map/ppermute | solution.py:428
  85.6 21.2 %collective-permute-start.21 = (bf16[384,1024]{1,0:T(8,128)(2,1)S(1)}, bf16[384,1024]{1,0:T(8,128)(2,1)S(1)}, u32[]{:S(2)}, u32[]{:S(2)}) collective-permute-start(bf16[384,1024]{1,0:T(8,128)(2,1)S(1)} %collective-permute-done.4.refs_2_), channel_id=1, source_target_pairs={{0,2},{2,0},{4,6},{6,4},{8,10},{10,8},{12,14},{14,12},{16,18},{18,... | collective-permute-start | bytes 2359304 | tf_op jit(solution)/shard_map/ppermute | solution.py:428
  91.5 15.3 %collective-permute-start.17 = (bf16[512,384]{1,0:T(8,128)(2,1)S(1)}, bf16[512,384]{1,0:T(8,128)(2,1)S(1)}, u32[]{:S(2)}, u32[]{:S(2)}) collective-permute-start(bf16[512,384]{1,0:T(8,128)(2,1)S(1)} %shard_map.74.refs_2_), channel_id=1, source_target_pairs={{0,1},{1,0},{2,3},{3,2},{4,5},{5,4},{6,7},{7,6},{8,9},{9,8},{10,11... | collective-permute-start | bytes 1179656 | tf_op jit(solution)/shard_map/ppermute | solution.py:434
  93.0 13.8 %collective-permute-start.23 = (bf16[384,512]{1,0:T(8,128)(2,1)S(1)}, bf16[384,512]{1,0:T(8,128)(2,1)S(1)}, u32[]{:S(2)}, u32[]{:S(2)}) collective-permute-start(bf16[384,512]{1,0:T(8,128)(2,1)S(1)} %collective-permute-done.20.refs_4_), channel_id=1, source_target_pairs={{0,2},{2,0},{4,6},{6,4},{8,10},{10,8},{12,14},{14,12},{16,18},{18,... | collective-permute-start | bytes 1179656 | tf_op jit(solution)/shard_map/ppermute | solution.py:428
  94.5 12.3 %collective-permute-start.22 = (bf16[384,512]{1,0:T(8,128)(2,1)S(1)}, bf16[384,512]{1,0:T(8,128)(2,1)S(1)}, u32[]{:S(2)}, u32[]{:S(2)}) collective-permute-start(bf16[384,512]{1,0:T(8,128)(2,1)S(1)} %collective-permute-done.19.refs_3_), channel_id=1, source_target_pairs={{0,2},{2,0},{4,6},{6,4},{8,10},{10,8},{12,14},{14,12},{16,18},{18,... | collective-permute-start | bytes 1179656 | tf_op jit(solution)/shard_map/ppermute | solution.py:428
  (10 other events, 144.7 us)

commit v4 on v3

--- a/solution.py
+++ b/solution.py
@@ -126,66 +126,76 @@
     return jnp.where(condition, 1.0, 0.0)
 
 
-def split_states(meta, key, value, doc_count):
+def split_states(meta, key, value, doc_count, slots):
     rows, width = key.shape
     part = width // 4
-
-    def slot(g):
-        return jnp.where(g < 2, 2 * g + 1, 2 * g - 4)
-
-    def kernel(meta_ref, k_ref, v_ref, send_ref, keep_ref):
+    count = len(slots)
+
+    def kernel(meta_ref, k_hbm, v_hbm, o_ref, k_ref, v_ref, sems):
+        copies = []
+        for i, s in enumerate(slots):
+            cols = pl.ds(pl.multiple_of((meta_ref[1] ^ s) * part, DH), part)
+            for n, (source, target) in enumerate(((k_hbm, k_ref), (v_hbm, v_ref))):
+                copies.append(pltpu.make_async_copy(source.at[:, cols], target.at[i], sems.at[i, n]))
+                copies[-1].start()
         offset = meta_ref[0] * rows
         first = doc_start(meta_ref, doc_count, offset + rows - 1) - offset
         live = lax.broadcasted_iota(jnp.int32, (rows, DH), 0) >= first
-        for h in range(part // DH):
-            cols = slice(h * DH, (h + 1) * DH)
-            k = jnp.where(live, k_ref[:, cols], jnp.zeros((), BF16))
-            s = lax.dot_general(k, v_ref[:, cols], (((0,), (0,)), ((), ())), preferred_element_type=F32)
-            s = s.astype(BF16)
-
-            @pl.when(pl.program_id(0) < 2)
-            def _():
-                send_ref[0, cols, :] = s
-
-            @pl.when(pl.program_id(0) >= 2)
-            def _():
-                keep_ref[0, cols, :] = s
-
-    return call(
-        kernel,
-        (4,),
-        [pl.BlockSpec((rows, part), lambda g, m: (0, slot(g) ^ m[1]))] * 2,
+        for i in range(count):
+            copies[2 * i].wait()
+            copies[2 * i + 1].wait()
+            for h in range(part // DH):
+                cols = slice(h * DH, (h + 1) * DH)
+                k = jnp.where(live, k_ref[i, :, cols], jnp.zeros((), BF16))
+                state = lax.dot_general(
+                    k, v_ref[i, :, cols], (((0,), (0,)), ((), ())), preferred_element_type=F32
+                )
+                o_ref[i, cols, :] = state.astype(BF16)
+
+    return call(
+        kernel,
+        (1,),
+        [pl.BlockSpec(memory_space=pltpu.HBM)] * 2,
+        whole((count, part, DH)),
+        jax.ShapeDtypeStruct((count, part, DH), BF16),
+        2 * rows * part * count * DH,
+        2 * 2 * rows * part * count,
         [
-            pl.BlockSpec((1, part, DH), lambda g, m: (jnp.minimum(g, 1), 0, 0)),
-            pl.BlockSpec((1, part, DH), lambda g, m: (jnp.maximum(g - 2, 0), 0, 0)),
+            pltpu.VMEM((count, rows, part), BF16),
+            pltpu.VMEM((count, rows, part), BF16),
+            pltpu.SemaphoreType.DMA((count, 2)),
         ],
-        [jax.ShapeDtypeStruct((2, part, DH), BF16)] * 2,
-        2 * rows * width * DH,
-        2 * 2 * rows * width,
     )(meta, key, value)
 
 
-def within_slots(meta, query, key, value, doc_count, slots, dtype, with_query):
+def seen_mask(meta_ref, rows, doc_count):
+    offset = meta_ref[0] * rows
+    t = lax.broadcasted_iota(jnp.int32, (rows, rows), 0)
+    s = lax.broadcasted_iota(jnp.int32, (rows, rows), 1)
+    pos = lax.broadcasted_iota(jnp.int32, (rows, 1), 0)
+    first = jnp.zeros((rows, 1), jnp.int32)
+    bound = -offset
+    for d in range(doc_count):
+        bound = bound + meta_ref[LENS + d]
+        first = jnp.where(bound <= pos, bound, first)
+    return jnp.where((s <= t) & (s >= first), 1.0, 0.0).astype(BF16)
+
+
+def within_slots(meta, query, key, value, doc_count, slots, mask=None):
     rows, width = query.shape
     part = width // 4
     tile = rows // 2
-
-    def kernel(meta_ref, q_ref, k_ref, v_ref, o_ref, *rest):
-        mask_ref = rest[-1]
-
-        @pl.when(pl.program_id(0) == 0)
-        def _():
-            offset = meta_ref[0] * rows
-            t = lax.broadcasted_iota(jnp.int32, (rows, rows), 0)
-            s = lax.broadcasted_iota(jnp.int32, (rows, rows), 1)
-            pos = lax.broadcasted_iota(jnp.int32, (rows, 1), 0)
-            first = jnp.zeros((rows, 1), jnp.int32)
-            bound = -offset
-            for d in range(doc_count):
-                bound = bound + meta_ref[LENS + d]
-                first = jnp.where(bound <= pos, bound, first)
-            mask_ref[...] = jnp.where((s <= t) & (s >= first), 1.0, 0.0).astype(BF16)
-
+    make = mask is None
+
+    def kernel(meta_ref, q_ref, k_ref, v_ref, *rest):
+        if make:
+            o_ref, mask_ref = rest
+
+            @pl.when(pl.program_id(0) == 0)
+            def _():
+                mask_ref[...] = seen_mask(meta_ref, rows, doc_count)
+        else:
+            mask_ref, o_ref = rest
         for h in range(part // DH):
             cols = slice(h * DH, (h + 1) * DH)
             for i in range(2):
@@ -195,24 +205,22 @@
                     q_ref[r, cols], k_ref[:seen, cols], (((1,), (1,)), ((), ())), preferred_element_type=F32
                 )
                 scores = scores.astype(BF16) * mask_ref[r, :seen]
-                o_ref[r, cols] = jnp.dot(scores, v_ref[:seen, cols], preferred_element_type=F32).astype(dtype)
-        if with_query:
-            rest[0][...] = q_ref[...]
+                o_ref[r, cols] = jnp.dot(scores, v_ref[:seen, cols], preferred_element_type=F32)
 
     count = len(slots)
     spec = pl.BlockSpec((rows, part), lambda g, m: (0, (g + slots[0]) ^ m[1]))
     out = pl.BlockSpec((rows, part), lambda g, m: (0, g))
-    shape = (rows, part * count)
+    shape = jax.ShapeDtypeStruct((rows, part * count), F32)
+    square = whole((rows, rows))
     return call(
         kernel,
         (count,),
-        [spec] * 3,
-        [out] * (1 + with_query),
-        [jax.ShapeDtypeStruct(shape, dtype)] + [jax.ShapeDtypeStruct(shape, BF16)] * with_query,
+        [spec] * 3 + [square] * (not make),
+        [out, square] if make else out,
+        [shape, jax.ShapeDtypeStruct((rows, rows), BF16)] if make else shape,
         3 * rows * rows * part * count,
         10 * rows * part * count,
-        [pltpu.VMEM((rows, rows), BF16)],
-    )(meta, query, key, value)
+    )(meta, query, key, value, *([] if make else [mask]))
 
 
 def small(kernel, meta, arrays, shape, count):
@@ -436,53 +444,48 @@
     def behind(x, *arrays):
         return lax.optimization_barrier((x, *arrays))[0]
 
+    send = split_states(meta, key, value, docs, (1, 3))
+    core_got = swap(send, 1)
+    keep = split_states(after(meta, send), key, value, docs, (0, 2))
+    chip0, chip2 = join_core(meta, keep, core_got, rows, docs)
+    chip_got = swap(chip2, 2)
+
     sent_weight = lax.dynamic_slice(
         weight, (member * part, (1 - group) * columns + side * half), (part, half)
     )
-    far_gain = flip(lax.dynamic_slice(gain, ((member ^ 3) * part,), (part,)))
-    w0 = [flip(sent_weight), None]
-
-    send, keep = split_states(after(meta, sent_weight), key, value, docs)
-    core_got = swap(send, 1)
-    within3, query3 = within_slots(after(meta, send), query, key, value, docs, (3,), BF16, True)
-    far_query, far_within = flip(query3), flip(within3)
-    chip0, chip2 = join_core(after(meta, within3, far_gain), keep, core_got, rows, docs)
-    chip_got = swap(chip2, 2)
-    (within,) = within_slots(after(meta, chip0), query, key, value, docs, (0, 1, 2), F32, False)
-    plane_sum = join_chips(after(meta, within, w0[0]), chip0, chip_got, rows, docs)
+    w0 = [flip(behind(sent_weight, chip2))]
+    within0, mask = within_slots(after(meta, chip0), query, key, value, docs, (0,))
+    plane_sum = join_chips(after(meta, within0), chip0, chip_got, rows, docs)
     near = shift(plane_sum, plane)
-    both = join_planes(after(meta, far_query), plane_sum, near, rows, docs)
+    within1 = within_slots(after(meta, plane_sum), query, key, value, docs, (1,), mask)
+    both = join_planes(after(meta, within1, w0[0]), plane_sum, near, rows, docs)
     w2 = [swap(w0[0], 2)]
     far = shift(both, 2 * plane)
     carry0, core_carry0, chip_carry = carry_first(
-        after(meta, far_within, w2[0]), near, far, chip0, chip_got, keep, core_got, rows, docs
+        meta, near, far, chip0, chip_got, keep, core_got, rows, docs
     )
     carry1 = swap(core_carry0, 1)
     chip_carry2 = swap(chip_carry, 2)
 
-    def norm(slot, carry):
+    def norm(slot, within, carry):
         return norm_heads(
-            meta,
-            query,
-            within3 if slot == 3 else within,
-            carry,
-            gain,
-            docs,
-            (("slot", slot), None if slot == 3 else slot, ("slot", slot)),
+            meta, query, within, carry, gain, docs, (("slot", slot), None, ("slot", slot))
         )
 
-    normed0 = norm(0, carry0)
+    normed0 = norm(0, within0, carry0)
     far0 = flip(normed0)
-    normed1 = norm(1, carry1)
+    normed1 = norm(1, within1, carry1)
     far1 = flip(normed1)
+    within2 = within_slots(after(meta, normed1), query, key, value, docs, (2,), mask)
+    within3 = within_slots(after(meta, within2), query, key, value, docs, (3,), mask)
     carry2, core_carry2 = carry_second(meta, chip_carry2, keep, core_got, rows, docs)
     carry3 = swap(core_carry2, 1)
-    far_carry3 = flip(carry3)
-    normed2 = norm(2, carry2)
-    far2 = flip(behind(normed2, carry3))
-    normed3 = norm(3, carry3)
-
-    w0[1] = swap(behind(w0[0], far), plane)
+    normed2 = norm(2, within2, carry2)
+    far2 = flip(normed2)
+    normed3 = norm(3, within3, carry3)
+    far3 = flip(normed3)
+
+    w0.append(swap(behind(w0[0], far), plane))
     quarter = half // 2
     w2.append(swap(w0[1][:, :quarter], 2))
     w2.append(swap(w2[0][:, quarter:], plane))
@@ -491,8 +494,8 @@
 
     total = project_own(meta, [normed0, normed1, normed2, normed3], weight, columns)
     total = project_more(meta, total, [far0, far1], [w0, w1], F32)
-    far3 = norm_heads(meta, far_query, far_within, far_carry3, far_gain, docs)
-    return project_more(meta, total, [far2, far3], [w2, w3], BF16)
+    total = project_more(meta, total, [far2], [w2], F32)
+    return project_more(meta, total, [far3], [w3], BF16)
 
 
 def body(n_seq, n_head, query, key, value, doc_lengths, gain, weight):

time: 112 us -> 105 us (0.938)
  waiting for transfers between devices: 39.8 us -> 35.6 us
  Pallas kernels: 35.9 us -> 33.9 us
    ppermute x8 -> x5, waiting for transfers between devices: 25.9 us -> 16.1 us  [flip(): return lax.ppermute(x, 'head', [(0, 1), (1, 0)])]
    ppermute x14, waiting for transfers between devices: 9.18 us -> 17.5 us  [swap(): return lax.ppermute(x, 'seq', [(i, i ^ bit) for i in range(n_seq)])]
    ppermute x14, starting transfers between devices: 7.8 us -> 12.7 us  [swap(): return lax.ppermute(x, 'seq', [(i, i ^ bit) for i in range(n_seq)])]
    ppermute x8 -> x5, starting transfers between devices: 11.7 us -> 7.83 us  [flip(): return lax.ppermute(x, 'head', [(0, 1), (1, 0)])]
    ppermute x2, waiting for transfers between devices: 4.79 us -> 2.01 us  [shift(): lax.ppermute(x, 'seq', [(i, i + count) for i in range(n_seq - count)])]
    pallas_call x5 -> x4, Pallas kernels: 6.09 us -> 4.04 us  [norm_heads(): call(kernel, (1,), [pl.BlockSpec((rows, part), block(slots[0])), pl.Block...]
    pallas_call x2 -> x3, Pallas kernels: 9.3 us -> 11.2 us  [project_more(): call(kernel, (TILES,), [out_spec] + [whole((rows, part))] * count + [pl.B...]
    pallas_call x3 -> x6, Pallas kernels: 12 us -> 10.2 us  [the longest x4 7.31 us: within_slots(): call(kernel, (count,), [spec] * 3 + [square] * (not make), [out, square]...]
  transfers between devices with their start and end apart: 24 -> 21, of which waited for: 9 -> 8; matrix products, arithmetic and copies ran while one was open for 1% -> 1% of each run, Pallas kernels for 28% -> 26%
where the time goes in v4:
time: 105 us
  waiting for transfers between devices  35.6 us (34%)
  Pallas kernels  33.9 us (32%)
  starting transfers between devices  28.9 us (28%)
  local copies, waits for them, and re-layouts  6.36 us (6%)
    ppermute x14, waiting for transfers between devices, swap(): return lax.ppermute(x, 'seq', [(i, i ^ bit) for i in range(n_seq)])  17.5 us
    ppermute x5, waiting for transfers between devices, flip(): return lax.ppermute(x, 'head', [(0, 1), (1, 0)])  16.1 us
    ppermute x14, starting transfers between devices, swap(): return lax.ppermute(x, 'seq', [(i, i ^ bit) for i in range(n_seq)])  12.7 us
    pallas_call x3, Pallas kernels, project_more(): call(kernel, (TILES,), [out_spec] + [whole((rows, part))] * count + [pl.B...  11.2 us
    ppermute x2, starting transfers between devices, shift(): lax.ppermute(x, 'seq', [(i, i + count) for i in range(n_seq - count)])  8.38 us
    ppermute x5, starting transfers between devices, flip(): return lax.ppermute(x, 'head', [(0, 1), (1, 0)])  7.83 us
    pallas_call x4, Pallas kernels, within_slots(): call(kernel, (count,), [spec] * 3 + [square] * (not make), [out, square]...  7.31 us
    pallas_call x1, Pallas kernels, project_own(): call(kernel, (TILES,), [whole((rows, part))] * count + [pl.BlockSpec((par...  5.34 us
  transfers between devices with their start and end apart: 21, of which 8 were waited for; matrix products, arithmetic and copies ran while one was open for 1% of the time, Pallas kernels for 26%

profile of v4, /device:TPU:0, one launch (start us, length us, event | category | flops | bytes accessed | tf_op | source)
XLA Modules:
  0.0 105.1 jit_solution(14963750901136106171)
XLA Ops:
  10.4 2.6 %collective-permute-start.3 = (bf16[384,1024]{1,0:T(8,128)(2,1)S(1)}, bf16[384,1024]{1,0:T(8,128)(2,1)S(1)}, u32[]{:S(2)}, u32[]{:S(2)}) collective-permute-start(bf16[384,1024]{1,0:T(8,128)(2,1)S(1)} %dynamic_slice.3), channel_id=1, source_target_pairs={{0,1},{1,0},{2,3},{3,2},{4,5},{5,4},{6,7},{7,6},{8,9},{9,8},{10,11... | collective-permute-start | bytes 2359304 | tf_op jit(solution)/shard_map/ppermute | solution.py:442
  13.0 1.5 %collective-permute-start.1 = (bf16[384,128]{1,0:T(8,128)(2,1)S(1)}, bf16[384,128]{1,0:T(8,128)(2,1)S(1)}, u32[]{:S(2)}, u32[]{:S(2)}) collective-permute-start(bf16[384,128]{1,0:T(8,128)(2,1)S(1)} %get-tuple-element.28), channel_id=1, source_target_pairs={{0,4},{2,6},{4,0},{6,2},{8,12},{10,14},{12,8},{14,10},{16,20},{18,... | collective-permute-start | bytes 294920 | tf_op jit(solution)/shard_map/ppermute | solution.py:436
  14.5 1.9 %shard_map.67 = (f32[512,384]{1,0:T(8,128)S(1)}, bf16[512,512]{1,0:T(8,128)(2,1)S(1)}) custom-call(s32[24]{0:T(128)S(1)} %concatenate.3.meta_ref, bf16[512,1536]{1,0:T(8,128)(2,1)S(1)} %copy-done, bf16[512,1536]{1,0:T(8,128)(2,1)S(1)} %copy-done.2, bf16[512,1536]{1,0:T(8,128)(2,1)S(1)} %copy-done.5), custom_call_target="tpu_custom_call" | custom-call | flops 301989888 | bytes 1966080 | tf_op jit(solution)/shard_map/pallas_call | solution.py:215
  18.5 3.5 %collective-permute-start.2 = (bf16[384,128]{1,0:T(8,128)(2,1)S(1)}, bf16[384,128]{1,0:T(8,128)(2,1)S(1)}, u32[]{:S(2)}, u32[]{:S(2)}) collective-permute-start(bf16[384,128]{1,0:T(8,128)(2,1)S(1)} %shard_map.68.a_ref), channel_id=1, source_target_pairs={{0,8},{2,10},{4,12},{6,14},{8,16},{10,18},{12,20},{14,22},{16,24},... | collective-permute-start | bytes 294920 | tf_op jit(solution)/shard_map/ppermute | solution.py:439
  22.0 1.8 %shard_map.69.w_ref = f32[512,384]{1,0:T(8,128)S(1)} custom-call(s32[24]{0:T(128)S(1)} %concatenate.3.meta_ref, bf16[512,1536]{1,0:T(8,128)(2,1)S(1)} %copy-done, bf16[512,1536]{1,0:T(8,128)(2,1)S(1)} %copy-done.2, bf16[512,1536]{1,0:T(8,128)(2,1)S(1)} %copy-done.5, bf16[512,512]{1,0:T(8,128)(2,1)S(1)} %get-tuple-element.30.rest_0_), custom_call_target="tpu_custom_call" | custom-call | flops 301989888 | bytes 1966080 | tf_op jit(solution)/shard_map/pallas_call | solution.py:215
  23.8 7.4 %collective-permute-done.3.refs_2_ = bf16[384,1024]{1,0:T(8,128)(2,1)S(1)} collective-permute-done((bf16[384,1024]{1,0:T(8,128)(2,1)S(1)}, bf16[384,1024]{1,0:T(8,128)(2,1)S(1)}, u32[]{:S(2)}, u32[]{:S(2)}) %collective-permute-start.3) | collective-permute-done | bytes 786464 | tf_op jit(solution)/shard_map/ppermute | solution.py:442
  31.7 4.9 %collective-permute-start.4 = (bf16[384,128]{1,0:T(8,128)(2,1)S(1)}, bf16[384,128]{1,0:T(8,128)(2,1)S(1)}, u32[]{:S(2)}, u32[]{:S(2)}) collective-permute-start(bf16[384,128]{1,0:T(8,128)(2,1)S(1)} %shard_map.70), channel_id=1, source_target_pairs={{0,16},{2,18},{4,20},{6,22},{8,24},{10,26},{12,28},{14,30},{1,17},... | collective-permute-start | bytes 294920 | tf_op jit(solution)/shard_map/ppermute | solution.py:439
  36.7 2.0 %collective-permute-done.4.far_ref = bf16[384,128]{1,0:T(8,128)(2,1)S(1)} collective-permute-done((bf16[384,128]{1,0:T(8,128)(2,1)S(1)}, bf16[384,128]{1,0:T(8,128)(2,1)S(1)}, u32[]{:S(2)}, u32[]{:S(2)}) %collective-permute-start.4) | collective-permute-done | bytes 98336 | tf_op jit(solution)/shard_map/ppermute | solution.py:439
  38.7 3.3 %collective-permute-start.10 = (bf16[384,1024]{1,0:T(8,128)(2,1)S(1)}, bf16[384,1024]{1,0:T(8,128)(2,1)S(1)}, u32[]{:S(2)}, u32[]{:S(2)}) collective-permute-start(bf16[384,1024]{1,0:T(8,128)(2,1)S(1)} %collective-permute-done.3.refs_2_), channel_id=1, source_target_pairs={{0,8},{2,10},{4,12},{6,14},{8,0},{10,2},{12,4},{14,6},{16,24},{18,... | collective-permute-start | bytes 2359304 | tf_op jit(solution)/shard_map/ppermute | solution.py:436
  45.8 1.6 %collective-permute-start.8 = (bf16[512,384]{1,0:T(8,128)(2,1)S(1)}, bf16[512,384]{1,0:T(8,128)(2,1)S(1)}, u32[]{:S(2)}, u32[]{:S(2)}) collective-permute-start(bf16[512,384]{1,0:T(8,128)(2,1)S(1)} %shard_map.72.refs_0_), channel_id=1, source_target_pairs={{0,1},{1,0},{2,3},{3,2},{4,5},{5,4},{6,7},{7,6},{8,9},{9,8},{10,11... | collective-permute-start | bytes 1179656 | tf_op jit(solution)/shard_map/ppermute | solution.py:442
  47.4 12.1 %collective-permute-done.10.refs_3_ = bf16[384,1024]{1,0:T(8,128)(2,1)S(1)} collective-permute-done((bf16[384,1024]{1,0:T(8,128)(2,1)S(1)}, bf16[384,1024]{1,0:T(8,128)(2,1)S(1)}, u32[]{:S(2)}, u32[]{:S(2)}) %collective-permute-start.10) | collective-permute-done | bytes 786464 | tf_op jit(solution)/shard_map/ppermute | solution.py:436
  62.0 2.7 %collective-permute-done.6.chip_ref = bf16[384,128]{1,0:T(8,128)(2,1)S(1)} collective-permute-done((bf16[384,128]{1,0:T(8,128)(2,1)S(1)}, bf16[384,128]{1,0:T(8,128)(2,1)S(1)}, u32[]{:S(2)}, u32[]{:S(2)}) %collective-permute-start.6) | collective-permute-done | bytes 98336 | tf_op jit(solution)/shard_map/ppermute | solution.py:436
  64.7 1.5 %collective-permute-start.9 = (bf16[512,384]{1,0:T(8,128)(2,1)S(1)}, bf16[512,384]{1,0:T(8,128)(2,1)S(1)}, u32[]{:S(2)}, u32[]{:S(2)}) collective-permute-start(bf16[512,384]{1,0:T(8,128)(2,1)S(1)} %shard_map.73.refs_1_), channel_id=1, source_target_pairs={{0,1},{1,0},{2,3},{3,2},{4,5},{5,4},{6,7},{7,6},{8,9},{9,8},{10,11... | collective-permute-start | bytes 1179656 | tf_op jit(solution)/shard_map/ppermute | solution.py:442
  68.2 1.7 %collective-permute-start.16 = (bf16[384,512]{1,0:T(8,128)(2,1)S(1)}, bf16[384,512]{1,0:T(8,128)(2,1)S(1)}, u32[]{:S(2)}, u32[]{:S(2)}) collective-permute-start(bf16[384,512]{1,0:T(8,128)(2,1)S(1)} %slice.9), channel_id=1, source_target_pairs={{0,8},{2,10},{4,12},{6,14},{8,0},{10,2},{12,4},{14,6},{16,24},{18,... | collective-permute-start | bytes 1179656 | tf_op jit(solution)/shard_map/ppermute | solution.py:436
  70.0 1.5 %collective-permute-start.15 = (bf16[384,512]{1,0:T(8,128)(2,1)S(1)}, bf16[384,512]{1,0:T(8,128)(2,1)S(1)}, u32[]{:S(2)}, u32[]{:S(2)}) collective-permute-start(bf16[384,512]{1,0:T(8,128)(2,1)S(1)} %slice.8), channel_id=1, source_target_pairs={{0,4},{2,6},{4,0},{6,2},{8,12},{10,14},{12,8},{14,10},{16,20},{18,... | collective-permute-start | bytes 1179656 | tf_op jit(solution)/shard_map/ppermute | solution.py:436
  71.5 4.0 %collective-permute-done.9.refs_1_ = bf16[512,384]{1,0:T(8,128)(2,1)S(1)} collective-permute-done((bf16[512,384]{1,0:T(8,128)(2,1)S(1)}, bf16[512,384]{1,0:T(8,128)(2,1)S(1)}, u32[]{:S(2)}, u32[]{:S(2)}) %collective-permute-start.9) | collective-permute-done | bytes 393248 | tf_op jit(solution)/shard_map/ppermute | solution.py:442
  75.5 1.8 %shard_map.74.w_ref = f32[512,384]{1,0:T(8,128)S(1)} custom-call(s32[24]{0:T(128)S(1)} %concatenate.3.meta_ref, bf16[512,1536]{1,0:T(8,128)(2,1)S(1)} %copy-done, bf16[512,1536]{1,0:T(8,128)(2,1)S(1)} %copy-done.2, bf16[512,1536]{1,0:T(8,128)(2,1)S(1)} %copy-done.5, bf16[512,512]{1,0:T(8,128)(2,1)S(1)} %get-tuple-element.30.rest_0_), custom_call_target="tpu_custom_call" | custom-call | flops 301989888 | bytes 1966080 | tf_op jit(solution)/shard_map/pallas_call | solution.py:215
  78.3 1.8 %shard_map.77.w_ref = f32[512,384]{1,0:T(8,128)S(1)} custom-call(s32[24]{0:T(128)S(1)} %concatenate.3.meta_ref, bf16[512,1536]{1,0:T(8,128)(2,1)S(1)} %copy-done, bf16[512,1536]{1,0:T(8,128)(2,1)S(1)} %copy-done.2, bf16[512,1536]{1,0:T(8,128)(2,1)S(1)} %copy-done.5, bf16[512,512]{1,0:T(8,128)(2,1)S(1)} %get-tuple-element.30.rest_0_), custom_call_target="tpu_custom_call" | custom-call | flops 301989888 | bytes 1966080 | tf_op jit(solution)/shard_map/pallas_call | solution.py:215
  81.1 1.6 %collective-permute-start.13 = (bf16[512,384]{1,0:T(8,128)(2,1)S(1)}, bf16[512,384]{1,0:T(8,128)(2,1)S(1)}, u32[]{:S(2)}, u32[]{:S(2)}) collective-permute-start(bf16[512,384]{1,0:T(8,128)(2,1)S(1)} %shard_map.76.refs_2_), channel_id=1, source_target_pairs={{0,1},{1,0},{2,3},{3,2},{4,5},{5,4},{6,7},{7,6},{8,9},{9,8},{10,11... | collective-permute-start | bytes 1179656 | tf_op jit(solution)/shard_map/ppermute | solution.py:442
  83.8 5.3 %shard_map.79.t_ref = f32[512,2048]{1,0:T(8,128)S(1)} custom-call(s32[24]{0:T(128)S(1)} %concatenate.3.meta_ref, bf16[512,384]{1,0:T(8,128)(2,1)S(1)} %shard_map.72.refs_0_, bf16[512,384]{1,0:T(8,128)(2,1)S(1)} %shard_map.73.refs_1_, bf16[512,384]{1,0:T(8,128)(2,1)S(1)} %shard_map.76.refs_2_, bf16[512,384]{1,0:T(8,128)(2,1)S(1)} %shard_map.78.refs_3_, ...), custom_call_target="tpu_custom_call" | custom-call | flops 3221225472 | bytes 10485760 | tf_op jit(solution)/shard_map/pallas_call | solution.py:368
  89.1 4.1 %shard_map.80.t_ref = f32[512,2048]{1,0:T(8,128)S(1)} custom-call(s32[24]{0:T(128)S(1)} %concatenate.3.meta_ref, f32[512,2048]{1,0:T(8,128)S(1)} %shard_map.79.t_ref, bf16[512,384]{1,0:T(8,128)(2,1)S(1)} %collective-permute-done.8.refs_0_, bf16[512,384]{1,0:T(8,128)(2,1)S(1)} %collective-permute-done.9.refs_1_, ...), custom_call_target="tpu_custom_call" | custom-call | flops 1610612736 | bytes 9437184 | tf_op jit(solution)/shard_map/pallas_call | solution.py:408
  93.2 3.2 %shard_map.81.t_ref = f32[512,2048]{1,0:T(8,128)S(1)} custom-call(s32[24]{0:T(128)S(1)} %concatenate.3.meta_ref, f32[512,2048]{1,0:T(8,128)S(1)} %shard_map.80.t_ref, bf16[512,384]{1,0:T(8,128)(2,1)S(1)} %collective-permute-done.13.refs_0_, bf16[384,1024]{1,0:T(8,128)(2,1)S(1)} %collective-permute-done.14.refs_1_, ...), custom_call_target="tpu_custom_call" | custom-call | flops 805306368 | bytes 7864320 | tf_op jit(solution)/shard_map/pallas_call | solution.py:408
  96.4 4.7 %collective-permute-done.17.refs_0_ = bf16[512,384]{1,0:T(8,128)(2,1)S(1)} collective-permute-done((bf16[512,384]{1,0:T(8,128)(2,1)S(1)}, bf16[512,384]{1,0:T(8,128)(2,1)S(1)}, u32[]{:S(2)}, u32[]{:S(2)}) %collective-permute-start.17) | collective-permute-done | bytes 393248 | tf_op jit(solution)/shard_map/ppermute | solution.py:442
  101.2 3.9 %shard_map.82 = bf16[512,2048]{1,0:T(8,128)(2,1)} custom-call(s32[24]{0:T(128)S(1)} %concatenate.3.meta_ref, f32[512,2048]{1,0:T(8,128)S(1)} %shard_map.81.t_ref, bf16[512,384]{1,0:T(8,128)(2,1)S(1)} %collective-permute-done.17.refs_0_, bf16[384,1024]{1,0:T(8,128)(2,1)S(1)} %collective-permute-done.18.refs_1_, ...), custom_call_target="tpu_custom_call" | custom-call | flops 805306368 | bytes 7864320 | tf_op jit(solution)/shard_map/pallas_call | solution.py:408
  (64 shorter events, 24.3 us)
Async XLA Ops:
  5.0 4.7 %collective-permute-start = (bf16[2,384,128]{2,1,0:T(8,128)(2,1)S(1)}, bf16[2,384,128]{2,1,0:T(8,128)(2,1)S(1)}, u32[]{:S(2)}, u32[]{:S(2)}) collective-permute-start(bf16[2,384,128]{2,1,0:T(8,128)(2,1)S(1)} %shard_map.64), channel_id=1, source_target_pairs={{0,2},{2,0},{4,6},{6,4},{8,10},{10,8},{12,14},{14,12},{16,18},{18,... | collective-permute-start | bytes 589832 | tf_op jit(solution)/shard_map/ppermute | solution.py:436
  10.4 20.8 %collective-permute-start.3 = (bf16[384,1024]{1,0:T(8,128)(2,1)S(1)}, bf16[384,1024]{1,0:T(8,128)(2,1)S(1)}, u32[]{:S(2)}, u32[]{:S(2)}) collective-permute-start(bf16[384,1024]{1,0:T(8,128)(2,1)S(1)} %dynamic_slice.3), channel_id=1, source_target_pairs={{0,1},{1,0},{2,3},{3,2},{4,5},{5,4},{6,7},{7,6},{8,9},{9,8},{10,11... | collective-permute-start | bytes 2359304 | tf_op jit(solution)/shard_map/ppermute | solution.py:442
  13.0 4.9 %collective-permute-start.1 = (bf16[384,128]{1,0:T(8,128)(2,1)S(1)}, bf16[384,128]{1,0:T(8,128)(2,1)S(1)}, u32[]{:S(2)}, u32[]{:S(2)}) collective-permute-start(bf16[384,128]{1,0:T(8,128)(2,1)S(1)} %get-tuple-element.28), channel_id=1, source_target_pairs={{0,4},{2,6},{4,0},{6,2},{8,12},{10,14},{12,8},{14,10},{16,20},{18,... | collective-permute-start | bytes 294920 | tf_op jit(solution)/shard_map/ppermute | solution.py:436
  16.4 27.8 %copy-start.6 = (f32[1536]{0:T(1024)S(1)}, f32[1536]{0:T(1024)}, u32[]{:S(2)}) copy-start(f32[1536]{0:T(1024)} %param.10) | copy-start | bytes 18436
  18.5 12.7 %collective-permute-start.2 = (bf16[384,128]{1,0:T(8,128)(2,1)S(1)}, bf16[384,128]{1,0:T(8,128)(2,1)S(1)}, u32[]{:S(2)}, u32[]{:S(2)}) collective-permute-start(bf16[384,128]{1,0:T(8,128)(2,1)S(1)} %shard_map.68.a_ref), channel_id=1, source_target_pairs={{0,8},{2,10},{4,12},{6,14},{8,16},{10,18},{12,20},{14,22},{16,24},... | collective-permute-start | bytes 294920 | tf_op jit(solution)/shard_map/ppermute | solution.py:439
  31.7 6.9 %collective-permute-start.4 = (bf16[384,128]{1,0:T(8,128)(2,1)S(1)}, bf16[384,128]{1,0:T(8,128)(2,1)S(1)}, u32[]{:S(2)}, u32[]{:S(2)}) collective-permute-start(bf16[384,128]{1,0:T(8,128)(2,1)S(1)} %shard_map.70), channel_id=1, source_target_pairs={{0,16},{2,18},{4,20},{6,22},{8,24},{10,26},{12,28},{14,30},{1,17},... | collective-permute-start | bytes 294920 | tf_op jit(solution)/shard_map/ppermute | solution.py:439
  38.7 20.8 %collective-permute-start.10 = (bf16[384,1024]{1,0:T(8,128)(2,1)S(1)}, bf16[384,1024]{1,0:T(8,128)(2,1)S(1)}, u32[]{:S(2)}, u32[]{:S(2)}) collective-permute-start(bf16[384,1024]{1,0:T(8,128)(2,1)S(1)} %collective-permute-done.3.refs_2_), channel_id=1, source_target_pairs={{0,8},{2,10},{4,12},{6,14},{8,0},{10,2},{12,4},{14,6},{16,24},{18,... | collective-permute-start | bytes 2359304 | tf_op jit(solution)/shard_map/ppermute | solution.py:436
  41.9 24.9 %collective-permute-start.14 = (bf16[384,1024]{1,0:T(8,128)(2,1)S(1)}, bf16[384,1024]{1,0:T(8,128)(2,1)S(1)}, u32[]{:S(2)}, u32[]{:S(2)}) collective-permute-start(bf16[384,1024]{1,0:T(8,128)(2,1)S(1)} %collective-permute-done.3.refs_2_), channel_id=1, source_target_pairs={{0,4},{2,6},{4,0},{6,2},{8,12},{10,14},{12,8},{14,10},{16,20},{18,... | collective-permute-start | bytes 2359304 | tf_op jit(solution)/shard_map/ppermute | solution.py:436
  44.1 15.4 %collective-permute-start.5 = (bf16[384,128]{1,0:T(8,128)(2,1)S(1)}, bf16[384,128]{1,0:T(8,128)(2,1)S(1)}, u32[]{:S(2)}, u32[]{:S(2)}) collective-permute-start(bf16[384,128]{1,0:T(8,128)(2,1)S(1)} %get-tuple-element.34), channel_id=1, source_target_pairs={{0,2},{2,0},{4,6},{6,4},{8,10},{10,8},{12,14},{14,12},{16,18},{18,... | collective-permute-start | bytes 294920 | tf_op jit(solution)/shard_map/ppermute | solution.py:436
  44.2 36.9 %collective-permute-start.11 = (bf16[384,1024]{1,0:T(8,128)(2,1)S(1)}, bf16[384,1024]{1,0:T(8,128)(2,1)S(1)}, u32[]{:S(2)}, u32[]{:S(2)}) collective-permute-start(bf16[384,1024]{1,0:T(8,128)(2,1)S(1)} %collective-permute-done.3.refs_2_), channel_id=1, source_target_pairs={{0,2},{2,0},{4,6},{6,4},{8,10},{10,8},{12,14},{14,12},{16,18},{18,... | collective-permute-start | bytes 2359304 | tf_op jit(solution)/shard_map/ppermute | solution.py:436
  45.8 24.2 %collective-permute-start.8 = (bf16[512,384]{1,0:T(8,128)(2,1)S(1)}, bf16[512,384]{1,0:T(8,128)(2,1)S(1)}, u32[]{:S(2)}, u32[]{:S(2)}) collective-permute-start(bf16[512,384]{1,0:T(8,128)(2,1)S(1)} %shard_map.72.refs_0_), channel_id=1, source_target_pairs={{0,1},{1,0},{2,3},{3,2},{4,5},{5,4},{6,7},{7,6},{8,9},{9,8},{10,11... | collective-permute-start | bytes 1179656 | tf_op jit(solution)/shard_map/ppermute | solution.py:442
  59.5 23.8 %collective-permute-start.12 = (bf16[384,1024]{1,0:T(8,128)(2,1)S(1)}, bf16[384,1024]{1,0:T(8,128)(2,1)S(1)}, u32[]{:S(2)}, u32[]{:S(2)}) collective-permute-start(bf16[384,1024]{1,0:T(8,128)(2,1)S(1)} %collective-permute-done.10.refs_3_), channel_id=1, source_target_pairs={{0,2},{2,0},{4,6},{6,4},{8,10},{10,8},{12,14},{14,12},{16,18},{18,... | collective-permute-start | bytes 2359304 | tf_op jit(solution)/shard_map/ppermute | solution.py:436
  59.5 5.2 %collective-permute-start.6 = (bf16[384,128]{1,0:T(8,128)(2,1)S(1)}, bf16[384,128]{1,0:T(8,128)(2,1)S(1)}, u32[]{:S(2)}, u32[]{:S(2)}) collective-permute-start(bf16[384,128]{1,0:T(8,128)(2,1)S(1)} %get-tuple-element.36), channel_id=1, source_target_pairs={{0,4},{2,6},{4,0},{6,2},{8,12},{10,14},{12,8},{14,10},{16,20},{18,... | collective-permute-start | bytes 294920 | tf_op jit(solution)/shard_map/ppermute | solution.py:436
  61.0 22.8 %slice-start = ((s8[12582912]{0:T(1024)(128)(4,1)}), s8[4194304]{0:T(1024)(128)(4,1)S(1)}, s32[]{:S(2)}) async-start(s8[12582912]{0:T(1024)(128)(4,1)} %bitcast.4), calls=%async_computation | async-start | bytes 8388608
  64.7 10.7 %collective-permute-start.9 = (bf16[512,384]{1,0:T(8,128)(2,1)S(1)}, bf16[512,384]{1,0:T(8,128)(2,1)S(1)}, u32[]{:S(2)}, u32[]{:S(2)}) collective-permute-start(bf16[512,384]{1,0:T(8,128)(2,1)S(1)} %shard_map.73.refs_1_), channel_id=1, source_target_pairs={{0,1},{1,0},{2,3},{3,2},{4,5},{5,4},{6,7},{7,6},{8,9},{9,8},{10,11... | collective-permute-start | bytes 1179656 | tf_op jit(solution)/shard_map/ppermute | solution.py:442
  66.9 1.4 %collective-permute-start.7 = (bf16[384,128]{1,0:T(8,128)(2,1)S(1)}, bf16[384,128]{1,0:T(8,128)(2,1)S(1)}, u32[]{:S(2)}, u32[]{:S(2)}) collective-permute-start(bf16[384,128]{1,0:T(8,128)(2,1)S(1)} %get-tuple-element.39), channel_id=1, source_target_pairs={{0,2},{2,0},{4,6},{6,4},{8,10},{10,8},{12,14},{14,12},{16,18},{18,... | collective-permute-start | bytes 294920 | tf_op jit(solution)/shard_map/ppermute | solution.py:436
  67.0 16.8 %slice-start.1 = ((s8[12582912]{0:T(1024)(128)(4,1)}), s8[4194304]{0:T(1024)(128)(4,1)S(1)}, s32[]{:S(2)}) async-start(s8[12582912]{0:T(1024)(128)(4,1)} %bitcast.4), calls=%async_computation.1 | async-start | bytes 8388608
  68.2 14.5 %collective-permute-start.16 = (bf16[384,512]{1,0:T(8,128)(2,1)S(1)}, bf16[384,512]{1,0:T(8,128)(2,1)S(1)}, u32[]{:S(2)}, u32[]{:S(2)}) collective-permute-start(bf16[384,512]{1,0:T(8,128)(2,1)S(1)} %slice.9), channel_id=1, source_target_pairs={{0,8},{2,10},{4,12},{6,14},{8,0},{10,2},{12,4},{14,6},{16,24},{18,... | collective-permute-start | bytes 1179656 | tf_op jit(solution)/shard_map/ppermute | solution.py:436
  70.0 13.3 %collective-permute-start.15 = (bf16[384,512]{1,0:T(8,128)(2,1)S(1)}, bf16[384,512]{1,0:T(8,128)(2,1)S(1)}, u32[]{:S(2)}, u32[]{:S(2)}) collective-permute-start(bf16[384,512]{1,0:T(8,128)(2,1)S(1)} %slice.8), channel_id=1, source_target_pairs={{0,4},{2,6},{4,0},{6,2},{8,12},{10,14},{12,8},{14,10},{16,20},{18,... | collective-permute-start | bytes 1179656 | tf_op jit(solution)/shard_map/ppermute | solution.py:436
  75.5 25.7 %collective-permute-start.18 = (bf16[384,1024]{1,0:T(8,128)(2,1)S(1)}, bf16[384,1024]{1,0:T(8,128)(2,1)S(1)}, u32[]{:S(2)}, u32[]{:S(2)}) collective-permute-start(bf16[384,1024]{1,0:T(8,128)(2,1)S(1)} %collective-permute-done.14.refs_1_), channel_id=1, source_target_pairs={{0,2},{2,0},{4,6},{6,4},{8,10},{10,8},{12,14},{14,12},{16,18},{18,... | collective-permute-start | bytes 2359304 | tf_op jit(solution)/shard_map/ppermute | solution.py:436
  81.1 12.1 %collective-permute-start.13 = (bf16[512,384]{1,0:T(8,128)(2,1)S(1)}, bf16[512,384]{1,0:T(8,128)(2,1)S(1)}, u32[]{:S(2)}, u32[]{:S(2)}) collective-permute-start(bf16[512,384]{1,0:T(8,128)(2,1)S(1)} %shard_map.76.refs_2_), channel_id=1, source_target_pairs={{0,1},{1,0},{2,3},{3,2},{4,5},{5,4},{6,7},{7,6},{8,9},{9,8},{10,11... | collective-permute-start | bytes 1179656 | tf_op jit(solution)/shard_map/ppermute | solution.py:442
  82.7 18.4 %collective-permute-start.17 = (bf16[512,384]{1,0:T(8,128)(2,1)S(1)}, bf16[512,384]{1,0:T(8,128)(2,1)S(1)}, u32[]{:S(2)}, u32[]{:S(2)}) collective-permute-start(bf16[512,384]{1,0:T(8,128)(2,1)S(1)} %shard_map.78.refs_3_), channel_id=1, source_target_pairs={{0,1},{1,0},{2,3},{3,2},{4,5},{5,4},{6,7},{7,6},{8,9},{9,8},{10,11... | collective-permute-start | bytes 1179656 | tf_op jit(solution)/shard_map/ppermute | solution.py:442
  83.2 17.9 %collective-permute-start.20 = (bf16[384,512]{1,0:T(8,128)(2,1)S(1)}, bf16[384,512]{1,0:T(8,128)(2,1)S(1)}, u32[]{:S(2)}, u32[]{:S(2)}) collective-permute-start(bf16[384,512]{1,0:T(8,128)(2,1)S(1)} %collective-permute-done.16.refs_3_), channel_id=1, source_target_pairs={{0,2},{2,0},{4,6},{6,4},{8,10},{10,8},{12,14},{14,12},{16,18},{18,... | collective-permute-start | bytes 1179656 | tf_op jit(solution)/shard_map/ppermute | solution.py:436
  83.2 17.9 %collective-permute-start.19 = (bf16[384,512]{1,0:T(8,128)(2,1)S(1)}, bf16[384,512]{1,0:T(8,128)(2,1)S(1)}, u32[]{:S(2)}, u32[]{:S(2)}) collective-permute-start(bf16[384,512]{1,0:T(8,128)(2,1)S(1)} %collective-permute-done.15.refs_2_), channel_id=1, source_target_pairs={{0,2},{2,0},{4,6},{6,4},{8,10},{10,8},{12,14},{14,12},{16,18},{18,... | collective-permute-start | bytes 1179656 | tf_op jit(solution)/shard_map/ppermute | solution.py:436
  (7 other events, 32.8 us)

commit v5 on v4

--- a/solution.py
+++ b/solution.py
@@ -12,6 +12,7 @@
 F32, BF16 = jnp.float32, jnp.bfloat16
 LENS = 8
 VMEM_LIMIT = 16 * 1024 * 1024
+VMEM_MOST = 60 * 1024 * 1024
 
 
 def doc_start(meta, doc_count, token):
@@ -23,7 +24,7 @@
     return start
 
 
-def call(kernel, grid, in_specs, out_specs, out_shape, flops, bytes_accessed, scratch=()):
+def call(kernel, grid, in_specs, out_specs, out_shape, flops, bytes_accessed, scratch=(), vmem=VMEM_LIMIT):
     return pl.pallas_call(
         kernel,
         grid_spec=pltpu.PrefetchScalarGridSpec(
@@ -34,7 +35,7 @@
             scratch_shapes=scratch,
         ),
         out_shape=out_shape,
-        compiler_params=pltpu.CompilerParams(vmem_limit_bytes=VMEM_LIMIT),
+        compiler_params=pltpu.CompilerParams(vmem_limit_bytes=vmem),
         cost_estimate=pl.CostEstimate(flops=flops, bytes_accessed=bytes_accessed, transcendentals=0),
     )
 
@@ -165,6 +166,7 @@
             pltpu.VMEM((count, rows, part), BF16),
             pltpu.SemaphoreType.DMA((count, 2)),
         ],
+        VMEM_MOST,
     )(meta, key, value)
 
 
@@ -453,16 +455,15 @@
     sent_weight = lax.dynamic_slice(
         weight, (member * part, (1 - group) * columns + side * half), (part, half)
     )
-    w0 = [flip(behind(sent_weight, chip2))]
     within0, mask = within_slots(after(meta, chip0), query, key, value, docs, (0,))
+    w0 = [flip(behind(sent_weight, within0))]
     plane_sum = join_chips(after(meta, within0), chip0, chip_got, rows, docs)
     near = shift(plane_sum, plane)
     within1 = within_slots(after(meta, plane_sum), query, key, value, docs, (1,), mask)
-    both = join_planes(after(meta, within1, w0[0]), plane_sum, near, rows, docs)
-    w2 = [swap(w0[0], 2)]
+    both = join_planes(after(meta, within1), plane_sum, near, rows, docs)
     far = shift(both, 2 * plane)
     carry0, core_carry0, chip_carry = carry_first(
-        meta, near, far, chip0, chip_got, keep, core_got, rows, docs
+        after(meta, w0[0]), near, far, chip0, chip_got, keep, core_got, rows, docs
     )
     carry1 = swap(core_carry0, 1)
     chip_carry2 = swap(chip_carry, 2)
@@ -485,11 +486,13 @@
     normed3 = norm(3, within3, carry3)
     far3 = flip(normed3)
 
-    w0.append(swap(behind(w0[0], far), plane))
+    held = behind(w0[0], normed0)
+    w0.append(behind(swap(held, plane), normed3))
+    w2 = [behind(swap(behind(w0[0], chip_carry2), 2), normed3)]
     quarter = half // 2
     w2.append(swap(w0[1][:, :quarter], 2))
     w2.append(swap(w2[0][:, quarter:], plane))
-    w1 = [swap(w, 1) for w in w0]
+    w1 = [swap(held, 1), swap(w0[1], 1)]
     w3 = [swap(w, 1) for w in w2]
 
     total = project_own(meta, [normed0, normed1, normed2, normed3], weight, columns)

time: 105 us -> 95.1 us (0.906)
  waiting for transfers between devices: 35.6 us -> 26 us
  starting transfers between devices: 28.9 us -> 25 us
  Pallas kernels: 33.9 us -> 37.6 us
    ppermute x5, waiting for transfers between devices: 16.1 us -> 8.88 us  [flip(): return lax.ppermute(x, 'head', [(0, 1), (1, 0)])]
    pallas_call x2, Pallas kernels: 2.87 us -> 6.54 us  [split_states(): call(kernel, (1,), [pl.BlockSpec(memory_space=pltpu.HBM)] * 2, whole((cou...]
    ppermute x14, starting transfers between devices: 12.7 us -> 10.2 us  [swap(): return lax.ppermute(x, 'seq', [(i, i ^ bit) for i in range(n_seq)])]
    ppermute x5, starting transfers between devices: 7.83 us -> 5.76 us  [flip(): return lax.ppermute(x, 'head', [(0, 1), (1, 0)])]
    unnamed x20 -> x24, local copies, waits for them, and re-layouts: 4.26 us -> 2.37 us
    ppermute x14, waiting for transfers between devices: 17.5 us -> 15.6 us  [swap(): return lax.ppermute(x, 'seq', [(i, i ^ bit) for i in range(n_seq)])]
  transfers between devices with their start and end apart: 21 -> 21, of which waited for: 8 -> 11; matrix products, arithmetic and copies ran while one was open for 1% -> 2% of each run, Pallas kernels for 26% -> 27%
where the time goes in v5:
time: 95.1 us; the launch traced here: 94.8 us
  Pallas kernels  37.6 us (40%)
  waiting for transfers between devices  26 us (27%)
  starting transfers between devices  25 us (26%)
  local copies, waits for them, and re-layouts  5.82 us (6%)
    ppermute x14, waiting for transfers between devices, swap(): return lax.ppermute(x, 'seq', [(i, i ^ bit) for i in range(n_seq)])  15.6 us
    pallas_call x3, Pallas kernels, project_more(): call(kernel, (TILES,), [out_spec] + [whole((rows, part))] * count + [pl.B...  11.2 us
    ppermute x14, starting transfers between devices, swap(): return lax.ppermute(x, 'seq', [(i, i ^ bit) for i in range(n_seq)])  10.2 us
    ppermute x2, starting transfers between devices, shift(): lax.ppermute(x, 'seq', [(i, i + count) for i in range(n_seq - count)])  8.99 us
    ppermute x5, waiting for transfers between devices, flip(): return lax.ppermute(x, 'head', [(0, 1), (1, 0)])  8.88 us
    pallas_call x4, Pallas kernels, within_slots(): call(kernel, (count,), [spec] * 3 + [square] * (not make), [out, square]...  7.29 us
    pallas_call x2, Pallas kernels, split_states(): call(kernel, (1,), [pl.BlockSpec(memory_space=pltpu.HBM)] * 2, whole((cou...  6.54 us
    ppermute x5, starting transfers between devices, flip(): return lax.ppermute(x, 'head', [(0, 1), (1, 0)])  5.76 us
  transfers between devices with their start and end apart: 21, of which 11 were waited for; matrix products, arithmetic and copies ran while one was open for 2% of the time, Pallas kernels for 27%

profile of v5, /device:TPU:0, one launch (start us, length us, event | category | flops | bytes accessed | tf_op | source)
XLA Modules:
  0.0 94.8 jit_solution(4928651485020787327)
XLA Ops:
  1.3 3.4 %shard_map.64 = bf16[2,384,128]{2,1,0:T(8,128)(2,1)} custom-call(s32[24]{0:T(128)} %concatenate.3.meta_ref, bf16[512,1536]{1,0:T(8,128)(2,1)} %k_ref.7, bf16[512,1536]{1,0:T(8,128)(2,1)} %v_ref.7), custom_call_target="tpu_custom_call" | custom-call | flops 100663296 | bytes 1572864 | tf_op jit(solution)/shard_map/pallas_call | solution.py:156
  5.3 2.1 %dynamic_slice.3 = bf16[384,1024]{1,0:T(8,128)(2,1)} dynamic-slice(bf16[1536,4096]{1,0:T(8,128)(2,1)} %refs_7_.1, s32[]{:T(128)S(6)} %select_n.24, s32[]{:T(128)S(6)} %select_n.25), dynamic_slice_sizes={384,1024} | dynamic-slice | bytes 1572868 | tf_op jit(solution)/shard_map/dynamic_slice | solution.py:455
  7.3 3.1 %shard_map.65.keep_ref = bf16[2,384,128]{2,1,0:T(8,128)(2,1)} custom-call(s32[24]{0:T(128)} %concatenate.3.meta_ref, bf16[512,1536]{1,0:T(8,128)(2,1)} %k_ref.7, bf16[512,1536]{1,0:T(8,128)(2,1)} %v_ref.7), custom_call_target="tpu_custom_call" | custom-call | flops 100663296 | bytes 1572864 | tf_op jit(solution)/shard_map/pallas_call | solution.py:156
  13.5 1.9 %shard_map.67 = (f32[512,384]{1,0:T(8,128)S(1)}, bf16[512,512]{1,0:T(8,128)(2,1)S(1)}) custom-call(s32[24]{0:T(128)S(1)} %copy-done.6, bf16[512,1536]{1,0:T(8,128)(2,1)S(1)} %copy-done, bf16[512,1536]{1,0:T(8,128)(2,1)S(1)} %copy-done.1, bf16[512,1536]{1,0:T(8,128)(2,1)S(1)} %copy-done.2), custom_call_target="tpu_custom_call" | custom-call | flops 301989888 | bytes 1966080 | tf_op jit(solution)/shard_map/pallas_call | solution.py:217
  15.5 2.6 %collective-permute-start.1 = (bf16[384,1024]{1,0:T(8,128)(2,1)S(1)}, bf16[384,1024]{1,0:T(8,128)(2,1)S(1)}, u32[]{:S(2)}, u32[]{:S(2)}) collective-permute-start(bf16[384,1024]{1,0:T(8,128)(2,1)S(1)} %copy-done.7), channel_id=1, source_target_pairs={{0,1},{1,0},{2,3},{3,2},{4,5},{5,4},{6,7},{7,6},{8,9},{9,8},{10,11... | collective-permute-start | bytes 2359304 | tf_op jit(solution)/shard_map/ppermute | solution.py:444
  19.6 3.4 %collective-permute-done.2.b_ref = bf16[384,128]{1,0:T(8,128)(2,1)S(1)} collective-permute-done((bf16[384,128]{1,0:T(8,128)(2,1)S(1)}, bf16[384,128]{1,0:T(8,128)(2,1)S(1)}, u32[]{:S(2)}, u32[]{:S(2)}) %collective-permute-start.2) | collective-permute-done | bytes 98336 | tf_op jit(solution)/shard_map/ppermute | solution.py:438
  23.6 3.5 %collective-permute-start.3 = (bf16[384,128]{1,0:T(8,128)(2,1)S(1)}, bf16[384,128]{1,0:T(8,128)(2,1)S(1)}, u32[]{:S(2)}, u32[]{:S(2)}) collective-permute-start(bf16[384,128]{1,0:T(8,128)(2,1)S(1)} %shard_map.68.a_ref), channel_id=1, source_target_pairs={{0,8},{2,10},{4,12},{6,14},{8,16},{10,18},{12,20},{14,22},{16,24},... | collective-permute-start | bytes 294920 | tf_op jit(solution)/shard_map/ppermute | solution.py:441
  27.1 1.8 %shard_map.69.w_ref = f32[512,384]{1,0:T(8,128)S(1)} custom-call(s32[24]{0:T(128)S(1)} %copy-done.6, bf16[512,1536]{1,0:T(8,128)(2,1)S(1)} %copy-done, bf16[512,1536]{1,0:T(8,128)(2,1)S(1)} %copy-done.1, bf16[512,1536]{1,0:T(8,128)(2,1)S(1)} %copy-done.3, bf16[512,512]{1,0:T(8,128)(2,1)S(1)} %get-tuple-element.36.rest_0_), custom_call_target="tpu_custom_call" | custom-call | flops 301989888 | bytes 1966080 | tf_op jit(solution)/shard_map/pallas_call | solution.py:217
  29.8 5.5 %collective-permute-start.4 = (bf16[384,128]{1,0:T(8,128)(2,1)S(1)}, bf16[384,128]{1,0:T(8,128)(2,1)S(1)}, u32[]{:S(2)}, u32[]{:S(2)}) collective-permute-start(bf16[384,128]{1,0:T(8,128)(2,1)S(1)} %shard_map.70), channel_id=1, source_target_pairs={{0,16},{2,18},{4,20},{6,22},{8,24},{10,26},{12,28},{14,30},{1,17},... | collective-permute-start | bytes 294920 | tf_op jit(solution)/shard_map/ppermute | solution.py:441
  39.1 2.5 %collective-permute-start.10 = (bf16[384,1024]{1,0:T(8,128)(2,1)S(1)}, bf16[384,1024]{1,0:T(8,128)(2,1)S(1)}, u32[]{:S(2)}, u32[]{:S(2)}) collective-permute-start(bf16[384,1024]{1,0:T(8,128)(2,1)S(1)} %collective-permute-done.1.refs_2_), channel_id=1, source_target_pairs={{0,8},{2,10},{4,12},{6,14},{8,0},{10,2},{12,4},{14,6},{16,24},{18,... | collective-permute-start | bytes 2359304 | tf_op jit(solution)/shard_map/ppermute | solution.py:438
  41.6 1.5 %collective-permute-start.6 = (bf16[384,128]{1,0:T(8,128)(2,1)S(1)}, bf16[384,128]{1,0:T(8,128)(2,1)S(1)}, u32[]{:S(2)}, u32[]{:S(2)}) collective-permute-start(bf16[384,128]{1,0:T(8,128)(2,1)S(1)} %get-tuple-element.41), channel_id=1, source_target_pairs={{0,4},{2,6},{4,0},{6,2},{8,12},{10,14},{12,8},{14,10},{16,20},{18,... | collective-permute-start | bytes 294920 | tf_op jit(solution)/shard_map/ppermute | solution.py:438
  43.1 4.0 %collective-permute-done.6.chip_ref = bf16[384,128]{1,0:T(8,128)(2,1)S(1)} collective-permute-done((bf16[384,128]{1,0:T(8,128)(2,1)S(1)}, bf16[384,128]{1,0:T(8,128)(2,1)S(1)}, u32[]{:S(2)}, u32[]{:S(2)}) %collective-permute-start.6) | collective-permute-done | bytes 98336 | tf_op jit(solution)/shard_map/ppermute | solution.py:438
  47.1 1.5 %collective-permute-start.14 = (bf16[384,1024]{1,0:T(8,128)(2,1)S(1)}, bf16[384,1024]{1,0:T(8,128)(2,1)S(1)}, u32[]{:S(2)}, u32[]{:S(2)}) collective-permute-start(bf16[384,1024]{1,0:T(8,128)(2,1)S(1)} %collective-permute-done.1.refs_2_), channel_id=1, source_target_pairs={{0,4},{2,6},{4,0},{6,2},{8,12},{10,14},{12,8},{14,10},{16,20},{18,... | collective-permute-start | bytes 2359304 | tf_op jit(solution)/shard_map/ppermute | solution.py:438
  51.0 1.8 %shard_map.74.w_ref = f32[512,384]{1,0:T(8,128)S(1)} custom-call(s32[24]{0:T(128)S(1)} %copy-done.6, bf16[512,1536]{1,0:T(8,128)(2,1)S(1)} %copy-done, bf16[512,1536]{1,0:T(8,128)(2,1)S(1)} %copy-done.1, bf16[512,1536]{1,0:T(8,128)(2,1)S(1)} %copy-done.3, bf16[512,512]{1,0:T(8,128)(2,1)S(1)} %get-tuple-element.36.rest_0_), custom_call_target="tpu_custom_call" | custom-call | flops 301989888 | bytes 1966080 | tf_op jit(solution)/shard_map/pallas_call | solution.py:217
  52.8 1.8 %shard_map.77.w_ref = f32[512,384]{1,0:T(8,128)S(1)} custom-call(s32[24]{0:T(128)S(1)} %copy-done.6, bf16[512,1536]{1,0:T(8,128)(2,1)S(1)} %copy-done, bf16[512,1536]{1,0:T(8,128)(2,1)S(1)} %copy-done.1, bf16[512,1536]{1,0:T(8,128)(2,1)S(1)} %copy-done.3, bf16[512,512]{1,0:T(8,128)(2,1)S(1)} %get-tuple-element.36.rest_0_), custom_call_target="tpu_custom_call" | custom-call | flops 301989888 | bytes 1966080 | tf_op jit(solution)/shard_map/pallas_call | solution.py:217
  55.7 1.7 %collective-permute-done.10.refs_3_ = bf16[384,1024]{1,0:T(8,128)(2,1)S(1)} collective-permute-done((bf16[384,1024]{1,0:T(8,128)(2,1)S(1)}, bf16[384,1024]{1,0:T(8,128)(2,1)S(1)}, u32[]{:S(2)}, u32[]{:S(2)}) %collective-permute-start.10) | collective-permute-done | bytes 786464 | tf_op jit(solution)/shard_map/ppermute | solution.py:438
  57.4 1.5 %collective-permute-start.9 = (bf16[512,384]{1,0:T(8,128)(2,1)S(1)}, bf16[512,384]{1,0:T(8,128)(2,1)S(1)}, u32[]{:S(2)}, u32[]{:S(2)}) collective-permute-start(bf16[512,384]{1,0:T(8,128)(2,1)S(1)} %shard_map.73.refs_1_), channel_id=1, source_target_pairs={{0,1},{1,0},{2,3},{3,2},{4,5},{5,4},{6,7},{7,6},{8,9},{9,8},{10,11... | collective-permute-start | bytes 1179656 | tf_op jit(solution)/shard_map/ppermute | solution.py:444
  59.0 5.3 %collective-permute-done.14.refs_1_ = bf16[384,1024]{1,0:T(8,128)(2,1)S(1)} collective-permute-done((bf16[384,1024]{1,0:T(8,128)(2,1)S(1)}, bf16[384,1024]{1,0:T(8,128)(2,1)S(1)}, u32[]{:S(2)}, u32[]{:S(2)}) %collective-permute-start.14) | collective-permute-done | bytes 786464 | tf_op jit(solution)/shard_map/ppermute | solution.py:438
  65.9 4.0 %collective-permute-done.9.refs_1_ = bf16[512,384]{1,0:T(8,128)(2,1)S(1)} collective-permute-done((bf16[512,384]{1,0:T(8,128)(2,1)S(1)}, bf16[512,384]{1,0:T(8,128)(2,1)S(1)}, u32[]{:S(2)}, u32[]{:S(2)}) %collective-permute-start.9) | collective-permute-done | bytes 393248 | tf_op jit(solution)/shard_map/ppermute | solution.py:444
  74.1 5.4 %shard_map.79.t_ref = f32[512,2048]{1,0:T(8,128)S(1)} custom-call(s32[24]{0:T(128)S(1)} %copy-done.6, bf16[512,384]{1,0:T(8,128)(2,1)S(1)} %shard_map.72.refs_0_, bf16[512,384]{1,0:T(8,128)(2,1)S(1)} %shard_map.73.refs_1_, bf16[512,384]{1,0:T(8,128)(2,1)S(1)} %shard_map.76.refs_2_, bf16[512,384]{1,0:T(8,128)(2,1)S(1)} %shard_map.78.refs_3_, ...), custom_call_target="tpu_custom_call" | custom-call | flops 3221225472 | bytes 10485760 | tf_op jit(solution)/shard_map/pallas_call | solution.py:370
  79.5 4.1 %shard_map.80.t_ref = f32[512,2048]{1,0:T(8,128)S(1)} custom-call(s32[24]{0:T(128)S(1)} %copy-done.6, f32[512,2048]{1,0:T(8,128)S(1)} %shard_map.79.t_ref, bf16[512,384]{1,0:T(8,128)(2,1)S(1)} %collective-permute-done.8.refs_0_, bf16[512,384]{1,0:T(8,128)(2,1)S(1)} %collective-permute-done.9.refs_1_, bf16[384,1024]{1,0:T(8,128)(2,1)S(1)} %collective-permute-done.1.refs_2_, ...), custom_call_target="tpu_custom_call" | custom-call | flops 1610612736 | bytes 9437184 | tf_op jit(solution)/shard_map/pallas_call | solution.py:410
  83.6 3.2 %shard_map.81.t_ref = f32[512,2048]{1,0:T(8,128)S(1)} custom-call(s32[24]{0:T(128)S(1)} %copy-done.6, f32[512,2048]{1,0:T(8,128)S(1)} %shard_map.80.t_ref, bf16[512,384]{1,0:T(8,128)(2,1)S(1)} %collective-permute-done.13.refs_0_, bf16[384,1024]{1,0:T(8,128)(2,1)S(1)} %collective-permute-done.14.refs_1_, ...), custom_call_target="tpu_custom_call" | custom-call | flops 805306368 | bytes 7864320 | tf_op jit(solution)/shard_map/pallas_call | solution.py:410
  86.9 4.0 %collective-permute-done.17.refs_0_ = bf16[512,384]{1,0:T(8,128)(2,1)S(1)} collective-permute-done((bf16[512,384]{1,0:T(8,128)(2,1)S(1)}, bf16[512,384]{1,0:T(8,128)(2,1)S(1)}, u32[]{:S(2)}, u32[]{:S(2)}) %collective-permute-start.17) | collective-permute-done | bytes 393248 | tf_op jit(solution)/shard_map/ppermute | solution.py:444
  90.9 3.9 %shard_map.82 = bf16[512,2048]{1,0:T(8,128)(2,1)} custom-call(s32[24]{0:T(128)S(1)} %copy-done.6, f32[512,2048]{1,0:T(8,128)S(1)} %shard_map.81.t_ref, bf16[512,384]{1,0:T(8,128)(2,1)S(1)} %collective-permute-done.17.refs_0_, bf16[384,1024]{1,0:T(8,128)(2,1)S(1)} %collective-permute-done.18.refs_1_, bf16[384,512]{1,0:T(8,128)(2,1)S(1)} %collective-permute-done.19.refs_2_, ...), custom_call_target="tpu_custom_call" | custom-call | flops 805306368 | bytes 7864320 | tf_op jit(solution)/shard_map/pallas_call | solution.py:410
  (68 shorter events, 20.9 us)
Async XLA Ops:
  4.7 5.7 %collective-permute-start = (bf16[2,384,128]{2,1,0:T(8,128)(2,1)}, bf16[2,384,128]{2,1,0:T(8,128)(2,1)S(1)}, u32[]{:S(2)}, u32[]{:S(2)}) collective-permute-start(bf16[2,384,128]{2,1,0:T(8,128)(2,1)} %shard_map.64), channel_id=1, source_target_pairs={{0,2},{2,0},{4,6},{6,4},{8,10},{10,8},{12,14},{14,12},{16,18},{18,... | collective-permute-start | bytes 589832 | tf_op jit(solution)/shard_map/ppermute | solution.py:438
  15.4 21.9 %copy-start.5 = (bf16[2,384,128]{2,1,0:T(8,128)(2,1)S(1)}, bf16[2,384,128]{2,1,0:T(8,128)(2,1)}, u32[]{:S(2)}) copy-start(bf16[2,384,128]{2,1,0:T(8,128)(2,1)} %shard_map.65.keep_ref) | copy-start | bytes 589828
  15.5 20.8 %collective-permute-start.1 = (bf16[384,1024]{1,0:T(8,128)(2,1)S(1)}, bf16[384,1024]{1,0:T(8,128)(2,1)S(1)}, u32[]{:S(2)}, u32[]{:S(2)}) collective-permute-start(bf16[384,1024]{1,0:T(8,128)(2,1)S(1)} %copy-done.7), channel_id=1, source_target_pairs={{0,1},{1,0},{2,3},{3,2},{4,5},{5,4},{6,7},{7,6},{8,9},{9,8},{10,11... | collective-permute-start | bytes 2359304 | tf_op jit(solution)/shard_map/ppermute | solution.py:444
  18.1 4.9 %collective-permute-start.2 = (bf16[384,128]{1,0:T(8,128)(2,1)S(1)}, bf16[384,128]{1,0:T(8,128)(2,1)S(1)}, u32[]{:S(2)}, u32[]{:S(2)}) collective-permute-start(bf16[384,128]{1,0:T(8,128)(2,1)S(1)} %get-tuple-element.34), channel_id=1, source_target_pairs={{0,4},{2,6},{4,0},{6,2},{8,12},{10,14},{12,8},{14,10},{16,20},{18,... | collective-permute-start | bytes 294920 | tf_op jit(solution)/shard_map/ppermute | solution.py:438
  23.6 5.7 %collective-permute-start.3 = (bf16[384,128]{1,0:T(8,128)(2,1)S(1)}, bf16[384,128]{1,0:T(8,128)(2,1)S(1)}, u32[]{:S(2)}, u32[]{:S(2)}) collective-permute-start(bf16[384,128]{1,0:T(8,128)(2,1)S(1)} %shard_map.68.a_ref), channel_id=1, source_target_pairs={{0,8},{2,10},{4,12},{6,14},{8,16},{10,18},{12,20},{14,22},{16,24},... | collective-permute-start | bytes 294920 | tf_op jit(solution)/shard_map/ppermute | solution.py:441
  29.8 7.5 %collective-permute-start.4 = (bf16[384,128]{1,0:T(8,128)(2,1)S(1)}, bf16[384,128]{1,0:T(8,128)(2,1)S(1)}, u32[]{:S(2)}, u32[]{:S(2)}) collective-permute-start(bf16[384,128]{1,0:T(8,128)(2,1)S(1)} %shard_map.70), channel_id=1, source_target_pairs={{0,16},{2,18},{4,20},{6,22},{8,24},{10,26},{12,28},{14,30},{1,17},... | collective-permute-start | bytes 294920 | tf_op jit(solution)/shard_map/ppermute | solution.py:441
  39.1 18.3 %collective-permute-start.10 = (bf16[384,1024]{1,0:T(8,128)(2,1)S(1)}, bf16[384,1024]{1,0:T(8,128)(2,1)S(1)}, u32[]{:S(2)}, u32[]{:S(2)}) collective-permute-start(bf16[384,1024]{1,0:T(8,128)(2,1)S(1)} %collective-permute-done.1.refs_2_), channel_id=1, source_target_pairs={{0,8},{2,10},{4,12},{6,14},{8,0},{10,2},{12,4},{14,6},{16,24},{18,... | collective-permute-start | bytes 2359304 | tf_op jit(solution)/shard_map/ppermute | solution.py:438
  41.6 5.5 %collective-permute-start.6 = (bf16[384,128]{1,0:T(8,128)(2,1)S(1)}, bf16[384,128]{1,0:T(8,128)(2,1)S(1)}, u32[]{:S(2)}, u32[]{:S(2)}) collective-permute-start(bf16[384,128]{1,0:T(8,128)(2,1)S(1)} %get-tuple-element.41), channel_id=1, source_target_pairs={{0,4},{2,6},{4,0},{6,2},{8,12},{10,14},{12,8},{14,10},{16,20},{18,... | collective-permute-start | bytes 294920 | tf_op jit(solution)/shard_map/ppermute | solution.py:438
  47.1 17.1 %collective-permute-start.14 = (bf16[384,1024]{1,0:T(8,128)(2,1)S(1)}, bf16[384,1024]{1,0:T(8,128)(2,1)S(1)}, u32[]{:S(2)}, u32[]{:S(2)}) collective-permute-start(bf16[384,1024]{1,0:T(8,128)(2,1)S(1)} %collective-permute-done.1.refs_2_), channel_id=1, source_target_pairs={{0,4},{2,6},{4,0},{6,2},{8,12},{10,14},{12,8},{14,10},{16,20},{18,... | collective-permute-start | bytes 2359304 | tf_op jit(solution)/shard_map/ppermute | solution.py:438
  48.7 1.3 %collective-permute-start.5 = (bf16[384,128]{1,0:T(8,128)(2,1)S(1)}, bf16[384,128]{1,0:T(8,128)(2,1)S(1)}, u32[]{:S(2)}, u32[]{:S(2)}) collective-permute-start(bf16[384,128]{1,0:T(8,128)(2,1)S(1)} %get-tuple-element.39), channel_id=1, source_target_pairs={{0,2},{2,0},{4,6},{6,4},{8,10},{10,8},{12,14},{14,12},{16,18},{18,... | collective-permute-start | bytes 294920 | tf_op jit(solution)/shard_map/ppermute | solution.py:438
  48.7 25.5 %slice-start = ((s8[12582912]{0:T(1024)(128)(4,1)}), s8[4194304]{0:T(1024)(128)(4,1)S(1)}, s32[]{:S(2)}) async-start(s8[12582912]{0:T(1024)(128)(4,1)} %bitcast.4), calls=%async_computation | async-start | bytes 8388608
  49.3 5.3 %collective-permute-start.7 = (bf16[384,128]{1,0:T(8,128)(2,1)S(1)}, bf16[384,128]{1,0:T(8,128)(2,1)S(1)}, u32[]{:S(2)}, u32[]{:S(2)}) collective-permute-start(bf16[384,128]{1,0:T(8,128)(2,1)S(1)} %get-tuple-element.44), channel_id=1, source_target_pairs={{0,2},{2,0},{4,6},{6,4},{8,10},{10,8},{12,14},{14,12},{16,18},{18,... | collective-permute-start | bytes 294920 | tf_op jit(solution)/shard_map/ppermute | solution.py:438
  49.9 21.0 %collective-permute-start.11 = (bf16[384,1024]{1,0:T(8,128)(2,1)S(1)}, bf16[384,1024]{1,0:T(8,128)(2,1)S(1)}, u32[]{:S(2)}, u32[]{:S(2)}) collective-permute-start(bf16[384,1024]{1,0:T(8,128)(2,1)S(1)} %collective-permute-done.1.refs_2_), channel_id=1, source_target_pairs={{0,2},{2,0},{4,6},{6,4},{8,10},{10,8},{12,14},{14,12},{16,18},{18,... | collective-permute-start | bytes 2359304 | tf_op jit(solution)/shard_map/ppermute | solution.py:438
  50.0 15.8 %collective-permute-start.8 = (bf16[512,384]{1,0:T(8,128)(2,1)S(1)}, bf16[512,384]{1,0:T(8,128)(2,1)S(1)}, u32[]{:S(2)}, u32[]{:S(2)}) collective-permute-start(bf16[512,384]{1,0:T(8,128)(2,1)S(1)} %shard_map.72.refs_0_), channel_id=1, source_target_pairs={{0,1},{1,0},{2,3},{3,2},{4,5},{5,4},{6,7},{7,6},{8,9},{9,8},{10,11... | collective-permute-start | bytes 1179656 | tf_op jit(solution)/shard_map/ppermute | solution.py:444
  51.0 23.2 %slice-start.1 = ((s8[12582912]{0:T(1024)(128)(4,1)}), s8[4194304]{0:T(1024)(128)(4,1)S(1)}, s32[]{:S(2)}) async-start(s8[12582912]{0:T(1024)(128)(4,1)} %bitcast.4), calls=%async_computation.1 | async-start | bytes 8388608
  57.4 16.2 %collective-permute-start.12 = (bf16[384,1024]{1,0:T(8,128)(2,1)S(1)}, bf16[384,1024]{1,0:T(8,128)(2,1)S(1)}, u32[]{:S(2)}, u32[]{:S(2)}) collective-permute-start(bf16[384,1024]{1,0:T(8,128)(2,1)S(1)} %collective-permute-done.10.refs_3_), channel_id=1, source_target_pairs={{0,2},{2,0},{4,6},{6,4},{8,10},{10,8},{12,14},{14,12},{16,18},{18,... | collective-permute-start | bytes 2359304 | tf_op jit(solution)/shard_map/ppermute | solution.py:438
  57.4 12.4 %collective-permute-start.9 = (bf16[512,384]{1,0:T(8,128)(2,1)S(1)}, bf16[512,384]{1,0:T(8,128)(2,1)S(1)}, u32[]{:S(2)}, u32[]{:S(2)}) collective-permute-start(bf16[512,384]{1,0:T(8,128)(2,1)S(1)} %shard_map.73.refs_1_), channel_id=1, source_target_pairs={{0,1},{1,0},{2,3},{3,2},{4,5},{5,4},{6,7},{7,6},{8,9},{9,8},{10,11... | collective-permute-start | bytes 1179656 | tf_op jit(solution)/shard_map/ppermute | solution.py:444
  64.3 7.8 %collective-permute-start.15 = (bf16[384,512]{1,0:T(8,128)(2,1)S(1)}, bf16[384,512]{1,0:T(8,128)(2,1)S(1)}, u32[]{:S(2)}, u32[]{:S(2)}) collective-permute-start(bf16[384,512]{1,0:T(8,128)(2,1)S(1)} %slice.6), channel_id=1, source_target_pairs={{0,4},{2,6},{4,0},{6,2},{8,12},{10,14},{12,8},{14,10},{16,20},{18,... | collective-permute-start | bytes 1179656 | tf_op jit(solution)/shard_map/ppermute | solution.py:438
  65.8 7.8 %collective-permute-start.16 = (bf16[384,512]{1,0:T(8,128)(2,1)S(1)}, bf16[384,512]{1,0:T(8,128)(2,1)S(1)}, u32[]{:S(2)}, u32[]{:S(2)}) collective-permute-start(bf16[384,512]{1,0:T(8,128)(2,1)S(1)} %slice.7), channel_id=1, source_target_pairs={{0,8},{2,10},{4,12},{6,14},{8,0},{10,2},{12,4},{14,6},{16,24},{18,... | collective-permute-start | bytes 1179656 | tf_op jit(solution)/shard_map/ppermute | solution.py:438
  69.8 21.1 %collective-permute-start.18 = (bf16[384,1024]{1,0:T(8,128)(2,1)S(1)}, bf16[384,1024]{1,0:T(8,128)(2,1)S(1)}, u32[]{:S(2)}, u32[]{:S(2)}) collective-permute-start(bf16[384,1024]{1,0:T(8,128)(2,1)S(1)} %collective-permute-done.14.refs_1_), channel_id=1, source_target_pairs={{0,2},{2,0},{4,6},{6,4},{8,10},{10,8},{12,14},{14,12},{16,18},{18,... | collective-permute-start | bytes 2359304 | tf_op jit(solution)/shard_map/ppermute | solution.py:438
  70.9 12.8 %collective-permute-start.13 = (bf16[512,384]{1,0:T(8,128)(2,1)S(1)}, bf16[512,384]{1,0:T(8,128)(2,1)S(1)}, u32[]{:S(2)}, u32[]{:S(2)}) collective-permute-start(bf16[512,384]{1,0:T(8,128)(2,1)S(1)} %shard_map.76.refs_2_), channel_id=1, source_target_pairs={{0,1},{1,0},{2,3},{3,2},{4,5},{5,4},{6,7},{7,6},{8,9},{9,8},{10,11... | collective-permute-start | bytes 1179656 | tf_op jit(solution)/shard_map/ppermute | solution.py:444
  72.0 18.8 %collective-permute-start.17 = (bf16[512,384]{1,0:T(8,128)(2,1)S(1)}, bf16[512,384]{1,0:T(8,128)(2,1)S(1)}, u32[]{:S(2)}, u32[]{:S(2)}) collective-permute-start(bf16[512,384]{1,0:T(8,128)(2,1)S(1)} %shard_map.78.refs_3_), channel_id=1, source_target_pairs={{0,1},{1,0},{2,3},{3,2},{4,5},{5,4},{6,7},{7,6},{8,9},{9,8},{10,11... | collective-permute-start | bytes 1179656 | tf_op jit(solution)/shard_map/ppermute | solution.py:444
  73.6 17.3 %collective-permute-start.19 = (bf16[384,512]{1,0:T(8,128)(2,1)S(1)}, bf16[384,512]{1,0:T(8,128)(2,1)S(1)}, u32[]{:S(2)}, u32[]{:S(2)}) collective-permute-start(bf16[384,512]{1,0:T(8,128)(2,1)S(1)} %collective-permute-done.15.refs_2_), channel_id=1, source_target_pairs={{0,2},{2,0},{4,6},{6,4},{8,10},{10,8},{12,14},{14,12},{16,18},{18,... | collective-permute-start | bytes 1179656 | tf_op jit(solution)/shard_map/ppermute | solution.py:438
  73.6 17.3 %collective-permute-start.20 = (bf16[384,512]{1,0:T(8,128)(2,1)S(1)}, bf16[384,512]{1,0:T(8,128)(2,1)S(1)}, u32[]{:S(2)}, u32[]{:S(2)}) collective-permute-start(bf16[384,512]{1,0:T(8,128)(2,1)S(1)} %collective-permute-done.16.refs_3_), channel_id=1, source_target_pairs={{0,2},{2,0},{4,6},{6,4},{8,10},{10,8},{12,14},{14,12},{16,18},{18,... | collective-permute-start | bytes 1179656 | tf_op jit(solution)/shard_map/ppermute | solution.py:438
  (9 other events, 89.8 us)

commit v6 on v5

--- a/solution.py
+++ b/solution.py
@@ -12,7 +12,7 @@
 F32, BF16 = jnp.float32, jnp.bfloat16
 LENS = 8
 VMEM_LIMIT = 16 * 1024 * 1024
-VMEM_MOST = 60 * 1024 * 1024
+VMEM_MOST = 62 * 1024 * 1024
 
 
 def doc_start(meta, doc_count, token):
@@ -127,14 +127,13 @@
     return jnp.where(condition, 1.0, 0.0)
 
 
-def split_states(meta, key, value, doc_count, slots):
+def split_states(meta, key, value, doc_count):
     rows, width = key.shape
     part = width // 4
-    count = len(slots)
-
-    def kernel(meta_ref, k_hbm, v_hbm, o_ref, k_ref, v_ref, sems):
+
+    def kernel(meta_ref, k_hbm, v_hbm, send_ref, keep_ref, k_ref, v_ref, sems):
         copies = []
-        for i, s in enumerate(slots):
+        for i, s in enumerate((1, 3, 0, 2)):
             cols = pl.ds(pl.multiple_of((meta_ref[1] ^ s) * part, DH), part)
             for n, (source, target) in enumerate(((k_hbm, k_ref), (v_hbm, v_ref))):
                 copies.append(pltpu.make_async_copy(source.at[:, cols], target.at[i], sems.at[i, n]))
@@ -142,29 +141,30 @@
         offset = meta_ref[0] * rows
         first = doc_start(meta_ref, doc_count, offset + rows - 1) - offset
         live = lax.broadcasted_iota(jnp.int32, (rows, DH), 0) >= first
-        for i in range(count):
+        for i in range(4):
             copies[2 * i].wait()
             copies[2 * i + 1].wait()
+            o_ref = (send_ref, keep_ref)[i // 2]
             for h in range(part // DH):
                 cols = slice(h * DH, (h + 1) * DH)
                 k = jnp.where(live, k_ref[i, :, cols], jnp.zeros((), BF16))
                 state = lax.dot_general(
                     k, v_ref[i, :, cols], (((0,), (0,)), ((), ())), preferred_element_type=F32
                 )
-                o_ref[i, cols, :] = state.astype(BF16)
+                o_ref[i % 2, cols, :] = state.astype(BF16)
 
     return call(
         kernel,
         (1,),
         [pl.BlockSpec(memory_space=pltpu.HBM)] * 2,
-        whole((count, part, DH)),
-        jax.ShapeDtypeStruct((count, part, DH), BF16),
-        2 * rows * part * count * DH,
-        2 * 2 * rows * part * count,
+        [whole((2, part, DH))] * 2,
+        [jax.ShapeDtypeStruct((2, part, DH), BF16)] * 2,
+        2 * rows * width * DH,
+        2 * 2 * rows * width,
         [
-            pltpu.VMEM((count, rows, part), BF16),
-            pltpu.VMEM((count, rows, part), BF16),
-            pltpu.SemaphoreType.DMA((count, 2)),
+            pltpu.VMEM((4, rows, part), BF16),
+            pltpu.VMEM((4, rows, part), BF16),
+            pltpu.SemaphoreType.DMA((4, 2)),
         ],
         VMEM_MOST,
     )(meta, key, value)
@@ -446,24 +446,29 @@
     def behind(x, *arrays):
         return lax.optimization_barrier((x, *arrays))[0]
 
-    send = split_states(meta, key, value, docs, (1, 3))
+    quarter = half // 2
+    sent = [(side * half, half), ((1 - side) * half, quarter)]
+    sent = [
+        lax.dynamic_slice(weight, (member * part, (1 - group) * columns + at), (part, size))
+        for at, size in sent
+    ]
+
+    send, keep = split_states(meta, key, value, docs)
     core_got = swap(send, 1)
-    keep = split_states(after(meta, send), key, value, docs, (0, 2))
+    w0 = [flip(behind(sent[0], send))]
     chip0, chip2 = join_core(meta, keep, core_got, rows, docs)
     chip_got = swap(chip2, 2)
-
-    sent_weight = lax.dynamic_slice(
-        weight, (member * part, (1 - group) * columns + side * half), (part, half)
-    )
     within0, mask = within_slots(after(meta, chip0), query, key, value, docs, (0,))
-    w0 = [flip(behind(sent_weight, within0))]
-    plane_sum = join_chips(after(meta, within0), chip0, chip_got, rows, docs)
+    within1 = within_slots(after(meta, within0), query, key, value, docs, (1,), mask)
+    plane_sum = join_chips(after(meta, within1), chip0, chip_got, rows, docs)
     near = shift(plane_sum, plane)
-    within1 = within_slots(after(meta, plane_sum), query, key, value, docs, (1,), mask)
-    both = join_planes(after(meta, within1), plane_sum, near, rows, docs)
+    within2 = within_slots(after(meta, plane_sum), query, key, value, docs, (2,), mask)
+    both = join_planes(after(meta, within2), plane_sum, near, rows, docs)
     far = shift(both, 2 * plane)
+    w0.append(flip(behind(sent[1], both)))
+    within3 = within_slots(after(meta, both), query, key, value, docs, (3,), mask)
     carry0, core_carry0, chip_carry = carry_first(
-        after(meta, w0[0]), near, far, chip0, chip_got, keep, core_got, rows, docs
+        after(meta, within3), near, far, chip0, chip_got, keep, core_got, rows, docs
     )
     carry1 = swap(core_carry0, 1)
     chip_carry2 = swap(chip_carry, 2)
@@ -477,8 +482,6 @@
     far0 = flip(normed0)
     normed1 = norm(1, within1, carry1)
     far1 = flip(normed1)
-    within2 = within_slots(after(meta, normed1), query, key, value, docs, (2,), mask)
-    within3 = within_slots(after(meta, within2), query, key, value, docs, (3,), mask)
     carry2, core_carry2 = carry_second(meta, chip_carry2, keep, core_got, rows, docs)
     carry3 = swap(core_carry2, 1)
     normed2 = norm(2, within2, carry2)
@@ -486,16 +489,14 @@
     normed3 = norm(3, within3, carry3)
     far3 = flip(normed3)
 
-    held = behind(w0[0], normed0)
-    w0.append(behind(swap(held, plane), normed3))
-    w2 = [behind(swap(behind(w0[0], chip_carry2), 2), normed3)]
-    quarter = half // 2
-    w2.append(swap(w0[1][:, :quarter], 2))
+    first, second = lax.optimization_barrier((*w0, chip_carry2, normed1))[:2]
+    w2 = [swap(first, 2), swap(second, 2)]
+    w0.append(swap(first[:, quarter:], plane))
     w2.append(swap(w2[0][:, quarter:], plane))
-    w1 = [swap(held, 1), swap(w0[1], 1)]
+    w1 = [swap(w, 1) for w in w0]
     w3 = [swap(w, 1) for w in w2]
 
-    total = project_own(meta, [normed0, normed1, normed2, normed3], weight, columns)
+    total = project_own(after(meta, far1), [normed0, normed1, normed2, normed3], weight, columns)
     total = project_more(meta, total, [far0, far1], [w0, w1], F32)
     total = project_more(meta, total, [far2], [w2], F32)
     return project_more(meta, total, [far3], [w3], BF16)

time: 95.1 us -> 99.9 us (1.050)
  local copies, waits for them, and re-layouts: 5.82 us -> 15.3 us
  starting transfers between devices: 25 us -> 21.3 us
    unnamed x24 -> x38, local copies, waits for them, and re-layouts: 2.37 us -> 9.76 us
    ppermute x14 -> x15, starting transfers between devices: 10.2 us -> 5.69 us  [swap(): return lax.ppermute(x, 'seq', [(i, i ^ bit) for i in range(n_seq)])]
    pallas_call x2 -> x1, Pallas kernels: 6.54 us -> 3.94 us  [split_states(): call(kernel, (1,), [pl.BlockSpec(memory_space=pltpu.HBM)] * 2, [whole((2,...]
    pallas_call x5, Pallas kernels: 3.15 us -> 4.9 us  [small(): call(kernel, (1,), [whole(a.shape) for a in arrays], [whole(shape)] * cou...]
    ppermute x2, waiting for transfers between devices: 1.51 us -> 0.01 us  [shift(): lax.ppermute(x, 'seq', [(i, i + count) for i in range(n_seq - count)])]
    ppermute x5 -> x6, starting transfers between devices: 5.76 us -> 7.25 us  [flip(): return lax.ppermute(x, 'head', [(0, 1), (1, 0)])]
    dynamic_slice x1 -> x2, local copies, waits for them, and re-layouts: 2.06 us -> 3.1 us  [pair_body(): lax.dynamic_slice(weight, (member * part, (1 - group) * columns + at), (p...]
    ppermute x5 -> x6, waiting for transfers between devices: 8.88 us -> 9.84 us  [flip(): return lax.ppermute(x, 'head', [(0, 1), (1, 0)])]
  transfers between devices with their start and end apart: 21 -> 23, of which waited for: 11 -> 9; matrix products, arithmetic and copies ran while one was open for 2% -> 4% of each run, Pallas kernels for 27% -> 30%
where the time goes in v6:
time: 99.9 us; the launch traced here: 99.3 us
  Pallas kernels  37.4 us (37%)
  waiting for transfers between devices  25.1 us (25%)
  starting transfers between devices  21.3 us (21%)
  local copies, waits for them, and re-layouts  15.3 us (15%)
    ppermute x15, waiting for transfers between devices, swap(): return lax.ppermute(x, 'seq', [(i, i ^ bit) for i in range(n_seq)])  15.3 us
    pallas_call x3, Pallas kernels, project_more(): call(kernel, (TILES,), [out_spec] + [whole((rows, part))] * count + [pl.B...  11.9 us
    ppermute x6, waiting for transfers between devices, flip(): return lax.ppermute(x, 'head', [(0, 1), (1, 0)])  9.84 us
    unnamed x38, local copies, waits for them, and re-layouts  9.76 us
    ppermute x2, starting transfers between devices, shift(): lax.ppermute(x, 'seq', [(i, i + count) for i in range(n_seq - count)])  8.31 us
    pallas_call x4, Pallas kernels, within_slots(): call(kernel, (count,), [spec] * 3 + [square] * (not make), [out, square]...  7.29 us
    ppermute x6, starting transfers between devices, flip(): return lax.ppermute(x, 'head', [(0, 1), (1, 0)])  7.25 us
    ppermute x15, starting transfers between devices, swap(): return lax.ppermute(x, 'seq', [(i, i ^ bit) for i in range(n_seq)])  5.69 us
  transfers between devices with their start and end apart: 23, of which 9 were waited for; matrix products, arithmetic and copies ran while one was open for 4% of the time, Pallas kernels for 30%

profile of v6, /device:TPU:0, one launch (start us, length us, event | category | flops | bytes accessed | tf_op | source)
XLA Modules:
  0.0 99.3 jit_solution(2646515039668082437)
XLA Ops:
  1.4 3.9 %shard_map.64 = (bf16[2,384,128]{2,1,0:T(8,128)(2,1)}, bf16[2,384,128]{2,1,0:T(8,128)(2,1)}) custom-call(s32[24]{0:T(128)} %concatenate.3.meta_ref, bf16[512,1536]{1,0:T(8,128)(2,1)} %k_ref.7, bf16[512,1536]{1,0:T(8,128)(2,1)} %v_ref.7), custom_call_target="tpu_custom_call" | custom-call | flops 201326592 | bytes 3145728 | tf_op jit(solution)/shard_map/pallas_call | solution.py:156
  5.9 2.1 %dynamic_slice.6 = bf16[384,1024]{1,0:T(8,128)(2,1)} dynamic-slice(bf16[1536,4096]{1,0:T(8,128)(2,1)} %refs_7_.1, s32[]{:T(128)S(6)} %select_n.28, s32[]{:T(128)S(6)} %select_n.29), dynamic_slice_sizes={384,1024} | dynamic-slice | bytes 1572868 | tf_op jit(solution)/shard_map/dynamic_slice | solution.py:452
  7.9 2.6 %collective-permute-start.9 = (bf16[384,1024]{1,0:T(8,128)(2,1)}, bf16[384,1024]{1,0:T(8,128)(2,1)}, u32[]{:S(2)}, u32[]{:S(2)}) collective-permute-start(bf16[384,1024]{1,0:T(8,128)(2,1)} %dynamic_slice.6), channel_id=1, source_target_pairs={{0,1},{1,0},{2,3},{3,2},{4,5},{5,4},{6,7},{7,6},{8,9},{9,8},{10,11... | collective-permute-start | bytes 2359304 | tf_op jit(solution)/shard_map/ppermute | solution.py:444
  12.1 1.6 %collective-permute-start.1 = (bf16[384,128]{1,0:T(8,128)(2,1)S(1)}, bf16[384,128]{1,0:T(8,128)(2,1)S(1)}, u32[]{:S(2)}, u32[]{:S(2)}) collective-permute-start(bf16[384,128]{1,0:T(8,128)(2,1)S(1)} %get-tuple-element.36), channel_id=1, source_target_pairs={{0,4},{2,6},{4,0},{6,2},{8,12},{10,14},{12,8},{14,10},{16,20},{18,... | collective-permute-start | bytes 294920 | tf_op jit(solution)/shard_map/ppermute | solution.py:438
  16.4 1.9 %shard_map.66 = (f32[512,384]{1,0:T(8,128)S(1)}, bf16[512,512]{1,0:T(8,128)(2,1)S(1)}) custom-call(s32[24]{0:T(128)S(1)} %copy-done.14, bf16[512,1536]{1,0:T(8,128)(2,1)S(1)} %copy-done, bf16[512,1536]{1,0:T(8,128)(2,1)S(1)} %copy-done.1, bf16[512,1536]{1,0:T(8,128)(2,1)S(1)} %copy-done.4), custom_call_target="tpu_custom_call" | custom-call | flops 301989888 | bytes 1966080 | tf_op jit(solution)/shard_map/pallas_call | solution.py:217
  19.2 1.8 %shard_map.67.w_ref = f32[512,384]{1,0:T(8,128)S(1)} custom-call(s32[24]{0:T(128)S(1)} %copy-done.14, bf16[512,1536]{1,0:T(8,128)(2,1)S(1)} %copy-done, bf16[512,1536]{1,0:T(8,128)(2,1)S(1)} %copy-done.1, bf16[512,1536]{1,0:T(8,128)(2,1)S(1)} %copy-done.4, bf16[512,512]{1,0:T(8,128)(2,1)S(1)} %get-tuple-element.34.rest_0_), custom_call_target="tpu_custom_call" | custom-call | flops 301989888 | bytes 1966080 | tf_op jit(solution)/shard_map/pallas_call | solution.py:217
  22.5 4.1 %collective-permute-start.2 = (bf16[384,128]{1,0:T(8,128)(2,1)S(1)}, bf16[384,128]{1,0:T(8,128)(2,1)}, u32[]{:S(2)}, u32[]{:S(2)}) collective-permute-start(bf16[384,128]{1,0:T(8,128)(2,1)S(1)} %shard_map.68.a_ref), channel_id=1, source_target_pairs={{0,8},{2,10},{4,12},{6,14},{8,16},{10,18},{12,20},{14,22},{16,24},... | collective-permute-start | bytes 294920 | tf_op jit(solution)/shard_map/ppermute | solution.py:441
  30.5 1.8 %shard_map.69.w_ref = f32[512,384]{1,0:T(8,128)S(1)} custom-call(s32[24]{0:T(128)S(1)} %copy-done.14, bf16[512,1536]{1,0:T(8,128)(2,1)S(1)} %copy-done, bf16[512,1536]{1,0:T(8,128)(2,1)S(1)} %copy-done.2, bf16[512,1536]{1,0:T(8,128)(2,1)S(1)} %copy-done.5, bf16[512,512]{1,0:T(8,128)(2,1)S(1)} %get-tuple-element.34.rest_0_), custom_call_target="tpu_custom_call" | custom-call | flops 301989888 | bytes 1966080 | tf_op jit(solution)/shard_map/pallas_call | solution.py:217
  32.4 1.5 %shard_map.70 = bf16[384,128]{1,0:T(8,128)(2,1)S(1)} custom-call(s32[24]{0:T(128)S(1)} %copy-done.14, bf16[384,128]{1,0:T(8,128)(2,1)S(1)} %shard_map.68.a_ref, bf16[384,128]{1,0:T(8,128)(2,1)} %collective-permute-done.2.b_ref.near_ref), custom_call_target="tpu_custom_call" | custom-call | flops 49152 | bytes 294912 | tf_op jit(solution)/shard_map/pallas_call | solution.py:229
  34.4 4.2 %collective-permute-start.3 = (bf16[384,128]{1,0:T(8,128)(2,1)S(1)}, bf16[384,128]{1,0:T(8,128)(2,1)S(1)}, u32[]{:S(2)}, u32[]{:S(2)}) collective-permute-start(bf16[384,128]{1,0:T(8,128)(2,1)S(1)} %shard_map.70), channel_id=1, source_target_pairs={{0,16},{2,18},{4,20},{6,22},{8,24},{10,26},{12,28},{14,30},{1,17},... | collective-permute-start | bytes 294920 | tf_op jit(solution)/shard_map/ppermute | solution.py:441
  40.0 1.8 %shard_map.71.w_ref = f32[512,384]{1,0:T(8,128)S(1)} custom-call(s32[24]{0:T(128)S(1)} %copy-done.14, bf16[512,1536]{1,0:T(8,128)(2,1)S(1)} %copy-done, bf16[512,1536]{1,0:T(8,128)(2,1)S(1)} %copy-done.3, bf16[512,1536]{1,0:T(8,128)(2,1)S(1)} %copy-done.5, bf16[512,512]{1,0:T(8,128)(2,1)S(1)} %get-tuple-element.34.rest_0_), custom_call_target="tpu_custom_call" | custom-call | flops 301989888 | bytes 1966080 | tf_op jit(solution)/shard_map/pallas_call | solution.py:217
  41.9 1.6 %shard_map.72 = (bf16[384,128]{1,0:T(8,128)(2,1)S(1)}, bf16[384,128]{1,0:T(8,128)(2,1)S(1)}, bf16[384,128]{1,0:T(8,128)(2,1)S(1)}) custom-call(s32[24]{0:T(128)S(1)} %copy-done.14, bf16[384,128]{1,0:T(8,128)(2,1)} %collective-permute-done.2.b_ref.near_ref, bf16[384,128]{1,0:T(8,128)(2,1)S(1)} %collective-permute-done.3.far_ref, ...), custom_call_target="tpu_custom_call" | custom-call | flops 49152 | bytes 884736 | tf_op jit(solution)/shard_map/pallas_call | solution.py:229
  45.8 2.9 %collective-permute-done.6.chip_ref = bf16[384,128]{1,0:T(8,128)(2,1)S(1)} collective-permute-done((bf16[384,128]{1,0:T(8,128)(2,1)S(1)}, bf16[384,128]{1,0:T(8,128)(2,1)S(1)}, u32[]{:S(2)}, u32[]{:S(2)}) %collective-permute-start.6) | collective-permute-done | bytes 98336 | tf_op jit(solution)/shard_map/ppermute | solution.py:438
  54.7 7.7 %collective-permute-done.8.refs_0_ = bf16[512,384]{1,0:T(8,128)(2,1)S(1)} collective-permute-done((bf16[512,384]{1,0:T(8,128)(2,1)S(1)}, bf16[512,384]{1,0:T(8,128)(2,1)S(1)}, u32[]{:S(2)}, u32[]{:S(2)}) %collective-permute-start.8) | collective-permute-done | bytes 393248 | tf_op jit(solution)/shard_map/ppermute | solution.py:444
  62.4 2.6 %collective-permute-done.11.refs_4_ = bf16[384,512]{1,0:T(8,128)(2,1)S(1)} collective-permute-done((bf16[384,512]{1,0:T(8,128)(2,1)S(1)}, bf16[384,512]{1,0:T(8,128)(2,1)S(1)}, u32[]{:S(2)}, u32[]{:S(2)}) %collective-permute-start.11) | collective-permute-done | bytes 393248 | tf_op jit(solution)/shard_map/ppermute | solution.py:438
  65.0 1.5 %collective-permute-start.17 = (bf16[384,512]{1,0:T(8,128)(2,1)S(1)}, bf16[384,512]{1,0:T(8,128)(2,1)S(1)}, u32[]{:S(2)}, u32[]{:S(2)}) collective-permute-start(bf16[384,512]{1,0:T(8,128)(2,1)S(1)} %collective-permute-done.10.refs_3_), channel_id=1, source_target_pairs={{0,4},{2,6},{4,0},{6,2},{8,12},{10,14},{12,8},{14,10},{16,20},{18,... | collective-permute-start | bytes 1179656 | tf_op jit(solution)/shard_map/ppermute | solution.py:438
  66.5 2.1 %collective-permute-done.16.refs_1_ = bf16[384,1024]{1,0:T(8,128)(2,1)S(1)} collective-permute-done((bf16[384,1024]{1,0:T(8,128)(2,1)}, bf16[384,1024]{1,0:T(8,128)(2,1)S(1)}, u32[]{:S(2)}, u32[]{:S(2)}) %collective-permute-start.16) | collective-permute-done | bytes 786464 | tf_op jit(solution)/shard_map/ppermute | solution.py:438
  71.4 5.1 %collective-permute-done.17.refs_2_ = bf16[384,512]{1,0:T(8,128)(2,1)S(1)} collective-permute-done((bf16[384,512]{1,0:T(8,128)(2,1)S(1)}, bf16[384,512]{1,0:T(8,128)(2,1)S(1)}, u32[]{:S(2)}, u32[]{:S(2)}) %collective-permute-start.17) | collective-permute-done | bytes 393248 | tf_op jit(solution)/shard_map/ppermute | solution.py:438
  78.5 1.8 %collective-permute-done.18.refs_3_ = bf16[384,512]{1,0:T(8,128)(2,1)S(1)} collective-permute-done((bf16[384,512]{1,0:T(8,128)(2,1)S(1)}, bf16[384,512]{1,0:T(8,128)(2,1)S(1)}, u32[]{:S(2)}, u32[]{:S(2)}) %collective-permute-start.18) | collective-permute-done | bytes 393248 | tf_op jit(solution)/shard_map/ppermute | solution.py:438
  80.4 5.3 %shard_map.78.t_ref = f32[512,2048]{1,0:T(8,128)S(1)} custom-call(s32[24]{0:T(128)S(1)} %copy-done.14, bf16[512,384]{1,0:T(8,128)(2,1)S(1)} %shard_map.74.refs_0_, bf16[512,384]{1,0:T(8,128)(2,1)S(1)} %shard_map.73.refs_1_, bf16[512,384]{1,0:T(8,128)(2,1)S(1)} %shard_map.76.refs_2_, bf16[512,384]{1,0:T(8,128)(2,1)S(1)} %shard_map.77.refs_3_, ...), custom_call_target="tpu_custom_call" | custom-call | flops 3221225472 | bytes 10485760 | tf_op jit(solution)/shard_map/pallas_call | solution.py:370
  85.7 4.7 %shard_map.79.t_ref = f32[512,2048]{1,0:T(8,128)S(1)} custom-call(s32[24]{0:T(128)S(1)} %copy-done.14, f32[512,2048]{1,0:T(8,128)S(1)} %shard_map.78.t_ref, bf16[512,384]{1,0:T(8,128)(2,1)S(1)} %collective-permute-done.8.refs_0_, bf16[512,384]{1,0:T(8,128)(2,1)S(1)} %collective-permute-done.5.refs_1_, bf16[384,1024]{1,0:T(8,128)(2,1)} %collective-permute-done.9.refs_2_, ...), custom_call_target="tpu_custom_call" | custom-call | flops 1610612736 | bytes 9437184 | tf_op jit(solution)/shard_map/pallas_call | solution.py:410
  90.5 3.2 %shard_map.80.t_ref = f32[512,2048]{1,0:T(8,128)S(1)} custom-call(s32[24]{0:T(128)S(1)} %copy-done.14, f32[512,2048]{1,0:T(8,128)S(1)} %shard_map.79.t_ref, bf16[512,384]{1,0:T(8,128)(2,1)S(1)} %collective-permute-done.15.refs_0_, bf16[384,1024]{1,0:T(8,128)(2,1)S(1)} %collective-permute-done.16.refs_1_, ...), custom_call_target="tpu_custom_call" | custom-call | flops 805306368 | bytes 7864320 | tf_op jit(solution)/shard_map/pallas_call | solution.py:410
  93.7 1.7 %collective-permute-done.19.refs_0_ = bf16[512,384]{1,0:T(8,128)(2,1)S(1)} collective-permute-done((bf16[512,384]{1,0:T(8,128)(2,1)S(1)}, bf16[512,384]{1,0:T(8,128)(2,1)S(1)}, u32[]{:S(2)}, u32[]{:S(2)}) %collective-permute-start.19) | collective-permute-done | bytes 393248 | tf_op jit(solution)/shard_map/ppermute | solution.py:444
  95.4 3.9 %shard_map.81 = bf16[512,2048]{1,0:T(8,128)(2,1)} custom-call(s32[24]{0:T(128)S(1)} %copy-done.14, f32[512,2048]{1,0:T(8,128)S(1)} %shard_map.80.t_ref, bf16[512,384]{1,0:T(8,128)(2,1)S(1)} %collective-permute-done.19.refs_0_, bf16[384,1024]{1,0:T(8,128)(2,1)S(1)} %collective-permute-done.20.refs_1_, bf16[384,512]{1,0:T(8,128)(2,1)S(1)} %collective-permute-done.21.refs_2_, ...), custom_call_target="tpu_custom_call" | custom-call | flops 805306368 | bytes 7864320 | tf_op jit(solution)/shard_map/pallas_call | solution.py:410
  (86 shorter events, 27.6 us)
Async XLA Ops:
  5.3 5.2 %collective-permute-start = (bf16[2,384,128]{2,1,0:T(8,128)(2,1)}, bf16[2,384,128]{2,1,0:T(8,128)(2,1)S(1)}, u32[]{:S(2)}, u32[]{:S(2)}) collective-permute-start(bf16[2,384,128]{2,1,0:T(8,128)(2,1)} %get-tuple-element.29), channel_id=1, source_target_pairs={{0,2},{2,0},{4,6},{6,4},{8,10},{10,8},{12,14},{14,12},{16,18},{18,... | collective-permute-start | bytes 589832 | tf_op jit(solution)/shard_map/ppermute | solution.py:438
  7.9 40.8 %collective-permute-start.9 = (bf16[384,1024]{1,0:T(8,128)(2,1)}, bf16[384,1024]{1,0:T(8,128)(2,1)}, u32[]{:S(2)}, u32[]{:S(2)}) collective-permute-start(bf16[384,1024]{1,0:T(8,128)(2,1)} %dynamic_slice.6), channel_id=1, source_target_pairs={{0,1},{1,0},{2,3},{3,2},{4,5},{5,4},{6,7},{7,6},{8,9},{9,8},{10,11... | collective-permute-start | bytes 2359304 | tf_op jit(solution)/shard_map/ppermute | solution.py:444
  12.1 9.9 %collective-permute-start.1 = (bf16[384,128]{1,0:T(8,128)(2,1)S(1)}, bf16[384,128]{1,0:T(8,128)(2,1)S(1)}, u32[]{:S(2)}, u32[]{:S(2)}) collective-permute-start(bf16[384,128]{1,0:T(8,128)(2,1)S(1)} %get-tuple-element.36), channel_id=1, source_target_pairs={{0,4},{2,6},{4,0},{6,2},{8,12},{10,14},{12,8},{14,10},{16,20},{18,... | collective-permute-start | bytes 294920 | tf_op jit(solution)/shard_map/ppermute | solution.py:438
  22.5 9.8 %collective-permute-start.2 = (bf16[384,128]{1,0:T(8,128)(2,1)S(1)}, bf16[384,128]{1,0:T(8,128)(2,1)}, u32[]{:S(2)}, u32[]{:S(2)}) collective-permute-start(bf16[384,128]{1,0:T(8,128)(2,1)S(1)} %shard_map.68.a_ref), channel_id=1, source_target_pairs={{0,8},{2,10},{4,12},{6,14},{8,16},{10,18},{12,20},{14,22},{16,24},... | collective-permute-start | bytes 294920 | tf_op jit(solution)/shard_map/ppermute | solution.py:441
  30.5 49.8 %slice-start = ((s8[12582912]{0:T(1024)(128)(4,1)}), s8[4194304]{0:T(1024)(128)(4,1)S(1)}, s32[]{:S(2)}) async-start(s8[12582912]{0:T(1024)(128)(4,1)} %bitcast.4), calls=%async_computation | async-start | bytes 8388608
  33.8 14.9 %collective-permute-start.10 = (bf16[384,512]{1,0:T(8,128)(2,1)S(1)}, bf16[384,512]{1,0:T(8,128)(2,1)S(1)}, u32[]{:S(2)}, u32[]{:S(2)}) collective-permute-start(bf16[384,512]{1,0:T(8,128)(2,1)S(1)} %dynamic_slice.7), channel_id=1, source_target_pairs={{0,1},{1,0},{2,3},{3,2},{4,5},{5,4},{6,7},{7,6},{8,9},{9,8},{10,11... | collective-permute-start | bytes 1179656 | tf_op jit(solution)/shard_map/ppermute | solution.py:444
  34.4 7.4 %collective-permute-start.3 = (bf16[384,128]{1,0:T(8,128)(2,1)S(1)}, bf16[384,128]{1,0:T(8,128)(2,1)S(1)}, u32[]{:S(2)}, u32[]{:S(2)}) collective-permute-start(bf16[384,128]{1,0:T(8,128)(2,1)S(1)} %shard_map.70), channel_id=1, source_target_pairs={{0,16},{2,18},{4,20},{6,22},{8,24},{10,26},{12,28},{14,30},{1,17},... | collective-permute-start | bytes 294920 | tf_op jit(solution)/shard_map/ppermute | solution.py:441
  43.4 1.4 %collective-permute-start.4 = (bf16[384,128]{1,0:T(8,128)(2,1)S(1)}, bf16[384,128]{1,0:T(8,128)(2,1)S(1)}, u32[]{:S(2)}, u32[]{:S(2)}) collective-permute-start(bf16[384,128]{1,0:T(8,128)(2,1)S(1)} %get-tuple-element.41), channel_id=1, source_target_pairs={{0,2},{2,0},{4,6},{6,4},{8,10},{10,8},{12,14},{14,12},{16,18},{18,... | collective-permute-start | bytes 294920 | tf_op jit(solution)/shard_map/ppermute | solution.py:438
  43.5 5.2 %collective-permute-start.6 = (bf16[384,128]{1,0:T(8,128)(2,1)S(1)}, bf16[384,128]{1,0:T(8,128)(2,1)S(1)}, u32[]{:S(2)}, u32[]{:S(2)}) collective-permute-start(bf16[384,128]{1,0:T(8,128)(2,1)S(1)} %get-tuple-element.44), channel_id=1, source_target_pairs={{0,4},{2,6},{4,0},{6,2},{8,12},{10,14},{12,8},{14,10},{16,20},{18,... | collective-permute-start | bytes 294920 | tf_op jit(solution)/shard_map/ppermute | solution.py:438
  48.7 20.0 %collective-permute-start.16 = (bf16[384,1024]{1,0:T(8,128)(2,1)}, bf16[384,1024]{1,0:T(8,128)(2,1)S(1)}, u32[]{:S(2)}, u32[]{:S(2)}) collective-permute-start(bf16[384,1024]{1,0:T(8,128)(2,1)} %collective-permute-done.9.refs_2_), channel_id=1, source_target_pairs={{0,4},{2,6},{4,0},{6,2},{8,12},{10,14},{12,8},{14,10},{16,20},{18,... | collective-permute-start | bytes 2359304 | tf_op jit(solution)/shard_map/ppermute | solution.py:438
  50.3 12.1 %collective-permute-start.8 = (bf16[512,384]{1,0:T(8,128)(2,1)S(1)}, bf16[512,384]{1,0:T(8,128)(2,1)S(1)}, u32[]{:S(2)}, u32[]{:S(2)}) collective-permute-start(bf16[512,384]{1,0:T(8,128)(2,1)S(1)} %shard_map.74.refs_0_), channel_id=1, source_target_pairs={{0,1},{1,0},{2,3},{3,2},{4,5},{5,4},{6,7},{7,6},{8,9},{9,8},{10,11... | collective-permute-start | bytes 1179656 | tf_op jit(solution)/shard_map/ppermute | solution.py:444
  52.4 1.7 %collective-permute-start.7 = (bf16[384,128]{1,0:T(8,128)(2,1)S(1)}, bf16[384,128]{1,0:T(8,128)(2,1)S(1)}, u32[]{:S(2)}, u32[]{:S(2)}) collective-permute-start(bf16[384,128]{1,0:T(8,128)(2,1)S(1)} %get-tuple-element.46), channel_id=1, source_target_pairs={{0,2},{2,0},{4,6},{6,4},{8,10},{10,8},{12,14},{14,12},{16,18},{18,... | collective-permute-start | bytes 294920 | tf_op jit(solution)/shard_map/ppermute | solution.py:438
  53.5 11.6 %collective-permute-start.11 = (bf16[384,512]{1,0:T(8,128)(2,1)S(1)}, bf16[384,512]{1,0:T(8,128)(2,1)S(1)}, u32[]{:S(2)}, u32[]{:S(2)}) collective-permute-start(bf16[384,512]{1,0:T(8,128)(2,1)S(1)} %slice.6), channel_id=1, source_target_pairs={{0,8},{2,10},{4,12},{6,14},{8,0},{10,2},{12,4},{14,6},{16,24},{18,... | collective-permute-start | bytes 1179656 | tf_op jit(solution)/shard_map/ppermute | solution.py:438
  53.5 25.0 %collective-permute-start.12 = (bf16[384,1024]{1,0:T(8,128)(2,1)}, bf16[384,1024]{1,0:T(8,128)(2,1)S(1)}, u32[]{:S(2)}, u32[]{:S(2)}) collective-permute-start(bf16[384,1024]{1,0:T(8,128)(2,1)} %collective-permute-done.9.refs_2_), channel_id=1, source_target_pairs={{0,2},{2,0},{4,6},{6,4},{8,10},{10,8},{12,14},{14,12},{16,18},{18,... | collective-permute-start | bytes 2359304 | tf_op jit(solution)/shard_map/ppermute | solution.py:438
  54.1 15.1 %collective-permute-start.5 = (bf16[512,384]{1,0:T(8,128)(2,1)S(1)}, bf16[512,384]{1,0:T(8,128)(2,1)S(1)}, u32[]{:S(2)}, u32[]{:S(2)}) collective-permute-start(bf16[512,384]{1,0:T(8,128)(2,1)S(1)} %shard_map.73.refs_1_), channel_id=1, source_target_pairs={{0,1},{1,0},{2,3},{3,2},{4,5},{5,4},{6,7},{7,6},{8,9},{9,8},{10,11... | collective-permute-start | bytes 1179656 | tf_op jit(solution)/shard_map/ppermute | solution.py:444
  62.4 6.8 %collective-permute-start.13 = (bf16[384,512]{1,0:T(8,128)(2,1)S(1)}, bf16[384,512]{1,0:T(8,128)(2,1)S(1)}, u32[]{:S(2)}, u32[]{:S(2)}) collective-permute-start(bf16[384,512]{1,0:T(8,128)(2,1)S(1)} %collective-permute-done.10.refs_3_), channel_id=1, source_target_pairs={{0,2},{2,0},{4,6},{6,4},{8,10},{10,8},{12,14},{14,12},{16,18},{18,... | collective-permute-start | bytes 1179656 | tf_op jit(solution)/shard_map/ppermute | solution.py:438
  65.0 11.4 %collective-permute-start.17 = (bf16[384,512]{1,0:T(8,128)(2,1)S(1)}, bf16[384,512]{1,0:T(8,128)(2,1)S(1)}, u32[]{:S(2)}, u32[]{:S(2)}) collective-permute-start(bf16[384,512]{1,0:T(8,128)(2,1)S(1)} %collective-permute-done.10.refs_3_), channel_id=1, source_target_pairs={{0,4},{2,6},{4,0},{6,2},{8,12},{10,14},{12,8},{14,10},{16,20},{18,... | collective-permute-start | bytes 1179656 | tf_op jit(solution)/shard_map/ppermute | solution.py:438
  68.7 9.2 %collective-permute-start.14 = (bf16[384,512]{1,0:T(8,128)(2,1)S(1)}, bf16[384,512]{1,0:T(8,128)(2,1)S(1)}, u32[]{:S(2)}, u32[]{:S(2)}) collective-permute-start(bf16[384,512]{1,0:T(8,128)(2,1)S(1)} %collective-permute-done.11.refs_4_), channel_id=1, source_target_pairs={{0,2},{2,0},{4,6},{6,4},{8,10},{10,8},{12,14},{14,12},{16,18},{18,... | collective-permute-start | bytes 1179656 | tf_op jit(solution)/shard_map/ppermute | solution.py:438
  69.2 11.2 %collective-permute-start.18 = (bf16[384,512]{1,0:T(8,128)(2,1)S(1)}, bf16[384,512]{1,0:T(8,128)(2,1)S(1)}, u32[]{:S(2)}, u32[]{:S(2)}) collective-permute-start(bf16[384,512]{1,0:T(8,128)(2,1)S(1)} %slice.8), channel_id=1, source_target_pairs={{0,8},{2,10},{4,12},{6,14},{8,0},{10,2},{12,4},{14,6},{16,24},{18,... | collective-permute-start | bytes 1179656 | tf_op jit(solution)/shard_map/ppermute | solution.py:438
  69.2 26.2 %collective-permute-start.20 = (bf16[384,1024]{1,0:T(8,128)(2,1)S(1)}, bf16[384,1024]{1,0:T(8,128)(2,1)S(1)}, u32[]{:S(2)}, u32[]{:S(2)}) collective-permute-start(bf16[384,1024]{1,0:T(8,128)(2,1)S(1)} %collective-permute-done.16.refs_1_), channel_id=1, source_target_pairs={{0,2},{2,0},{4,6},{6,4},{8,10},{10,8},{12,14},{14,12},{16,18},{18,... | collective-permute-start | bytes 2359304 | tf_op jit(solution)/shard_map/ppermute | solution.py:438
  76.5 14.0 %collective-permute-start.15 = (bf16[512,384]{1,0:T(8,128)(2,1)S(1)}, bf16[512,384]{1,0:T(8,128)(2,1)S(1)}, u32[]{:S(2)}, u32[]{:S(2)}) collective-permute-start(bf16[512,384]{1,0:T(8,128)(2,1)S(1)} %shard_map.76.refs_2_), channel_id=1, source_target_pairs={{0,1},{1,0},{2,3},{3,2},{4,5},{5,4},{6,7},{7,6},{8,9},{9,8},{10,11... | collective-permute-start | bytes 1179656 | tf_op jit(solution)/shard_map/ppermute | solution.py:444
  77.9 17.5 %collective-permute-start.19 = (bf16[512,384]{1,0:T(8,128)(2,1)S(1)}, bf16[512,384]{1,0:T(8,128)(2,1)S(1)}, u32[]{:S(2)}, u32[]{:S(2)}) collective-permute-start(bf16[512,384]{1,0:T(8,128)(2,1)S(1)} %shard_map.77.refs_3_), channel_id=1, source_target_pairs={{0,1},{1,0},{2,3},{3,2},{4,5},{5,4},{6,7},{7,6},{8,9},{9,8},{10,11... | collective-permute-start | bytes 1179656 | tf_op jit(solution)/shard_map/ppermute | solution.py:444
  78.5 16.9 %collective-permute-start.21 = (bf16[384,512]{1,0:T(8,128)(2,1)S(1)}, bf16[384,512]{1,0:T(8,128)(2,1)S(1)}, u32[]{:S(2)}, u32[]{:S(2)}) collective-permute-start(bf16[384,512]{1,0:T(8,128)(2,1)S(1)} %collective-permute-done.17.refs_2_), channel_id=1, source_target_pairs={{0,2},{2,0},{4,6},{6,4},{8,10},{10,8},{12,14},{14,12},{16,18},{18,... | collective-permute-start | bytes 1179656 | tf_op jit(solution)/shard_map/ppermute | solution.py:438
  80.3 15.1 %collective-permute-start.22 = (bf16[384,512]{1,0:T(8,128)(2,1)S(1)}, bf16[384,512]{1,0:T(8,128)(2,1)S(1)}, u32[]{:S(2)}, u32[]{:S(2)}) collective-permute-start(bf16[384,512]{1,0:T(8,128)(2,1)S(1)} %collective-permute-done.18.refs_3_), channel_id=1, source_target_pairs={{0,2},{2,0},{4,6},{6,4},{8,10},{10,8},{12,14},{14,12},{16,18},{18,... | collective-permute-start | bytes 1179656 | tf_op jit(solution)/shard_map/ppermute | solution.py:438
  (18 other events, 172.0 us)

commit v7 on v6

--- a/solution.py
+++ b/solution.py
@@ -115,6 +115,18 @@
     )(meta, query, key, value)
 
 
+def local(kernel, meta, arrays, shapes, micros, limit=4):
+    vmem = pl.BlockSpec(memory_space=pltpu.VMEM)
+    return pl.pallas_call(
+        kernel,
+        out_shape=shapes,
+        in_specs=[pl.BlockSpec(memory_space=pltpu.SMEM)] + [vmem] * len(arrays),
+        out_specs=[vmem] * len(shapes),
+        compiler_params=pltpu.CompilerParams(vmem_limit_bytes=limit * 1024 * 1024),
+        cost_estimate=pl.CostEstimate(flops=int(micros * 1e9), bytes_accessed=1024, transcendentals=0),
+    )(meta, *arrays)
+
+
 def whole(shape):
     return pl.BlockSpec(shape, lambda *_: (0,) * len(shape))
 
@@ -125,49 +137,31 @@
 
 def factor(condition):
     return jnp.where(condition, 1.0, 0.0)
+
+
+def head_columns(meta_ref, slot, part, h):
+    return pl.ds(pl.multiple_of((meta_ref[1] ^ slot) * part + h * DH, DH), DH)
 
 
 def split_states(meta, key, value, doc_count):
     rows, width = key.shape
     part = width // 4
 
-    def kernel(meta_ref, k_hbm, v_hbm, send_ref, keep_ref, k_ref, v_ref, sems):
-        copies = []
-        for i, s in enumerate((1, 3, 0, 2)):
-            cols = pl.ds(pl.multiple_of((meta_ref[1] ^ s) * part, DH), part)
-            for n, (source, target) in enumerate(((k_hbm, k_ref), (v_hbm, v_ref))):
-                copies.append(pltpu.make_async_copy(source.at[:, cols], target.at[i], sems.at[i, n]))
-                copies[-1].start()
+    def kernel(meta_ref, k_ref, v_ref, send_ref, keep_ref):
         offset = meta_ref[0] * rows
         first = doc_start(meta_ref, doc_count, offset + rows - 1) - offset
         live = lax.broadcasted_iota(jnp.int32, (rows, DH), 0) >= first
-        for i in range(4):
-            copies[2 * i].wait()
-            copies[2 * i + 1].wait()
+        for i, s in enumerate((1, 3, 0, 2)):
             o_ref = (send_ref, keep_ref)[i // 2]
             for h in range(part // DH):
-                cols = slice(h * DH, (h + 1) * DH)
-                k = jnp.where(live, k_ref[i, :, cols], jnp.zeros((), BF16))
+                cols = head_columns(meta_ref, s, part, h)
+                k = jnp.where(live, k_ref[:, cols], jnp.zeros((), BF16))
                 state = lax.dot_general(
-                    k, v_ref[i, :, cols], (((0,), (0,)), ((), ())), preferred_element_type=F32
+                    k, v_ref[:, cols], (((0,), (0,)), ((), ())), preferred_element_type=F32
                 )
-                o_ref[i % 2, cols, :] = state.astype(BF16)
-
-    return call(
-        kernel,
-        (1,),
-        [pl.BlockSpec(memory_space=pltpu.HBM)] * 2,
-        [whole((2, part, DH))] * 2,
-        [jax.ShapeDtypeStruct((2, part, DH), BF16)] * 2,
-        2 * rows * width * DH,
-        2 * 2 * rows * width,
-        [
-            pltpu.VMEM((4, rows, part), BF16),
-            pltpu.VMEM((4, rows, part), BF16),
-            pltpu.SemaphoreType.DMA((4, 2)),
-        ],
-        VMEM_MOST,
-    )(meta, key, value)
+                o_ref[i % 2, h * DH : (h + 1) * DH, :] = state.astype(BF16)
+
+    return local(kernel, meta, (key, value), [jax.ShapeDtypeStruct((2, part, DH), BF16)] * 2, 2, 8)
 
 
 def seen_mask(meta_ref, rows, doc_count):
@@ -183,7 +177,7 @@
     return jnp.where((s <= t) & (s >= first), 1.0, 0.0).astype(BF16)
 
 
-def within_slots(meta, query, key, value, doc_count, slots, mask=None):
+def within_slot(meta, query, key, value, doc_count, slot, mask=None):
     rows, width = query.shape
     part = width // 4
     tile = rows // 2
@@ -192,14 +186,11 @@
     def kernel(meta_ref, q_ref, k_ref, v_ref, *rest):
         if make:
             o_ref, mask_ref = rest
-
-            @pl.when(pl.program_id(0) == 0)
-            def _():
-                mask_ref[...] = seen_mask(meta_ref, rows, doc_count)
+            mask_ref[...] = seen_mask(meta_ref, rows, doc_count)
         else:
             mask_ref, o_ref = rest
         for h in range(part // DH):
-            cols = slice(h * DH, (h + 1) * DH)
+            cols = head_columns(meta_ref, slot, part, h)
             for i in range(2):
                 r = slice(i * tile, (i + 1) * tile)
                 seen = (i + 1) * tile
@@ -207,34 +198,17 @@
                     q_ref[r, cols], k_ref[:seen, cols], (((1,), (1,)), ((), ())), preferred_element_type=F32
                 )
                 scores = scores.astype(BF16) * mask_ref[r, :seen]
-                o_ref[r, cols] = jnp.dot(scores, v_ref[:seen, cols], preferred_element_type=F32)
-
-    count = len(slots)
-    spec = pl.BlockSpec((rows, part), lambda g, m: (0, (g + slots[0]) ^ m[1]))
-    out = pl.BlockSpec((rows, part), lambda g, m: (0, g))
-    shape = jax.ShapeDtypeStruct((rows, part * count), F32)
-    square = whole((rows, rows))
-    return call(
-        kernel,
-        (count,),
-        [spec] * 3 + [square] * (not make),
-        [out, square] if make else out,
-        [shape, jax.ShapeDtypeStruct((rows, rows), BF16)] if make else shape,
-        3 * rows * rows * part * count,
-        10 * rows * part * count,
-    )(meta, query, key, value, *([] if make else [mask]))
+                o_ref[r, h * DH : (h + 1) * DH] = jnp.dot(scores, v_ref[:seen, cols], preferred_element_type=F32)
+
+    shapes = [jax.ShapeDtypeStruct((rows, part), F32)]
+    arrays = (query, key, value)
+    if make:
+        return local(kernel, meta, arrays, shapes + [jax.ShapeDtypeStruct((rows, rows), BF16)], 2, 12)
+    return local(kernel, meta, (*arrays, mask), shapes, 2, 12)[0]
 
 
 def small(kernel, meta, arrays, shape, count):
-    return call(
-        kernel,
-        (1,),
-        [whole(a.shape) for a in arrays],
-        [whole(shape)] * count,
-        [jax.ShapeDtypeStruct(shape, BF16)] * count,
-        shape[0] * shape[1],
-        2 * shape[0] * shape[1] * (len(arrays) + count),
-    )(meta, *arrays)
+    return local(kernel, meta, arrays, [jax.ShapeDtypeStruct(shape, BF16)] * count, 0.6)
 
 
 def join_core(meta, keep, got, rows, doc_count):
@@ -308,7 +282,7 @@
     return small(kernel, meta, (chip, keep, core_got), chip.shape, 2)
 
 
-def norm_heads(meta, query, within, carry, gain, doc_count, slots=(None, None, None)):
+def norm_heads(meta, query, within, carry, gain, doc_count, slot=None):
     rows = query.shape[0]
     part = carry.shape[0]
 
@@ -324,33 +298,15 @@
         stop = jnp.where(begins < offset, end - offset, 0)
         cross = lax.broadcasted_iota(jnp.int32, (rows, DH), 0) < stop
         for h in range(part // DH):
-            cols = slice(h * DH, (h + 1) * DH)
-            term = jnp.dot(q_ref[:, cols], c_ref[cols, :], preferred_element_type=F32)
-            mixture = w_ref[:, cols].astype(F32) + jnp.where(cross, term, 0.0)
+            here = slice(h * DH, (h + 1) * DH)
+            cols = here if slot is None else head_columns(meta_ref, slot, part, h)
+            term = jnp.dot(q_ref[:, cols], c_ref[here, :], preferred_element_type=F32)
+            mixture = w_ref[:, here] + jnp.where(cross, term, 0.0)
             mean = jnp.mean(mixture * mixture, axis=-1, keepdims=True)
-            o_ref[:, cols] = (mixture * lax.rsqrt(mean + 1e-06) * g_ref[:, cols]).astype(BF16)
-
-    def block(place):
-        if place is None:
-            return lambda i, m: (0, 0)
-        if isinstance(place, int):
-            return lambda i, m: (0, place)
-        return lambda i, m: (0, m[1] ^ place[1])
-
-    return call(
-        kernel,
-        (1,),
-        [
-            pl.BlockSpec((rows, part), block(slots[0])),
-            pl.BlockSpec((rows, part), block(slots[1])),
-            whole((part, DH)),
-            pl.BlockSpec((1, part), block(slots[2])),
-        ],
-        whole((rows, part)),
-        jax.ShapeDtypeStruct((rows, part), BF16),
-        2 * rows * part * DH,
-        8 * rows * part,
-    )(meta, query, within, carry, gain.reshape(1, -1))
+            o_ref[:, here] = (mixture * lax.rsqrt(mean + 1e-06) * g_ref[:, cols]).astype(BF16)
+
+    shapes = [jax.ShapeDtypeStruct((rows, part), BF16)]
+    return local(kernel, meta, (query, within, carry, gain.reshape(1, -1)), shapes, 1, 8)[0]
 
 
 TILES = 4
@@ -374,8 +330,8 @@
         + [pl.BlockSpec((part, tile), lambda n, m, s=s: (m[1] ^ s, m[2] * TILES + n)) for s in range(count)],
         pl.BlockSpec((rows, tile), lambda n, m: (0, n)),
         jax.ShapeDtypeStruct((rows, columns), F32),
-        2 * rows * part * count * columns,
-        2 * part * count * columns + 4 * rows * columns,
+        5 * 10**9,
+        1024,
     )(meta, *pieces, *[weight] * count)
 
 
@@ -415,8 +371,8 @@
         + [pl.BlockSpec((part, tile), column(start, tiles)) for _, start, tiles in flat],
         out_spec,
         jax.ShapeDtypeStruct((rows, columns), dtype),
-        2 * rows * part * count * columns,
-        2 * part * count * columns + 6 * rows * columns,
+        3 * 10**9,
+        1024,
     )(meta, total, *pieces, *[w for w, _, _ in flat])
 
 
@@ -452,21 +408,21 @@
         lax.dynamic_slice(weight, (member * part, (1 - group) * columns + at), (part, size))
         for at, size in sent
     ]
-
-    send, keep = split_states(meta, key, value, docs)
+    w0 = [flip(x) for x in sent]
+
+    send, keep = split_states(after(meta, sent[0]), key, value, docs)
     core_got = swap(send, 1)
-    w0 = [flip(behind(sent[0], send))]
-    chip0, chip2 = join_core(meta, keep, core_got, rows, docs)
+    query = behind(query, send)
+    within0, mask = within_slot(after(meta, send), query, key, value, docs, 0)
+    chip0, chip2 = join_core(after(meta, within0), keep, core_got, rows, docs)
     chip_got = swap(chip2, 2)
-    within0, mask = within_slots(after(meta, chip0), query, key, value, docs, (0,))
-    within1 = within_slots(after(meta, within0), query, key, value, docs, (1,), mask)
+    within1 = within_slot(after(meta, chip0), query, key, value, docs, 1, mask)
     plane_sum = join_chips(after(meta, within1), chip0, chip_got, rows, docs)
     near = shift(plane_sum, plane)
-    within2 = within_slots(after(meta, plane_sum), query, key, value, docs, (2,), mask)
+    within2 = within_slot(after(meta, plane_sum), query, key, value, docs, 2, mask)
     both = join_planes(after(meta, within2), plane_sum, near, rows, docs)
     far = shift(both, 2 * plane)
-    w0.append(flip(behind(sent[1], both)))
-    within3 = within_slots(after(meta, both), query, key, value, docs, (3,), mask)
+    within3 = within_slot(after(meta, both), query, key, value, docs, 3, mask)
     carry0, core_carry0, chip_carry = carry_first(
         after(meta, within3), near, far, chip0, chip_got, keep, core_got, rows, docs
     )
@@ -474,9 +430,7 @@
     chip_carry2 = swap(chip_carry, 2)
 
     def norm(slot, within, carry):
-        return norm_heads(
-            meta, query, within, carry, gain, docs, (("slot", slot), None, ("slot", slot))
-        )
+        return norm_heads(meta, query, within, carry, gain, docs, slot)
 
     normed0 = norm(0, within0, carry0)
     far0 = flip(normed0)
@@ -489,14 +443,14 @@
     normed3 = norm(3, within3, carry3)
     far3 = flip(normed3)
 
-    first, second = lax.optimization_barrier((*w0, chip_carry2, normed1))[:2]
+    first, second = lax.optimization_barrier((*w0, chip_carry2, normed0, normed1))[:2]
+    total = project_own(after(meta, far0), [normed0, normed1, normed2, normed3], weight, columns)
     w2 = [swap(first, 2), swap(second, 2)]
     w0.append(swap(first[:, quarter:], plane))
-    w2.append(swap(w2[0][:, quarter:], plane))
+    w2.append(swap(behind(w2[0], total)[:, quarter:], plane))
     w1 = [swap(w, 1) for w in w0]
     w3 = [swap(w, 1) for w in w2]
 
-    total = project_own(after(meta, far1), [normed0, normed1, normed2, normed3], weight, columns)
     total = project_more(meta, total, [far0, far1], [w0, w1], F32)
     total = project_more(meta, total, [far2], [w2], F32)
     return project_more(meta, total, [far3], [w3], BF16)

time: 99.9 us -> 94.7 us (0.948)
  starting transfers between devices: 21.3 us -> 27.1 us
  local copies, waits for them, and re-layouts: 15.3 us -> 9.67 us
  Pallas kernels: 37.4 us -> 31.8 us
    pallas_call x14, Pallas kernels: 20.2 us -> 15.4 us  [local(): pl.pallas_call(kernel, out_shape=shapes, in_specs=[pl.BlockSpec(memory_sp...]
    ppermute x15, starting transfers between devices: 5.69 us -> 9.97 us  [swap(): return lax.ppermute(x, 'seq', [(i, i ^ bit) for i in range(n_seq)])]
    unnamed x38 -> x20, local copies, waits for them, and re-layouts: 9.76 us -> 5.67 us
    ppermute x6, waiting for transfers between devices: 9.84 us -> 6.32 us  [flip(): return lax.ppermute(x, 'head', [(0, 1), (1, 0)])]
    ppermute x15, waiting for transfers between devices: 15.3 us -> 18.4 us  [swap(): return lax.ppermute(x, 'seq', [(i, i ^ bit) for i in range(n_seq)])]
  transfers between devices with their start and end apart: 23 -> 23, of which waited for: 9 -> 10; matrix products, arithmetic and copies ran while one was open for 4% -> 1% of each run, Pallas kernels for 30% -> 28%
where the time goes in v7:
time: 94.7 us; the launch traced here: 94.3 us
  Pallas kernels  31.8 us (34%)
  starting transfers between devices  27.1 us (29%)
  waiting for transfers between devices  25.4 us (27%)
  local copies, waits for them, and re-layouts  9.67 us (10%)
    ppermute x15, waiting for transfers between devices, swap(): return lax.ppermute(x, 'seq', [(i, i ^ bit) for i in range(n_seq)])  18.4 us
    pallas_call x14, Pallas kernels, local(): pl.pallas_call(kernel, out_shape=shapes, in_specs=[pl.BlockSpec(memory_sp...  15.4 us
    pallas_call x3, Pallas kernels, project_more(): call(kernel, (TILES,), [out_spec] + [whole((rows, part))] * count + [pl.B...  11 us
    ppermute x15, starting transfers between devices, swap(): return lax.ppermute(x, 'seq', [(i, i ^ bit) for i in range(n_seq)])  9.97 us
    ppermute x2, starting transfers between devices, shift(): lax.ppermute(x, 'seq', [(i, i + count) for i in range(n_seq - count)])  9.22 us
    ppermute x6, starting transfers between devices, flip(): return lax.ppermute(x, 'head', [(0, 1), (1, 0)])  7.89 us
    ppermute x6, waiting for transfers between devices, flip(): return lax.ppermute(x, 'head', [(0, 1), (1, 0)])  6.32 us
    unnamed x20, local copies, waits for them, and re-layouts  5.67 us
  transfers between devices with their start and end apart: 23, of which 10 were waited for; matrix products, arithmetic and copies ran while one was open for 1% of the time, Pallas kernels for 28%

profile of v7, /device:TPU:0, one launch (start us, length us, event | category | flops | bytes accessed | tf_op | source)
XLA Modules:
  0.0 94.3 jit_solution(3516266217947090976)
XLA Ops:
  0.0 2.2 %dynamic_slice.6 = bf16[384,1024]{1,0:T(8,128)(2,1)} dynamic-slice(bf16[1536,4096]{1,0:T(8,128)(2,1)} %refs_7_.1, s32[]{:T(128)S(6)} %select_n.28, s32[]{:T(128)S(6)} %select_n.29), dynamic_slice_sizes={384,1024} | dynamic-slice | bytes 1572868 | tf_op jit(solution)/shard_map/dynamic_slice | solution.py:408
  7.6 2.6 %collective-permute-start.9 = (bf16[384,1024]{1,0:T(8,128)(2,1)}, bf16[384,1024]{1,0:T(8,128)(2,1)S(1)}, u32[]{:S(2)}, u32[]{:S(2)}) collective-permute-start(bf16[384,1024]{1,0:T(8,128)(2,1)} %dynamic_slice.6), channel_id=1, source_target_pairs={{0,1},{1,0},{2,3},{3,2},{4,5},{5,4},{6,7},{7,6},{8,9},{9,8},{10,11... | collective-permute-start | bytes 2359304 | tf_op jit(solution)/shard_map/ppermute | solution.py:400
  14.1 1.8 %shard_map.65 = (f32[512,384]{1,0:T(8,128)S(1)}, bf16[512,512]{1,0:T(8,128)(2,1)S(1)}) custom-call(s32[24]{0:T(128)S(1)} %concatenate.3.meta_ref, bf16[512,1536]{1,0:T(8,128)(2,1)S(1)} %copy-done.4, bf16[512,1536]{1,0:T(8,128)(2,1)S(1)} %copy-done.1, bf16[512,1536]{1,0:T(8,128)(2,1)S(1)} %copy-done.3), custom_call_target="tpu_custom_call" | custom-call | flops 2000000000 | bytes 1024 | tf_op jit(solution)/shard_map/pallas_call | solution.py:120
  16.6 2.0 %collective-permute-start.1 = (bf16[384,128]{1,0:T(8,128)(2,1)S(1)}, bf16[384,128]{1,0:T(8,128)(2,1)S(1)}, u32[]{:S(2)}, u32[]{:S(2)}) collective-permute-start(bf16[384,128]{1,0:T(8,128)(2,1)S(1)} %get-tuple-element.41), channel_id=1, source_target_pairs={{0,4},{2,6},{4,0},{6,2},{8,12},{10,14},{12,8},{14,10},{16,20},{18,... | collective-permute-start | bytes 294920 | tf_op jit(solution)/shard_map/ppermute | solution.py:394
  18.6 1.7 %shard_map.67.w_ref = f32[512,384]{1,0:T(8,128)S(1)} custom-call(s32[24]{0:T(128)S(1)} %concatenate.3.meta_ref, bf16[512,1536]{1,0:T(8,128)(2,1)S(1)} %copy-done.4, bf16[512,1536]{1,0:T(8,128)(2,1)S(1)} %copy-done.1, bf16[512,1536]{1,0:T(8,128)(2,1)S(1)} %copy-done.3, bf16[512,512]{1,0:T(8,128)(2,1)S(1)} %get-tuple-element.39.rest_0_), custom_call_target="tpu_custom_call" | custom-call | flops 2000000000 | bytes 1024 | tf_op jit(solution)/shard_map/pallas_call | solution.py:120
  22.2 3.7 %collective-permute-start.2 = (bf16[384,128]{1,0:T(8,128)(2,1)S(1)}, bf16[384,128]{1,0:T(8,128)(2,1)S(1)}, u32[]{:S(2)}, u32[]{:S(2)}) collective-permute-start(bf16[384,128]{1,0:T(8,128)(2,1)S(1)} %shard_map.68.a_ref), channel_id=1, source_target_pairs={{0,8},{2,10},{4,12},{6,14},{8,16},{10,18},{12,20},{14,22},{16,24},... | collective-permute-start | bytes 294920 | tf_op jit(solution)/shard_map/ppermute | solution.py:397
  25.9 1.7 %shard_map.69.w_ref = f32[512,384]{1,0:T(8,128)S(1)} custom-call(s32[24]{0:T(128)S(1)} %concatenate.3.meta_ref, bf16[512,1536]{1,0:T(8,128)(2,1)S(1)} %copy-done.4, bf16[512,1536]{1,0:T(8,128)(2,1)S(1)} %copy-done.1, bf16[512,1536]{1,0:T(8,128)(2,1)S(1)} %copy-done.3, bf16[512,512]{1,0:T(8,128)(2,1)S(1)} %get-tuple-element.39.rest_0_), custom_call_target="tpu_custom_call" | custom-call | flops 2000000000 | bytes 1024 | tf_op jit(solution)/shard_map/pallas_call | solution.py:120
  28.7 5.5 %collective-permute-start.3 = (bf16[384,128]{1,0:T(8,128)(2,1)S(1)}, bf16[384,128]{1,0:T(8,128)(2,1)S(1)}, u32[]{:S(2)}, u32[]{:S(2)}) collective-permute-start(bf16[384,128]{1,0:T(8,128)(2,1)S(1)} %shard_map.70), channel_id=1, source_target_pairs={{0,16},{2,18},{4,20},{6,22},{8,24},{10,26},{12,28},{14,30},{1,17},... | collective-permute-start | bytes 294920 | tf_op jit(solution)/shard_map/ppermute | solution.py:397
  34.2 1.7 %shard_map.71.w_ref = f32[512,384]{1,0:T(8,128)S(1)} custom-call(s32[24]{0:T(128)S(1)} %concatenate.3.meta_ref, bf16[512,1536]{1,0:T(8,128)(2,1)S(1)} %copy-done.4, bf16[512,1536]{1,0:T(8,128)(2,1)S(1)} %copy-done.1, bf16[512,1536]{1,0:T(8,128)(2,1)S(1)} %copy-done.3, bf16[512,512]{1,0:T(8,128)(2,1)S(1)} %get-tuple-element.39.rest_0_), custom_call_target="tpu_custom_call" | custom-call | flops 2000000000 | bytes 1024 | tf_op jit(solution)/shard_map/pallas_call | solution.py:120
  37.0 1.5 %collective-permute-start.6 = (bf16[384,128]{1,0:T(8,128)(2,1)S(1)}, bf16[384,128]{1,0:T(8,128)(2,1)S(1)}, u32[]{:S(2)}, u32[]{:S(2)}) collective-permute-start(bf16[384,128]{1,0:T(8,128)(2,1)S(1)} %get-tuple-element.49), channel_id=1, source_target_pairs={{0,4},{2,6},{4,0},{6,2},{8,12},{10,14},{12,8},{14,10},{16,20},{18,... | collective-permute-start | bytes 294920 | tf_op jit(solution)/shard_map/ppermute | solution.py:394
  39.6 1.6 %collective-permute-start.4 = (bf16[512,384]{1,0:T(8,128)(2,1)S(1)}, bf16[512,384]{1,0:T(8,128)(2,1)S(1)}, u32[]{:S(2)}, u32[]{:S(2)}) collective-permute-start(bf16[512,384]{1,0:T(8,128)(2,1)S(1)} %shard_map.73.refs_0_), channel_id=1, source_target_pairs={{0,1},{1,0},{2,3},{3,2},{4,5},{5,4},{6,7},{7,6},{8,9},{9,8},{10,11... | collective-permute-start | bytes 1179656 | tf_op jit(solution)/shard_map/ppermute | solution.py:400
  42.3 2.5 %collective-permute-start.11 = (bf16[384,512]{1,0:T(8,128)(2,1)S(1)}, bf16[384,512]{1,0:T(8,128)(2,1)S(1)}, u32[]{:S(2)}, u32[]{:S(2)}) collective-permute-start(bf16[384,512]{1,0:T(8,128)(2,1)S(1)} %slice.6), channel_id=1, source_target_pairs={{0,8},{2,10},{4,12},{6,14},{8,0},{10,2},{12,4},{14,6},{16,24},{18,... | collective-permute-start | bytes 1179656 | tf_op jit(solution)/shard_map/ppermute | solution.py:394
  44.8 1.5 %collective-permute-start.16 = (bf16[384,1024]{1,0:T(8,128)(2,1)S(1)}, bf16[384,1024]{1,0:T(8,128)(2,1)S(1)}, u32[]{:S(2)}, u32[]{:S(2)}) collective-permute-start(bf16[384,1024]{1,0:T(8,128)(2,1)S(1)} %collective-permute-done.9.refs_2_), channel_id=1, source_target_pairs={{0,4},{2,6},{4,0},{6,2},{8,12},{10,14},{12,8},{14,10},{16,20},{18,... | collective-permute-start | bytes 2359304 | tf_op jit(solution)/shard_map/ppermute | solution.py:394
  48.5 1.6 %collective-permute-start.8 = (bf16[512,384]{1,0:T(8,128)(2,1)S(1)}, bf16[512,384]{1,0:T(8,128)(2,1)S(1)}, u32[]{:S(2)}, u32[]{:S(2)}) collective-permute-start(bf16[512,384]{1,0:T(8,128)(2,1)S(1)} %shard_map.74.refs_1_), channel_id=1, source_target_pairs={{0,1},{1,0},{2,3},{3,2},{4,5},{5,4},{6,7},{7,6},{8,9},{9,8},{10,11... | collective-permute-start | bytes 1179656 | tf_op jit(solution)/shard_map/ppermute | solution.py:400
  51.7 2.2 %collective-permute-done.11.refs_4_ = bf16[384,512]{1,0:T(8,128)(2,1)S(1)} collective-permute-done((bf16[384,512]{1,0:T(8,128)(2,1)S(1)}, bf16[384,512]{1,0:T(8,128)(2,1)S(1)}, u32[]{:S(2)}, u32[]{:S(2)}) %collective-permute-start.11) | collective-permute-done | bytes 393248 | tf_op jit(solution)/shard_map/ppermute | solution.py:394
  54.0 5.3 %shard_map.78.t_ref = f32[512,2048]{1,0:T(8,128)S(1)} custom-call(s32[24]{0:T(128)S(1)} %concatenate.3.meta_ref, bf16[512,384]{1,0:T(8,128)(2,1)S(1)} %shard_map.73.refs_0_, bf16[512,384]{1,0:T(8,128)(2,1)S(1)} %shard_map.74.refs_1_, bf16[512,384]{1,0:T(8,128)(2,1)S(1)} %shard_map.76.refs_2_, bf16[512,384]{1,0:T(8,128)(2,1)S(1)} %shard_map.77.refs_3_, ...), custom_call_target="tpu_custom_call" | custom-call | flops 5000000000 | bytes 1024 | tf_op jit(solution)/shard_map/pallas_call | solution.py:326
  59.3 6.0 %collective-permute-done.16.refs_1_ = bf16[384,1024]{1,0:T(8,128)(2,1)S(1)} collective-permute-done((bf16[384,1024]{1,0:T(8,128)(2,1)S(1)}, bf16[384,1024]{1,0:T(8,128)(2,1)S(1)}, u32[]{:S(2)}, u32[]{:S(2)}) %collective-permute-start.16) | collective-permute-done | bytes 786464 | tf_op jit(solution)/shard_map/ppermute | solution.py:394
  66.0 6.3 %collective-permute-done.17.refs_2_ = bf16[384,512]{1,0:T(8,128)(2,1)S(1)} collective-permute-done((bf16[384,512]{1,0:T(8,128)(2,1)S(1)}, bf16[384,512]{1,0:T(8,128)(2,1)S(1)}, u32[]{:S(2)}, u32[]{:S(2)}) %collective-permute-start.17) | collective-permute-done | bytes 393248 | tf_op jit(solution)/shard_map/ppermute | solution.py:394
  74.3 2.6 %collective-permute-done.18.refs_3_ = bf16[384,512]{1,0:T(8,128)(2,1)S(1)} collective-permute-done((bf16[384,512]{1,0:T(8,128)(2,1)S(1)}, bf16[384,512]{1,0:T(8,128)(2,1)S(1)}, u32[]{:S(2)}, u32[]{:S(2)}) %collective-permute-start.18) | collective-permute-done | bytes 393248 | tf_op jit(solution)/shard_map/ppermute | solution.py:394
  76.9 3.9 %shard_map.79.t_ref = f32[512,2048]{1,0:T(8,128)S(1)} custom-call(s32[24]{0:T(128)S(1)} %concatenate.3.meta_ref, f32[512,2048]{1,0:T(8,128)S(1)} %shard_map.78.t_ref, bf16[512,384]{1,0:T(8,128)(2,1)S(1)} %collective-permute-done.4.refs_0_, bf16[512,384]{1,0:T(8,128)(2,1)S(1)} %collective-permute-done.8.refs_1_, ...), custom_call_target="tpu_custom_call" | custom-call | flops 3000000000 | bytes 1024 | tf_op jit(solution)/shard_map/pallas_call | solution.py:366
  80.8 3.5 %collective-permute-done.15.refs_0_ = bf16[512,384]{1,0:T(8,128)(2,1)S(1)} collective-permute-done((bf16[512,384]{1,0:T(8,128)(2,1)S(1)}, bf16[512,384]{1,0:T(8,128)(2,1)S(1)}, u32[]{:S(2)}, u32[]{:S(2)}) %collective-permute-start.15) | collective-permute-done | bytes 393248 | tf_op jit(solution)/shard_map/ppermute | solution.py:400
  84.3 3.2 %shard_map.80.t_ref = f32[512,2048]{1,0:T(8,128)S(1)} custom-call(s32[24]{0:T(128)S(1)} %concatenate.3.meta_ref, f32[512,2048]{1,0:T(8,128)S(1)} %shard_map.79.t_ref, bf16[512,384]{1,0:T(8,128)(2,1)S(1)} %collective-permute-done.15.refs_0_, bf16[384,1024]{1,0:T(8,128)(2,1)S(1)} %collective-permute-done.16.refs_1_, ...), custom_call_target="tpu_custom_call" | custom-call | flops 3000000000 | bytes 1024 | tf_op jit(solution)/shard_map/pallas_call | solution.py:366
  87.5 2.8 %collective-permute-done.19.refs_0_ = bf16[512,384]{1,0:T(8,128)(2,1)S(1)} collective-permute-done((bf16[512,384]{1,0:T(8,128)(2,1)S(1)}, bf16[512,384]{1,0:T(8,128)(2,1)S(1)}, u32[]{:S(2)}, u32[]{:S(2)}) %collective-permute-start.19) | collective-permute-done | bytes 393248 | tf_op jit(solution)/shard_map/ppermute | solution.py:400
  90.4 3.9 %shard_map.81 = bf16[512,2048]{1,0:T(8,128)(2,1)} custom-call(s32[24]{0:T(128)S(1)} %concatenate.3.meta_ref, f32[512,2048]{1,0:T(8,128)S(1)} %shard_map.80.t_ref, bf16[512,384]{1,0:T(8,128)(2,1)S(1)} %collective-permute-done.19.refs_0_, bf16[384,1024]{1,0:T(8,128)(2,1)S(1)} %collective-permute-done.20.refs_1_, ...), custom_call_target="tpu_custom_call" | custom-call | flops 3000000000 | bytes 1024 | tf_op jit(solution)/shard_map/pallas_call | solution.py:366
  (68 shorter events, 22.5 us)
Async XLA Ops:
  7.1 8.9 %collective-permute-start = (bf16[2,384,128]{2,1,0:T(8,128)(2,1)S(1)}, bf16[2,384,128]{2,1,0:T(8,128)(2,1)S(1)}, u32[]{:S(2)}, u32[]{:S(2)}) collective-permute-start(bf16[2,384,128]{2,1,0:T(8,128)(2,1)S(1)} %get-tuple-element.31), channel_id=1, source_target_pairs={{0,2},{2,0},{4,6},{6,4},{8,10},{10,8},{12,14},{14,12},{16,18},{18,... | collective-permute-start | bytes 589832 | tf_op jit(solution)/shard_map/ppermute | solution.py:394
  7.6 34.7 %collective-permute-start.9 = (bf16[384,1024]{1,0:T(8,128)(2,1)}, bf16[384,1024]{1,0:T(8,128)(2,1)S(1)}, u32[]{:S(2)}, u32[]{:S(2)}) collective-permute-start(bf16[384,1024]{1,0:T(8,128)(2,1)} %dynamic_slice.6), channel_id=1, source_target_pairs={{0,1},{1,0},{2,3},{3,2},{4,5},{5,4},{6,7},{7,6},{8,9},{9,8},{10,11... | collective-permute-start | bytes 2359304 | tf_op jit(solution)/shard_map/ppermute | solution.py:400
  11.2 31.0 %collective-permute-start.10 = (bf16[384,512]{1,0:T(8,128)(2,1)S(1)}, bf16[384,512]{1,0:T(8,128)(2,1)S(1)}, u32[]{:S(2)}, u32[]{:S(2)}) collective-permute-start(bf16[384,512]{1,0:T(8,128)(2,1)S(1)} %dynamic_slice.7), channel_id=1, source_target_pairs={{0,1},{1,0},{2,3},{3,2},{4,5},{5,4},{6,7},{7,6},{8,9},{9,8},{10,11... | collective-permute-start | bytes 1179656 | tf_op jit(solution)/shard_map/ppermute | solution.py:400
  16.6 4.9 %collective-permute-start.1 = (bf16[384,128]{1,0:T(8,128)(2,1)S(1)}, bf16[384,128]{1,0:T(8,128)(2,1)S(1)}, u32[]{:S(2)}, u32[]{:S(2)}) collective-permute-start(bf16[384,128]{1,0:T(8,128)(2,1)S(1)} %get-tuple-element.41), channel_id=1, source_target_pairs={{0,4},{2,6},{4,0},{6,2},{8,12},{10,14},{12,8},{14,10},{16,20},{18,... | collective-permute-start | bytes 294920 | tf_op jit(solution)/shard_map/ppermute | solution.py:394
  22.2 5.9 %collective-permute-start.2 = (bf16[384,128]{1,0:T(8,128)(2,1)S(1)}, bf16[384,128]{1,0:T(8,128)(2,1)S(1)}, u32[]{:S(2)}, u32[]{:S(2)}) collective-permute-start(bf16[384,128]{1,0:T(8,128)(2,1)S(1)} %shard_map.68.a_ref), channel_id=1, source_target_pairs={{0,8},{2,10},{4,12},{6,14},{8,16},{10,18},{12,20},{14,22},{16,24},... | collective-permute-start | bytes 294920 | tf_op jit(solution)/shard_map/ppermute | solution.py:397
  28.7 7.5 %collective-permute-start.3 = (bf16[384,128]{1,0:T(8,128)(2,1)S(1)}, bf16[384,128]{1,0:T(8,128)(2,1)S(1)}, u32[]{:S(2)}, u32[]{:S(2)}) collective-permute-start(bf16[384,128]{1,0:T(8,128)(2,1)S(1)} %shard_map.70), channel_id=1, source_target_pairs={{0,16},{2,18},{4,20},{6,22},{8,24},{10,26},{12,28},{14,30},{1,17},... | collective-permute-start | bytes 294920 | tf_op jit(solution)/shard_map/ppermute | solution.py:397
  34.2 19.8 %slice-start = ((s8[12582912]{0:T(1024)(128)(4,1)}), s8[4194304]{0:T(1024)(128)(4,1)S(1)}, s32[]{:S(2)}) async-start(s8[12582912]{0:T(1024)(128)(4,1)} %bitcast.4), calls=%async_computation | async-start | bytes 8388608
  36.9 4.3 %collective-permute-start.5 = (bf16[384,128]{1,0:T(8,128)(2,1)S(1)}, bf16[384,128]{1,0:T(8,128)(2,1)S(1)}, u32[]{:S(2)}, u32[]{:S(2)}) collective-permute-start(bf16[384,128]{1,0:T(8,128)(2,1)S(1)} %get-tuple-element.48), channel_id=1, source_target_pairs={{0,2},{2,0},{4,6},{6,4},{8,10},{10,8},{12,14},{14,12},{16,18},{18,... | collective-permute-start | bytes 294920 | tf_op jit(solution)/shard_map/ppermute | solution.py:394
  37.0 5.2 %collective-permute-start.6 = (bf16[384,128]{1,0:T(8,128)(2,1)S(1)}, bf16[384,128]{1,0:T(8,128)(2,1)S(1)}, u32[]{:S(2)}, u32[]{:S(2)}) collective-permute-start(bf16[384,128]{1,0:T(8,128)(2,1)S(1)} %get-tuple-element.49), channel_id=1, source_target_pairs={{0,4},{2,6},{4,0},{6,2},{8,12},{10,14},{12,8},{14,10},{16,20},{18,... | collective-permute-start | bytes 294920 | tf_op jit(solution)/shard_map/ppermute | solution.py:394
  39.6 11.5 %collective-permute-start.4 = (bf16[512,384]{1,0:T(8,128)(2,1)S(1)}, bf16[512,384]{1,0:T(8,128)(2,1)S(1)}, u32[]{:S(2)}, u32[]{:S(2)}) collective-permute-start(bf16[512,384]{1,0:T(8,128)(2,1)S(1)} %shard_map.73.refs_0_), channel_id=1, source_target_pairs={{0,1},{1,0},{2,3},{3,2},{4,5},{5,4},{6,7},{7,6},{8,9},{9,8},{10,11... | collective-permute-start | bytes 1179656 | tf_op jit(solution)/shard_map/ppermute | solution.py:400
  42.3 11.6 %collective-permute-start.11 = (bf16[384,512]{1,0:T(8,128)(2,1)S(1)}, bf16[384,512]{1,0:T(8,128)(2,1)S(1)}, u32[]{:S(2)}, u32[]{:S(2)}) collective-permute-start(bf16[384,512]{1,0:T(8,128)(2,1)S(1)} %slice.6), channel_id=1, source_target_pairs={{0,8},{2,10},{4,12},{6,14},{8,0},{10,2},{12,4},{14,6},{16,24},{18,... | collective-permute-start | bytes 1179656 | tf_op jit(solution)/shard_map/ppermute | solution.py:394
  44.8 20.5 %collective-permute-start.16 = (bf16[384,1024]{1,0:T(8,128)(2,1)S(1)}, bf16[384,1024]{1,0:T(8,128)(2,1)S(1)}, u32[]{:S(2)}, u32[]{:S(2)}) collective-permute-start(bf16[384,1024]{1,0:T(8,128)(2,1)S(1)} %collective-permute-done.9.refs_2_), channel_id=1, source_target_pairs={{0,4},{2,6},{4,0},{6,2},{8,12},{10,14},{12,8},{14,10},{16,20},{18,... | collective-permute-start | bytes 2359304 | tf_op jit(solution)/shard_map/ppermute | solution.py:394
  46.9 1.6 %collective-permute-start.7 = (bf16[384,128]{1,0:T(8,128)(2,1)S(1)}, bf16[384,128]{1,0:T(8,128)(2,1)S(1)}, u32[]{:S(2)}, u32[]{:S(2)}) collective-permute-start(bf16[384,128]{1,0:T(8,128)(2,1)S(1)} %get-tuple-element.51), channel_id=1, source_target_pairs={{0,2},{2,0},{4,6},{6,4},{8,10},{10,8},{12,14},{14,12},{16,18},{18,... | collective-permute-start | bytes 294920 | tf_op jit(solution)/shard_map/ppermute | solution.py:394
  47.0 18.3 %collective-permute-start.13 = (bf16[384,512]{1,0:T(8,128)(2,1)S(1)}, bf16[384,512]{1,0:T(8,128)(2,1)S(1)}, u32[]{:S(2)}, u32[]{:S(2)}) collective-permute-start(bf16[384,512]{1,0:T(8,128)(2,1)S(1)} %collective-permute-done.10.refs_3_), channel_id=1, source_target_pairs={{0,2},{2,0},{4,6},{6,4},{8,10},{10,8},{12,14},{14,12},{16,18},{18,... | collective-permute-start | bytes 1179656 | tf_op jit(solution)/shard_map/ppermute | solution.py:394
  48.5 16.9 %collective-permute-start.8 = (bf16[512,384]{1,0:T(8,128)(2,1)S(1)}, bf16[512,384]{1,0:T(8,128)(2,1)S(1)}, u32[]{:S(2)}, u32[]{:S(2)}) collective-permute-start(bf16[512,384]{1,0:T(8,128)(2,1)S(1)} %shard_map.74.refs_1_), channel_id=1, source_target_pairs={{0,1},{1,0},{2,3},{3,2},{4,5},{5,4},{6,7},{7,6},{8,9},{9,8},{10,11... | collective-permute-start | bytes 1179656 | tf_op jit(solution)/shard_map/ppermute | solution.py:400
  51.1 21.2 %collective-permute-start.17 = (bf16[384,512]{1,0:T(8,128)(2,1)S(1)}, bf16[384,512]{1,0:T(8,128)(2,1)S(1)}, u32[]{:S(2)}, u32[]{:S(2)}) collective-permute-start(bf16[384,512]{1,0:T(8,128)(2,1)S(1)} %collective-permute-done.10.refs_3_), channel_id=1, source_target_pairs={{0,4},{2,6},{4,0},{6,2},{8,12},{10,14},{12,8},{14,10},{16,20},{18,... | collective-permute-start | bytes 1179656 | tf_op jit(solution)/shard_map/ppermute | solution.py:394
  54.0 19.7 %collective-permute-start.12 = (bf16[384,1024]{1,0:T(8,128)(2,1)S(1)}, bf16[384,1024]{1,0:T(8,128)(2,1)S(1)}, u32[]{:S(2)}, u32[]{:S(2)}) collective-permute-start(bf16[384,1024]{1,0:T(8,128)(2,1)S(1)} %collective-permute-done.9.refs_2_), channel_id=1, source_target_pairs={{0,2},{2,0},{4,6},{6,4},{8,10},{10,8},{12,14},{14,12},{16,18},{18,... | collective-permute-start | bytes 2359304 | tf_op jit(solution)/shard_map/ppermute | solution.py:394
  65.3 9.0 %collective-permute-start.14 = (bf16[384,512]{1,0:T(8,128)(2,1)S(1)}, bf16[384,512]{1,0:T(8,128)(2,1)S(1)}, u32[]{:S(2)}, u32[]{:S(2)}) collective-permute-start(bf16[384,512]{1,0:T(8,128)(2,1)S(1)} %collective-permute-done.11.refs_4_), channel_id=1, source_target_pairs={{0,2},{2,0},{4,6},{6,4},{8,10},{10,8},{12,14},{14,12},{16,18},{18,... | collective-permute-start | bytes 1179656 | tf_op jit(solution)/shard_map/ppermute | solution.py:394
  65.3 11.6 %collective-permute-start.18 = (bf16[384,512]{1,0:T(8,128)(2,1)S(1)}, bf16[384,512]{1,0:T(8,128)(2,1)S(1)}, u32[]{:S(2)}, u32[]{:S(2)}) collective-permute-start(bf16[384,512]{1,0:T(8,128)(2,1)S(1)} %slice.7), channel_id=1, source_target_pairs={{0,8},{2,10},{4,12},{6,14},{8,0},{10,2},{12,4},{14,6},{16,24},{18,... | collective-permute-start | bytes 1179656 | tf_op jit(solution)/shard_map/ppermute | solution.py:394
  65.4 24.9 %collective-permute-start.20 = (bf16[384,1024]{1,0:T(8,128)(2,1)S(1)}, bf16[384,1024]{1,0:T(8,128)(2,1)S(1)}, u32[]{:S(2)}, u32[]{:S(2)}) collective-permute-start(bf16[384,1024]{1,0:T(8,128)(2,1)S(1)} %collective-permute-done.16.refs_1_), channel_id=1, source_target_pairs={{0,2},{2,0},{4,6},{6,4},{8,10},{10,8},{12,14},{14,12},{16,18},{18,... | collective-permute-start | bytes 2359304 | tf_op jit(solution)/shard_map/ppermute | solution.py:394
  72.3 12.1 %collective-permute-start.15 = (bf16[512,384]{1,0:T(8,128)(2,1)S(1)}, bf16[512,384]{1,0:T(8,128)(2,1)S(1)}, u32[]{:S(2)}, u32[]{:S(2)}) collective-permute-start(bf16[512,384]{1,0:T(8,128)(2,1)S(1)} %shard_map.76.refs_2_), channel_id=1, source_target_pairs={{0,1},{1,0},{2,3},{3,2},{4,5},{5,4},{6,7},{7,6},{8,9},{9,8},{10,11... | collective-permute-start | bytes 1179656 | tf_op jit(solution)/shard_map/ppermute | solution.py:400
  73.6 16.7 %collective-permute-start.19 = (bf16[512,384]{1,0:T(8,128)(2,1)S(1)}, bf16[512,384]{1,0:T(8,128)(2,1)S(1)}, u32[]{:S(2)}, u32[]{:S(2)}) collective-permute-start(bf16[512,384]{1,0:T(8,128)(2,1)S(1)} %shard_map.77.refs_3_), channel_id=1, source_target_pairs={{0,1},{1,0},{2,3},{3,2},{4,5},{5,4},{6,7},{7,6},{8,9},{9,8},{10,11... | collective-permute-start | bytes 1179656 | tf_op jit(solution)/shard_map/ppermute | solution.py:400
  74.3 16.1 %collective-permute-start.21 = (bf16[384,512]{1,0:T(8,128)(2,1)S(1)}, bf16[384,512]{1,0:T(8,128)(2,1)S(1)}, u32[]{:S(2)}, u32[]{:S(2)}) collective-permute-start(bf16[384,512]{1,0:T(8,128)(2,1)S(1)} %collective-permute-done.17.refs_2_), channel_id=1, source_target_pairs={{0,2},{2,0},{4,6},{6,4},{8,10},{10,8},{12,14},{14,12},{16,18},{18,... | collective-permute-start | bytes 1179656 | tf_op jit(solution)/shard_map/ppermute | solution.py:394
  76.9 13.5 %collective-permute-start.22 = (bf16[384,512]{1,0:T(8,128)(2,1)S(1)}, bf16[384,512]{1,0:T(8,128)(2,1)S(1)}, u32[]{:S(2)}, u32[]{:S(2)}) collective-permute-start(bf16[384,512]{1,0:T(8,128)(2,1)S(1)} %collective-permute-done.18.refs_3_), channel_id=1, source_target_pairs={{0,2},{2,0},{4,6},{6,4},{8,10},{10,8},{12,14},{14,12},{16,18},{18,... | collective-permute-start | bytes 1179656 | tf_op jit(solution)/shard_map/ppermute | solution.py:394
  (9 other events, 62.9 us)

commit v8 on v7

--- a/solution.py
+++ b/solution.py
@@ -12,7 +12,6 @@
 F32, BF16 = jnp.float32, jnp.bfloat16
 LENS = 8
 VMEM_LIMIT = 16 * 1024 * 1024
-VMEM_MOST = 62 * 1024 * 1024
 
 
 def doc_start(meta, doc_count, token):
@@ -115,53 +114,57 @@
     )(meta, query, key, value)
 
 
-def local(kernel, meta, arrays, shapes, micros, limit=4):
-    vmem = pl.BlockSpec(memory_space=pltpu.VMEM)
-    return pl.pallas_call(
-        kernel,
-        out_shape=shapes,
-        in_specs=[pl.BlockSpec(memory_space=pltpu.SMEM)] + [vmem] * len(arrays),
-        out_specs=[vmem] * len(shapes),
-        compiler_params=pltpu.CompilerParams(vmem_limit_bytes=limit * 1024 * 1024),
-        cost_estimate=pl.CostEstimate(flops=int(micros * 1e9), bytes_accessed=1024, transcendentals=0),
-    )(meta, *arrays)
-
-
 def whole(shape):
     return pl.BlockSpec(shape, lambda *_: (0,) * len(shape))
 
 
+def local(kernel, meta, arrays, shapes, micros, limit=4, specs=None):
+    return call(
+        kernel,
+        (1,),
+        specs or [whole(a.shape) for a in arrays],
+        [whole(s.shape) for s in shapes],
+        shapes,
+        int(micros * 1e9),
+        1024,
+        (),
+        limit * 1024 * 1024,
+    )(meta, *arrays)
+
+
+def group(rows, part, slot):
+    return pl.BlockSpec((rows, part), lambda i, m: (0, m[1] ^ slot))
+
+
 def after(meta, *arrays):
     return lax.optimization_barrier((meta, *arrays))[0]
 
 
 def factor(condition):
     return jnp.where(condition, 1.0, 0.0)
-
-
-def head_columns(meta_ref, slot, part, h):
-    return pl.ds(pl.multiple_of((meta_ref[1] ^ slot) * part + h * DH, DH), DH)
 
 
 def split_states(meta, key, value, doc_count):
     rows, width = key.shape
     part = width // 4
-
-    def kernel(meta_ref, k_ref, v_ref, send_ref, keep_ref):
+    order = (1, 3, 0, 2)
+
+    def kernel(meta_ref, *refs):
         offset = meta_ref[0] * rows
         first = doc_start(meta_ref, doc_count, offset + rows - 1) - offset
         live = lax.broadcasted_iota(jnp.int32, (rows, DH), 0) >= first
-        for i, s in enumerate((1, 3, 0, 2)):
-            o_ref = (send_ref, keep_ref)[i // 2]
+        for i in range(4):
+            k_ref, v_ref, o_ref = refs[i], refs[4 + i], refs[8 + i // 2]
             for h in range(part // DH):
-                cols = head_columns(meta_ref, s, part, h)
+                cols = slice(h * DH, (h + 1) * DH)
                 k = jnp.where(live, k_ref[:, cols], jnp.zeros((), BF16))
                 state = lax.dot_general(
                     k, v_ref[:, cols], (((0,), (0,)), ((), ())), preferred_element_type=F32
                 )
-                o_ref[i % 2, h * DH : (h + 1) * DH, :] = state.astype(BF16)
-
-    return local(kernel, meta, (key, value), [jax.ShapeDtypeStruct((2, part, DH), BF16)] * 2, 2, 8)
+                o_ref[i % 2, cols, :] = state.astype(BF16)
+
+    arrays, specs = [key] * 4 + [value] * 4, [group(rows, part, s) for s in order] * 2
+    return local(kernel, meta, arrays, [jax.ShapeDtypeStruct((2, part, DH), BF16)] * 2, 2, 16, specs)
 
 
 def seen_mask(meta_ref, rows, doc_count):
@@ -190,7 +193,7 @@
         else:
             mask_ref, o_ref = rest
         for h in range(part // DH):
-            cols = head_columns(meta_ref, slot, part, h)
+            cols = slice(h * DH, (h + 1) * DH)
             for i in range(2):
                 r = slice(i * tile, (i + 1) * tile)
                 seen = (i + 1) * tile
@@ -198,13 +201,14 @@
                     q_ref[r, cols], k_ref[:seen, cols], (((1,), (1,)), ((), ())), preferred_element_type=F32
                 )
                 scores = scores.astype(BF16) * mask_ref[r, :seen]
-                o_ref[r, h * DH : (h + 1) * DH] = jnp.dot(scores, v_ref[:seen, cols], preferred_element_type=F32)
+                o_ref[r, cols] = jnp.dot(scores, v_ref[:seen, cols], preferred_element_type=F32)
 
     shapes = [jax.ShapeDtypeStruct((rows, part), F32)]
-    arrays = (query, key, value)
+    arrays, specs = [query, key, value], [group(rows, part, slot)] * 3
     if make:
-        return local(kernel, meta, arrays, shapes + [jax.ShapeDtypeStruct((rows, rows), BF16)], 2, 12)
-    return local(kernel, meta, (*arrays, mask), shapes, 2, 12)[0]
+        shapes = shapes + [jax.ShapeDtypeStruct((rows, rows), BF16)]
+        return local(kernel, meta, arrays, shapes, 2, 16, specs)
+    return local(kernel, meta, [*arrays, mask], shapes, 2, 16, [*specs, whole(mask.shape)])[0]
 
 
 def small(kernel, meta, arrays, shape, count):
@@ -282,11 +286,12 @@
     return small(kernel, meta, (chip, keep, core_got), chip.shape, 2)
 
 
-def norm_heads(meta, query, within, carry, gain, doc_count, slot=None):
+def norm_heads(meta, query, withins, carries, gain, doc_count, slots=None):
     rows = query.shape[0]
-    part = carry.shape[0]
-
-    def kernel(meta_ref, q_ref, w_ref, c_ref, g_ref, o_ref):
+    part = carries[0].shape[0]
+    count = len(carries)
+
+    def kernel(meta_ref, *refs):
         offset = meta_ref[0] * rows
         begins = doc_start(meta_ref, doc_count, offset)
         bound = jnp.int32(0)
@@ -297,28 +302,41 @@
             end = jnp.where(previous <= offset, bound, end)
         stop = jnp.where(begins < offset, end - offset, 0)
         cross = lax.broadcasted_iota(jnp.int32, (rows, DH), 0) < stop
-        for h in range(part // DH):
-            here = slice(h * DH, (h + 1) * DH)
-            cols = here if slot is None else head_columns(meta_ref, slot, part, h)
-            term = jnp.dot(q_ref[:, cols], c_ref[here, :], preferred_element_type=F32)
-            mixture = w_ref[:, here] + jnp.where(cross, term, 0.0)
-            mean = jnp.mean(mixture * mixture, axis=-1, keepdims=True)
-            o_ref[:, here] = (mixture * lax.rsqrt(mean + 1e-06) * g_ref[:, cols]).astype(BF16)
-
-    shapes = [jax.ShapeDtypeStruct((rows, part), BF16)]
-    return local(kernel, meta, (query, within, carry, gain.reshape(1, -1)), shapes, 1, 8)[0]
+        o_ref = refs[-1]
+        for n in range(count):
+            q_ref, w_ref, c_ref, g_ref = refs[4 * n : 4 * n + 4]
+            for h in range(part // DH):
+                cols = slice(h * DH, (h + 1) * DH)
+                term = jnp.dot(q_ref[:, cols], c_ref[cols, :], preferred_element_type=F32)
+                mixture = w_ref[:, cols] + jnp.where(cross, term, 0.0)
+                mean = jnp.mean(mixture * mixture, axis=-1, keepdims=True)
+                o_ref[:, n * part + h * DH : n * part + (h + 1) * DH] = (
+                    mixture * lax.rsqrt(mean + 1e-06) * g_ref[:, cols]
+                ).astype(BF16)
+
+    gain = gain.reshape(1, -1)
+    arrays, specs = [], []
+    for n in range(count):
+        arrays += [query, withins[n], carries[n], gain]
+        wide = [whole((rows, part)), whole((1, part))] if slots is None else [
+            group(rows, part, slots[n]), group(1, part, slots[n])
+        ]
+        specs += [wide[0], whole((rows, part)), whole((part, DH)), wide[1]]
+    shapes = [jax.ShapeDtypeStruct((rows, part * count), BF16)]
+    return local(kernel, meta, arrays, shapes, count, 16, specs)[0]
 
 
 TILES = 4
 
 
 def project_own(meta, pieces, weight, columns):
-    rows, part = pieces[0].shape
+    rows = pieces[0].shape[0]
+    part = weight.shape[0] // 4
     tile = columns // TILES
     count = len(pieces)
 
     def kernel(meta_ref, *refs):
-        ns, ws, o_ref = refs[:count], refs[count : 2 * count], refs[-1]
+        ns, ws, o_ref = refs[:count], refs[count:-1], refs[-1]
         n = jnp.concatenate([r[...] for r in ns], axis=1)
         w = jnp.concatenate([r[...] for r in ws], axis=0)
         o_ref[...] = jnp.dot(n, w, preferred_element_type=F32)
@@ -326,27 +344,34 @@
     return call(
         kernel,
         (TILES,),
-        [whole((rows, part))] * count
-        + [pl.BlockSpec((part, tile), lambda n, m, s=s: (m[1] ^ s, m[2] * TILES + n)) for s in range(count)],
+        [whole(p.shape) for p in pieces]
+        + [pl.BlockSpec((part, tile), lambda n, m, s=s: (m[1] ^ s, m[2] * TILES + n)) for s in range(4)],
         pl.BlockSpec((rows, tile), lambda n, m: (0, n)),
         jax.ShapeDtypeStruct((rows, columns), F32),
-        5 * 10**9,
+        10**6,
         1024,
-    )(meta, *pieces, *[weight] * count)
+    )(meta, *pieces, *[weight] * 4)
 
 
 def project_more(meta, total, pieces, weights, dtype):
     rows, columns = total.shape
-    part = pieces[0].shape[1]
     tile = columns // TILES
     count = len(pieces)
-    flat = []
+    flat, specs, places = [], [], []
     for ws in weights:
         start = 0
         for w in ws:
-            tiles = w.shape[1] // tile
-            flat.append((w, start, tiles))
-            start += tiles
+            first, last = start // tile, (start + w.shape[1] - 1) // tile
+            places.append((first, last))
+            flat.append(w)
+            specs.append(
+                pl.BlockSpec(
+                    (w.shape[0], min(tile, w.shape[1])),
+                    lambda n, m, first=first, last=last: (0, jnp.clip(n - first, 0, last - first)),
+                )
+            )
+            start += w.shape[1]
+    per_slot = [len(ws) for ws in weights]
 
     def kernel(meta_ref, t_ref, *refs):
         ns, ws, o_ref = refs[:count], refs[count:-1], refs[-1]
@@ -355,25 +380,25 @@
 
             @pl.when(pl.program_id(0) == c)
             def _():
-                held = [r[...] for r, (_, start, tiles) in zip(ws, flat) if start <= c < start + tiles]
-                w = jnp.concatenate(held, axis=0)
+                rows_of, at = [], 0
+                for size in per_slot:
+                    here = range(at, at + size)
+                    held = [ws[i][...] for i in here if places[i][0] <= c <= places[i][1]]
+                    rows_of.append(jnp.concatenate(held, axis=1))
+                    at += size
+                w = jnp.concatenate(rows_of, axis=0)
                 o_ref[...] = (t_ref[...] + jnp.dot(n, w, preferred_element_type=F32)).astype(dtype)
-
-    def column(start, tiles):
-        return lambda n, m: (0, jnp.clip(n - start, 0, tiles - 1))
 
     out_spec = pl.BlockSpec((rows, tile), lambda n, m: (0, n ^ (m[3] * (TILES // 2))))
     return call(
         kernel,
         (TILES,),
-        [out_spec]
-        + [whole((rows, part))] * count
-        + [pl.BlockSpec((part, tile), column(start, tiles)) for _, start, tiles in flat],
+        [out_spec] + [whole(p.shape) for p in pieces] + specs,
         out_spec,
         jax.ShapeDtypeStruct((rows, columns), dtype),
-        3 * 10**9,
+        10**6,
         1024,
-    )(meta, total, *pieces, *[w for w, _, _ in flat])
+    )(meta, total, *pieces, *flat)
 
 
 def pair_body(n_seq, query, key, value, doc_lengths, gain, weight):
@@ -429,31 +454,32 @@
     carry1 = swap(core_carry0, 1)
     chip_carry2 = swap(chip_carry, 2)
 
-    def norm(slot, within, carry):
-        return norm_heads(meta, query, within, carry, gain, docs, slot)
-
-    normed0 = norm(0, within0, carry0)
+    def norm(slots, withins, carries):
+        return norm_heads(meta, query, withins, carries, gain, docs, slots)
+
+    normed0 = norm((0,), [within0], [carry0])
     far0 = flip(normed0)
-    normed1 = norm(1, within1, carry1)
+    normed1 = norm((1,), [within1], [carry1])
     far1 = flip(normed1)
     carry2, core_carry2 = carry_second(meta, chip_carry2, keep, core_got, rows, docs)
     carry3 = swap(core_carry2, 1)
-    normed2 = norm(2, within2, carry2)
+    normed2 = norm((2, 3), [within2, within3], [carry2, carry3])
     far2 = flip(normed2)
-    normed3 = norm(3, within3, carry3)
-    far3 = flip(normed3)
 
     first, second = lax.optimization_barrier((*w0, chip_carry2, normed0, normed1))[:2]
-    total = project_own(after(meta, far0), [normed0, normed1, normed2, normed3], weight, columns)
+    total = project_own(after(meta, far0), [normed0, normed1, normed2], weight, columns)
     w2 = [swap(first, 2), swap(second, 2)]
     w0.append(swap(first[:, quarter:], plane))
     w2.append(swap(behind(w2[0], total)[:, quarter:], plane))
-    w1 = [swap(w, 1) for w in w0]
-    w3 = [swap(w, 1) for w in w2]
+
+    def cut(w, width):
+        return [w[:, at : at + width] for at in range(0, w.shape[1], width)]
+
+    w1 = [swap(x, 1) for w in w0 for x in cut(w, quarter)]
+    w3 = [swap(x, 1) for w, width in zip(w2, (quarter, quarter // 2, quarter // 2)) for x in cut(w, width)]
 
     total = project_more(meta, total, [far0, far1], [w0, w1], F32)
-    total = project_more(meta, total, [far2], [w2], F32)
-    return project_more(meta, total, [far3], [w3], BF16)
+    return project_more(meta, total, [far2], [w2, w3], BF16)
 
 
 def body(n_seq, n_head, query, key, value, doc_lengths, gain, weight):
@@ -529,7 +555,7 @@
 
     within = within_block(meta, query, key, value, doc_count)
     natural = jnp.stack(carries)[jnp.arange(plane, dtype=jnp.int32) ^ member].reshape(width, DH)
-    normed = norm_heads(meta, query, within, natural, gain, doc_count)
+    normed = norm_heads(meta, query, [within], [natural], gain, doc_count)
     partial_sum = jnp.dot(normed, weight, preferred_element_type=F32)
     return lax.psum_scatter(partial_sum.astype(BF16), "head", scatter_dimension=1, tiled=True)
 

time: 94.7 us -> 92.6 us (0.978)
  waiting for transfers between devices: 25.4 us -> 23.2 us
  starting transfers between devices: 27.1 us -> 28.8 us
  Pallas kernels: 31.8 us -> 30.4 us
    ppermute x15 -> x19, starting transfers between devices: 9.97 us -> 13.4 us  [swap(): return lax.ppermute(x, 'seq', [(i, i ^ bit) for i in range(n_seq)])]
    unnamed x20 -> x16, local copies, waits for them, and re-layouts: 5.67 us -> 2.85 us
    ppermute x15 -> x19, waiting for transfers between devices: 18.4 us -> 16 us  [swap(): return lax.ppermute(x, 'seq', [(i, i ^ bit) for i in range(n_seq)])]
    ppermute x6 -> x5, starting transfers between devices: 7.89 us -> 6.2 us  [flip(): return lax.ppermute(x, 'head', [(0, 1), (1, 0)])]
    pallas_call x18 -> x16, Pallas kernels: 31.8 us -> 30.4 us  [the longest x13 16 us: local(): call(kernel, (1,), specs or [whole(a.shape) for a in arrays], [whole(s.sh...]
    slice x0 -> x4, local copies, waits for them, and re-layouts: none -> 1.27 us  [cut(): return [w[:, at:at + width] for at in range(0, w.shape[1], width)]]
    slice x1, local copies, waits for them, and re-layouts: 0.03 us -> 1.19 us  [pair_body(): w0.append(swap(first[:, quarter:], plane))]
    ppermute x6 -> x5, waiting for transfers between devices: 6.32 us -> 6.64 us  [flip(): return lax.ppermute(x, 'head', [(0, 1), (1, 0)])]
  transfers between devices with their start and end apart: 23 -> 26, of which waited for: 10 -> 9; matrix products, arithmetic and copies ran while one was open for 1% -> 4% of each run, Pallas kernels for 28% -> 26%
where the time goes in v8:
time: 92.6 us; the launch traced here: 92.1 us
  Pallas kernels  30.4 us (33%)
  starting transfers between devices  28.8 us (31%)
  waiting for transfers between devices  23.2 us (25%)
  local copies, waits for them, and re-layouts  9.27 us (10%)
    ppermute x19, waiting for transfers between devices, swap(): return lax.ppermute(x, 'seq', [(i, i ^ bit) for i in range(n_seq)])  16 us
    pallas_call x13, Pallas kernels, local(): call(kernel, (1,), specs or [whole(a.shape) for a in arrays], [whole(s.sh...  16 us
    ppermute x19, starting transfers between devices, swap(): return lax.ppermute(x, 'seq', [(i, i ^ bit) for i in range(n_seq)])  13.4 us
    ppermute x2, starting transfers between devices, shift(): lax.ppermute(x, 'seq', [(i, i + count) for i in range(n_seq - count)])  9.2 us
    pallas_call x2, Pallas kernels, project_more(): call(kernel, (TILES,), [out_spec] + [whole(p.shape) for p in pieces] + sp...  9.11 us
    ppermute x5, waiting for transfers between devices, flip(): return lax.ppermute(x, 'head', [(0, 1), (1, 0)])  6.64 us
    ppermute x5, starting transfers between devices, flip(): return lax.ppermute(x, 'head', [(0, 1), (1, 0)])  6.2 us
    pallas_call x1, Pallas kernels, project_own(): call(kernel, (TILES,), [whole(p.shape) for p in pieces] + [pl.BlockSpec((...  5.34 us
  transfers between devices with their start and end apart: 26, of which 9 were waited for; matrix products, arithmetic and copies ran while one was open for 4% of the time, Pallas kernels for 26%

profile of v8, /device:TPU:0, one launch (start us, length us, event | category | flops | bytes accessed | tf_op | source)
XLA Modules:
  0.0 92.1 jit_solution(2145160356963744827)
XLA Ops:
  0.0 2.2 %dynamic_slice.6 = bf16[384,1024]{1,0:T(8,128)(2,1)} dynamic-slice(bf16[1536,4096]{1,0:T(8,128)(2,1)} %refs_6_.3, s32[]{:T(128)S(6)} %select_n.28, s32[]{:T(128)S(6)} %select_n.29), dynamic_slice_sizes={384,1024} | dynamic-slice | bytes 1572868 | tf_op jit(solution)/shard_map/dynamic_slice | solution.py:433
  2.9 1.4 %copy-done.1 = bf16[512,1536]{1,0:T(8,128)(2,1)S(1)} copy-done((bf16[512,1536]{1,0:T(8,128)(2,1)S(1)}, bf16[512,1536]{1,0:T(8,128)(2,1)}, u32[]{:S(2)}) %copy-start.1) | copy-done | bytes 1572888
  4.3 2.2 %shard_map.64 = (bf16[2,384,128]{2,1,0:T(8,128)(2,1)}, bf16[2,384,128]{2,1,0:T(8,128)(2,1)S(1)}) custom-call(s32[24]{0:T(128)S(1)} %concatenate.3.meta_ref, bf16[512,1536]{1,0:T(8,128)(2,1)S(1)} %copy-done, bf16[512,1536]{1,0:T(8,128)(2,1)S(1)} %copy-done, bf16[512,1536]{1,0:T(8,128)(2,1)S(1)} %copy-done, bf16[512,1536]{1,0:T(8,128)(2,1)S(1)} %copy-done, ...), custom_call_target="tpu_custom_call" | custom-call | flops 2000000000 | bytes 1024 | tf_op jit(solution)/shard_map/pallas_call | solution.py:122
  7.0 2.5 %collective-permute-start.9 = (bf16[384,1024]{1,0:T(8,128)(2,1)}, bf16[384,1024]{1,0:T(8,128)(2,1)}, u32[]{:S(2)}, u32[]{:S(2)}) collective-permute-start(bf16[384,1024]{1,0:T(8,128)(2,1)} %dynamic_slice.6), channel_id=1, source_target_pairs={{0,1},{1,0},{2,3},{3,2},{4,5},{5,4},{6,7},{7,6},{8,9},{9,8},{10,11... | collective-permute-start | bytes 2359304 | tf_op jit(solution)/shard_map/ppermute | solution.py:425
  12.0 1.9 %shard_map.65 = (f32[512,384]{1,0:T(8,128)S(1)}, bf16[512,512]{1,0:T(8,128)(2,1)S(1)}) custom-call(s32[24]{0:T(128)S(1)} %concatenate.3.meta_ref, bf16[512,1536]{1,0:T(8,128)(2,1)S(1)} %copy-done.3, bf16[512,1536]{1,0:T(8,128)(2,1)S(1)} %copy-done, bf16[512,1536]{1,0:T(8,128)(2,1)S(1)} %copy-done.2), custom_call_target="tpu_custom_call" | custom-call | flops 2000000000 | bytes 1024 | tf_op jit(solution)/shard_map/pallas_call | solution.py:122
  14.6 2.1 %collective-permute-start.1 = (bf16[384,128]{1,0:T(8,128)(2,1)S(1)}, bf16[384,128]{1,0:T(8,128)(2,1)S(1)}, u32[]{:S(2)}, u32[]{:S(2)}) collective-permute-start(bf16[384,128]{1,0:T(8,128)(2,1)S(1)} %get-tuple-element.41), channel_id=1, source_target_pairs={{0,4},{2,6},{4,0},{6,2},{8,12},{10,14},{12,8},{14,10},{16,20},{18,... | collective-permute-start | bytes 294920 | tf_op jit(solution)/shard_map/ppermute | solution.py:419
  16.6 1.8 %shard_map.67.refs_1_ = f32[512,384]{1,0:T(8,128)S(1)} custom-call(s32[24]{0:T(128)S(1)} %concatenate.3.meta_ref, bf16[512,1536]{1,0:T(8,128)(2,1)S(1)} %copy-done.3, bf16[512,1536]{1,0:T(8,128)(2,1)S(1)} %copy-done, bf16[512,1536]{1,0:T(8,128)(2,1)S(1)} %copy-done.2, bf16[512,512]{1,0:T(8,128)(2,1)S(1)} %get-tuple-element.39.rest_0_), custom_call_target="tpu_custom_call" | custom-call | flops 2000000000 | bytes 1024 | tf_op jit(solution)/shard_map/pallas_call | solution.py:122
  20.2 3.7 %collective-permute-start.2 = (bf16[384,128]{1,0:T(8,128)(2,1)S(1)}, bf16[384,128]{1,0:T(8,128)(2,1)S(1)}, u32[]{:S(2)}, u32[]{:S(2)}) collective-permute-start(bf16[384,128]{1,0:T(8,128)(2,1)S(1)} %shard_map.68.a_ref), channel_id=1, source_target_pairs={{0,8},{2,10},{4,12},{6,14},{8,16},{10,18},{12,20},{14,22},{16,24},... | collective-permute-start | bytes 294920 | tf_op jit(solution)/shard_map/ppermute | solution.py:422
  23.9 1.8 %shard_map.69.refs_1_ = f32[512,384]{1,0:T(8,128)S(1)} custom-call(s32[24]{0:T(128)S(1)} %concatenate.3.meta_ref, bf16[512,1536]{1,0:T(8,128)(2,1)S(1)} %copy-done.3, bf16[512,1536]{1,0:T(8,128)(2,1)S(1)} %copy-done, bf16[512,1536]{1,0:T(8,128)(2,1)S(1)} %copy-done.2, bf16[512,512]{1,0:T(8,128)(2,1)S(1)} %get-tuple-element.39.rest_0_), custom_call_target="tpu_custom_call" | custom-call | flops 2000000000 | bytes 1024 | tf_op jit(solution)/shard_map/pallas_call | solution.py:122
  26.7 5.5 %collective-permute-start.3 = (bf16[384,128]{1,0:T(8,128)(2,1)S(1)}, bf16[384,128]{1,0:T(8,128)(2,1)S(1)}, u32[]{:S(2)}, u32[]{:S(2)}) collective-permute-start(bf16[384,128]{1,0:T(8,128)(2,1)S(1)} %shard_map.70), channel_id=1, source_target_pairs={{0,16},{2,18},{4,20},{6,22},{8,24},{10,26},{12,28},{14,30},{1,17},... | collective-permute-start | bytes 294920 | tf_op jit(solution)/shard_map/ppermute | solution.py:422
  32.2 1.8 %shard_map.71.refs_5_ = f32[512,384]{1,0:T(8,128)S(1)} custom-call(s32[24]{0:T(128)S(1)} %concatenate.3.meta_ref, bf16[512,1536]{1,0:T(8,128)(2,1)S(1)} %copy-done.3, bf16[512,1536]{1,0:T(8,128)(2,1)S(1)} %copy-done, bf16[512,1536]{1,0:T(8,128)(2,1)S(1)} %copy-done.2, bf16[512,512]{1,0:T(8,128)(2,1)S(1)} %get-tuple-element.39.rest_0_), custom_call_target="tpu_custom_call" | custom-call | flops 2000000000 | bytes 1024 | tf_op jit(solution)/shard_map/pallas_call | solution.py:122
  35.0 1.6 %collective-permute-start.6 = (bf16[384,128]{1,0:T(8,128)(2,1)S(1)}, bf16[384,128]{1,0:T(8,128)(2,1)S(1)}, u32[]{:S(2)}, u32[]{:S(2)}) collective-permute-start(bf16[384,128]{1,0:T(8,128)(2,1)S(1)} %get-tuple-element.49), channel_id=1, source_target_pairs={{0,4},{2,6},{4,0},{6,2},{8,12},{10,14},{12,8},{14,10},{16,20},{18,... | collective-permute-start | bytes 294920 | tf_op jit(solution)/shard_map/ppermute | solution.py:419
  38.7 1.6 %collective-permute-done.6.chip_ref = bf16[384,128]{1,0:T(8,128)(2,1)S(1)} collective-permute-done((bf16[384,128]{1,0:T(8,128)(2,1)S(1)}, bf16[384,128]{1,0:T(8,128)(2,1)S(1)}, u32[]{:S(2)}, u32[]{:S(2)}) %collective-permute-start.6) | collective-permute-done | bytes 98336 | tf_op jit(solution)/shard_map/ppermute | solution.py:419
  40.3 1.5 %collective-permute-start.17 = (bf16[384,1024]{1,0:T(8,128)(2,1)}, bf16[384,1024]{1,0:T(8,128)(2,1)S(1)}, u32[]{:S(2)}, u32[]{:S(2)}) collective-permute-start(bf16[384,1024]{1,0:T(8,128)(2,1)} %collective-permute-done.9.refs_2_), channel_id=1, source_target_pairs={{0,4},{2,6},{4,0},{6,2},{8,12},{10,14},{12,8},{14,10},{16,20},{18,... | collective-permute-start | bytes 2359304 | tf_op jit(solution)/shard_map/ppermute | solution.py:419
  41.8 1.5 %collective-permute-start.4 = (bf16[512,384]{1,0:T(8,128)(2,1)S(1)}, bf16[512,384]{1,0:T(8,128)(2,1)S(1)}, u32[]{:S(2)}, u32[]{:S(2)}) collective-permute-start(bf16[512,384]{1,0:T(8,128)(2,1)S(1)} %shard_map.73.refs_0_), channel_id=1, source_target_pairs={{0,1},{1,0},{2,3},{3,2},{4,5},{5,4},{6,7},{7,6},{8,9},{9,8},{10,11... | collective-permute-start | bytes 1179656 | tf_op jit(solution)/shard_map/ppermute | solution.py:425
  48.0 5.9 %collective-permute-done.4.refs_0_ = bf16[512,384]{1,0:T(8,128)(2,1)S(1)} collective-permute-done((bf16[512,384]{1,0:T(8,128)(2,1)S(1)}, bf16[512,384]{1,0:T(8,128)(2,1)S(1)}, u32[]{:S(2)}, u32[]{:S(2)}) %collective-permute-start.4) | collective-permute-done | bytes 393248 | tf_op jit(solution)/shard_map/ppermute | solution.py:425
  53.8 2.4 %collective-permute-start.11 = (bf16[384,512]{1,0:T(8,128)(2,1)S(1)}, bf16[384,512]{1,0:T(8,128)(2,1)S(1)}, u32[]{:S(2)}, u32[]{:S(2)}) collective-permute-start(bf16[384,512]{1,0:T(8,128)(2,1)S(1)} %slice.30), channel_id=1, source_target_pairs={{0,8},{2,10},{4,12},{6,14},{8,0},{10,2},{12,4},{14,6},{16,24},{18,... | collective-permute-start | bytes 1179656 | tf_op jit(solution)/shard_map/ppermute | solution.py:419
  56.3 4.7 %collective-permute-done.17.refs_1_ = bf16[384,1024]{1,0:T(8,128)(2,1)S(1)} collective-permute-done((bf16[384,1024]{1,0:T(8,128)(2,1)}, bf16[384,1024]{1,0:T(8,128)(2,1)S(1)}, u32[]{:S(2)}, u32[]{:S(2)}) %collective-permute-start.17) | collective-permute-done | bytes 786464 | tf_op jit(solution)/shard_map/ppermute | solution.py:419
  62.3 5.3 %shard_map.77.t_ref = f32[512,2048]{1,0:T(8,128)S(1)} custom-call(s32[24]{0:T(128)S(1)} %concatenate.3.meta_ref, bf16[512,384]{1,0:T(8,128)(2,1)S(1)} %shard_map.73.refs_0_, bf16[512,384]{1,0:T(8,128)(2,1)S(1)} %shard_map.74.refs_1_, bf16[512,768]{1,0:T(8,128)(2,1)S(1)} %shard_map.76.refs_2_, bf16[1536,4096]{1,0:T(8,128)(2,1)S(1)} %bitcast.5, ...), custom_call_target="tpu_custom_call" | custom-call | flops 1000000 | bytes 1024 | tf_op jit(solution)/shard_map/pallas_call | solution.py:344
  67.7 1.6 %collective-permute-start.16 = (bf16[512,768]{1,0:T(8,128)(2,1)S(1)}, bf16[512,768]{1,0:T(8,128)(2,1)S(1)}, u32[]{:S(2)}, u32[]{:S(2)}) collective-permute-start(bf16[512,768]{1,0:T(8,128)(2,1)S(1)} %shard_map.76.refs_2_), channel_id=1, source_target_pairs={{0,1},{1,0},{2,3},{3,2},{4,5},{5,4},{6,7},{7,6},{8,9},{9,8},{10,11... | collective-permute-start | bytes 2359304 | tf_op jit(solution)/shard_map/ppermute | solution.py:425
  69.5 2.4 %collective-permute-start.19 = (bf16[384,512]{1,0:T(8,128)(2,1)S(1)}, bf16[384,512]{1,0:T(8,128)(2,1)S(1)}, u32[]{:S(2)}, u32[]{:S(2)}) collective-permute-start(bf16[384,512]{1,0:T(8,128)(2,1)S(1)} %slice.33), channel_id=1, source_target_pairs={{0,8},{2,10},{4,12},{6,14},{8,0},{10,2},{12,4},{14,6},{16,24},{18,... | collective-permute-start | bytes 1179656 | tf_op jit(solution)/shard_map/ppermute | solution.py:419
  73.6 7.9 %collective-permute-done.19.refs_3_ = bf16[384,512]{1,0:T(8,128)(2,1)S(1)} collective-permute-done((bf16[384,512]{1,0:T(8,128)(2,1)S(1)}, bf16[384,512]{1,0:T(8,128)(2,1)S(1)}, u32[]{:S(2)}, u32[]{:S(2)}) %collective-permute-start.19) | collective-permute-done | bytes 393248 | tf_op jit(solution)/shard_map/ppermute | solution.py:419
  82.2 4.7 %shard_map.78.t_ref = f32[512,2048]{1,0:T(8,128)S(1)} custom-call(s32[24]{0:T(128)S(1)} %concatenate.3.meta_ref, f32[512,2048]{1,0:T(8,128)S(1)} %shard_map.77.t_ref, bf16[512,384]{1,0:T(8,128)(2,1)S(1)} %collective-permute-done.4.refs_0_, bf16[512,384]{1,0:T(8,128)(2,1)S(1)} %collective-permute-done.8.refs_1_, ...), custom_call_target="tpu_custom_call" | custom-call | flops 1000000 | bytes 1024 | tf_op jit(solution)/shard_map/pallas_call | solution.py:393
  87.7 4.4 %shard_map.79 = bf16[512,2048]{1,0:T(8,128)(2,1)} custom-call(s32[24]{0:T(128)S(1)} %concatenate.3.meta_ref, f32[512,2048]{1,0:T(8,128)S(1)} %shard_map.78.t_ref, bf16[512,768]{1,0:T(8,128)(2,1)S(1)} %collective-permute-done.16.refs_0_, bf16[384,1024]{1,0:T(8,128)(2,1)S(1)} %collective-permute-done.17.refs_1_, ...), custom_call_target="tpu_custom_call" | custom-call | flops 1000000 | bytes 1024 | tf_op jit(solution)/shard_map/pallas_call | solution.py:393
  (72 shorter events, 19.4 us)
Async XLA Ops:
  6.5 7.4 %collective-permute-start = (bf16[2,384,128]{2,1,0:T(8,128)(2,1)}, bf16[2,384,128]{2,1,0:T(8,128)(2,1)S(1)}, u32[]{:S(2)}, u32[]{:S(2)}) collective-permute-start(bf16[2,384,128]{2,1,0:T(8,128)(2,1)} %get-tuple-element.31), channel_id=1, source_target_pairs={{0,2},{2,0},{4,6},{6,4},{8,10},{10,8},{12,14},{14,12},{16,18},{18,... | collective-permute-start | bytes 589832 | tf_op jit(solution)/shard_map/ppermute | solution.py:419
  7.0 33.3 %collective-permute-start.9 = (bf16[384,1024]{1,0:T(8,128)(2,1)}, bf16[384,1024]{1,0:T(8,128)(2,1)}, u32[]{:S(2)}, u32[]{:S(2)}) collective-permute-start(bf16[384,1024]{1,0:T(8,128)(2,1)} %dynamic_slice.6), channel_id=1, source_target_pairs={{0,1},{1,0},{2,3},{3,2},{4,5},{5,4},{6,7},{7,6},{8,9},{9,8},{10,11... | collective-permute-start | bytes 2359304 | tf_op jit(solution)/shard_map/ppermute | solution.py:425
  10.5 28.1 %collective-permute-start.10 = (bf16[384,512]{1,0:T(8,128)(2,1)S(1)}, bf16[384,512]{1,0:T(8,128)(2,1)S(1)}, u32[]{:S(2)}, u32[]{:S(2)}) collective-permute-start(bf16[384,512]{1,0:T(8,128)(2,1)S(1)} %dynamic_slice.7), channel_id=1, source_target_pairs={{0,1},{1,0},{2,3},{3,2},{4,5},{5,4},{6,7},{7,6},{8,9},{9,8},{10,11... | collective-permute-start | bytes 1179656 | tf_op jit(solution)/shard_map/ppermute | solution.py:425
  14.6 5.0 %collective-permute-start.1 = (bf16[384,128]{1,0:T(8,128)(2,1)S(1)}, bf16[384,128]{1,0:T(8,128)(2,1)S(1)}, u32[]{:S(2)}, u32[]{:S(2)}) collective-permute-start(bf16[384,128]{1,0:T(8,128)(2,1)S(1)} %get-tuple-element.41), channel_id=1, source_target_pairs={{0,4},{2,6},{4,0},{6,2},{8,12},{10,14},{12,8},{14,10},{16,20},{18,... | collective-permute-start | bytes 294920 | tf_op jit(solution)/shard_map/ppermute | solution.py:419
  20.2 5.9 %collective-permute-start.2 = (bf16[384,128]{1,0:T(8,128)(2,1)S(1)}, bf16[384,128]{1,0:T(8,128)(2,1)S(1)}, u32[]{:S(2)}, u32[]{:S(2)}) collective-permute-start(bf16[384,128]{1,0:T(8,128)(2,1)S(1)} %shard_map.68.a_ref), channel_id=1, source_target_pairs={{0,8},{2,10},{4,12},{6,14},{8,16},{10,18},{12,20},{14,22},{16,24},... | collective-permute-start | bytes 294920 | tf_op jit(solution)/shard_map/ppermute | solution.py:422
  26.7 7.5 %collective-permute-start.3 = (bf16[384,128]{1,0:T(8,128)(2,1)S(1)}, bf16[384,128]{1,0:T(8,128)(2,1)S(1)}, u32[]{:S(2)}, u32[]{:S(2)}) collective-permute-start(bf16[384,128]{1,0:T(8,128)(2,1)S(1)} %shard_map.70), channel_id=1, source_target_pairs={{0,16},{2,18},{4,20},{6,22},{8,24},{10,26},{12,28},{14,30},{1,17},... | collective-permute-start | bytes 294920 | tf_op jit(solution)/shard_map/ppermute | solution.py:422
  34.9 2.7 %collective-permute-start.5 = (bf16[384,128]{1,0:T(8,128)(2,1)S(1)}, bf16[384,128]{1,0:T(8,128)(2,1)S(1)}, u32[]{:S(2)}, u32[]{:S(2)}) collective-permute-start(bf16[384,128]{1,0:T(8,128)(2,1)S(1)} %get-tuple-element.48), channel_id=1, source_target_pairs={{0,2},{2,0},{4,6},{6,4},{8,10},{10,8},{12,14},{14,12},{16,18},{18,... | collective-permute-start | bytes 294920 | tf_op jit(solution)/shard_map/ppermute | solution.py:419
  35.0 5.2 %collective-permute-start.6 = (bf16[384,128]{1,0:T(8,128)(2,1)S(1)}, bf16[384,128]{1,0:T(8,128)(2,1)S(1)}, u32[]{:S(2)}, u32[]{:S(2)}) collective-permute-start(bf16[384,128]{1,0:T(8,128)(2,1)S(1)} %get-tuple-element.49), channel_id=1, source_target_pairs={{0,4},{2,6},{4,0},{6,2},{8,12},{10,14},{12,8},{14,10},{16,20},{18,... | collective-permute-start | bytes 294920 | tf_op jit(solution)/shard_map/ppermute | solution.py:419
  40.3 20.7 %collective-permute-start.17 = (bf16[384,1024]{1,0:T(8,128)(2,1)}, bf16[384,1024]{1,0:T(8,128)(2,1)S(1)}, u32[]{:S(2)}, u32[]{:S(2)}) collective-permute-start(bf16[384,1024]{1,0:T(8,128)(2,1)} %collective-permute-done.9.refs_2_), channel_id=1, source_target_pairs={{0,4},{2,6},{4,0},{6,2},{8,12},{10,14},{12,8},{14,10},{16,20},{18,... | collective-permute-start | bytes 2359304 | tf_op jit(solution)/shard_map/ppermute | solution.py:419
  41.8 12.1 %collective-permute-start.4 = (bf16[512,384]{1,0:T(8,128)(2,1)S(1)}, bf16[512,384]{1,0:T(8,128)(2,1)S(1)}, u32[]{:S(2)}, u32[]{:S(2)}) collective-permute-start(bf16[512,384]{1,0:T(8,128)(2,1)S(1)} %shard_map.73.refs_0_), channel_id=1, source_target_pairs={{0,1},{1,0},{2,3},{3,2},{4,5},{5,4},{6,7},{7,6},{8,9},{9,8},{10,11... | collective-permute-start | bytes 1179656 | tf_op jit(solution)/shard_map/ppermute | solution.py:425
  44.0 23.6 %collective-permute-start.14 = (bf16[384,512]{1,0:T(8,128)(2,1)S(1)}, bf16[384,512]{1,0:T(8,128)(2,1)S(1)}, u32[]{:S(2)}, u32[]{:S(2)}) collective-permute-start(bf16[384,512]{1,0:T(8,128)(2,1)S(1)} %collective-permute-done.10.refs_3_), channel_id=1, source_target_pairs={{0,2},{2,0},{4,6},{6,4},{8,10},{10,8},{12,14},{14,12},{16,18},{18,... | collective-permute-start | bytes 1179656 | tf_op jit(solution)/shard_map/ppermute | solution.py:419
  44.5 24.7 %collective-permute-start.8 = (bf16[512,384]{1,0:T(8,128)(2,1)S(1)}, bf16[512,384]{1,0:T(8,128)(2,1)S(1)}, u32[]{:S(2)}, u32[]{:S(2)}) collective-permute-start(bf16[512,384]{1,0:T(8,128)(2,1)S(1)} %shard_map.74.refs_1_), channel_id=1, source_target_pairs={{0,1},{1,0},{2,3},{3,2},{4,5},{5,4},{6,7},{7,6},{8,9},{9,8},{10,11... | collective-permute-start | bytes 1179656 | tf_op jit(solution)/shard_map/ppermute | solution.py:425
  46.2 23.3 %collective-permute-start.18 = (bf16[384,512]{1,0:T(8,128)(2,1)S(1)}, bf16[384,512]{1,0:T(8,128)(2,1)S(1)}, u32[]{:S(2)}, u32[]{:S(2)}) collective-permute-start(bf16[384,512]{1,0:T(8,128)(2,1)S(1)} %collective-permute-done.10.refs_3_), channel_id=1, source_target_pairs={{0,4},{2,6},{4,0},{6,2},{8,12},{10,14},{12,8},{14,10},{16,20},{18,... | collective-permute-start | bytes 1179656 | tf_op jit(solution)/shard_map/ppermute | solution.py:419
  53.8 18.1 %collective-permute-start.11 = (bf16[384,512]{1,0:T(8,128)(2,1)S(1)}, bf16[384,512]{1,0:T(8,128)(2,1)S(1)}, u32[]{:S(2)}, u32[]{:S(2)}) collective-permute-start(bf16[384,512]{1,0:T(8,128)(2,1)S(1)} %slice.30), channel_id=1, source_target_pairs={{0,8},{2,10},{4,12},{6,14},{8,0},{10,2},{12,4},{14,6},{16,24},{18,... | collective-permute-start | bytes 1179656 | tf_op jit(solution)/shard_map/ppermute | solution.py:419
  60.9 11.1 %collective-permute-start.12 = (bf16[384,512]{1,0:T(8,128)(2,1)S(1)}, bf16[384,512]{1,0:T(8,128)(2,1)S(1)}, u32[]{:S(2)}, u32[]{:S(2)}) collective-permute-start(bf16[384,512]{1,0:T(8,128)(2,1)S(1)} %get-tuple-element.58), channel_id=1, source_target_pairs={{0,2},{2,0},{4,6},{6,4},{8,10},{10,8},{12,14},{14,12},{16,18},{18,... | collective-permute-start | bytes 1179656 | tf_op jit(solution)/shard_map/ppermute | solution.py:419
  67.7 20.0 %collective-permute-start.16 = (bf16[512,768]{1,0:T(8,128)(2,1)S(1)}, bf16[512,768]{1,0:T(8,128)(2,1)S(1)}, u32[]{:S(2)}, u32[]{:S(2)}) collective-permute-start(bf16[512,768]{1,0:T(8,128)(2,1)S(1)} %shard_map.76.refs_2_), channel_id=1, source_target_pairs={{0,1},{1,0},{2,3},{3,2},{4,5},{5,4},{6,7},{7,6},{8,9},{9,8},{10,11... | collective-permute-start | bytes 2359304 | tf_op jit(solution)/shard_map/ppermute | solution.py:425
  69.3 3.4 %collective-permute-start.13 = (bf16[384,512]{1,0:T(8,128)(2,1)S(1)}, bf16[384,512]{1,0:T(8,128)(2,1)S(1)}, u32[]{:S(2)}, u32[]{:S(2)}) collective-permute-start(bf16[384,512]{1,0:T(8,128)(2,1)S(1)} %get-tuple-element.57), channel_id=1, source_target_pairs={{0,2},{2,0},{4,6},{6,4},{8,10},{10,8},{12,14},{14,12},{16,18},{18,... | collective-permute-start | bytes 1179656 | tf_op jit(solution)/shard_map/ppermute | solution.py:419
  69.5 12.0 %collective-permute-start.19 = (bf16[384,512]{1,0:T(8,128)(2,1)S(1)}, bf16[384,512]{1,0:T(8,128)(2,1)S(1)}, u32[]{:S(2)}, u32[]{:S(2)}) collective-permute-start(bf16[384,512]{1,0:T(8,128)(2,1)S(1)} %slice.33), channel_id=1, source_target_pairs={{0,8},{2,10},{4,12},{6,14},{8,0},{10,2},{12,4},{14,6},{16,24},{18,... | collective-permute-start | bytes 1179656 | tf_op jit(solution)/shard_map/ppermute | solution.py:419
  72.1 10.0 %collective-permute-start.15 = (bf16[384,512]{1,0:T(8,128)(2,1)S(1)}, bf16[384,512]{1,0:T(8,128)(2,1)S(1)}, u32[]{:S(2)}, u32[]{:S(2)}) collective-permute-start(bf16[384,512]{1,0:T(8,128)(2,1)S(1)} %collective-permute-done.11.refs_4_), channel_id=1, source_target_pairs={{0,2},{2,0},{4,6},{6,4},{8,10},{10,8},{12,14},{14,12},{16,18},{18,... | collective-permute-start | bytes 1179656 | tf_op jit(solution)/shard_map/ppermute | solution.py:419
  72.6 8.9 %collective-permute-start.23 = (bf16[384,256]{1,0:T(8,128)(2,1)S(1)}, bf16[384,256]{1,0:T(8,128)(2,1)S(1)}, u32[]{:S(2)}, u32[]{:S(2)}) collective-permute-start(bf16[384,256]{1,0:T(8,128)(2,1)S(1)} %get-tuple-element.61), channel_id=1, source_target_pairs={{0,2},{2,0},{4,6},{6,4},{8,10},{10,8},{12,14},{14,12},{16,18},{18,... | collective-permute-start | bytes 589832 | tf_op jit(solution)/shard_map/ppermute | solution.py:419
  73.5 14.2 %collective-permute-start.20 = (bf16[384,512]{1,0:T(8,128)(2,1)S(1)}, bf16[384,512]{1,0:T(8,128)(2,1)S(1)}, u32[]{:S(2)}, u32[]{:S(2)}) collective-permute-start(bf16[384,512]{1,0:T(8,128)(2,1)S(1)} %get-tuple-element.56), channel_id=1, source_target_pairs={{0,2},{2,0},{4,6},{6,4},{8,10},{10,8},{12,14},{14,12},{16,18},{18,... | collective-permute-start | bytes 1179656 | tf_op jit(solution)/shard_map/ppermute | solution.py:419
  81.5 6.2 %collective-permute-start.21 = (bf16[384,512]{1,0:T(8,128)(2,1)S(1)}, bf16[384,512]{1,0:T(8,128)(2,1)S(1)}, u32[]{:S(2)}, u32[]{:S(2)}) collective-permute-start(bf16[384,512]{1,0:T(8,128)(2,1)S(1)} %get-tuple-element.55), channel_id=1, source_target_pairs={{0,2},{2,0},{4,6},{6,4},{8,10},{10,8},{12,14},{14,12},{16,18},{18,... | collective-permute-start | bytes 1179656 | tf_op jit(solution)/shard_map/ppermute | solution.py:419
  81.5 6.2 %collective-permute-start.24 = (bf16[384,256]{1,0:T(8,128)(2,1)S(1)}, bf16[384,256]{1,0:T(8,128)(2,1)S(1)}, u32[]{:S(2)}, u32[]{:S(2)}) collective-permute-start(bf16[384,256]{1,0:T(8,128)(2,1)S(1)} %get-tuple-element.60), channel_id=1, source_target_pairs={{0,2},{2,0},{4,6},{6,4},{8,10},{10,8},{12,14},{14,12},{16,18},{18,... | collective-permute-start | bytes 589832 | tf_op jit(solution)/shard_map/ppermute | solution.py:419
  82.1 5.6 %collective-permute-start.25 = (bf16[384,256]{1,0:T(8,128)(2,1)S(1)}, bf16[384,256]{1,0:T(8,128)(2,1)S(1)}, u32[]{:S(2)}, u32[]{:S(2)}) collective-permute-start(bf16[384,256]{1,0:T(8,128)(2,1)S(1)} %get-tuple-element.59), channel_id=1, source_target_pairs={{0,2},{2,0},{4,6},{6,4},{8,10},{10,8},{12,14},{14,12},{16,18},{18,... | collective-permute-start | bytes 589832 | tf_op jit(solution)/shard_map/ppermute | solution.py:419
  (10 other events, 90.8 us)

commit v9 on v8

--- a/solution.py
+++ b/solution.py
@@ -164,7 +164,7 @@
                 o_ref[i % 2, cols, :] = state.astype(BF16)
 
     arrays, specs = [key] * 4 + [value] * 4, [group(rows, part, s) for s in order] * 2
-    return local(kernel, meta, arrays, [jax.ShapeDtypeStruct((2, part, DH), BF16)] * 2, 2, 16, specs)
+    return local(kernel, meta, arrays, [jax.ShapeDtypeStruct((2, part, DH), BF16)] * 2, 2, 10, specs)
 
 
 def seen_mask(meta_ref, rows, doc_count):
@@ -207,8 +207,8 @@
     arrays, specs = [query, key, value], [group(rows, part, slot)] * 3
     if make:
         shapes = shapes + [jax.ShapeDtypeStruct((rows, rows), BF16)]
-        return local(kernel, meta, arrays, shapes, 2, 16, specs)
-    return local(kernel, meta, [*arrays, mask], shapes, 2, 16, [*specs, whole(mask.shape)])[0]
+        return local(kernel, meta, arrays, shapes, 2, 10, specs)
+    return local(kernel, meta, [*arrays, mask], shapes, 2, 10, [*specs, whole(mask.shape)])[0]
 
 
 def small(kernel, meta, arrays, shape, count):
@@ -323,7 +323,7 @@
         ]
         specs += [wide[0], whole((rows, part)), whole((part, DH)), wide[1]]
     shapes = [jax.ShapeDtypeStruct((rows, part * count), BF16)]
-    return local(kernel, meta, arrays, shapes, count, 16, specs)[0]
+    return local(kernel, meta, arrays, shapes, count, 10, specs)[0]
 
 
 TILES = 4
@@ -435,7 +435,7 @@
     ]
     w0 = [flip(x) for x in sent]
 
-    send, keep = split_states(after(meta, sent[0]), key, value, docs)
+    send, keep = split_states(after(meta, *sent), key, value, docs)
     core_got = swap(send, 1)
     query = behind(query, send)
     within0, mask = within_slot(after(meta, send), query, key, value, docs, 0)
@@ -447,6 +447,7 @@
     within2 = within_slot(after(meta, plane_sum), query, key, value, docs, 2, mask)
     both = join_planes(after(meta, within2), plane_sum, near, rows, docs)
     far = shift(both, 2 * plane)
+    w2 = [swap(behind(w0[0], both), 2)]
     within3 = within_slot(after(meta, both), query, key, value, docs, 3, mask)
     carry0, core_carry0, chip_carry = carry_first(
         after(meta, within3), near, far, chip0, chip_got, keep, core_got, rows, docs
@@ -461,16 +462,15 @@
     far0 = flip(normed0)
     normed1 = norm((1,), [within1], [carry1])
     far1 = flip(normed1)
-    carry2, core_carry2 = carry_second(meta, chip_carry2, keep, core_got, rows, docs)
+    carry2, core_carry2 = carry_second(after(meta, far0, w2[0]), chip_carry2, keep, core_got, rows, docs)
     carry3 = swap(core_carry2, 1)
     normed2 = norm((2, 3), [within2, within3], [carry2, carry3])
     far2 = flip(normed2)
 
-    first, second = lax.optimization_barrier((*w0, chip_carry2, normed0, normed1))[:2]
-    total = project_own(after(meta, far0), [normed0, normed1, normed2], weight, columns)
-    w2 = [swap(first, 2), swap(second, 2)]
-    w0.append(swap(first[:, quarter:], plane))
-    w2.append(swap(behind(w2[0], total)[:, quarter:], plane))
+    total = project_own(after(meta, far1), [normed0, normed1, normed2], weight, columns)
+    w0.append(swap(behind(w0[0], normed0)[:, quarter:], plane))
+    w2.append(swap(behind(w0[1], chip_carry2), 2))
+    w2.append(swap(behind(w2[0], carry2)[:, quarter:], plane))
 
     def cut(w, width):
         return [w[:, at : at + width] for at in range(0, w.shape[1], width)]

time: 92.6 us -> 77.4 us (0.84)
  waiting for transfers between devices: 23.2 us -> 15.5 us
  local copies, waits for them, and re-layouts: 9.27 us -> 4.2 us
  Pallas kernels: 30.4 us -> 29.1 us
    ppermute x5, waiting for transfers between devices: 6.64 us -> 0.45 us  [flip(): return lax.ppermute(x, 'head', [(0, 1), (1, 0)])]
    ppermute x19, starting transfers between devices: 13.4 us -> 11.9 us  [swap(): return lax.ppermute(x, 'seq', [(i, i ^ bit) for i in range(n_seq)])]
    ppermute x19, waiting for transfers between devices: 16 us -> 14.5 us  [swap(): return lax.ppermute(x, 'seq', [(i, i ^ bit) for i in range(n_seq)])]
    unnamed x16 -> x18, local copies, waits for them, and re-layouts: 2.85 us -> 1.57 us
    slice x2, local copies, waits for them, and re-layouts: 1.21 us -> 0.05 us  [the longest x1 0.03 us: pair_body(): w2.append(swap(behind(w2[0], carry2)[:, quarter:], plane))]
    slice x4, local copies, waits for them, and re-layouts: 1.27 us -> 0.16 us  [cut(): return [w[:, at:at + width] for at in range(0, w.shape[1], width)]]
    ppermute x5, starting transfers between devices: 6.2 us -> 7.13 us  [flip(): return lax.ppermute(x, 'head', [(0, 1), (1, 0)])]
  transfers between devices with their start and end apart: 26 -> 26, of which waited for: 9 -> 9; matrix products, arithmetic and copies ran while one was open for 4% -> 2% of each run, Pallas kernels for 26% -> 32%
where the time goes in v9:
time: 77.4 us; the launch traced here: 77.1 us
  Pallas kernels  29.1 us (38%)
  starting transfers between devices  28 us (36%)
  waiting for transfers between devices  15.5 us (20%)
  local copies, waits for them, and re-layouts  4.2 us (5%)
    pallas_call x13, Pallas kernels, local(): call(kernel, (1,), specs or [whole(a.shape) for a in arrays], [whole(s.sh...  15.5 us
    ppermute x19, waiting for transfers between devices, swap(): return lax.ppermute(x, 'seq', [(i, i ^ bit) for i in range(n_seq)])  14.5 us
    ppermute x19, starting transfers between devices, swap(): return lax.ppermute(x, 'seq', [(i, i ^ bit) for i in range(n_seq)])  11.9 us
    ppermute x2, starting transfers between devices, shift(): lax.ppermute(x, 'seq', [(i, i + count) for i in range(n_seq - count)])  8.99 us
    pallas_call x2, Pallas kernels, project_more(): call(kernel, (TILES,), [out_spec] + [whole(p.shape) for p in pieces] + sp...  8.25 us
    ppermute x5, starting transfers between devices, flip(): return lax.ppermute(x, 'head', [(0, 1), (1, 0)])  7.13 us
    pallas_call x1, Pallas kernels, project_own(): call(kernel, (TILES,), [whole(p.shape) for p in pieces] + [pl.BlockSpec((...  5.34 us
    dynamic_slice x2, local copies, waits for them, and re-layouts, pair_body(): lax.dynamic_slice(weight, (member * part, (1 - group) * columns + at), (p...  2.32 us
  transfers between devices with their start and end apart: 26, of which 9 were waited for; matrix products, arithmetic and copies ran while one was open for 2% of the time, Pallas kernels for 32%

profile of v9, /device:TPU:0, one launch (start us, length us, event | category | flops | bytes accessed | tf_op | source)
XLA Modules:
  0.0 77.1 jit_solution(12621436700594779844)
XLA Ops:
  0.0 1.3 %dynamic_slice.6 = bf16[384,1024]{1,0:T(8,128)(2,1)S(1)} dynamic-slice(bf16[1536,4096]{1,0:T(8,128)(2,1)} %refs_6_.3, s32[]{:T(128)S(6)} %select_n.28, s32[]{:T(128)S(6)} %select_n.29), dynamic_slice_sizes={384,1024} | dynamic-slice | bytes 1572868 | tf_op jit(solution)/shard_map/dynamic_slice | solution.py:433
  1.3 3.0 %collective-permute-start.7 = (bf16[384,1024]{1,0:T(8,128)(2,1)S(1)}, bf16[384,1024]{1,0:T(8,128)(2,1)S(1)}, u32[]{:S(2)}, u32[]{:S(2)}) collective-permute-start(bf16[384,1024]{1,0:T(8,128)(2,1)S(1)} %dynamic_slice.6), channel_id=1, source_target_pairs={{0,1},{1,0},{2,3},{3,2},{4,5},{5,4},{6,7},{7,6},{8,9},{9,8},{10,11... | collective-permute-start | bytes 2359304 | tf_op jit(solution)/shard_map/ppermute | solution.py:425
  5.5 1.4 %copy-done.1 = bf16[512,1536]{1,0:T(8,128)(2,1)S(1)} copy-done((bf16[512,1536]{1,0:T(8,128)(2,1)S(1)}, bf16[512,1536]{1,0:T(8,128)(2,1)}, u32[]{:S(2)}) %copy-start.1) | copy-done | bytes 1572888
  6.9 1.7 %shard_map.64 = (bf16[2,384,128]{2,1,0:T(8,128)(2,1)S(1)}, bf16[2,384,128]{2,1,0:T(8,128)(2,1)S(1)}) custom-call(s32[24]{0:T(128)S(1)} %concatenate.3.meta_ref, bf16[512,1536]{1,0:T(8,128)(2,1)S(1)} %copy-done, bf16[512,1536]{1,0:T(8,128)(2,1)S(1)} %copy-done, bf16[512,1536]{1,0:T(8,128)(2,1)S(1)} %copy-done, bf16[512,1536]{1,0:T(8,128)(2,1)S(1)} %copy-done, ...), custom_call_target="tpu_custom_call" | custom-call | flops 2000000000 | bytes 1024 | tf_op jit(solution)/shard_map/pallas_call | solution.py:122
  8.8 1.9 %shard_map.65 = (f32[512,384]{1,0:T(8,128)S(1)}, bf16[512,512]{1,0:T(8,128)(2,1)S(1)}) custom-call(s32[24]{0:T(128)S(1)} %concatenate.3.meta_ref, bf16[512,1536]{1,0:T(8,128)(2,1)S(1)} %copy-done.3, bf16[512,1536]{1,0:T(8,128)(2,1)S(1)} %copy-done, bf16[512,1536]{1,0:T(8,128)(2,1)S(1)} %copy-done.2), custom_call_target="tpu_custom_call" | custom-call | flops 2000000000 | bytes 1024 | tf_op jit(solution)/shard_map/pallas_call | solution.py:122
  11.3 1.6 %collective-permute-start.1 = (bf16[384,128]{1,0:T(8,128)(2,1)S(1)}, bf16[384,128]{1,0:T(8,128)(2,1)S(1)}, u32[]{:S(2)}, u32[]{:S(2)}) collective-permute-start(bf16[384,128]{1,0:T(8,128)(2,1)S(1)} %get-tuple-element.43), channel_id=1, source_target_pairs={{0,4},{2,6},{4,0},{6,2},{8,12},{10,14},{12,8},{14,10},{16,20},{18,... | collective-permute-start | bytes 294920 | tf_op jit(solution)/shard_map/ppermute | solution.py:419
  12.9 1.8 %shard_map.67.refs_1_ = f32[512,384]{1,0:T(8,128)S(1)} custom-call(s32[24]{0:T(128)S(1)} %concatenate.3.meta_ref, bf16[512,1536]{1,0:T(8,128)(2,1)S(1)} %copy-done.3, bf16[512,1536]{1,0:T(8,128)(2,1)S(1)} %copy-done, bf16[512,1536]{1,0:T(8,128)(2,1)S(1)} %copy-done.2, bf16[512,512]{1,0:T(8,128)(2,1)S(1)} %get-tuple-element.41.rest_0_), custom_call_target="tpu_custom_call" | custom-call | flops 2000000000 | bytes 1024 | tf_op jit(solution)/shard_map/pallas_call | solution.py:122
  14.7 1.8 %collective-permute-done.1.b_ref = bf16[384,128]{1,0:T(8,128)(2,1)S(1)} collective-permute-done((bf16[384,128]{1,0:T(8,128)(2,1)S(1)}, bf16[384,128]{1,0:T(8,128)(2,1)S(1)}, u32[]{:S(2)}, u32[]{:S(2)}) %collective-permute-start.1) | collective-permute-done | bytes 98336 | tf_op jit(solution)/shard_map/ppermute | solution.py:419
  17.1 3.5 %collective-permute-start.2 = (bf16[384,128]{1,0:T(8,128)(2,1)S(1)}, bf16[384,128]{1,0:T(8,128)(2,1)S(1)}, u32[]{:S(2)}, u32[]{:S(2)}) collective-permute-start(bf16[384,128]{1,0:T(8,128)(2,1)S(1)} %shard_map.68.a_ref), channel_id=1, source_target_pairs={{0,8},{2,10},{4,12},{6,14},{8,16},{10,18},{12,20},{14,22},{16,24},... | collective-permute-start | bytes 294920 | tf_op jit(solution)/shard_map/ppermute | solution.py:422
  20.6 1.8 %shard_map.69.refs_1_ = f32[512,384]{1,0:T(8,128)S(1)} custom-call(s32[24]{0:T(128)S(1)} %concatenate.3.meta_ref, bf16[512,1536]{1,0:T(8,128)(2,1)S(1)} %copy-done.3, bf16[512,1536]{1,0:T(8,128)(2,1)S(1)} %copy-done, bf16[512,1536]{1,0:T(8,128)(2,1)S(1)} %copy-done.2, bf16[512,512]{1,0:T(8,128)(2,1)S(1)} %get-tuple-element.41.rest_0_), custom_call_target="tpu_custom_call" | custom-call | flops 2000000000 | bytes 1024 | tf_op jit(solution)/shard_map/pallas_call | solution.py:122
  23.4 1.6 %collective-permute-start.8 = (bf16[384,1024]{1,0:T(8,128)(2,1)S(1)}, bf16[384,1024]{1,0:T(8,128)(2,1)S(1)}, u32[]{:S(2)}, u32[]{:S(2)}) collective-permute-start(bf16[384,1024]{1,0:T(8,128)(2,1)S(1)} %collective-permute-done.7.refs_2_), channel_id=1, source_target_pairs={{0,4},{2,6},{4,0},{6,2},{8,12},{10,14},{12,8},{14,10},{16,20},{18,... | collective-permute-start | bytes 2359304 | tf_op jit(solution)/shard_map/ppermute | solution.py:419
  25.5 5.5 %collective-permute-start.3 = (bf16[384,128]{1,0:T(8,128)(2,1)S(1)}, bf16[384,128]{1,0:T(8,128)(2,1)S(1)}, u32[]{:S(2)}, u32[]{:S(2)}) collective-permute-start(bf16[384,128]{1,0:T(8,128)(2,1)S(1)} %shard_map.70), channel_id=1, source_target_pairs={{0,16},{2,18},{4,20},{6,22},{8,24},{10,26},{12,28},{14,30},{1,17},... | collective-permute-start | bytes 294920 | tf_op jit(solution)/shard_map/ppermute | solution.py:422
  31.0 1.8 %shard_map.71.refs_5_ = f32[512,384]{1,0:T(8,128)S(1)} custom-call(s32[24]{0:T(128)S(1)} %concatenate.3.meta_ref, bf16[512,1536]{1,0:T(8,128)(2,1)S(1)} %copy-done.3, bf16[512,1536]{1,0:T(8,128)(2,1)S(1)} %copy-done, bf16[512,1536]{1,0:T(8,128)(2,1)S(1)} %copy-done.2, bf16[512,512]{1,0:T(8,128)(2,1)S(1)} %get-tuple-element.41.rest_0_), custom_call_target="tpu_custom_call" | custom-call | flops 2000000000 | bytes 1024 | tf_op jit(solution)/shard_map/pallas_call | solution.py:122
  34.7 1.6 %collective-permute-start.6 = (bf16[512,384]{1,0:T(8,128)(2,1)S(1)}, bf16[512,384]{1,0:T(8,128)(2,1)S(1)}, u32[]{:S(2)}, u32[]{:S(2)}) collective-permute-start(bf16[512,384]{1,0:T(8,128)(2,1)S(1)} %shard_map.74.refs_0_), channel_id=1, source_target_pairs={{0,1},{1,0},{2,3},{3,2},{4,5},{5,4},{6,7},{7,6},{8,9},{9,8},{10,11... | collective-permute-start | bytes 1179656 | tf_op jit(solution)/shard_map/ppermute | solution.py:425
  39.3 4.7 %collective-permute-done.9.chip_ref = bf16[384,128]{1,0:T(8,128)(2,1)S(1)} collective-permute-done((bf16[384,128]{1,0:T(8,128)(2,1)S(1)}, bf16[384,128]{1,0:T(8,128)(2,1)S(1)}, u32[]{:S(2)}, u32[]{:S(2)}) %collective-permute-start.9) | collective-permute-done | bytes 98336 | tf_op jit(solution)/shard_map/ppermute | solution.py:419
  43.9 1.5 %collective-permute-start.18 = (bf16[384,512]{1,0:T(8,128)(2,1)S(1)}, bf16[384,512]{1,0:T(8,128)(2,1)S(1)}, u32[]{:S(2)}, u32[]{:S(2)}) collective-permute-start(bf16[384,512]{1,0:T(8,128)(2,1)S(1)} %collective-permute-done.11.refs_3_), channel_id=1, source_target_pairs={{0,4},{2,6},{4,0},{6,2},{8,12},{10,14},{12,8},{14,10},{16,20},{18,... | collective-permute-start | bytes 1179656 | tf_op jit(solution)/shard_map/ppermute | solution.py:419
  45.5 2.1 %collective-permute-start.12 = (bf16[384,512]{1,0:T(8,128)(2,1)S(1)}, bf16[384,512]{1,0:T(8,128)(2,1)S(1)}, u32[]{:S(2)}, u32[]{:S(2)}) collective-permute-start(bf16[384,512]{1,0:T(8,128)(2,1)S(1)} %slice.30), channel_id=1, source_target_pairs={{0,8},{2,10},{4,12},{6,14},{8,0},{10,2},{12,4},{14,6},{16,24},{18,... | collective-permute-start | bytes 1179656 | tf_op jit(solution)/shard_map/ppermute | solution.py:419
  49.8 1.3 %shard_map.76.refs_2_ = bf16[512,768]{1,0:T(8,128)(2,1)S(1)} custom-call(s32[24]{0:T(128)S(1)} %concatenate.3.meta_ref, bf16[512,1536]{1,0:T(8,128)(2,1)S(1)} %copy-done.3, f32[512,384]{1,0:T(8,128)S(1)} %shard_map.69.refs_1_, bf16[384,128]{1,0:T(8,128)(2,1)S(1)} %get-tuple-element.54.refs_2_, f32[1,1536]{1,0:T(1,128)S(1)} %reshape.2.refs_3_.refs_7_, ...), custom_call_target="tpu_custom_call" | custom-call | flops 2000000000 | bytes 1024 | tf_op jit(solution)/shard_map/pallas_call | solution.py:122
  51.9 2.1 %collective-permute-start.19 = (bf16[384,512]{1,0:T(8,128)(2,1)S(1)}, bf16[384,512]{1,0:T(8,128)(2,1)S(1)}, u32[]{:S(2)}, u32[]{:S(2)}) collective-permute-start(bf16[384,512]{1,0:T(8,128)(2,1)S(1)} %slice.33), channel_id=1, source_target_pairs={{0,8},{2,10},{4,12},{6,14},{8,0},{10,2},{12,4},{14,6},{16,24},{18,... | collective-permute-start | bytes 1179656 | tf_op jit(solution)/shard_map/ppermute | solution.py:419
  54.0 1.4 %collective-permute-start.17 = (bf16[512,768]{1,0:T(8,128)(2,1)S(1)}, bf16[512,768]{1,0:T(8,128)(2,1)S(1)}, u32[]{:S(2)}, u32[]{:S(2)}) collective-permute-start(bf16[512,768]{1,0:T(8,128)(2,1)S(1)} %shard_map.76.refs_2_), channel_id=1, source_target_pairs={{0,1},{1,0},{2,3},{3,2},{4,5},{5,4},{6,7},{7,6},{8,9},{9,8},{10,11... | collective-permute-start | bytes 2359304 | tf_op jit(solution)/shard_map/ppermute | solution.py:425
  57.1 5.6 %collective-permute-done.19.refs_3_ = bf16[384,512]{1,0:T(8,128)(2,1)S(1)} collective-permute-done((bf16[384,512]{1,0:T(8,128)(2,1)S(1)}, bf16[384,512]{1,0:T(8,128)(2,1)S(1)}, u32[]{:S(2)}, u32[]{:S(2)}) %collective-permute-start.19) | collective-permute-done | bytes 393248 | tf_op jit(solution)/shard_map/ppermute | solution.py:419
  63.5 5.3 %shard_map.77.t_ref = f32[512,2048]{1,0:T(8,128)S(1)} custom-call(s32[24]{0:T(128)S(1)} %concatenate.3.meta_ref, bf16[512,384]{1,0:T(8,128)(2,1)S(1)} %shard_map.74.refs_0_, bf16[512,384]{1,0:T(8,128)(2,1)S(1)} %shard_map.73.refs_1_, bf16[512,768]{1,0:T(8,128)(2,1)S(1)} %shard_map.76.refs_2_, bf16[1536,4096]{1,0:T(8,128)(2,1)S(1)} %bitcast.5, ...), custom_call_target="tpu_custom_call" | custom-call | flops 1000000 | bytes 1024 | tf_op jit(solution)/shard_map/pallas_call | solution.py:344
  68.8 3.9 %shard_map.78.t_ref = f32[512,2048]{1,0:T(8,128)S(1)} custom-call(s32[24]{0:T(128)S(1)} %concatenate.3.meta_ref, f32[512,2048]{1,0:T(8,128)S(1)} %shard_map.77.t_ref, bf16[512,384]{1,0:T(8,128)(2,1)S(1)} %collective-permute-done.6.refs_0_, bf16[512,384]{1,0:T(8,128)(2,1)S(1)} %collective-permute-done.5.refs_1_, ...), custom_call_target="tpu_custom_call" | custom-call | flops 1000000 | bytes 1024 | tf_op jit(solution)/shard_map/pallas_call | solution.py:393
  72.7 4.4 %shard_map.79 = bf16[512,2048]{1,0:T(8,128)(2,1)} custom-call(s32[24]{0:T(128)S(1)} %concatenate.3.meta_ref, f32[512,2048]{1,0:T(8,128)S(1)} %shard_map.78.t_ref, bf16[512,768]{1,0:T(8,128)(2,1)S(1)} %collective-permute-done.17.refs_0_, bf16[384,1024]{1,0:T(8,128)(2,1)S(1)} %collective-permute-done.8.refs_1_, ...), custom_call_target="tpu_custom_call" | custom-call | flops 1000000 | bytes 1024 | tf_op jit(solution)/shard_map/pallas_call | solution.py:393
  (74 shorter events, 14.3 us)
Async XLA Ops:
  1.3 22.1 %collective-permute-start.7 = (bf16[384,1024]{1,0:T(8,128)(2,1)S(1)}, bf16[384,1024]{1,0:T(8,128)(2,1)S(1)}, u32[]{:S(2)}, u32[]{:S(2)}) collective-permute-start(bf16[384,1024]{1,0:T(8,128)(2,1)S(1)} %dynamic_slice.6), channel_id=1, source_target_pairs={{0,1},{1,0},{2,3},{3,2},{4,5},{5,4},{6,7},{7,6},{8,9},{9,8},{10,11... | collective-permute-start | bytes 2359304 | tf_op jit(solution)/shard_map/ppermute | solution.py:425
  8.6 2.1 %collective-permute-start = (bf16[2,384,128]{2,1,0:T(8,128)(2,1)S(1)}, bf16[2,384,128]{2,1,0:T(8,128)(2,1)S(1)}, u32[]{:S(2)}, u32[]{:S(2)}) collective-permute-start(bf16[2,384,128]{2,1,0:T(8,128)(2,1)S(1)} %get-tuple-element.33), channel_id=1, source_target_pairs={{0,2},{2,0},{4,6},{6,4},{8,10},{10,8},{12,14},{14,12},{16,18},{18,... | collective-permute-start | bytes 589832 | tf_op jit(solution)/shard_map/ppermute | solution.py:419
  11.3 5.1 %collective-permute-start.1 = (bf16[384,128]{1,0:T(8,128)(2,1)S(1)}, bf16[384,128]{1,0:T(8,128)(2,1)S(1)}, u32[]{:S(2)}, u32[]{:S(2)}) collective-permute-start(bf16[384,128]{1,0:T(8,128)(2,1)S(1)} %get-tuple-element.43), channel_id=1, source_target_pairs={{0,4},{2,6},{4,0},{6,2},{8,12},{10,14},{12,8},{14,10},{16,20},{18,... | collective-permute-start | bytes 294920 | tf_op jit(solution)/shard_map/ppermute | solution.py:419
  17.1 5.7 %collective-permute-start.2 = (bf16[384,128]{1,0:T(8,128)(2,1)S(1)}, bf16[384,128]{1,0:T(8,128)(2,1)S(1)}, u32[]{:S(2)}, u32[]{:S(2)}) collective-permute-start(bf16[384,128]{1,0:T(8,128)(2,1)S(1)} %shard_map.68.a_ref), channel_id=1, source_target_pairs={{0,8},{2,10},{4,12},{6,14},{8,16},{10,18},{12,20},{14,22},{16,24},... | collective-permute-start | bytes 294920 | tf_op jit(solution)/shard_map/ppermute | solution.py:422
  23.4 24.2 %collective-permute-start.8 = (bf16[384,1024]{1,0:T(8,128)(2,1)S(1)}, bf16[384,1024]{1,0:T(8,128)(2,1)S(1)}, u32[]{:S(2)}, u32[]{:S(2)}) collective-permute-start(bf16[384,1024]{1,0:T(8,128)(2,1)S(1)} %collective-permute-done.7.refs_2_), channel_id=1, source_target_pairs={{0,4},{2,6},{4,0},{6,2},{8,12},{10,14},{12,8},{14,10},{16,20},{18,... | collective-permute-start | bytes 2359304 | tf_op jit(solution)/shard_map/ppermute | solution.py:419
  24.9 11.9 %collective-permute-start.11 = (bf16[384,512]{1,0:T(8,128)(2,1)S(1)}, bf16[384,512]{1,0:T(8,128)(2,1)S(1)}, u32[]{:S(2)}, u32[]{:S(2)}) collective-permute-start(bf16[384,512]{1,0:T(8,128)(2,1)S(1)} %dynamic_slice.7), channel_id=1, source_target_pairs={{0,1},{1,0},{2,3},{3,2},{4,5},{5,4},{6,7},{7,6},{8,9},{9,8},{10,11... | collective-permute-start | bytes 1179656 | tf_op jit(solution)/shard_map/ppermute | solution.py:425
  25.5 7.5 %collective-permute-start.3 = (bf16[384,128]{1,0:T(8,128)(2,1)S(1)}, bf16[384,128]{1,0:T(8,128)(2,1)S(1)}, u32[]{:S(2)}, u32[]{:S(2)}) collective-permute-start(bf16[384,128]{1,0:T(8,128)(2,1)S(1)} %shard_map.70), channel_id=1, source_target_pairs={{0,16},{2,18},{4,20},{6,22},{8,24},{10,26},{12,28},{14,30},{1,17},... | collective-permute-start | bytes 294920 | tf_op jit(solution)/shard_map/ppermute | solution.py:422
  34.7 10.7 %collective-permute-start.6 = (bf16[512,384]{1,0:T(8,128)(2,1)S(1)}, bf16[512,384]{1,0:T(8,128)(2,1)S(1)}, u32[]{:S(2)}, u32[]{:S(2)}) collective-permute-start(bf16[512,384]{1,0:T(8,128)(2,1)S(1)} %shard_map.74.refs_0_), channel_id=1, source_target_pairs={{0,1},{1,0},{2,3},{3,2},{4,5},{5,4},{6,7},{7,6},{8,9},{9,8},{10,11... | collective-permute-start | bytes 1179656 | tf_op jit(solution)/shard_map/ppermute | solution.py:425
  36.3 7.6 %collective-permute-start.9 = (bf16[384,128]{1,0:T(8,128)(2,1)S(1)}, bf16[384,128]{1,0:T(8,128)(2,1)S(1)}, u32[]{:S(2)}, u32[]{:S(2)}) collective-permute-start(bf16[384,128]{1,0:T(8,128)(2,1)S(1)} %get-tuple-element.53), channel_id=1, source_target_pairs={{0,4},{2,6},{4,0},{6,2},{8,12},{10,14},{12,8},{14,10},{16,20},{18,... | collective-permute-start | bytes 294920 | tf_op jit(solution)/shard_map/ppermute | solution.py:419
  36.9 14.2 %collective-permute-start.15 = (bf16[384,512]{1,0:T(8,128)(2,1)S(1)}, bf16[384,512]{1,0:T(8,128)(2,1)S(1)}, u32[]{:S(2)}, u32[]{:S(2)}) collective-permute-start(bf16[384,512]{1,0:T(8,128)(2,1)S(1)} %collective-permute-done.11.refs_3_), channel_id=1, source_target_pairs={{0,2},{2,0},{4,6},{6,4},{8,10},{10,8},{12,14},{14,12},{16,18},{18,... | collective-permute-start | bytes 1179656 | tf_op jit(solution)/shard_map/ppermute | solution.py:419
  38.7 13.3 %collective-permute-start.5 = (bf16[512,384]{1,0:T(8,128)(2,1)S(1)}, bf16[512,384]{1,0:T(8,128)(2,1)S(1)}, u32[]{:S(2)}, u32[]{:S(2)}) collective-permute-start(bf16[512,384]{1,0:T(8,128)(2,1)S(1)} %shard_map.73.refs_1_), channel_id=1, source_target_pairs={{0,1},{1,0},{2,3},{3,2},{4,5},{5,4},{6,7},{7,6},{8,9},{9,8},{10,11... | collective-permute-start | bytes 1179656 | tf_op jit(solution)/shard_map/ppermute | solution.py:425
  43.9 10.1 %collective-permute-start.18 = (bf16[384,512]{1,0:T(8,128)(2,1)S(1)}, bf16[384,512]{1,0:T(8,128)(2,1)S(1)}, u32[]{:S(2)}, u32[]{:S(2)}) collective-permute-start(bf16[384,512]{1,0:T(8,128)(2,1)S(1)} %collective-permute-done.11.refs_3_), channel_id=1, source_target_pairs={{0,4},{2,6},{4,0},{6,2},{8,12},{10,14},{12,8},{14,10},{16,20},{18,... | collective-permute-start | bytes 1179656 | tf_op jit(solution)/shard_map/ppermute | solution.py:419
  45.5 10.0 %collective-permute-start.12 = (bf16[384,512]{1,0:T(8,128)(2,1)S(1)}, bf16[384,512]{1,0:T(8,128)(2,1)S(1)}, u32[]{:S(2)}, u32[]{:S(2)}) collective-permute-start(bf16[384,512]{1,0:T(8,128)(2,1)S(1)} %slice.30), channel_id=1, source_target_pairs={{0,8},{2,10},{4,12},{6,14},{8,0},{10,2},{12,4},{14,6},{16,24},{18,... | collective-permute-start | bytes 1179656 | tf_op jit(solution)/shard_map/ppermute | solution.py:419
  49.6 5.9 %collective-permute-start.13 = (bf16[384,512]{1,0:T(8,128)(2,1)S(1)}, bf16[384,512]{1,0:T(8,128)(2,1)S(1)}, u32[]{:S(2)}, u32[]{:S(2)}) collective-permute-start(bf16[384,512]{1,0:T(8,128)(2,1)S(1)} %get-tuple-element.62), channel_id=1, source_target_pairs={{0,2},{2,0},{4,6},{6,4},{8,10},{10,8},{12,14},{14,12},{16,18},{18,... | collective-permute-start | bytes 1179656 | tf_op jit(solution)/shard_map/ppermute | solution.py:419
  51.1 5.0 %collective-permute-start.14 = (bf16[384,512]{1,0:T(8,128)(2,1)S(1)}, bf16[384,512]{1,0:T(8,128)(2,1)S(1)}, u32[]{:S(2)}, u32[]{:S(2)}) collective-permute-start(bf16[384,512]{1,0:T(8,128)(2,1)S(1)} %get-tuple-element.61), channel_id=1, source_target_pairs={{0,2},{2,0},{4,6},{6,4},{8,10},{10,8},{12,14},{14,12},{16,18},{18,... | collective-permute-start | bytes 1179656 | tf_op jit(solution)/shard_map/ppermute | solution.py:419
  51.9 10.8 %collective-permute-start.19 = (bf16[384,512]{1,0:T(8,128)(2,1)S(1)}, bf16[384,512]{1,0:T(8,128)(2,1)S(1)}, u32[]{:S(2)}, u32[]{:S(2)}) collective-permute-start(bf16[384,512]{1,0:T(8,128)(2,1)S(1)} %slice.33), channel_id=1, source_target_pairs={{0,8},{2,10},{4,12},{6,14},{8,0},{10,2},{12,4},{14,6},{16,24},{18,... | collective-permute-start | bytes 1179656 | tf_op jit(solution)/shard_map/ppermute | solution.py:419
  54.0 18.7 %collective-permute-start.17 = (bf16[512,768]{1,0:T(8,128)(2,1)S(1)}, bf16[512,768]{1,0:T(8,128)(2,1)S(1)}, u32[]{:S(2)}, u32[]{:S(2)}) collective-permute-start(bf16[512,768]{1,0:T(8,128)(2,1)S(1)} %shard_map.76.refs_2_), channel_id=1, source_target_pairs={{0,1},{1,0},{2,3},{3,2},{4,5},{5,4},{6,7},{7,6},{8,9},{9,8},{10,11... | collective-permute-start | bytes 2359304 | tf_op jit(solution)/shard_map/ppermute | solution.py:425
  55.5 1.5 %collective-permute-start.22 = (bf16[384,256]{1,0:T(8,128)(2,1)S(1)}, bf16[384,256]{1,0:T(8,128)(2,1)S(1)}, u32[]{:S(2)}, u32[]{:S(2)}) collective-permute-start(bf16[384,256]{1,0:T(8,128)(2,1)S(1)} %get-tuple-element.66), channel_id=1, source_target_pairs={{0,2},{2,0},{4,6},{6,4},{8,10},{10,8},{12,14},{14,12},{16,18},{18,... | collective-permute-start | bytes 589832 | tf_op jit(solution)/shard_map/ppermute | solution.py:419
  55.6 7.8 %collective-permute-start.16 = (bf16[384,512]{1,0:T(8,128)(2,1)S(1)}, bf16[384,512]{1,0:T(8,128)(2,1)S(1)}, u32[]{:S(2)}, u32[]{:S(2)}) collective-permute-start(bf16[384,512]{1,0:T(8,128)(2,1)S(1)} %collective-permute-done.12.refs_4_), channel_id=1, source_target_pairs={{0,2},{2,0},{4,6},{6,4},{8,10},{10,8},{12,14},{14,12},{16,18},{18,... | collective-permute-start | bytes 1179656 | tf_op jit(solution)/shard_map/ppermute | solution.py:419
  56.1 6.7 %collective-permute-start.23 = (bf16[384,256]{1,0:T(8,128)(2,1)S(1)}, bf16[384,256]{1,0:T(8,128)(2,1)S(1)}, u32[]{:S(2)}, u32[]{:S(2)}) collective-permute-start(bf16[384,256]{1,0:T(8,128)(2,1)S(1)} %get-tuple-element.65), channel_id=1, source_target_pairs={{0,2},{2,0},{4,6},{6,4},{8,10},{10,8},{12,14},{14,12},{16,18},{18,... | collective-permute-start | bytes 589832 | tf_op jit(solution)/shard_map/ppermute | solution.py:419
  57.0 15.7 %collective-permute-start.20 = (bf16[384,512]{1,0:T(8,128)(2,1)S(1)}, bf16[384,512]{1,0:T(8,128)(2,1)S(1)}, u32[]{:S(2)}, u32[]{:S(2)}) collective-permute-start(bf16[384,512]{1,0:T(8,128)(2,1)S(1)} %get-tuple-element.60), channel_id=1, source_target_pairs={{0,2},{2,0},{4,6},{6,4},{8,10},{10,8},{12,14},{14,12},{16,18},{18,... | collective-permute-start | bytes 1179656 | tf_op jit(solution)/shard_map/ppermute | solution.py:419
  62.7 9.9 %collective-permute-start.21 = (bf16[384,512]{1,0:T(8,128)(2,1)S(1)}, bf16[384,512]{1,0:T(8,128)(2,1)S(1)}, u32[]{:S(2)}, u32[]{:S(2)}) collective-permute-start(bf16[384,512]{1,0:T(8,128)(2,1)S(1)} %get-tuple-element.59), channel_id=1, source_target_pairs={{0,2},{2,0},{4,6},{6,4},{8,10},{10,8},{12,14},{14,12},{16,18},{18,... | collective-permute-start | bytes 1179656 | tf_op jit(solution)/shard_map/ppermute | solution.py:419
  62.8 9.9 %collective-permute-start.24 = (bf16[384,256]{1,0:T(8,128)(2,1)S(1)}, bf16[384,256]{1,0:T(8,128)(2,1)S(1)}, u32[]{:S(2)}, u32[]{:S(2)}) collective-permute-start(bf16[384,256]{1,0:T(8,128)(2,1)S(1)} %get-tuple-element.64), channel_id=1, source_target_pairs={{0,2},{2,0},{4,6},{6,4},{8,10},{10,8},{12,14},{14,12},{16,18},{18,... | collective-permute-start | bytes 589832 | tf_op jit(solution)/shard_map/ppermute | solution.py:419
  63.4 9.3 %collective-permute-start.25 = (bf16[384,256]{1,0:T(8,128)(2,1)S(1)}, bf16[384,256]{1,0:T(8,128)(2,1)S(1)}, u32[]{:S(2)}, u32[]{:S(2)}) collective-permute-start(bf16[384,256]{1,0:T(8,128)(2,1)S(1)} %get-tuple-element.63), channel_id=1, source_target_pairs={{0,2},{2,0},{4,6},{6,4},{8,10},{10,8},{12,14},{14,12},{16,18},{18,... | collective-permute-start | bytes 589832 | tf_op jit(solution)/shard_map/ppermute | solution.py:419
  (11 other events, 90.0 us)

commit v10 on v9

--- a/solution.py
+++ b/solution.py
@@ -23,7 +23,7 @@
     return start
 
 
-def call(kernel, grid, in_specs, out_specs, out_shape, flops, bytes_accessed, scratch=(), vmem=VMEM_LIMIT):
+def call(kernel, grid, in_specs, out_specs, out_shape, flops, bytes_accessed, scratch=(), vmem=VMEM_LIMIT, aliases={}):
     return pl.pallas_call(
         kernel,
         grid_spec=pltpu.PrefetchScalarGridSpec(
@@ -34,6 +34,7 @@
             scratch_shapes=scratch,
         ),
         out_shape=out_shape,
+        input_output_aliases=aliases,
         compiler_params=pltpu.CompilerParams(vmem_limit_bytes=vmem),
         cost_estimate=pl.CostEstimate(flops=flops, bytes_accessed=bytes_accessed, transcendentals=0),
     )
@@ -142,6 +143,35 @@
 
 def factor(condition):
     return jnp.where(condition, 1.0, 0.0)
+
+
+def slice_weights(meta, weight, columns):
+    part, half = weight.shape[0] // 4, columns // 2
+    shapes = [jax.ShapeDtypeStruct((part, half), BF16), jax.ShapeDtypeStruct((part, half // 2), BF16)]
+
+    def kernel(meta_ref, w_ref, a_ref, b_ref, sems):
+        rows = pl.ds(pl.multiple_of(meta_ref[1] * part, DH), part)
+        base = (1 - meta_ref[2]) * columns
+        starts = (base + meta_ref[3] * half, base + (1 - meta_ref[3]) * half)
+        copies = []
+        for n, (o_ref, start) in enumerate(zip((a_ref, b_ref), starts)):
+            cols = pl.ds(pl.multiple_of(start, DH), shapes[n].shape[1])
+            copies.append(pltpu.make_async_copy(w_ref.at[rows, cols], o_ref, sems.at[n]))
+            copies[-1].start()
+        for copy in copies:
+            copy.wait()
+
+    return call(
+        kernel,
+        (1,),
+        [pl.BlockSpec(memory_space=pl.ANY)],
+        [pl.BlockSpec(memory_space=pl.ANY)] * 2,
+        shapes,
+        6 * 10**9,
+        1024,
+        [pltpu.SemaphoreType.DMA((2,))],
+        50 * 1024 * 1024,
+    )(meta, weight)
 
 
 def split_states(meta, key, value, doc_count):
@@ -286,10 +316,11 @@
     return small(kernel, meta, (chip, keep, core_got), chip.shape, 2)
 
 
-def norm_heads(meta, query, withins, carries, gain, doc_count, slots=None):
+def norm_heads(meta, query, withins, carries, gain, doc_count, slots=None, split=None):
     rows = query.shape[0]
     part = carries[0].shape[0]
     count = len(carries)
+    heights = split or (rows,)
 
     def kernel(meta_ref, *refs):
         offset = meta_ref[0] * rows
@@ -302,7 +333,7 @@
             end = jnp.where(previous <= offset, bound, end)
         stop = jnp.where(begins < offset, end - offset, 0)
         cross = lax.broadcasted_iota(jnp.int32, (rows, DH), 0) < stop
-        o_ref = refs[-1]
+        outs = refs[4 * count :]
         for n in range(count):
             q_ref, w_ref, c_ref, g_ref = refs[4 * n : 4 * n + 4]
             for h in range(part // DH):
@@ -310,9 +341,11 @@
                 term = jnp.dot(q_ref[:, cols], c_ref[cols, :], preferred_element_type=F32)
                 mixture = w_ref[:, cols] + jnp.where(cross, term, 0.0)
                 mean = jnp.mean(mixture * mixture, axis=-1, keepdims=True)
-                o_ref[:, n * part + h * DH : n * part + (h + 1) * DH] = (
-                    mixture * lax.rsqrt(mean + 1e-06) * g_ref[:, cols]
-                ).astype(BF16)
+                normed = (mixture * lax.rsqrt(mean + 1e-06) * g_ref[:, cols]).astype(BF16)
+                top = 0
+                for o_ref, height in zip(outs, heights):
+                    o_ref[:, n * part + h * DH : n * part + (h + 1) * DH] = normed[top : top + height]
+                    top += height
 
     gain = gain.reshape(1, -1)
     arrays, specs = [], []
@@ -322,8 +355,9 @@
             group(rows, part, slots[n]), group(1, part, slots[n])
         ]
         specs += [wide[0], whole((rows, part)), whole((part, DH)), wide[1]]
-    shapes = [jax.ShapeDtypeStruct((rows, part * count), BF16)]
-    return local(kernel, meta, arrays, shapes, count, 10, specs)[0]
+    shapes = [jax.ShapeDtypeStruct((height, part * count), BF16) for height in heights]
+    outs = local(kernel, meta, arrays, shapes, count, 10, specs)
+    return outs if split else outs[0]
 
 
 TILES = 4
@@ -337,7 +371,8 @@
 
     def kernel(meta_ref, *refs):
         ns, ws, o_ref = refs[:count], refs[count:-1], refs[-1]
-        n = jnp.concatenate([r[...] for r in ns], axis=1)
+        last = jnp.concatenate([r[...] for r in ns[-2:]], axis=0)
+        n = jnp.concatenate([*[r[...] for r in ns[:-2]], last], axis=1)
         w = jnp.concatenate([r[...] for r in ws], axis=0)
         o_ref[...] = jnp.dot(n, w, preferred_element_type=F32)
 
@@ -353,8 +388,8 @@
     )(meta, *pieces, *[weight] * 4)
 
 
-def project_more(meta, total, pieces, weights, dtype):
-    rows, columns = total.shape
+def project_more(meta, total, pieces, weights, dtype, row_block=0, into=None):
+    rows, columns = pieces[0].shape[0], total.shape[1]
     tile = columns // TILES
     count = len(pieces)
     flat, specs, places = [], [], []
@@ -374,7 +409,7 @@
     per_slot = [len(ws) for ws in weights]
 
     def kernel(meta_ref, t_ref, *refs):
-        ns, ws, o_ref = refs[:count], refs[count:-1], refs[-1]
+        ns, ws, o_ref = refs[:count], refs[count : count + len(flat)], refs[-1]
         n = jnp.concatenate([r[...] for r in ns], axis=1)
         for c in range(TILES):
 
@@ -389,16 +424,18 @@
                 w = jnp.concatenate(rows_of, axis=0)
                 o_ref[...] = (t_ref[...] + jnp.dot(n, w, preferred_element_type=F32)).astype(dtype)
 
-    out_spec = pl.BlockSpec((rows, tile), lambda n, m: (0, n ^ (m[3] * (TILES // 2))))
+    out_spec = pl.BlockSpec((rows, tile), lambda n, m: (row_block, n ^ (m[3] * (TILES // 2))))
+    held = [] if into is None else [into]
     return call(
         kernel,
         (TILES,),
-        [out_spec] + [whole(p.shape) for p in pieces] + specs,
+        [out_spec] + [whole(p.shape) for p in pieces] + specs + [pl.BlockSpec(memory_space=pl.ANY)] * len(held),
         out_spec,
-        jax.ShapeDtypeStruct((rows, columns), dtype),
+        jax.ShapeDtypeStruct(total.shape, dtype),
         10**6,
         1024,
-    )(meta, total, *pieces, *flat)
+        aliases={2 + count + len(flat): 0} if held else {},
+    )(meta, total, *pieces, *flat, *held)
 
 
 def pair_body(n_seq, query, key, value, doc_lengths, gain, weight):
@@ -428,11 +465,7 @@
         return lax.optimization_barrier((x, *arrays))[0]
 
     quarter = half // 2
-    sent = [(side * half, half), ((1 - side) * half, quarter)]
-    sent = [
-        lax.dynamic_slice(weight, (member * part, (1 - group) * columns + at), (part, size))
-        for at, size in sent
-    ]
+    sent = slice_weights(meta, weight, columns)
     w0 = [flip(x) for x in sent]
 
     send, keep = split_states(after(meta, *sent), key, value, docs)
@@ -455,8 +488,8 @@
     carry1 = swap(core_carry0, 1)
     chip_carry2 = swap(chip_carry, 2)
 
-    def norm(slots, withins, carries):
-        return norm_heads(meta, query, withins, carries, gain, docs, slots)
+    def norm(slots, withins, carries, split=None):
+        return norm_heads(meta, query, withins, carries, gain, docs, slots, split)
 
     normed0 = norm((0,), [within0], [carry0])
     far0 = flip(normed0)
@@ -464,22 +497,25 @@
     far1 = flip(normed1)
     carry2, core_carry2 = carry_second(after(meta, far0, w2[0]), chip_carry2, keep, core_got, rows, docs)
     carry3 = swap(core_carry2, 1)
-    normed2 = norm((2, 3), [within2, within3], [carry2, carry3])
-    far2 = flip(normed2)
-
-    total = project_own(after(meta, far1), [normed0, normed1, normed2], weight, columns)
-    w0.append(swap(behind(w0[0], normed0)[:, quarter:], plane))
+    low = rows // 4
+    normed2 = norm((2, 3), [within2, within3], [carry2, carry3], (rows - low, low))
+    far2 = [flip(x) for x in normed2]
+
+    total = project_own(after(meta, far1), [normed0, normed1, *normed2], weight, columns)
+    w0.append(swap(behind(w0[0], *normed2)[:, quarter:], plane))
     w2.append(swap(behind(w0[1], chip_carry2), 2))
-    w2.append(swap(behind(w2[0], carry2)[:, quarter:], plane))
+    w2.append(swap(behind(w2[0], *normed2)[:, quarter:], plane))
 
     def cut(w, width):
         return [w[:, at : at + width] for at in range(0, w.shape[1], width)]
 
     w1 = [swap(x, 1) for w in w0 for x in cut(w, quarter)]
+    w2 = [w2[0], *lax.optimization_barrier((*w2[1:], total))[:2]]
     w3 = [swap(x, 1) for w, width in zip(w2, (quarter, quarter // 2, quarter // 2)) for x in cut(w, width)]
 
     total = project_more(meta, total, [far0, far1], [w0, w1], F32)
-    return project_more(meta, total, [far2], [w2, w3], BF16)
+    out = project_more(meta, total, [far2[0]], [w2, w3], BF16)
+    return project_more(meta, total, [far2[1]], [w2, w3], BF16, (rows - low) // low, out)
 
 
 def body(n_seq, n_head, query, key, value, doc_lengths, gain, weight):

time: 77.4 us -> 95.3 us (1.23)
  waiting for transfers between devices: 15.5 us -> 32.2 us
  Pallas kernels: 29.1 us -> 33.6 us
  local copies, waits for them, and re-layouts: 4.2 us -> 0.98 us
    ppermute x5 -> x6, waiting for transfers between devices: 0.45 us -> 26.9 us  [flip(): return lax.ppermute(x, 'head', [(0, 1), (1, 0)])]
    ppermute x19, waiting for transfers between devices: 14.5 us -> 4.67 us  [swap(): return lax.ppermute(x, 'seq', [(i, i ^ bit) for i in range(n_seq)])]
    pallas_call x2 -> x3, Pallas kernels: 8.25 us -> 10.7 us  [project_more(): call(kernel, (TILES,), [out_spec] + [whole(p.shape) for p in pieces] + sp...]
    dynamic_slice x2 -> x0, local copies, waits for them, and re-layouts: 2.32 us -> none  [pair_body(): lax.dynamic_slice(weight, (member * part, (1 - group) * columns + at), (p...]
    pallas_call x0 -> x1, Pallas kernels: none -> 2.07 us  [slice_weights(): call(kernel, (1,), [pl.BlockSpec(memory_space=pl.ANY)], [pl.BlockSpec(mem...]
    ppermute x5 -> x6, starting transfers between devices: 7.13 us -> 9.14 us  [flip(): return lax.ppermute(x, 'head', [(0, 1), (1, 0)])]
    unnamed x18 -> x14, local copies, waits for them, and re-layouts: 1.57 us -> 0.03 us
    ppermute x19, starting transfers between devices: 11.9 us -> 10.7 us  [swap(): return lax.ppermute(x, 'seq', [(i, i ^ bit) for i in range(n_seq)])]
  transfers between devices with their start and end apart: 26 -> 27, of which waited for: 9 -> 10; matrix products, arithmetic and copies ran while one was open for 2% -> 0% of each run, Pallas kernels for 32% -> 30%
where the time goes in v10:
time: 95.3 us; the launch traced here: 95.1 us
  Pallas kernels  33.6 us (35%)
  waiting for transfers between devices  32.2 us (34%)
  starting transfers between devices  28 us (29%)
  local copies, waits for them, and re-layouts  0.98 us (1%)
    ppermute x6, waiting for transfers between devices, flip(): return lax.ppermute(x, 'head', [(0, 1), (1, 0)])  26.9 us
    pallas_call x13, Pallas kernels, local(): call(kernel, (1,), specs or [whole(a.shape) for a in arrays], [whole(s.sh...  15.5 us
    pallas_call x3, Pallas kernels, project_more(): call(kernel, (TILES,), [out_spec] + [whole(p.shape) for p in pieces] + sp...  10.7 us
    ppermute x19, starting transfers between devices, swap(): return lax.ppermute(x, 'seq', [(i, i ^ bit) for i in range(n_seq)])  10.7 us
    ppermute x6, starting transfers between devices, flip(): return lax.ppermute(x, 'head', [(0, 1), (1, 0)])  9.14 us
    ppermute x2, starting transfers between devices, shift(): lax.ppermute(x, 'seq', [(i, i + count) for i in range(n_seq - count)])  8.17 us
    pallas_call x1, Pallas kernels, project_own(): call(kernel, (TILES,), [whole(p.shape) for p in pieces] + [pl.BlockSpec((...  5.34 us
    ppermute x19, waiting for transfers between devices, swap(): return lax.ppermute(x, 'seq', [(i, i ^ bit) for i in range(n_seq)])  4.67 us
  transfers between devices with their start and end apart: 27, of which 10 were waited for; matrix products, arithmetic and copies ran while one was open for 0% of the time, Pallas kernels for 30%

profile of v10, /device:TPU:0, one launch (start us, length us, event | category | flops | bytes accessed | tf_op | source)
XLA Modules:
  0.0 95.1 jit_solution(14567615690652816962)
XLA Ops:
  0.7 2.1 %shard_map.64 = (bf16[384,1024]{1,0:T(8,128)(2,1)S(1)}, bf16[384,512]{1,0:T(8,128)(2,1)S(1)}) custom-call(s32[24]{0:T(128)S(1)} %concatenate.3.meta_ref, bf16[1536,4096]{1,0:T(8,128)(2,1)} %refs_7_.3), custom_call_target="tpu_custom_call" | custom-call | flops 6000000000 | bytes 1024 | tf_op jit(solution)/shard_map/pallas_call | solution.py:164
  2.8 3.0 %collective-permute-start.7 = (bf16[384,1024]{1,0:T(8,128)(2,1)S(1)}, bf16[384,1024]{1,0:T(8,128)(2,1)S(1)}, u32[]{:S(2)}, u32[]{:S(2)}) collective-permute-start(bf16[384,1024]{1,0:T(8,128)(2,1)S(1)} %get-tuple-element.38), channel_id=1, source_target_pairs={{0,1},{1,0},{2,3},{3,2},{4,5},{5,4},{6,7},{7,6},{8,9},{9,8},{10,11... | collective-permute-start | bytes 2359304 | tf_op jit(solution)/shard_map/ppermute | solution.py:462
  5.9 1.7 %shard_map.65 = (bf16[2,384,128]{2,1,0:T(8,128)(2,1)S(1)}, bf16[2,384,128]{2,1,0:T(8,128)(2,1)S(1)}) custom-call(s32[24]{0:T(128)S(1)} %concatenate.3.meta_ref, bf16[512,1536]{1,0:T(8,128)(2,1)S(1)} %copy-done, bf16[512,1536]{1,0:T(8,128)(2,1)S(1)} %copy-done, bf16[512,1536]{1,0:T(8,128)(2,1)S(1)} %copy-done, bf16[512,1536]{1,0:T(8,128)(2,1)S(1)} %copy-done, ...), custom_call_target="tpu_custom_call" | custom-call | flops 2000000000 | bytes 1024 | tf_op jit(solution)/shard_map/pallas_call | solution.py:123
  7.6 1.9 %shard_map.66 = (f32[512,384]{1,0:T(8,128)S(1)}, bf16[512,512]{1,0:T(8,128)(2,1)S(1)}) custom-call(s32[24]{0:T(128)S(1)} %concatenate.3.meta_ref, bf16[512,1536]{1,0:T(8,128)(2,1)S(1)} %copy-done.2, bf16[512,1536]{1,0:T(8,128)(2,1)S(1)} %copy-done, bf16[512,1536]{1,0:T(8,128)(2,1)S(1)} %copy-done.1), custom_call_target="tpu_custom_call" | custom-call | flops 2000000000 | bytes 1024 | tf_op jit(solution)/shard_map/pallas_call | solution.py:123
  11.8 1.8 %shard_map.68.refs_1_ = f32[512,384]{1,0:T(8,128)S(1)} custom-call(s32[24]{0:T(128)S(1)} %concatenate.3.meta_ref, bf16[512,1536]{1,0:T(8,128)(2,1)S(1)} %copy-done.2, bf16[512,1536]{1,0:T(8,128)(2,1)S(1)} %copy-done, bf16[512,1536]{1,0:T(8,128)(2,1)S(1)} %copy-done.1, bf16[512,512]{1,0:T(8,128)(2,1)S(1)} %get-tuple-element.49.rest_0_), custom_call_target="tpu_custom_call" | custom-call | flops 2000000000 | bytes 1024 | tf_op jit(solution)/shard_map/pallas_call | solution.py:123
  13.6 1.9 %collective-permute-done.1.b_ref = bf16[384,128]{1,0:T(8,128)(2,1)S(1)} collective-permute-done((bf16[384,128]{1,0:T(8,128)(2,1)S(1)}, bf16[384,128]{1,0:T(8,128)(2,1)S(1)}, u32[]{:S(2)}, u32[]{:S(2)}) %collective-permute-start.1) | collective-permute-done | bytes 98336 | tf_op jit(solution)/shard_map/ppermute | solution.py:456
  16.1 3.5 %collective-permute-start.2 = (bf16[384,128]{1,0:T(8,128)(2,1)S(1)}, bf16[384,128]{1,0:T(8,128)(2,1)S(1)}, u32[]{:S(2)}, u32[]{:S(2)}) collective-permute-start(bf16[384,128]{1,0:T(8,128)(2,1)S(1)} %shard_map.69.a_ref), channel_id=1, source_target_pairs={{0,8},{2,10},{4,12},{6,14},{8,16},{10,18},{12,20},{14,22},{16,24},... | collective-permute-start | bytes 294920 | tf_op jit(solution)/shard_map/ppermute | solution.py:459
  19.6 1.8 %shard_map.70.refs_1_ = f32[512,384]{1,0:T(8,128)S(1)} custom-call(s32[24]{0:T(128)S(1)} %concatenate.3.meta_ref, bf16[512,1536]{1,0:T(8,128)(2,1)S(1)} %copy-done.2, bf16[512,1536]{1,0:T(8,128)(2,1)S(1)} %copy-done, bf16[512,1536]{1,0:T(8,128)(2,1)S(1)} %copy-done.1, bf16[512,512]{1,0:T(8,128)(2,1)S(1)} %get-tuple-element.49.rest_0_), custom_call_target="tpu_custom_call" | custom-call | flops 2000000000 | bytes 1024 | tf_op jit(solution)/shard_map/pallas_call | solution.py:123
  23.4 1.7 %collective-permute-start.8 = (bf16[384,1024]{1,0:T(8,128)(2,1)S(1)}, bf16[384,1024]{1,0:T(8,128)(2,1)S(1)}, u32[]{:S(2)}, u32[]{:S(2)}) collective-permute-start(bf16[384,1024]{1,0:T(8,128)(2,1)S(1)} %collective-permute-done.7.refs_2_), channel_id=1, source_target_pairs={{0,4},{2,6},{4,0},{6,2},{8,12},{10,14},{12,8},{14,10},{16,20},{18,... | collective-permute-start | bytes 2359304 | tf_op jit(solution)/shard_map/ppermute | solution.py:456
  25.1 4.7 %collective-permute-start.3 = (bf16[384,128]{1,0:T(8,128)(2,1)S(1)}, bf16[384,128]{1,0:T(8,128)(2,1)S(1)}, u32[]{:S(2)}, u32[]{:S(2)}) collective-permute-start(bf16[384,128]{1,0:T(8,128)(2,1)S(1)} %shard_map.71), channel_id=1, source_target_pairs={{0,16},{2,18},{4,20},{6,22},{8,24},{10,26},{12,28},{14,30},{1,17},... | collective-permute-start | bytes 294920 | tf_op jit(solution)/shard_map/ppermute | solution.py:459
  29.8 1.8 %shard_map.72.refs_5_ = f32[512,384]{1,0:T(8,128)S(1)} custom-call(s32[24]{0:T(128)S(1)} %concatenate.3.meta_ref, bf16[512,1536]{1,0:T(8,128)(2,1)S(1)} %copy-done.2, bf16[512,1536]{1,0:T(8,128)(2,1)S(1)} %copy-done, bf16[512,1536]{1,0:T(8,128)(2,1)S(1)} %copy-done.1, bf16[512,512]{1,0:T(8,128)(2,1)S(1)} %get-tuple-element.49.rest_0_), custom_call_target="tpu_custom_call" | custom-call | flops 2000000000 | bytes 1024 | tf_op jit(solution)/shard_map/pallas_call | solution.py:123
  33.6 1.6 %collective-permute-start.6 = (bf16[512,384]{1,0:T(8,128)(2,1)S(1)}, bf16[512,384]{1,0:T(8,128)(2,1)S(1)}, u32[]{:S(2)}, u32[]{:S(2)}) collective-permute-start(bf16[512,384]{1,0:T(8,128)(2,1)S(1)} %shard_map.75.refs_0_), channel_id=1, source_target_pairs={{0,1},{1,0},{2,3},{3,2},{4,5},{5,4},{6,7},{7,6},{8,9},{9,8},{10,11... | collective-permute-start | bytes 1179656 | tf_op jit(solution)/shard_map/ppermute | solution.py:462
  36.2 9.5 %collective-permute-done.6.refs_0_ = bf16[512,384]{1,0:T(8,128)(2,1)S(1)} collective-permute-done((bf16[512,384]{1,0:T(8,128)(2,1)S(1)}, bf16[512,384]{1,0:T(8,128)(2,1)S(1)}, u32[]{:S(2)}, u32[]{:S(2)}) %collective-permute-start.6) | collective-permute-done | bytes 393248 | tf_op jit(solution)/shard_map/ppermute | solution.py:462
  46.4 4.9 %collective-permute-done.11.refs_3_ = bf16[384,512]{1,0:T(8,128)(2,1)S(1)} collective-permute-done((bf16[384,512]{1,0:T(8,128)(2,1)S(1)}, bf16[384,512]{1,0:T(8,128)(2,1)S(1)}, u32[]{:S(2)}, u32[]{:S(2)}) %collective-permute-start.11) | collective-permute-done | bytes 393248 | tf_op jit(solution)/shard_map/ppermute | solution.py:462
  52.3 1.6 %collective-permute-start.5 = (bf16[512,384]{1,0:T(8,128)(2,1)S(1)}, bf16[512,384]{1,0:T(8,128)(2,1)S(1)}, u32[]{:S(2)}, u32[]{:S(2)}) collective-permute-start(bf16[512,384]{1,0:T(8,128)(2,1)S(1)} %shard_map.74.refs_1_), channel_id=1, source_target_pairs={{0,1},{1,0},{2,3},{3,2},{4,5},{5,4},{6,7},{7,6},{8,9},{9,8},{10,11... | collective-permute-start | bytes 1179656 | tf_op jit(solution)/shard_map/ppermute | solution.py:462
  55.8 2.1 %collective-permute-start.19 = (bf16[384,512]{1,0:T(8,128)(2,1)S(1)}, bf16[384,512]{1,0:T(8,128)(2,1)S(1)}, u32[]{:S(2)}, u32[]{:S(2)}) collective-permute-start(bf16[384,512]{1,0:T(8,128)(2,1)S(1)} %slice.33), channel_id=1, source_target_pairs={{0,8},{2,10},{4,12},{6,14},{8,0},{10,2},{12,4},{14,6},{16,24},{18,... | collective-permute-start | bytes 1179656 | tf_op jit(solution)/shard_map/ppermute | solution.py:456
  58.1 5.8 %collective-permute-done.5.refs_1_ = bf16[512,384]{1,0:T(8,128)(2,1)S(1)} collective-permute-done((bf16[512,384]{1,0:T(8,128)(2,1)S(1)}, bf16[512,384]{1,0:T(8,128)(2,1)S(1)}, u32[]{:S(2)}, u32[]{:S(2)}) %collective-permute-start.5) | collective-permute-done | bytes 393248 | tf_op jit(solution)/shard_map/ppermute | solution.py:462
  63.9 2.1 %collective-permute-start.12 = (bf16[384,512]{1,0:T(8,128)(2,1)S(1)}, bf16[384,512]{1,0:T(8,128)(2,1)S(1)}, u32[]{:S(2)}, u32[]{:S(2)}) collective-permute-start(bf16[384,512]{1,0:T(8,128)(2,1)S(1)} %slice.30), channel_id=1, source_target_pairs={{0,8},{2,10},{4,12},{6,14},{8,0},{10,2},{12,4},{14,6},{16,24},{18,... | collective-permute-start | bytes 1179656 | tf_op jit(solution)/shard_map/ppermute | solution.py:456
  66.1 5.3 %shard_map.78.t_ref = f32[512,2048]{1,0:T(8,128)S(1)} custom-call(s32[24]{0:T(128)S(1)} %concatenate.3.meta_ref, bf16[512,384]{1,0:T(8,128)(2,1)S(1)} %shard_map.75.refs_0_, bf16[512,384]{1,0:T(8,128)(2,1)S(1)} %shard_map.74.refs_1_, bf16[384,768]{1,0:T(8,128)(2,1)S(1)} %get-tuple-element.64.refs_2_, bf16[128,768]{1,0:T(8,128)(2,1)S(1)} %get-tuple-element.65.refs_3_, ...), custom_call_target="tpu_custom_call" | custom-call | flops 1000000 | bytes 1024 | tf_op jit(solution)/shard_map/pallas_call | solution.py:379
  73.6 2.0 %collective-permute-done.12.refs_4_ = bf16[384,512]{1,0:T(8,128)(2,1)S(1)} collective-permute-done((bf16[384,512]{1,0:T(8,128)(2,1)S(1)}, bf16[384,512]{1,0:T(8,128)(2,1)S(1)}, u32[]{:S(2)}, u32[]{:S(2)}) %collective-permute-start.12) | collective-permute-done | bytes 393248 | tf_op jit(solution)/shard_map/ppermute | solution.py:456
  78.7 3.9 %shard_map.79.t_ref = f32[512,2048]{1,0:T(8,128)S(1)} custom-call(s32[24]{0:T(128)S(1)} %concatenate.3.meta_ref, f32[512,2048]{1,0:T(8,128)S(1)} %shard_map.78.t_ref, bf16[512,384]{1,0:T(8,128)(2,1)S(1)} %collective-permute-done.6.refs_0_, bf16[512,384]{1,0:T(8,128)(2,1)S(1)} %collective-permute-done.5.refs_1_, ...), custom_call_target="tpu_custom_call" | custom-call | flops 1000000 | bytes 1024 | tf_op jit(solution)/shard_map/pallas_call | solution.py:429
  82.5 5.7 %collective-permute-done.26.refs_0_ = bf16[384,768]{1,0:T(8,128)(2,1)S(1)} collective-permute-done((bf16[384,768]{1,0:T(8,128)(2,1)S(1)}, bf16[384,768]{1,0:T(8,128)(2,1)S(1)}, u32[]{:S(2)}, u32[]{:S(2)}) %collective-permute-start.26) | collective-permute-done | bytes 589856 | tf_op jit(solution)/shard_map/ppermute | solution.py:462
  88.2 3.9 %shard_map.80.refs_10_ = bf16[512,2048]{1,0:T(8,128)(2,1)} custom-call(s32[24]{0:T(128)S(1)} %concatenate.3.meta_ref, f32[512,2048]{1,0:T(8,128)S(1)} %shard_map.79.t_ref, bf16[384,768]{1,0:T(8,128)(2,1)S(1)} %collective-permute-done.26.refs_0_, bf16[384,1024]{1,0:T(8,128)(2,1)S(1)} %collective-permute-done.8.refs_1_, ...), custom_call_target="tpu_custom_call" | custom-call | flops 1000000 | bytes 1024 | tf_op jit(solution)/shard_map/pallas_call | solution.py:429
  92.1 2.9 %shard_map.81 = bf16[512,2048]{1,0:T(8,128)(2,1)} custom-call(s32[24]{0:T(128)S(1)} %concatenate.3.meta_ref, f32[512,2048]{1,0:T(8,128)S(1)} %shard_map.79.t_ref, bf16[128,768]{1,0:T(8,128)(2,1)S(1)} %collective-permute-done.17.refs_0_, bf16[384,1024]{1,0:T(8,128)(2,1)S(1)} %collective-permute-done.8.refs_1_, ...), custom_call_target="tpu_custom_call", output_to_operand_aliasing={{}: (12, {})} | custom-call | flops 1000000 | bytes 1024 | tf_op jit(solution)/shard_map/pallas_call | solution.py:429
  (72 shorter events, 17.7 us)
Async XLA Ops:
  2.8 20.6 %collective-permute-start.7 = (bf16[384,1024]{1,0:T(8,128)(2,1)S(1)}, bf16[384,1024]{1,0:T(8,128)(2,1)S(1)}, u32[]{:S(2)}, u32[]{:S(2)}) collective-permute-start(bf16[384,1024]{1,0:T(8,128)(2,1)S(1)} %get-tuple-element.38), channel_id=1, source_target_pairs={{0,1},{1,0},{2,3},{3,2},{4,5},{5,4},{6,7},{7,6},{8,9},{9,8},{10,11... | collective-permute-start | bytes 2359304 | tf_op jit(solution)/shard_map/ppermute | solution.py:462
  10.2 5.3 %collective-permute-start.1 = (bf16[384,128]{1,0:T(8,128)(2,1)S(1)}, bf16[384,128]{1,0:T(8,128)(2,1)S(1)}, u32[]{:S(2)}, u32[]{:S(2)}) collective-permute-start(bf16[384,128]{1,0:T(8,128)(2,1)S(1)} %get-tuple-element.51), channel_id=1, source_target_pairs={{0,4},{2,6},{4,0},{6,2},{8,12},{10,14},{12,8},{14,10},{16,20},{18,... | collective-permute-start | bytes 294920 | tf_op jit(solution)/shard_map/ppermute | solution.py:456
  16.1 5.7 %collective-permute-start.2 = (bf16[384,128]{1,0:T(8,128)(2,1)S(1)}, bf16[384,128]{1,0:T(8,128)(2,1)S(1)}, u32[]{:S(2)}, u32[]{:S(2)}) collective-permute-start(bf16[384,128]{1,0:T(8,128)(2,1)S(1)} %shard_map.69.a_ref), channel_id=1, source_target_pairs={{0,8},{2,10},{4,12},{6,14},{8,16},{10,18},{12,20},{14,22},{16,24},... | collective-permute-start | bytes 294920 | tf_op jit(solution)/shard_map/ppermute | solution.py:459
  23.4 22.3 %collective-permute-start.8 = (bf16[384,1024]{1,0:T(8,128)(2,1)S(1)}, bf16[384,1024]{1,0:T(8,128)(2,1)S(1)}, u32[]{:S(2)}, u32[]{:S(2)}) collective-permute-start(bf16[384,1024]{1,0:T(8,128)(2,1)S(1)} %collective-permute-done.7.refs_2_), channel_id=1, source_target_pairs={{0,4},{2,6},{4,0},{6,2},{8,12},{10,14},{12,8},{14,10},{16,20},{18,... | collective-permute-start | bytes 2359304 | tf_op jit(solution)/shard_map/ppermute | solution.py:456
  25.1 6.7 %collective-permute-start.3 = (bf16[384,128]{1,0:T(8,128)(2,1)S(1)}, bf16[384,128]{1,0:T(8,128)(2,1)S(1)}, u32[]{:S(2)}, u32[]{:S(2)}) collective-permute-start(bf16[384,128]{1,0:T(8,128)(2,1)S(1)} %shard_map.71), channel_id=1, source_target_pairs={{0,16},{2,18},{4,20},{6,22},{8,24},{10,26},{12,28},{14,30},{1,17},... | collective-permute-start | bytes 294920 | tf_op jit(solution)/shard_map/ppermute | solution.py:459
  33.6 12.1 %collective-permute-start.6 = (bf16[512,384]{1,0:T(8,128)(2,1)S(1)}, bf16[512,384]{1,0:T(8,128)(2,1)S(1)}, u32[]{:S(2)}, u32[]{:S(2)}) collective-permute-start(bf16[512,384]{1,0:T(8,128)(2,1)S(1)} %shard_map.75.refs_0_), channel_id=1, source_target_pairs={{0,1},{1,0},{2,3},{3,2},{4,5},{5,4},{6,7},{7,6},{8,9},{9,8},{10,11... | collective-permute-start | bytes 1179656 | tf_op jit(solution)/shard_map/ppermute | solution.py:462
  35.2 16.1 %collective-permute-start.11 = (bf16[384,512]{1,0:T(8,128)(2,1)S(1)}, bf16[384,512]{1,0:T(8,128)(2,1)S(1)}, u32[]{:S(2)}, u32[]{:S(2)}) collective-permute-start(bf16[384,512]{1,0:T(8,128)(2,1)S(1)} %get-tuple-element.39), channel_id=1, source_target_pairs={{0,1},{1,0},{2,3},{3,2},{4,5},{5,4},{6,7},{7,6},{8,9},{9,8},{10,11... | collective-permute-start | bytes 1179656 | tf_op jit(solution)/shard_map/ppermute | solution.py:462
  35.7 10.0 %collective-permute-start.9 = (bf16[384,128]{1,0:T(8,128)(2,1)S(1)}, bf16[384,128]{1,0:T(8,128)(2,1)S(1)}, u32[]{:S(2)}, u32[]{:S(2)}) collective-permute-start(bf16[384,128]{1,0:T(8,128)(2,1)S(1)} %get-tuple-element.61), channel_id=1, source_target_pairs={{0,4},{2,6},{4,0},{6,2},{8,12},{10,14},{12,8},{14,10},{16,20},{18,... | collective-permute-start | bytes 294920 | tf_op jit(solution)/shard_map/ppermute | solution.py:456
  36.2 15.1 %collective-permute-start.4 = (bf16[384,128]{1,0:T(8,128)(2,1)S(1)}, bf16[384,128]{1,0:T(8,128)(2,1)S(1)}, u32[]{:S(2)}, u32[]{:S(2)}) collective-permute-start(bf16[384,128]{1,0:T(8,128)(2,1)S(1)} %get-tuple-element.56), channel_id=1, source_target_pairs={{0,2},{2,0},{4,6},{6,4},{8,10},{10,8},{12,14},{14,12},{16,18},{18,... | collective-permute-start | bytes 294920 | tf_op jit(solution)/shard_map/ppermute | solution.py:456
  46.3 8.2 %collective-permute-start.10 = (bf16[384,128]{1,0:T(8,128)(2,1)S(1)}, bf16[384,128]{1,0:T(8,128)(2,1)S(1)}, u32[]{:S(2)}, u32[]{:S(2)}) collective-permute-start(bf16[384,128]{1,0:T(8,128)(2,1)S(1)} %get-tuple-element.63), channel_id=1, source_target_pairs={{0,2},{2,0},{4,6},{6,4},{8,10},{10,8},{12,14},{14,12},{16,18},{18,... | collective-permute-start | bytes 294920 | tf_op jit(solution)/shard_map/ppermute | solution.py:456
  51.3 20.7 %collective-permute-start.15 = (bf16[384,512]{1,0:T(8,128)(2,1)S(1)}, bf16[384,512]{1,0:T(8,128)(2,1)S(1)}, u32[]{:S(2)}, u32[]{:S(2)}) collective-permute-start(bf16[384,512]{1,0:T(8,128)(2,1)S(1)} %collective-permute-done.11.refs_3_), channel_id=1, source_target_pairs={{0,2},{2,0},{4,6},{6,4},{8,10},{10,8},{12,14},{14,12},{16,18},{18,... | collective-permute-start | bytes 1179656 | tf_op jit(solution)/shard_map/ppermute | solution.py:456
  52.3 11.6 %collective-permute-start.5 = (bf16[512,384]{1,0:T(8,128)(2,1)S(1)}, bf16[512,384]{1,0:T(8,128)(2,1)S(1)}, u32[]{:S(2)}, u32[]{:S(2)}) collective-permute-start(bf16[512,384]{1,0:T(8,128)(2,1)S(1)} %shard_map.74.refs_1_), channel_id=1, source_target_pairs={{0,1},{1,0},{2,3},{3,2},{4,5},{5,4},{6,7},{7,6},{8,9},{9,8},{10,11... | collective-permute-start | bytes 1179656 | tf_op jit(solution)/shard_map/ppermute | solution.py:462
  53.9 12.1 %collective-permute-start.18 = (bf16[384,512]{1,0:T(8,128)(2,1)S(1)}, bf16[384,512]{1,0:T(8,128)(2,1)S(1)}, u32[]{:S(2)}, u32[]{:S(2)}) collective-permute-start(bf16[384,512]{1,0:T(8,128)(2,1)S(1)} %collective-permute-done.11.refs_3_), channel_id=1, source_target_pairs={{0,4},{2,6},{4,0},{6,2},{8,12},{10,14},{12,8},{14,10},{16,20},{18,... | collective-permute-start | bytes 1179656 | tf_op jit(solution)/shard_map/ppermute | solution.py:456
  55.8 15.6 %collective-permute-start.19 = (bf16[384,512]{1,0:T(8,128)(2,1)S(1)}, bf16[384,512]{1,0:T(8,128)(2,1)S(1)}, u32[]{:S(2)}, u32[]{:S(2)}) collective-permute-start(bf16[384,512]{1,0:T(8,128)(2,1)S(1)} %slice.33), channel_id=1, source_target_pairs={{0,8},{2,10},{4,12},{6,14},{8,0},{10,2},{12,4},{14,6},{16,24},{18,... | collective-permute-start | bytes 1179656 | tf_op jit(solution)/shard_map/ppermute | solution.py:456
  58.0 14.1 %collective-permute-start.13 = (bf16[384,512]{1,0:T(8,128)(2,1)S(1)}, bf16[384,512]{1,0:T(8,128)(2,1)S(1)}, u32[]{:S(2)}, u32[]{:S(2)}) collective-permute-start(bf16[384,512]{1,0:T(8,128)(2,1)S(1)} %get-tuple-element.74), channel_id=1, source_target_pairs={{0,2},{2,0},{4,6},{6,4},{8,10},{10,8},{12,14},{14,12},{16,18},{18,... | collective-permute-start | bytes 1179656 | tf_op jit(solution)/shard_map/ppermute | solution.py:456
  63.9 11.7 %collective-permute-start.12 = (bf16[384,512]{1,0:T(8,128)(2,1)S(1)}, bf16[384,512]{1,0:T(8,128)(2,1)S(1)}, u32[]{:S(2)}, u32[]{:S(2)}) collective-permute-start(bf16[384,512]{1,0:T(8,128)(2,1)S(1)} %slice.30), channel_id=1, source_target_pairs={{0,8},{2,10},{4,12},{6,14},{8,0},{10,2},{12,4},{14,6},{16,24},{18,... | collective-permute-start | bytes 1179656 | tf_op jit(solution)/shard_map/ppermute | solution.py:456
  66.0 9.6 %collective-permute-start.14 = (bf16[384,512]{1,0:T(8,128)(2,1)S(1)}, bf16[384,512]{1,0:T(8,128)(2,1)S(1)}, u32[]{:S(2)}, u32[]{:S(2)}) collective-permute-start(bf16[384,512]{1,0:T(8,128)(2,1)S(1)} %get-tuple-element.73), channel_id=1, source_target_pairs={{0,2},{2,0},{4,6},{6,4},{8,10},{10,8},{12,14},{14,12},{16,18},{18,... | collective-permute-start | bytes 1179656 | tf_op jit(solution)/shard_map/ppermute | solution.py:456
  71.4 4.8 %collective-permute-start.20 = (bf16[384,512]{1,0:T(8,128)(2,1)S(1)}, bf16[384,512]{1,0:T(8,128)(2,1)S(1)}, u32[]{:S(2)}, u32[]{:S(2)}) collective-permute-start(bf16[384,512]{1,0:T(8,128)(2,1)S(1)} %get-tuple-element.72), channel_id=1, source_target_pairs={{0,2},{2,0},{4,6},{6,4},{8,10},{10,8},{12,14},{14,12},{16,18},{18,... | collective-permute-start | bytes 1179656 | tf_op jit(solution)/shard_map/ppermute | solution.py:456
  72.0 4.3 %collective-permute-start.21 = (bf16[384,512]{1,0:T(8,128)(2,1)S(1)}, bf16[384,512]{1,0:T(8,128)(2,1)S(1)}, u32[]{:S(2)}, u32[]{:S(2)}) collective-permute-start(bf16[384,512]{1,0:T(8,128)(2,1)S(1)} %get-tuple-element.71), channel_id=1, source_target_pairs={{0,2},{2,0},{4,6},{6,4},{8,10},{10,8},{12,14},{14,12},{16,18},{18,... | collective-permute-start | bytes 1179656 | tf_op jit(solution)/shard_map/ppermute | solution.py:456
  72.1 16.1 %collective-permute-start.26 = (bf16[384,768]{1,0:T(8,128)(2,1)S(1)}, bf16[384,768]{1,0:T(8,128)(2,1)S(1)}, u32[]{:S(2)}, u32[]{:S(2)}) collective-permute-start(bf16[384,768]{1,0:T(8,128)(2,1)S(1)} %get-tuple-element.64.refs_2_), channel_id=1, source_target_pairs={{0,1},{1,0},{2,3},{3,2},{4,5},{5,4},{6,7},{7,6},{8,9},{9,8},{10,11... | collective-permute-start | bytes 1769480 | tf_op jit(solution)/shard_map/ppermute | solution.py:462
  76.2 6.3 %collective-permute-start.23 = (bf16[384,256]{1,0:T(8,128)(2,1)S(1)}, bf16[384,256]{1,0:T(8,128)(2,1)S(1)}, u32[]{:S(2)}, u32[]{:S(2)}) collective-permute-start(bf16[384,256]{1,0:T(8,128)(2,1)S(1)} %get-tuple-element.77), channel_id=1, source_target_pairs={{0,2},{2,0},{4,6},{6,4},{8,10},{10,8},{12,14},{14,12},{16,18},{18,... | collective-permute-start | bytes 589832 | tf_op jit(solution)/shard_map/ppermute | solution.py:456
  76.3 6.2 %collective-permute-start.24 = (bf16[384,256]{1,0:T(8,128)(2,1)S(1)}, bf16[384,256]{1,0:T(8,128)(2,1)S(1)}, u32[]{:S(2)}, u32[]{:S(2)}) collective-permute-start(bf16[384,256]{1,0:T(8,128)(2,1)S(1)} %get-tuple-element.76), channel_id=1, source_target_pairs={{0,2},{2,0},{4,6},{6,4},{8,10},{10,8},{12,14},{14,12},{16,18},{18,... | collective-permute-start | bytes 589832 | tf_op jit(solution)/shard_map/ppermute | solution.py:456
  77.6 4.9 %collective-permute-start.25 = (bf16[384,256]{1,0:T(8,128)(2,1)S(1)}, bf16[384,256]{1,0:T(8,128)(2,1)S(1)}, u32[]{:S(2)}, u32[]{:S(2)}) collective-permute-start(bf16[384,256]{1,0:T(8,128)(2,1)S(1)} %get-tuple-element.75), channel_id=1, source_target_pairs={{0,2},{2,0},{4,6},{6,4},{8,10},{10,8},{12,14},{14,12},{16,18},{18,... | collective-permute-start | bytes 589832 | tf_op jit(solution)/shard_map/ppermute | solution.py:456
  77.7 14.4 %collective-permute-start.17 = (bf16[128,768]{1,0:T(8,128)(2,1)S(1)}, bf16[128,768]{1,0:T(8,128)(2,1)S(1)}, u32[]{:S(2)}, u32[]{:S(2)}) collective-permute-start(bf16[128,768]{1,0:T(8,128)(2,1)S(1)} %get-tuple-element.65.refs_3_), channel_id=1, source_target_pairs={{0,1},{1,0},{2,3},{3,2},{4,5},{5,4},{6,7},{7,6},{8,9},{9,8},{10,11... | collective-permute-start | bytes 589832 | tf_op jit(solution)/shard_map/ppermute | solution.py:462
  (10 other events, 97.6 us)

commit v11 on v10

--- a/solution.py
+++ b/solution.py
@@ -11,7 +11,7 @@
 PLANES = 4
 F32, BF16 = jnp.float32, jnp.bfloat16
 LENS = 8
-VMEM_LIMIT = 16 * 1024 * 1024
+VMEM_LIMIT = 24 * 1024 * 1024
 
 
 def doc_start(meta, doc_count, token):
@@ -361,26 +361,26 @@
 
 
 TILES = 4
+OWN_TILES = 2
 
 
 def project_own(meta, pieces, weight, columns):
     rows = pieces[0].shape[0]
     part = weight.shape[0] // 4
-    tile = columns // TILES
+    tile = columns // OWN_TILES
     count = len(pieces)
 
     def kernel(meta_ref, *refs):
         ns, ws, o_ref = refs[:count], refs[count:-1], refs[-1]
-        last = jnp.concatenate([r[...] for r in ns[-2:]], axis=0)
-        n = jnp.concatenate([*[r[...] for r in ns[:-2]], last], axis=1)
+        n = jnp.concatenate([r[...] for r in ns], axis=1)
         w = jnp.concatenate([r[...] for r in ws], axis=0)
         o_ref[...] = jnp.dot(n, w, preferred_element_type=F32)
 
     return call(
         kernel,
-        (TILES,),
+        (OWN_TILES,),
         [whole(p.shape) for p in pieces]
-        + [pl.BlockSpec((part, tile), lambda n, m, s=s: (m[1] ^ s, m[2] * TILES + n)) for s in range(4)],
+        + [pl.BlockSpec((part, tile), lambda n, m, s=s: (m[1] ^ s, m[2] * OWN_TILES + n)) for s in range(4)],
         pl.BlockSpec((rows, tile), lambda n, m: (0, n)),
         jax.ShapeDtypeStruct((rows, columns), F32),
         10**6,
@@ -388,54 +388,60 @@
     )(meta, *pieces, *[weight] * 4)
 
 
-def project_more(meta, total, pieces, weights, dtype, row_block=0, into=None):
-    rows, columns = pieces[0].shape[0], total.shape[1]
+def project_more(meta, total, pieces, weights, final):
+    rows, columns = total.shape
     tile = columns // TILES
     count = len(pieces)
-    flat, specs, places = [], [], []
+    flat = [w for ws in weights for w in ws]
+    places = []
     for ws in weights:
-        start = 0
+        start, slot = 0, []
         for w in ws:
-            first, last = start // tile, (start + w.shape[1] - 1) // tile
-            places.append((first, last))
-            flat.append(w)
-            specs.append(
-                pl.BlockSpec(
-                    (w.shape[0], min(tile, w.shape[1])),
-                    lambda n, m, first=first, last=last: (0, jnp.clip(n - first, 0, last - first)),
-                )
-            )
+            slot.append((start, start + w.shape[1]))
             start += w.shape[1]
-    per_slot = [len(ws) for ws in weights]
+        places.append(slot)
 
     def kernel(meta_ref, t_ref, *refs):
-        ns, ws, o_ref = refs[:count], refs[count : count + len(flat)], refs[-1]
+        ns, ws, rest = refs[:count], refs[count : count + len(flat)], refs[count + len(flat) :]
         n = jnp.concatenate([r[...] for r in ns], axis=1)
+        copies = []
         for c in range(TILES):
-
-            @pl.when(pl.program_id(0) == c)
-            def _():
-                rows_of, at = [], 0
-                for size in per_slot:
-                    here = range(at, at + size)
-                    held = [ws[i][...] for i in here if places[i][0] <= c <= places[i][1]]
-                    rows_of.append(jnp.concatenate(held, axis=1))
-                    at += size
-                w = jnp.concatenate(rows_of, axis=0)
-                o_ref[...] = (t_ref[...] + jnp.dot(n, w, preferred_element_type=F32)).astype(dtype)
-
-    out_spec = pl.BlockSpec((rows, tile), lambda n, m: (row_block, n ^ (m[3] * (TILES // 2))))
-    held = [] if into is None else [into]
+            low, high = c * tile, (c + 1) * tile
+            rows_of, at = [], 0
+            for slot in places:
+                held = []
+                for k, (start, stop) in enumerate(slot):
+                    first, last = max(start, low), min(stop, high)
+                    if first < last:
+                        held.append(ws[at + k][:, first - start : last - start])
+                rows_of.append(jnp.concatenate(held, axis=1))
+                at += len(slot)
+            w = jnp.concatenate(rows_of, axis=0)
+            cols = pl.ds(pl.multiple_of((c ^ (meta_ref[3] * (TILES // 2))) * tile, DH), tile)
+            value = t_ref[:, cols] + jnp.dot(n, w, preferred_element_type=F32)
+            if final:
+                o_ref, held_ref, sems = rest
+                held_ref[c] = value.astype(BF16)
+                copies.append(pltpu.make_async_copy(held_ref.at[c], o_ref.at[:, cols], sems.at[c]))
+                copies[-1].start()
+            else:
+                rest[0][:, cols] = value
+        for copy in copies:
+            copy.wait()
+
+    vmem = pl.BlockSpec(memory_space=pltpu.VMEM)
+    scratch = [pltpu.VMEM((TILES, rows, tile), BF16), pltpu.SemaphoreType.DMA((TILES,))]
     return call(
         kernel,
-        (TILES,),
-        [out_spec] + [whole(p.shape) for p in pieces] + specs + [pl.BlockSpec(memory_space=pl.ANY)] * len(held),
-        out_spec,
-        jax.ShapeDtypeStruct(total.shape, dtype),
+        (1,),
+        [vmem] * (1 + count + len(flat)),
+        pl.BlockSpec(memory_space=pl.ANY) if final else vmem,
+        jax.ShapeDtypeStruct((rows, columns), BF16 if final else F32),
         10**6,
         1024,
-        aliases={2 + count + len(flat): 0} if held else {},
-    )(meta, total, *pieces, *flat, *held)
+        scratch if final else (),
+        aliases={} if final else {1: 0},
+    )(meta, total, *pieces, *flat)
 
 
 def pair_body(n_seq, query, key, value, doc_lengths, gain, weight):
@@ -466,8 +472,8 @@
 
     quarter = half // 2
     sent = slice_weights(meta, weight, columns)
-    w0 = [flip(x) for x in sent]
-
+    w0 = [flip(sent[0])]
+    w0.append(flip(sent[1]))
     send, keep = split_states(after(meta, *sent), key, value, docs)
     core_got = swap(send, 1)
     query = behind(query, send)
@@ -480,42 +486,39 @@
     within2 = within_slot(after(meta, plane_sum), query, key, value, docs, 2, mask)
     both = join_planes(after(meta, within2), plane_sum, near, rows, docs)
     far = shift(both, 2 * plane)
-    w2 = [swap(behind(w0[0], both), 2)]
-    within3 = within_slot(after(meta, both), query, key, value, docs, 3, mask)
     carry0, core_carry0, chip_carry = carry_first(
-        after(meta, within3), near, far, chip0, chip_got, keep, core_got, rows, docs
+        meta, near, far, chip0, chip_got, keep, core_got, rows, docs
     )
     carry1 = swap(core_carry0, 1)
     chip_carry2 = swap(chip_carry, 2)
 
-    def norm(slots, withins, carries, split=None):
-        return norm_heads(meta, query, withins, carries, gain, docs, slots, split)
+    def norm(slots, withins, carries):
+        return norm_heads(meta, query, withins, carries, gain, docs, slots)
 
     normed0 = norm((0,), [within0], [carry0])
     far0 = flip(normed0)
+    within3 = within_slot(after(meta, normed0), query, key, value, docs, 3, mask)
     normed1 = norm((1,), [within1], [carry1])
     far1 = flip(normed1)
-    carry2, core_carry2 = carry_second(after(meta, far0, w2[0]), chip_carry2, keep, core_got, rows, docs)
+    w2 = [swap(behind(w0[0], both), 2)]
+    carry2, core_carry2 = carry_second(after(meta, far0, w2[0], normed1), chip_carry2, keep, core_got, rows, docs)
     carry3 = swap(core_carry2, 1)
-    low = rows // 4
-    normed2 = norm((2, 3), [within2, within3], [carry2, carry3], (rows - low, low))
-    far2 = [flip(x) for x in normed2]
-
-    total = project_own(after(meta, far1), [normed0, normed1, *normed2], weight, columns)
-    w0.append(swap(behind(w0[0], *normed2)[:, quarter:], plane))
-    w2.append(swap(behind(w0[1], chip_carry2), 2))
-    w2.append(swap(behind(w2[0], *normed2)[:, quarter:], plane))
+    normed2 = norm((2, 3), [within2, within3], [carry2, carry3])
+    far2 = flip(normed2)
+
+    total = project_own(after(meta, far1), [normed0, normed1, normed2], weight, columns)
+    w0.append(swap(behind(w0[0], normed1)[:, quarter:], plane))
+    w2.append(swap(behind(w0[1], far0), 2))
+    w2.append(swap(behind(w2[0], carry2)[:, quarter:], plane))
 
     def cut(w, width):
         return [w[:, at : at + width] for at in range(0, w.shape[1], width)]
 
     w1 = [swap(x, 1) for w in w0 for x in cut(w, quarter)]
-    w2 = [w2[0], *lax.optimization_barrier((*w2[1:], total))[:2]]
     w3 = [swap(x, 1) for w, width in zip(w2, (quarter, quarter // 2, quarter // 2)) for x in cut(w, width)]
 
-    total = project_more(meta, total, [far0, far1], [w0, w1], F32)
-    out = project_more(meta, total, [far2[0]], [w2, w3], BF16)
-    return project_more(meta, total, [far2[1]], [w2, w3], BF16, (rows - low) // low, out)
+    total = project_more(meta, total, [far0, far1], [w0, w1], False)
+    return project_more(meta, total, [far2], [w2, w3], True)
 
 
 def body(n_seq, n_head, query, key, value, doc_lengths, gain, weight):

time: 95.3 us -> 75.6 us (0.79)
  waiting for transfers between devices: 32.2 us -> 19.3 us
  Pallas kernels: 33.6 us -> 28.4 us
  starting transfers between devices: 28 us -> 26.3 us
    ppermute x6 -> x5, waiting for transfers between devices: 26.9 us -> 6.47 us  [flip(): return lax.ppermute(x, 'head', [(0, 1), (1, 0)])]
    ppermute x19, waiting for transfers between devices: 4.67 us -> 10.5 us  [swap(): return lax.ppermute(x, 'seq', [(i, i ^ bit) for i in range(n_seq)])]
    pallas_call x4 -> x3, Pallas kernels: 16 us -> 10.8 us  [the longest x2 5.81 us: project_more(): call(kernel, (1,), [vmem] * (1 + count + len(flat)), pl.BlockSpec(memory_...]
    ppermute x6 -> x5, starting transfers between devices: 9.14 us -> 6.71 us  [flip(): return lax.ppermute(x, 'head', [(0, 1), (1, 0)])]
    ppermute x2, waiting for transfers between devices: 0.59 us -> 2.37 us  [shift(): lax.ppermute(x, 'seq', [(i, i + count) for i in range(n_seq - count)])]
  transfers between devices with their start and end apart: 27 -> 26, of which waited for: 10 -> 11; matrix products, arithmetic and copies ran while one was open for 0% -> 0% of each run, Pallas kernels for 30% -> 31%
where the time goes in v11:
time: 75.6 us; the launch traced here: 75.5 us
  Pallas kernels  28.4 us (38%)
  starting transfers between devices  26.3 us (35%)
  waiting for transfers between devices  19.3 us (26%)
  local copies, waits for them, and re-layouts  0.99 us (1%)
    pallas_call x13, Pallas kernels, local(): call(kernel, (1,), specs or [whole(a.shape) for a in arrays], [whole(s.sh...  15.5 us
    ppermute x19, starting transfers between devices, swap(): return lax.ppermute(x, 'seq', [(i, i ^ bit) for i in range(n_seq)])  11.4 us
    ppermute x19, waiting for transfers between devices, swap(): return lax.ppermute(x, 'seq', [(i, i ^ bit) for i in range(n_seq)])  10.5 us
    ppermute x2, starting transfers between devices, shift(): lax.ppermute(x, 'seq', [(i, i + count) for i in range(n_seq - count)])  8.15 us
    ppermute x5, starting transfers between devices, flip(): return lax.ppermute(x, 'head', [(0, 1), (1, 0)])  6.71 us
    ppermute x5, waiting for transfers between devices, flip(): return lax.ppermute(x, 'head', [(0, 1), (1, 0)])  6.47 us
    pallas_call x2, Pallas kernels, project_more(): call(kernel, (1,), [vmem] * (1 + count + len(flat)), pl.BlockSpec(memory_...  5.81 us
    pallas_call x1, Pallas kernels, project_own(): call(kernel, (OWN_TILES,), [whole(p.shape) for p in pieces] + [pl.BlockSp...  4.97 us
  transfers between devices with their start and end apart: 26, of which 11 were waited for; matrix products, arithmetic and copies ran while one was open for 0% of the time, Pallas kernels for 31%

profile of v11, /device:TPU:0, one launch (start us, length us, event | category | flops | bytes accessed | tf_op | source)
XLA Modules:
  0.0 75.5 jit_solution(3865665397929231480)
XLA Ops:
  0.7 2.1 %shard_map.64 = (bf16[384,1024]{1,0:T(8,128)(2,1)S(1)}, bf16[384,512]{1,0:T(8,128)(2,1)S(1)}) custom-call(s32[24]{0:T(128)S(1)} %concatenate.3.meta_ref, bf16[1536,4096]{1,0:T(8,128)(2,1)} %refs_6_.3), custom_call_target="tpu_custom_call" | custom-call | flops 6000000000 | bytes 1024 | tf_op jit(solution)/shard_map/pallas_call | solution.py:164
  2.8 3.0 %collective-permute-start.7 = (bf16[384,1024]{1,0:T(8,128)(2,1)S(1)}, bf16[384,1024]{1,0:T(8,128)(2,1)S(1)}, u32[]{:S(2)}, u32[]{:S(2)}) collective-permute-start(bf16[384,1024]{1,0:T(8,128)(2,1)S(1)} %get-tuple-element.33), channel_id=1, source_target_pairs={{0,1},{1,0},{2,3},{3,2},{4,5},{5,4},{6,7},{7,6},{8,9},{9,8},{10,11... | collective-permute-start | bytes 2359304 | tf_op jit(solution)/shard_map/ppermute | solution.py:468
  5.9 1.7 %shard_map.65 = (bf16[2,384,128]{2,1,0:T(8,128)(2,1)S(1)}, bf16[2,384,128]{2,1,0:T(8,128)(2,1)S(1)}) custom-call(s32[24]{0:T(128)S(1)} %concatenate.3.meta_ref, bf16[512,1536]{1,0:T(8,128)(2,1)S(1)} %copy-done, bf16[512,1536]{1,0:T(8,128)(2,1)S(1)} %copy-done, bf16[512,1536]{1,0:T(8,128)(2,1)S(1)} %copy-done, bf16[512,1536]{1,0:T(8,128)(2,1)S(1)} %copy-done, ...), custom_call_target="tpu_custom_call" | custom-call | flops 2000000000 | bytes 1024 | tf_op jit(solution)/shard_map/pallas_call | solution.py:123
  7.6 1.9 %shard_map.66 = (f32[512,384]{1,0:T(8,128)S(1)}, bf16[512,512]{1,0:T(8,128)(2,1)S(1)}) custom-call(s32[24]{0:T(128)S(1)} %concatenate.3.meta_ref, bf16[512,1536]{1,0:T(8,128)(2,1)S(1)} %copy-done.2, bf16[512,1536]{1,0:T(8,128)(2,1)S(1)} %copy-done, bf16[512,1536]{1,0:T(8,128)(2,1)S(1)} %copy-done.1), custom_call_target="tpu_custom_call" | custom-call | flops 2000000000 | bytes 1024 | tf_op jit(solution)/shard_map/pallas_call | solution.py:123
  10.2 1.6 %collective-permute-start.1 = (bf16[384,128]{1,0:T(8,128)(2,1)S(1)}, bf16[384,128]{1,0:T(8,128)(2,1)S(1)}, u32[]{:S(2)}, u32[]{:S(2)}) collective-permute-start(bf16[384,128]{1,0:T(8,128)(2,1)S(1)} %get-tuple-element.46), channel_id=1, source_target_pairs={{0,4},{2,6},{4,0},{6,2},{8,12},{10,14},{12,8},{14,10},{16,20},{18,... | collective-permute-start | bytes 294920 | tf_op jit(solution)/shard_map/ppermute | solution.py:462
  11.8 1.8 %shard_map.68.refs_1_ = f32[512,384]{1,0:T(8,128)S(1)} custom-call(s32[24]{0:T(128)S(1)} %concatenate.3.meta_ref, bf16[512,1536]{1,0:T(8,128)(2,1)S(1)} %copy-done.2, bf16[512,1536]{1,0:T(8,128)(2,1)S(1)} %copy-done, bf16[512,1536]{1,0:T(8,128)(2,1)S(1)} %copy-done.1, bf16[512,512]{1,0:T(8,128)(2,1)S(1)} %get-tuple-element.44.rest_0_), custom_call_target="tpu_custom_call" | custom-call | flops 2000000000 | bytes 1024 | tf_op jit(solution)/shard_map/pallas_call | solution.py:123
  13.6 1.9 %collective-permute-done.1.b_ref = bf16[384,128]{1,0:T(8,128)(2,1)S(1)} collective-permute-done((bf16[384,128]{1,0:T(8,128)(2,1)S(1)}, bf16[384,128]{1,0:T(8,128)(2,1)S(1)}, u32[]{:S(2)}, u32[]{:S(2)}) %collective-permute-start.1) | collective-permute-done | bytes 98336 | tf_op jit(solution)/shard_map/ppermute | solution.py:462
  16.1 3.5 %collective-permute-start.2 = (bf16[384,128]{1,0:T(8,128)(2,1)S(1)}, bf16[384,128]{1,0:T(8,128)(2,1)S(1)}, u32[]{:S(2)}, u32[]{:S(2)}) collective-permute-start(bf16[384,128]{1,0:T(8,128)(2,1)S(1)} %shard_map.69.a_ref), channel_id=1, source_target_pairs={{0,8},{2,10},{4,12},{6,14},{8,16},{10,18},{12,20},{14,22},{16,24},... | collective-permute-start | bytes 294920 | tf_op jit(solution)/shard_map/ppermute | solution.py:465
  19.6 1.8 %shard_map.70.refs_1_ = f32[512,384]{1,0:T(8,128)S(1)} custom-call(s32[24]{0:T(128)S(1)} %concatenate.3.meta_ref, bf16[512,1536]{1,0:T(8,128)(2,1)S(1)} %copy-done.2, bf16[512,1536]{1,0:T(8,128)(2,1)S(1)} %copy-done, bf16[512,1536]{1,0:T(8,128)(2,1)S(1)} %copy-done.1, bf16[512,512]{1,0:T(8,128)(2,1)S(1)} %get-tuple-element.44.rest_0_), custom_call_target="tpu_custom_call" | custom-call | flops 2000000000 | bytes 1024 | tf_op jit(solution)/shard_map/pallas_call | solution.py:123
  23.4 1.7 %collective-permute-start.8 = (bf16[384,1024]{1,0:T(8,128)(2,1)S(1)}, bf16[384,1024]{1,0:T(8,128)(2,1)S(1)}, u32[]{:S(2)}, u32[]{:S(2)}) collective-permute-start(bf16[384,1024]{1,0:T(8,128)(2,1)S(1)} %collective-permute-done.7.refs_2_), channel_id=1, source_target_pairs={{0,4},{2,6},{4,0},{6,2},{8,12},{10,14},{12,8},{14,10},{16,20},{18,... | collective-permute-start | bytes 2359304 | tf_op jit(solution)/shard_map/ppermute | solution.py:462
  25.1 1.5 %collective-permute-start.11 = (bf16[384,512]{1,0:T(8,128)(2,1)S(1)}, bf16[384,512]{1,0:T(8,128)(2,1)S(1)}, u32[]{:S(2)}, u32[]{:S(2)}) collective-permute-start(bf16[384,512]{1,0:T(8,128)(2,1)S(1)} %get-tuple-element.34), channel_id=1, source_target_pairs={{0,1},{1,0},{2,3},{3,2},{4,5},{5,4},{6,7},{7,6},{8,9},{9,8},{10,11... | collective-permute-start | bytes 1179656 | tf_op jit(solution)/shard_map/ppermute | solution.py:468
  26.6 4.7 %collective-permute-start.3 = (bf16[384,128]{1,0:T(8,128)(2,1)S(1)}, bf16[384,128]{1,0:T(8,128)(2,1)S(1)}, u32[]{:S(2)}, u32[]{:S(2)}) collective-permute-start(bf16[384,128]{1,0:T(8,128)(2,1)S(1)} %shard_map.71), channel_id=1, source_target_pairs={{0,16},{2,18},{4,20},{6,22},{8,24},{10,26},{12,28},{14,30},{1,17},... | collective-permute-start | bytes 294920 | tf_op jit(solution)/shard_map/ppermute | solution.py:465
  31.3 2.0 %collective-permute-done.3.far_ref = bf16[384,128]{1,0:T(8,128)(2,1)S(1)} collective-permute-done((bf16[384,128]{1,0:T(8,128)(2,1)S(1)}, bf16[384,128]{1,0:T(8,128)(2,1)S(1)}, u32[]{:S(2)}, u32[]{:S(2)}) %collective-permute-start.3) | collective-permute-done | bytes 98336 | tf_op jit(solution)/shard_map/ppermute | solution.py:465
  36.7 1.8 %shard_map.76.refs_5_ = f32[512,384]{1,0:T(8,128)S(1)} custom-call(s32[24]{0:T(128)S(1)} %concatenate.3.meta_ref, bf16[512,1536]{1,0:T(8,128)(2,1)S(1)} %copy-done.2, bf16[512,1536]{1,0:T(8,128)(2,1)S(1)} %copy-done, bf16[512,1536]{1,0:T(8,128)(2,1)S(1)} %copy-done.1, bf16[512,512]{1,0:T(8,128)(2,1)S(1)} %get-tuple-element.44.rest_0_), custom_call_target="tpu_custom_call" | custom-call | flops 2000000000 | bytes 1024 | tf_op jit(solution)/shard_map/pallas_call | solution.py:123
  39.5 1.6 %collective-permute-start.5 = (bf16[512,384]{1,0:T(8,128)(2,1)S(1)}, bf16[512,384]{1,0:T(8,128)(2,1)S(1)}, u32[]{:S(2)}, u32[]{:S(2)}) collective-permute-start(bf16[512,384]{1,0:T(8,128)(2,1)S(1)} %shard_map.73.refs_1_), channel_id=1, source_target_pairs={{0,1},{1,0},{2,3},{3,2},{4,5},{5,4},{6,7},{7,6},{8,9},{9,8},{10,11... | collective-permute-start | bytes 1179656 | tf_op jit(solution)/shard_map/ppermute | solution.py:468
  41.2 4.3 %collective-permute-done.6.refs_0_ = bf16[512,384]{1,0:T(8,128)(2,1)S(1)} collective-permute-done((bf16[512,384]{1,0:T(8,128)(2,1)S(1)}, bf16[512,384]{1,0:T(8,128)(2,1)S(1)}, u32[]{:S(2)}, u32[]{:S(2)}) %collective-permute-start.6) | collective-permute-done | bytes 393248 | tf_op jit(solution)/shard_map/ppermute | solution.py:468
  45.4 2.4 %collective-permute-start.12 = (bf16[384,512]{1,0:T(8,128)(2,1)S(1)}, bf16[384,512]{1,0:T(8,128)(2,1)S(1)}, u32[]{:S(2)}, u32[]{:S(2)}) collective-permute-start(bf16[384,512]{1,0:T(8,128)(2,1)S(1)} %slice.30), channel_id=1, source_target_pairs={{0,8},{2,10},{4,12},{6,14},{8,0},{10,2},{12,4},{14,6},{16,24},{18,... | collective-permute-start | bytes 1179656 | tf_op jit(solution)/shard_map/ppermute | solution.py:462
  50.0 1.3 %shard_map.77.refs_2_ = bf16[512,768]{1,0:T(8,128)(2,1)S(1)} custom-call(s32[24]{0:T(128)S(1)} %concatenate.3.meta_ref, bf16[512,1536]{1,0:T(8,128)(2,1)S(1)} %copy-done.2, f32[512,384]{1,0:T(8,128)S(1)} %shard_map.70.refs_1_, bf16[384,128]{1,0:T(8,128)(2,1)S(1)} %get-tuple-element.55.refs_2_, f32[1,1536]{1,0:T(1,128)S(1)} %reshape.2.refs_3_.refs_7_, ...), custom_call_target="tpu_custom_call" | custom-call | flops 2000000000 | bytes 1024 | tf_op jit(solution)/shard_map/pallas_call | solution.py:123
  52.1 2.4 %collective-permute-start.19 = (bf16[384,512]{1,0:T(8,128)(2,1)S(1)}, bf16[384,512]{1,0:T(8,128)(2,1)S(1)}, u32[]{:S(2)}, u32[]{:S(2)}) collective-permute-start(bf16[384,512]{1,0:T(8,128)(2,1)S(1)} %slice.33), channel_id=1, source_target_pairs={{0,8},{2,10},{4,12},{6,14},{8,0},{10,2},{12,4},{14,6},{16,24},{18,... | collective-permute-start | bytes 1179656 | tf_op jit(solution)/shard_map/ppermute | solution.py:462
  56.5 1.3 %collective-permute-done.22.refs_6_ = bf16[384,256]{1,0:T(8,128)(2,1)S(1)} collective-permute-done((bf16[384,256]{1,0:T(8,128)(2,1)S(1)}, bf16[384,256]{1,0:T(8,128)(2,1)S(1)}, u32[]{:S(2)}, u32[]{:S(2)}) %collective-permute-start.22) | collective-permute-done | bytes 196640 | tf_op jit(solution)/shard_map/ppermute | solution.py:462
  57.9 5.1 %collective-permute-done.19.refs_3_ = bf16[384,512]{1,0:T(8,128)(2,1)S(1)} collective-permute-done((bf16[384,512]{1,0:T(8,128)(2,1)S(1)}, bf16[384,512]{1,0:T(8,128)(2,1)S(1)}, u32[]{:S(2)}, u32[]{:S(2)}) %collective-permute-start.19) | collective-permute-done | bytes 393248 | tf_op jit(solution)/shard_map/ppermute | solution.py:462
  63.7 5.0 %shard_map.78.t_ref = f32[512,2048]{1,0:T(8,128)S(1)} custom-call(s32[24]{0:T(128)S(1)} %concatenate.3.meta_ref, bf16[512,384]{1,0:T(8,128)(2,1)S(1)} %shard_map.74.refs_0_, bf16[512,384]{1,0:T(8,128)(2,1)S(1)} %shard_map.73.refs_1_, bf16[512,768]{1,0:T(8,128)(2,1)S(1)} %shard_map.77.refs_2_, bf16[1536,4096]{1,0:T(8,128)(2,1)S(1)} %bitcast.5, ...), custom_call_target="tpu_custom_call" | custom-call | flops 1000000 | bytes 1024 | tf_op jit(solution)/shard_map/pallas_call | solution.py:379
  68.6 2.6 %shard_map.79.t_ref = f32[512,2048]{1,0:T(8,128)S(1)} custom-call(s32[24]{0:T(128)S(1)} %concatenate.3.meta_ref, f32[512,2048]{1,0:T(8,128)S(1)} %shard_map.78.t_ref, bf16[512,384]{1,0:T(8,128)(2,1)S(1)} %collective-permute-done.6.refs_0_, bf16[512,384]{1,0:T(8,128)(2,1)S(1)} %collective-permute-done.5.refs_1_, ...), custom_call_target="tpu_custom_call", output_to_operand_aliasing={{}: (1, {})} | custom-call | flops 1000000 | bytes 1024 | tf_op jit(solution)/shard_map/pallas_call | solution.py:434
  72.1 3.2 %shard_map.80 = bf16[512,2048]{1,0:T(8,128)(2,1)} custom-call(s32[24]{0:T(128)S(1)} %concatenate.3.meta_ref, f32[512,2048]{1,0:T(8,128)S(1)} %shard_map.79.t_ref, bf16[512,768]{1,0:T(8,128)(2,1)S(1)} %collective-permute-done.17.refs_0_, bf16[384,1024]{1,0:T(8,128)(2,1)S(1)} %collective-permute-done.8.refs_1_, ...), custom_call_target="tpu_custom_call" | custom-call | flops 1000000 | bytes 1024 | tf_op jit(solution)/shard_map/pallas_call | solution.py:434
  (69 shorter events, 14.9 us)
Async XLA Ops:
  2.8 20.6 %collective-permute-start.7 = (bf16[384,1024]{1,0:T(8,128)(2,1)S(1)}, bf16[384,1024]{1,0:T(8,128)(2,1)S(1)}, u32[]{:S(2)}, u32[]{:S(2)}) collective-permute-start(bf16[384,1024]{1,0:T(8,128)(2,1)S(1)} %get-tuple-element.33), channel_id=1, source_target_pairs={{0,1},{1,0},{2,3},{3,2},{4,5},{5,4},{6,7},{7,6},{8,9},{9,8},{10,11... | collective-permute-start | bytes 2359304 | tf_op jit(solution)/shard_map/ppermute | solution.py:468
  7.5 2.0 %collective-permute-start = (bf16[2,384,128]{2,1,0:T(8,128)(2,1)S(1)}, bf16[2,384,128]{2,1,0:T(8,128)(2,1)S(1)}, u32[]{:S(2)}, u32[]{:S(2)}) collective-permute-start(bf16[2,384,128]{2,1,0:T(8,128)(2,1)S(1)} %get-tuple-element.36), channel_id=1, source_target_pairs={{0,2},{2,0},{4,6},{6,4},{8,10},{10,8},{12,14},{14,12},{16,18},{18,... | collective-permute-start | bytes 589832 | tf_op jit(solution)/shard_map/ppermute | solution.py:462
  10.2 5.3 %collective-permute-start.1 = (bf16[384,128]{1,0:T(8,128)(2,1)S(1)}, bf16[384,128]{1,0:T(8,128)(2,1)S(1)}, u32[]{:S(2)}, u32[]{:S(2)}) collective-permute-start(bf16[384,128]{1,0:T(8,128)(2,1)S(1)} %get-tuple-element.46), channel_id=1, source_target_pairs={{0,4},{2,6},{4,0},{6,2},{8,12},{10,14},{12,8},{14,10},{16,20},{18,... | collective-permute-start | bytes 294920 | tf_op jit(solution)/shard_map/ppermute | solution.py:462
  16.1 5.7 %collective-permute-start.2 = (bf16[384,128]{1,0:T(8,128)(2,1)S(1)}, bf16[384,128]{1,0:T(8,128)(2,1)S(1)}, u32[]{:S(2)}, u32[]{:S(2)}) collective-permute-start(bf16[384,128]{1,0:T(8,128)(2,1)S(1)} %shard_map.69.a_ref), channel_id=1, source_target_pairs={{0,8},{2,10},{4,12},{6,14},{8,16},{10,18},{12,20},{14,22},{16,24},... | collective-permute-start | bytes 294920 | tf_op jit(solution)/shard_map/ppermute | solution.py:465
  23.4 24.5 %collective-permute-start.8 = (bf16[384,1024]{1,0:T(8,128)(2,1)S(1)}, bf16[384,1024]{1,0:T(8,128)(2,1)S(1)}, u32[]{:S(2)}, u32[]{:S(2)}) collective-permute-start(bf16[384,1024]{1,0:T(8,128)(2,1)S(1)} %collective-permute-done.7.refs_2_), channel_id=1, source_target_pairs={{0,4},{2,6},{4,0},{6,2},{8,12},{10,14},{12,8},{14,10},{16,20},{18,... | collective-permute-start | bytes 2359304 | tf_op jit(solution)/shard_map/ppermute | solution.py:462
  25.1 10.5 %collective-permute-start.11 = (bf16[384,512]{1,0:T(8,128)(2,1)S(1)}, bf16[384,512]{1,0:T(8,128)(2,1)S(1)}, u32[]{:S(2)}, u32[]{:S(2)}) collective-permute-start(bf16[384,512]{1,0:T(8,128)(2,1)S(1)} %get-tuple-element.34), channel_id=1, source_target_pairs={{0,1},{1,0},{2,3},{3,2},{4,5},{5,4},{6,7},{7,6},{8,9},{9,8},{10,11... | collective-permute-start | bytes 1179656 | tf_op jit(solution)/shard_map/ppermute | solution.py:468
  26.6 6.7 %collective-permute-start.3 = (bf16[384,128]{1,0:T(8,128)(2,1)S(1)}, bf16[384,128]{1,0:T(8,128)(2,1)S(1)}, u32[]{:S(2)}, u32[]{:S(2)}) collective-permute-start(bf16[384,128]{1,0:T(8,128)(2,1)S(1)} %shard_map.71), channel_id=1, source_target_pairs={{0,16},{2,18},{4,20},{6,22},{8,24},{10,26},{12,28},{14,30},{1,17},... | collective-permute-start | bytes 294920 | tf_op jit(solution)/shard_map/ppermute | solution.py:465
  35.1 10.3 %collective-permute-start.6 = (bf16[512,384]{1,0:T(8,128)(2,1)S(1)}, bf16[512,384]{1,0:T(8,128)(2,1)S(1)}, u32[]{:S(2)}, u32[]{:S(2)}) collective-permute-start(bf16[512,384]{1,0:T(8,128)(2,1)S(1)} %shard_map.74.refs_0_), channel_id=1, source_target_pairs={{0,1},{1,0},{2,3},{3,2},{4,5},{5,4},{6,7},{7,6},{8,9},{9,8},{10,11... | collective-permute-start | bytes 1179656 | tf_op jit(solution)/shard_map/ppermute | solution.py:468
  35.6 15.7 %collective-permute-start.15 = (bf16[384,512]{1,0:T(8,128)(2,1)S(1)}, bf16[384,512]{1,0:T(8,128)(2,1)S(1)}, u32[]{:S(2)}, u32[]{:S(2)}) collective-permute-start(bf16[384,512]{1,0:T(8,128)(2,1)S(1)} %collective-permute-done.11.refs_3_), channel_id=1, source_target_pairs={{0,2},{2,0},{4,6},{6,4},{8,10},{10,8},{12,14},{14,12},{16,18},{18,... | collective-permute-start | bytes 1179656 | tf_op jit(solution)/shard_map/ppermute | solution.py:462
  35.6 2.9 %collective-permute-start.4 = (bf16[384,128]{1,0:T(8,128)(2,1)S(1)}, bf16[384,128]{1,0:T(8,128)(2,1)S(1)}, u32[]{:S(2)}, u32[]{:S(2)}) collective-permute-start(bf16[384,128]{1,0:T(8,128)(2,1)S(1)} %get-tuple-element.49), channel_id=1, source_target_pairs={{0,2},{2,0},{4,6},{6,4},{8,10},{10,8},{12,14},{14,12},{16,18},{18,... | collective-permute-start | bytes 294920 | tf_op jit(solution)/shard_map/ppermute | solution.py:462
  36.1 11.7 %collective-permute-start.9 = (bf16[384,128]{1,0:T(8,128)(2,1)S(1)}, bf16[384,128]{1,0:T(8,128)(2,1)S(1)}, u32[]{:S(2)}, u32[]{:S(2)}) collective-permute-start(bf16[384,128]{1,0:T(8,128)(2,1)S(1)} %get-tuple-element.54), channel_id=1, source_target_pairs={{0,4},{2,6},{4,0},{6,2},{8,12},{10,14},{12,8},{14,10},{16,20},{18,... | collective-permute-start | bytes 294920 | tf_op jit(solution)/shard_map/ppermute | solution.py:462
  39.5 12.6 %collective-permute-start.5 = (bf16[512,384]{1,0:T(8,128)(2,1)S(1)}, bf16[512,384]{1,0:T(8,128)(2,1)S(1)}, u32[]{:S(2)}, u32[]{:S(2)}) collective-permute-start(bf16[512,384]{1,0:T(8,128)(2,1)S(1)} %shard_map.73.refs_1_), channel_id=1, source_target_pairs={{0,1},{1,0},{2,3},{3,2},{4,5},{5,4},{6,7},{7,6},{8,9},{9,8},{10,11... | collective-permute-start | bytes 1179656 | tf_op jit(solution)/shard_map/ppermute | solution.py:468
  45.4 10.3 %collective-permute-start.12 = (bf16[384,512]{1,0:T(8,128)(2,1)S(1)}, bf16[384,512]{1,0:T(8,128)(2,1)S(1)}, u32[]{:S(2)}, u32[]{:S(2)}) collective-permute-start(bf16[384,512]{1,0:T(8,128)(2,1)S(1)} %slice.30), channel_id=1, source_target_pairs={{0,8},{2,10},{4,12},{6,14},{8,0},{10,2},{12,4},{14,6},{16,24},{18,... | collective-permute-start | bytes 1179656 | tf_op jit(solution)/shard_map/ppermute | solution.py:462
  47.9 7.8 %collective-permute-start.18 = (bf16[384,512]{1,0:T(8,128)(2,1)S(1)}, bf16[384,512]{1,0:T(8,128)(2,1)S(1)}, u32[]{:S(2)}, u32[]{:S(2)}) collective-permute-start(bf16[384,512]{1,0:T(8,128)(2,1)S(1)} %collective-permute-done.11.refs_3_), channel_id=1, source_target_pairs={{0,4},{2,6},{4,0},{6,2},{8,12},{10,14},{12,8},{14,10},{16,20},{18,... | collective-permute-start | bytes 1179656 | tf_op jit(solution)/shard_map/ppermute | solution.py:462
  49.9 5.9 %collective-permute-start.13 = (bf16[384,512]{1,0:T(8,128)(2,1)S(1)}, bf16[384,512]{1,0:T(8,128)(2,1)S(1)}, u32[]{:S(2)}, u32[]{:S(2)}) collective-permute-start(bf16[384,512]{1,0:T(8,128)(2,1)S(1)} %get-tuple-element.64), channel_id=1, source_target_pairs={{0,2},{2,0},{4,6},{6,4},{8,10},{10,8},{12,14},{14,12},{16,18},{18,... | collective-permute-start | bytes 1179656 | tf_op jit(solution)/shard_map/ppermute | solution.py:462
  51.3 5.0 %collective-permute-start.14 = (bf16[384,512]{1,0:T(8,128)(2,1)S(1)}, bf16[384,512]{1,0:T(8,128)(2,1)S(1)}, u32[]{:S(2)}, u32[]{:S(2)}) collective-permute-start(bf16[384,512]{1,0:T(8,128)(2,1)S(1)} %get-tuple-element.63), channel_id=1, source_target_pairs={{0,2},{2,0},{4,6},{6,4},{8,10},{10,8},{12,14},{14,12},{16,18},{18,... | collective-permute-start | bytes 1179656 | tf_op jit(solution)/shard_map/ppermute | solution.py:462
  52.1 10.8 %collective-permute-start.19 = (bf16[384,512]{1,0:T(8,128)(2,1)S(1)}, bf16[384,512]{1,0:T(8,128)(2,1)S(1)}, u32[]{:S(2)}, u32[]{:S(2)}) collective-permute-start(bf16[384,512]{1,0:T(8,128)(2,1)S(1)} %slice.33), channel_id=1, source_target_pairs={{0,8},{2,10},{4,12},{6,14},{8,0},{10,2},{12,4},{14,6},{16,24},{18,... | collective-permute-start | bytes 1179656 | tf_op jit(solution)/shard_map/ppermute | solution.py:462
  55.6 16.5 %collective-permute-start.17 = (bf16[512,768]{1,0:T(8,128)(2,1)S(1)}, bf16[512,768]{1,0:T(8,128)(2,1)S(1)}, u32[]{:S(2)}, u32[]{:S(2)}) collective-permute-start(bf16[512,768]{1,0:T(8,128)(2,1)S(1)} %shard_map.77.refs_2_), channel_id=1, source_target_pairs={{0,1},{1,0},{2,3},{3,2},{4,5},{5,4},{6,7},{7,6},{8,9},{9,8},{10,11... | collective-permute-start | bytes 2359304 | tf_op jit(solution)/shard_map/ppermute | solution.py:468
  55.7 7.9 %collective-permute-start.16 = (bf16[384,512]{1,0:T(8,128)(2,1)S(1)}, bf16[384,512]{1,0:T(8,128)(2,1)S(1)}, u32[]{:S(2)}, u32[]{:S(2)}) collective-permute-start(bf16[384,512]{1,0:T(8,128)(2,1)S(1)} %collective-permute-done.12.refs_4_), channel_id=1, source_target_pairs={{0,2},{2,0},{4,6},{6,4},{8,10},{10,8},{12,14},{14,12},{16,18},{18,... | collective-permute-start | bytes 1179656 | tf_op jit(solution)/shard_map/ppermute | solution.py:462
  56.3 6.7 %collective-permute-start.23 = (bf16[384,256]{1,0:T(8,128)(2,1)S(1)}, bf16[384,256]{1,0:T(8,128)(2,1)S(1)}, u32[]{:S(2)}, u32[]{:S(2)}) collective-permute-start(bf16[384,256]{1,0:T(8,128)(2,1)S(1)} %get-tuple-element.67), channel_id=1, source_target_pairs={{0,2},{2,0},{4,6},{6,4},{8,10},{10,8},{12,14},{14,12},{16,18},{18,... | collective-permute-start | bytes 589832 | tf_op jit(solution)/shard_map/ppermute | solution.py:462
  57.7 13.5 %collective-permute-start.20 = (bf16[384,512]{1,0:T(8,128)(2,1)S(1)}, bf16[384,512]{1,0:T(8,128)(2,1)S(1)}, u32[]{:S(2)}, u32[]{:S(2)}) collective-permute-start(bf16[384,512]{1,0:T(8,128)(2,1)S(1)} %get-tuple-element.62), channel_id=1, source_target_pairs={{0,2},{2,0},{4,6},{6,4},{8,10},{10,8},{12,14},{14,12},{16,18},{18,... | collective-permute-start | bytes 1179656 | tf_op jit(solution)/shard_map/ppermute | solution.py:462
  62.9 8.3 %collective-permute-start.21 = (bf16[384,512]{1,0:T(8,128)(2,1)S(1)}, bf16[384,512]{1,0:T(8,128)(2,1)S(1)}, u32[]{:S(2)}, u32[]{:S(2)}) collective-permute-start(bf16[384,512]{1,0:T(8,128)(2,1)S(1)} %get-tuple-element.61), channel_id=1, source_target_pairs={{0,2},{2,0},{4,6},{6,4},{8,10},{10,8},{12,14},{14,12},{16,18},{18,... | collective-permute-start | bytes 1179656 | tf_op jit(solution)/shard_map/ppermute | solution.py:462
  63.0 8.3 %collective-permute-start.24 = (bf16[384,256]{1,0:T(8,128)(2,1)S(1)}, bf16[384,256]{1,0:T(8,128)(2,1)S(1)}, u32[]{:S(2)}, u32[]{:S(2)}) collective-permute-start(bf16[384,256]{1,0:T(8,128)(2,1)S(1)} %get-tuple-element.66), channel_id=1, source_target_pairs={{0,2},{2,0},{4,6},{6,4},{8,10},{10,8},{12,14},{14,12},{16,18},{18,... | collective-permute-start | bytes 589832 | tf_op jit(solution)/shard_map/ppermute | solution.py:462
  63.6 7.8 %collective-permute-start.25 = (bf16[384,256]{1,0:T(8,128)(2,1)S(1)}, bf16[384,256]{1,0:T(8,128)(2,1)S(1)}, u32[]{:S(2)}, u32[]{:S(2)}) collective-permute-start(bf16[384,256]{1,0:T(8,128)(2,1)S(1)} %get-tuple-element.65), channel_id=1, source_target_pairs={{0,2},{2,0},{4,6},{6,4},{8,10},{10,8},{12,14},{14,12},{16,18},{18,... | collective-permute-start | bytes 589832 | tf_op jit(solution)/shard_map/ppermute | solution.py:462
  (9 other events, 91.2 us)

commit v12 on v11

--- a/solution.py
+++ b/solution.py
@@ -147,29 +147,24 @@
 
 def slice_weights(meta, weight, columns):
     part, half = weight.shape[0] // 4, columns // 2
-    shapes = [jax.ShapeDtypeStruct((part, half), BF16), jax.ShapeDtypeStruct((part, half // 2), BF16)]
-
-    def kernel(meta_ref, w_ref, a_ref, b_ref, sems):
+    shapes = [jax.ShapeDtypeStruct((part, half), BF16)]
+
+    def kernel(meta_ref, w_ref, o_ref, sem):
         rows = pl.ds(pl.multiple_of(meta_ref[1] * part, DH), part)
-        base = (1 - meta_ref[2]) * columns
-        starts = (base + meta_ref[3] * half, base + (1 - meta_ref[3]) * half)
-        copies = []
-        for n, (o_ref, start) in enumerate(zip((a_ref, b_ref), starts)):
-            cols = pl.ds(pl.multiple_of(start, DH), shapes[n].shape[1])
-            copies.append(pltpu.make_async_copy(w_ref.at[rows, cols], o_ref, sems.at[n]))
-            copies[-1].start()
-        for copy in copies:
-            copy.wait()
+        start = (1 - meta_ref[2]) * columns + meta_ref[3] * half
+        copy = pltpu.make_async_copy(w_ref.at[rows, pl.ds(pl.multiple_of(start, DH), half)], o_ref, sem)
+        copy.start()
+        copy.wait()
 
     return call(
         kernel,
         (1,),
         [pl.BlockSpec(memory_space=pl.ANY)],
-        [pl.BlockSpec(memory_space=pl.ANY)] * 2,
+        [pl.BlockSpec(memory_space=pltpu.VMEM)] * len(shapes),
         shapes,
         6 * 10**9,
         1024,
-        [pltpu.SemaphoreType.DMA((2,))],
+        [pltpu.SemaphoreType.DMA],
         50 * 1024 * 1024,
     )(meta, weight)
 
@@ -473,7 +468,6 @@
     quarter = half // 2
     sent = slice_weights(meta, weight, columns)
     w0 = [flip(sent[0])]
-    w0.append(flip(sent[1]))
     send, keep = split_states(after(meta, *sent), key, value, docs)
     core_got = swap(send, 1)
     query = behind(query, send)
@@ -506,10 +500,10 @@
     normed2 = norm((2, 3), [within2, within3], [carry2, carry3])
     far2 = flip(normed2)
 
-    total = project_own(after(meta, far1), [normed0, normed1, normed2], weight, columns)
-    w0.append(swap(behind(w0[0], normed1)[:, quarter:], plane))
-    w2.append(swap(behind(w0[1], far0), 2))
-    w2.append(swap(behind(w2[0], carry2)[:, quarter:], plane))
+    total = project_own(after(meta, far0), [normed0, normed1, normed2], weight, columns)
+    w0.append(swap(behind(w0[0], normed0), plane))
+    w2.append(swap(behind(w0[1], normed2)[:, :quarter], 2))
+    w2.append(swap(behind(w2[0], normed2)[:, quarter:], plane))
 
     def cut(w, width):
         return [w[:, at : at + width] for at in range(0, w.shape[1], width)]

time: 75.6 us -> 74.6 us (0.987)
  starting transfers between devices: 26.3 us -> 24.8 us
    ppermute x19, waiting for transfers between devices: 10.5 us -> 15.2 us  [swap(): return lax.ppermute(x, 'seq', [(i, i ^ bit) for i in range(n_seq)])]
    ppermute x5 -> x4, waiting for transfers between devices: 6.47 us -> 2.19 us  [flip(): return lax.ppermute(x, 'head', [(0, 1), (1, 0)])]
    ppermute x5 -> x4, starting transfers between devices: 6.71 us -> 5.76 us  [flip(): return lax.ppermute(x, 'head', [(0, 1), (1, 0)])]
  transfers between devices with their start and end apart: 26 -> 25, of which waited for: 11 -> 14; matrix products, arithmetic and copies ran while one was open for 0% -> 0% of each run, Pallas kernels for 31% -> 31%
where the time goes in v12:
time: 74.6 us; the launch traced here: 74.3 us
  Pallas kernels  28.2 us (38%)
  starting transfers between devices  24.8 us (33%)
  waiting for transfers between devices  19.8 us (27%)
  local copies, waits for them, and re-layouts  1.04 us (1%)
    pallas_call x13, Pallas kernels, local(): call(kernel, (1,), specs or [whole(a.shape) for a in arrays], [whole(s.sh...  15.5 us
    ppermute x19, waiting for transfers between devices, swap(): return lax.ppermute(x, 'seq', [(i, i ^ bit) for i in range(n_seq)])  15.2 us
    ppermute x19, starting transfers between devices, swap(): return lax.ppermute(x, 'seq', [(i, i ^ bit) for i in range(n_seq)])  10.9 us
    ppermute x2, starting transfers between devices, shift(): lax.ppermute(x, 'seq', [(i, i + count) for i in range(n_seq - count)])  8.15 us
    pallas_call x2, Pallas kernels, project_more(): call(kernel, (1,), [vmem] * (1 + count + len(flat)), pl.BlockSpec(memory_...  5.76 us
    ppermute x4, starting transfers between devices, flip(): return lax.ppermute(x, 'head', [(0, 1), (1, 0)])  5.76 us
    pallas_call x1, Pallas kernels, project_own(): call(kernel, (OWN_TILES,), [whole(p.shape) for p in pieces] + [pl.BlockSp...  4.97 us
    ppermute x2, waiting for transfers between devices, shift(): lax.ppermute(x, 'seq', [(i, i + count) for i in range(n_seq - count)])  2.37 us
  transfers between devices with their start and end apart: 25, of which 14 were waited for; matrix products, arithmetic and copies ran while one was open for 0% of the time, Pallas kernels for 31%

profile of v12, /device:TPU:0, one launch (start us, length us, event | category | flops | bytes accessed | tf_op | source)
XLA Modules:
  0.0 74.3 jit_solution(3282266724831055916)
XLA Ops:
  0.7 2.0 %shard_map.64 = bf16[384,1024]{1,0:T(8,128)(2,1)S(1)} custom-call(s32[24]{0:T(128)S(1)} %concatenate.3.meta_ref, bf16[1536,4096]{1,0:T(8,128)(2,1)} %refs_6_.3), custom_call_target="tpu_custom_call" | custom-call | flops 6000000000 | bytes 1024 | tf_op jit(solution)/shard_map/pallas_call | solution.py:159
  2.7 3.0 %collective-permute-start.6 = (bf16[384,1024]{1,0:T(8,128)(2,1)S(1)}, bf16[384,1024]{1,0:T(8,128)(2,1)S(1)}, u32[]{:S(2)}, u32[]{:S(2)}) collective-permute-start(bf16[384,1024]{1,0:T(8,128)(2,1)S(1)} %shard_map.64), channel_id=1, source_target_pairs={{0,1},{1,0},{2,3},{3,2},{4,5},{5,4},{6,7},{7,6},{8,9},{9,8},{10,11... | collective-permute-start | bytes 2359304 | tf_op jit(solution)/shard_map/ppermute | solution.py:463
  5.8 1.7 %shard_map.65 = (bf16[2,384,128]{2,1,0:T(8,128)(2,1)S(1)}, bf16[2,384,128]{2,1,0:T(8,128)(2,1)S(1)}) custom-call(s32[24]{0:T(128)S(1)} %concatenate.3.meta_ref, bf16[512,1536]{1,0:T(8,128)(2,1)S(1)} %copy-done, bf16[512,1536]{1,0:T(8,128)(2,1)S(1)} %copy-done, bf16[512,1536]{1,0:T(8,128)(2,1)S(1)} %copy-done, bf16[512,1536]{1,0:T(8,128)(2,1)S(1)} %copy-done, ...), custom_call_target="tpu_custom_call" | custom-call | flops 2000000000 | bytes 1024 | tf_op jit(solution)/shard_map/pallas_call | solution.py:123
  7.5 1.9 %shard_map.66 = (f32[512,384]{1,0:T(8,128)S(1)}, bf16[512,512]{1,0:T(8,128)(2,1)S(1)}) custom-call(s32[24]{0:T(128)S(1)} %concatenate.3.meta_ref, bf16[512,1536]{1,0:T(8,128)(2,1)S(1)} %copy-done.2, bf16[512,1536]{1,0:T(8,128)(2,1)S(1)} %copy-done, bf16[512,1536]{1,0:T(8,128)(2,1)S(1)} %copy-done.1), custom_call_target="tpu_custom_call" | custom-call | flops 2000000000 | bytes 1024 | tf_op jit(solution)/shard_map/pallas_call | solution.py:123
  10.1 1.6 %collective-permute-start.1 = (bf16[384,128]{1,0:T(8,128)(2,1)S(1)}, bf16[384,128]{1,0:T(8,128)(2,1)S(1)}, u32[]{:S(2)}, u32[]{:S(2)}) collective-permute-start(bf16[384,128]{1,0:T(8,128)(2,1)S(1)} %get-tuple-element.42), channel_id=1, source_target_pairs={{0,4},{2,6},{4,0},{6,2},{8,12},{10,14},{12,8},{14,10},{16,20},{18,... | collective-permute-start | bytes 294920 | tf_op jit(solution)/shard_map/ppermute | solution.py:457
  11.7 1.8 %shard_map.68.refs_1_ = f32[512,384]{1,0:T(8,128)S(1)} custom-call(s32[24]{0:T(128)S(1)} %concatenate.3.meta_ref, bf16[512,1536]{1,0:T(8,128)(2,1)S(1)} %copy-done.2, bf16[512,1536]{1,0:T(8,128)(2,1)S(1)} %copy-done, bf16[512,1536]{1,0:T(8,128)(2,1)S(1)} %copy-done.1, bf16[512,512]{1,0:T(8,128)(2,1)S(1)} %get-tuple-element.40.rest_0_), custom_call_target="tpu_custom_call" | custom-call | flops 2000000000 | bytes 1024 | tf_op jit(solution)/shard_map/pallas_call | solution.py:123
  13.5 1.9 %collective-permute-done.1.b_ref = bf16[384,128]{1,0:T(8,128)(2,1)S(1)} collective-permute-done((bf16[384,128]{1,0:T(8,128)(2,1)S(1)}, bf16[384,128]{1,0:T(8,128)(2,1)S(1)}, u32[]{:S(2)}, u32[]{:S(2)}) %collective-permute-start.1) | collective-permute-done | bytes 98336 | tf_op jit(solution)/shard_map/ppermute | solution.py:457
  16.0 3.5 %collective-permute-start.2 = (bf16[384,128]{1,0:T(8,128)(2,1)S(1)}, bf16[384,128]{1,0:T(8,128)(2,1)S(1)}, u32[]{:S(2)}, u32[]{:S(2)}) collective-permute-start(bf16[384,128]{1,0:T(8,128)(2,1)S(1)} %shard_map.69.a_ref), channel_id=1, source_target_pairs={{0,8},{2,10},{4,12},{6,14},{8,16},{10,18},{12,20},{14,22},{16,24},... | collective-permute-start | bytes 294920 | tf_op jit(solution)/shard_map/ppermute | solution.py:460
  19.5 1.8 %shard_map.70.refs_1_ = f32[512,384]{1,0:T(8,128)S(1)} custom-call(s32[24]{0:T(128)S(1)} %concatenate.3.meta_ref, bf16[512,1536]{1,0:T(8,128)(2,1)S(1)} %copy-done.2, bf16[512,1536]{1,0:T(8,128)(2,1)S(1)} %copy-done, bf16[512,1536]{1,0:T(8,128)(2,1)S(1)} %copy-done.1, bf16[512,512]{1,0:T(8,128)(2,1)S(1)} %get-tuple-element.40.rest_0_), custom_call_target="tpu_custom_call" | custom-call | flops 2000000000 | bytes 1024 | tf_op jit(solution)/shard_map/pallas_call | solution.py:123
  22.3 1.0 %collective-permute-done.6.refs_2_ = bf16[384,1024]{1,0:T(8,128)(2,1)S(1)} collective-permute-done((bf16[384,1024]{1,0:T(8,128)(2,1)S(1)}, bf16[384,1024]{1,0:T(8,128)(2,1)S(1)}, u32[]{:S(2)}, u32[]{:S(2)}) %collective-permute-start.6) | collective-permute-done | bytes 786464 | tf_op jit(solution)/shard_map/ppermute | solution.py:463
  23.3 1.7 %collective-permute-start.7 = (bf16[384,1024]{1,0:T(8,128)(2,1)S(1)}, bf16[384,1024]{1,0:T(8,128)(2,1)S(1)}, u32[]{:S(2)}, u32[]{:S(2)}) collective-permute-start(bf16[384,1024]{1,0:T(8,128)(2,1)S(1)} %collective-permute-done.6.refs_2_), channel_id=1, source_target_pairs={{0,4},{2,6},{4,0},{6,2},{8,12},{10,14},{12,8},{14,10},{16,20},{18,... | collective-permute-start | bytes 2359304 | tf_op jit(solution)/shard_map/ppermute | solution.py:457
  25.0 4.7 %collective-permute-start.3 = (bf16[384,128]{1,0:T(8,128)(2,1)S(1)}, bf16[384,128]{1,0:T(8,128)(2,1)S(1)}, u32[]{:S(2)}, u32[]{:S(2)}) collective-permute-start(bf16[384,128]{1,0:T(8,128)(2,1)S(1)} %shard_map.71), channel_id=1, source_target_pairs={{0,16},{2,18},{4,20},{6,22},{8,24},{10,26},{12,28},{14,30},{1,17},... | collective-permute-start | bytes 294920 | tf_op jit(solution)/shard_map/ppermute | solution.py:460
  29.7 2.0 %collective-permute-done.3.far_ref = bf16[384,128]{1,0:T(8,128)(2,1)S(1)} collective-permute-done((bf16[384,128]{1,0:T(8,128)(2,1)S(1)}, bf16[384,128]{1,0:T(8,128)(2,1)S(1)}, u32[]{:S(2)}, u32[]{:S(2)}) %collective-permute-start.3) | collective-permute-done | bytes 98336 | tf_op jit(solution)/shard_map/ppermute | solution.py:460
  33.4 1.6 %collective-permute-start.4 = (bf16[512,384]{1,0:T(8,128)(2,1)S(1)}, bf16[512,384]{1,0:T(8,128)(2,1)S(1)}, u32[]{:S(2)}, u32[]{:S(2)}) collective-permute-start(bf16[512,384]{1,0:T(8,128)(2,1)S(1)} %shard_map.73.refs_0_), channel_id=1, source_target_pairs={{0,1},{1,0},{2,3},{3,2},{4,5},{5,4},{6,7},{7,6},{8,9},{9,8},{10,11... | collective-permute-start | bytes 1179656 | tf_op jit(solution)/shard_map/ppermute | solution.py:463
  35.0 2.4 %collective-permute-start.11 = (bf16[384,1024]{1,0:T(8,128)(2,1)S(1)}, bf16[384,1024]{1,0:T(8,128)(2,1)S(1)}, u32[]{:S(2)}, u32[]{:S(2)}) collective-permute-start(bf16[384,1024]{1,0:T(8,128)(2,1)S(1)} %collective-permute-done.6.refs_2_), channel_id=1, source_target_pairs={{0,8},{2,10},{4,12},{6,14},{8,0},{10,2},{12,4},{14,6},{16,24},{18,... | collective-permute-start | bytes 2359304 | tf_op jit(solution)/shard_map/ppermute | solution.py:457
  38.0 1.8 %shard_map.76.refs_5_ = f32[512,384]{1,0:T(8,128)S(1)} custom-call(s32[24]{0:T(128)S(1)} %concatenate.3.meta_ref, bf16[512,1536]{1,0:T(8,128)(2,1)S(1)} %copy-done.2, bf16[512,1536]{1,0:T(8,128)(2,1)S(1)} %copy-done, bf16[512,1536]{1,0:T(8,128)(2,1)S(1)} %copy-done.1, bf16[512,512]{1,0:T(8,128)(2,1)S(1)} %get-tuple-element.40.rest_0_), custom_call_target="tpu_custom_call" | custom-call | flops 2000000000 | bytes 1024 | tf_op jit(solution)/shard_map/pallas_call | solution.py:123
  43.1 1.1 %collective-permute-done.8.chip_ref = bf16[384,128]{1,0:T(8,128)(2,1)S(1)} collective-permute-done((bf16[384,128]{1,0:T(8,128)(2,1)S(1)}, bf16[384,128]{1,0:T(8,128)(2,1)S(1)}, u32[]{:S(2)}, u32[]{:S(2)}) %collective-permute-start.8) | collective-permute-done | bytes 98336 | tf_op jit(solution)/shard_map/ppermute | solution.py:457
  46.1 1.3 %shard_map.77.refs_2_ = bf16[512,768]{1,0:T(8,128)(2,1)S(1)} custom-call(s32[24]{0:T(128)S(1)} %concatenate.3.meta_ref, bf16[512,1536]{1,0:T(8,128)(2,1)S(1)} %copy-done.2, f32[512,384]{1,0:T(8,128)S(1)} %shard_map.70.refs_1_, bf16[384,128]{1,0:T(8,128)(2,1)S(1)} %get-tuple-element.51.refs_2_, f32[1,1536]{1,0:T(1,128)S(1)} %reshape.2.refs_3_.refs_7_, ...), custom_call_target="tpu_custom_call" | custom-call | flops 2000000000 | bytes 1024 | tf_op jit(solution)/shard_map/pallas_call | solution.py:123
  47.5 5.3 %collective-permute-done.11.refs_3_ = bf16[384,1024]{1,0:T(8,128)(2,1)S(1)} collective-permute-done((bf16[384,1024]{1,0:T(8,128)(2,1)S(1)}, bf16[384,1024]{1,0:T(8,128)(2,1)S(1)}, u32[]{:S(2)}, u32[]{:S(2)}) %collective-permute-start.11) | collective-permute-done | bytes 786464 | tf_op jit(solution)/shard_map/ppermute | solution.py:457
  53.4 1.8 %collective-permute-start.18 = (bf16[384,512]{1,0:T(8,128)(2,1)S(1)}, bf16[384,512]{1,0:T(8,128)(2,1)S(1)}, u32[]{:S(2)}, u32[]{:S(2)}) collective-permute-start(bf16[384,512]{1,0:T(8,128)(2,1)S(1)} %slice.41), channel_id=1, source_target_pairs={{0,8},{2,10},{4,12},{6,14},{8,0},{10,2},{12,4},{14,6},{16,24},{18,... | collective-permute-start | bytes 1179656 | tf_op jit(solution)/shard_map/ppermute | solution.py:457
  56.5 4.3 %collective-permute-done.17.refs_2_ = bf16[384,512]{1,0:T(8,128)(2,1)S(1)} collective-permute-done((bf16[384,512]{1,0:T(8,128)(2,1)S(1)}, bf16[384,512]{1,0:T(8,128)(2,1)S(1)}, u32[]{:S(2)}, u32[]{:S(2)}) %collective-permute-start.17) | collective-permute-done | bytes 393248 | tf_op jit(solution)/shard_map/ppermute | solution.py:457
  63.2 5.0 %shard_map.78.t_ref = f32[512,2048]{1,0:T(8,128)S(1)} custom-call(s32[24]{0:T(128)S(1)} %concatenate.3.meta_ref, bf16[512,384]{1,0:T(8,128)(2,1)S(1)} %shard_map.73.refs_0_, bf16[512,384]{1,0:T(8,128)(2,1)S(1)} %shard_map.74.refs_1_, bf16[512,768]{1,0:T(8,128)(2,1)S(1)} %shard_map.77.refs_2_, bf16[1536,4096]{1,0:T(8,128)(2,1)S(1)} %bitcast.5, ...), custom_call_target="tpu_custom_call" | custom-call | flops 1000000 | bytes 1024 | tf_op jit(solution)/shard_map/pallas_call | solution.py:374
  68.2 2.6 %shard_map.79.t_ref = f32[512,2048]{1,0:T(8,128)S(1)} custom-call(s32[24]{0:T(128)S(1)} %concatenate.3.meta_ref, f32[512,2048]{1,0:T(8,128)S(1)} %shard_map.78.t_ref, bf16[512,384]{1,0:T(8,128)(2,1)S(1)} %collective-permute-done.4.refs_0_, bf16[512,384]{1,0:T(8,128)(2,1)S(1)} %collective-permute-done.10.refs_1_, ...), custom_call_target="tpu_custom_call", output_to_operand_aliasing={{}: (1, {})} | custom-call | flops 1000000 | bytes 1024 | tf_op jit(solution)/shard_map/pallas_call | solution.py:429
  71.0 3.2 %shard_map.80 = bf16[512,2048]{1,0:T(8,128)(2,1)} custom-call(s32[24]{0:T(128)S(1)} %concatenate.3.meta_ref, f32[512,2048]{1,0:T(8,128)S(1)} %shard_map.79.t_ref, bf16[512,768]{1,0:T(8,128)(2,1)S(1)} %collective-permute-done.16.refs_0_, bf16[384,1024]{1,0:T(8,128)(2,1)S(1)} %collective-permute-done.7.refs_1_, ...), custom_call_target="tpu_custom_call" | custom-call | flops 1000000 | bytes 1024 | tf_op jit(solution)/shard_map/pallas_call | solution.py:429
  (68 shorter events, 15.1 us)
Async XLA Ops:
  2.7 20.6 %collective-permute-start.6 = (bf16[384,1024]{1,0:T(8,128)(2,1)S(1)}, bf16[384,1024]{1,0:T(8,128)(2,1)S(1)}, u32[]{:S(2)}, u32[]{:S(2)}) collective-permute-start(bf16[384,1024]{1,0:T(8,128)(2,1)S(1)} %shard_map.64), channel_id=1, source_target_pairs={{0,1},{1,0},{2,3},{3,2},{4,5},{5,4},{6,7},{7,6},{8,9},{9,8},{10,11... | collective-permute-start | bytes 2359304 | tf_op jit(solution)/shard_map/ppermute | solution.py:463
  7.4 2.0 %collective-permute-start = (bf16[2,384,128]{2,1,0:T(8,128)(2,1)S(1)}, bf16[2,384,128]{2,1,0:T(8,128)(2,1)S(1)}, u32[]{:S(2)}, u32[]{:S(2)}) collective-permute-start(bf16[2,384,128]{2,1,0:T(8,128)(2,1)S(1)} %get-tuple-element.32), channel_id=1, source_target_pairs={{0,2},{2,0},{4,6},{6,4},{8,10},{10,8},{12,14},{14,12},{16,18},{18,... | collective-permute-start | bytes 589832 | tf_op jit(solution)/shard_map/ppermute | solution.py:457
  10.1 5.3 %collective-permute-start.1 = (bf16[384,128]{1,0:T(8,128)(2,1)S(1)}, bf16[384,128]{1,0:T(8,128)(2,1)S(1)}, u32[]{:S(2)}, u32[]{:S(2)}) collective-permute-start(bf16[384,128]{1,0:T(8,128)(2,1)S(1)} %get-tuple-element.42), channel_id=1, source_target_pairs={{0,4},{2,6},{4,0},{6,2},{8,12},{10,14},{12,8},{14,10},{16,20},{18,... | collective-permute-start | bytes 294920 | tf_op jit(solution)/shard_map/ppermute | solution.py:457
  16.0 5.7 %collective-permute-start.2 = (bf16[384,128]{1,0:T(8,128)(2,1)S(1)}, bf16[384,128]{1,0:T(8,128)(2,1)S(1)}, u32[]{:S(2)}, u32[]{:S(2)}) collective-permute-start(bf16[384,128]{1,0:T(8,128)(2,1)S(1)} %shard_map.69.a_ref), channel_id=1, source_target_pairs={{0,8},{2,10},{4,12},{6,14},{8,16},{10,18},{12,20},{14,22},{16,24},... | collective-permute-start | bytes 294920 | tf_op jit(solution)/shard_map/ppermute | solution.py:460
  23.3 19.8 %collective-permute-start.7 = (bf16[384,1024]{1,0:T(8,128)(2,1)S(1)}, bf16[384,1024]{1,0:T(8,128)(2,1)S(1)}, u32[]{:S(2)}, u32[]{:S(2)}) collective-permute-start(bf16[384,1024]{1,0:T(8,128)(2,1)S(1)} %collective-permute-done.6.refs_2_), channel_id=1, source_target_pairs={{0,4},{2,6},{4,0},{6,2},{8,12},{10,14},{12,8},{14,10},{16,20},{18,... | collective-permute-start | bytes 2359304 | tf_op jit(solution)/shard_map/ppermute | solution.py:457
  25.0 6.7 %collective-permute-start.3 = (bf16[384,128]{1,0:T(8,128)(2,1)S(1)}, bf16[384,128]{1,0:T(8,128)(2,1)S(1)}, u32[]{:S(2)}, u32[]{:S(2)}) collective-permute-start(bf16[384,128]{1,0:T(8,128)(2,1)S(1)} %shard_map.71), channel_id=1, source_target_pairs={{0,16},{2,18},{4,20},{6,22},{8,24},{10,26},{12,28},{14,30},{1,17},... | collective-permute-start | bytes 294920 | tf_op jit(solution)/shard_map/ppermute | solution.py:460
  33.4 8.9 %collective-permute-start.4 = (bf16[512,384]{1,0:T(8,128)(2,1)S(1)}, bf16[512,384]{1,0:T(8,128)(2,1)S(1)}, u32[]{:S(2)}, u32[]{:S(2)}) collective-permute-start(bf16[512,384]{1,0:T(8,128)(2,1)S(1)} %shard_map.73.refs_0_), channel_id=1, source_target_pairs={{0,1},{1,0},{2,3},{3,2},{4,5},{5,4},{6,7},{7,6},{8,9},{9,8},{10,11... | collective-permute-start | bytes 1179656 | tf_op jit(solution)/shard_map/ppermute | solution.py:463
  35.0 17.7 %collective-permute-start.11 = (bf16[384,1024]{1,0:T(8,128)(2,1)S(1)}, bf16[384,1024]{1,0:T(8,128)(2,1)S(1)}, u32[]{:S(2)}, u32[]{:S(2)}) collective-permute-start(bf16[384,1024]{1,0:T(8,128)(2,1)S(1)} %collective-permute-done.6.refs_2_), channel_id=1, source_target_pairs={{0,8},{2,10},{4,12},{6,14},{8,0},{10,2},{12,4},{14,6},{16,24},{18,... | collective-permute-start | bytes 2359304 | tf_op jit(solution)/shard_map/ppermute | solution.py:457
  37.5 2.4 %collective-permute-start.5 = (bf16[384,128]{1,0:T(8,128)(2,1)S(1)}, bf16[384,128]{1,0:T(8,128)(2,1)S(1)}, u32[]{:S(2)}, u32[]{:S(2)}) collective-permute-start(bf16[384,128]{1,0:T(8,128)(2,1)S(1)} %get-tuple-element.47), channel_id=1, source_target_pairs={{0,2},{2,0},{4,6},{6,4},{8,10},{10,8},{12,14},{14,12},{16,18},{18,... | collective-permute-start | bytes 294920 | tf_op jit(solution)/shard_map/ppermute | solution.py:457
  37.5 6.7 %collective-permute-start.8 = (bf16[384,128]{1,0:T(8,128)(2,1)S(1)}, bf16[384,128]{1,0:T(8,128)(2,1)S(1)}, u32[]{:S(2)}, u32[]{:S(2)}) collective-permute-start(bf16[384,128]{1,0:T(8,128)(2,1)S(1)} %get-tuple-element.50), channel_id=1, source_target_pairs={{0,4},{2,6},{4,0},{6,2},{8,12},{10,14},{12,8},{14,10},{16,20},{18,... | collective-permute-start | bytes 294920 | tf_op jit(solution)/shard_map/ppermute | solution.py:457
  40.9 14.4 %collective-permute-start.10 = (bf16[512,384]{1,0:T(8,128)(2,1)S(1)}, bf16[512,384]{1,0:T(8,128)(2,1)S(1)}, u32[]{:S(2)}, u32[]{:S(2)}) collective-permute-start(bf16[512,384]{1,0:T(8,128)(2,1)S(1)} %shard_map.74.refs_1_), channel_id=1, source_target_pairs={{0,1},{1,0},{2,3},{3,2},{4,5},{5,4},{6,7},{7,6},{8,9},{9,8},{10,11... | collective-permute-start | bytes 1179656 | tf_op jit(solution)/shard_map/ppermute | solution.py:463
  44.9 11.0 %collective-permute-start.12 = (bf16[384,512]{1,0:T(8,128)(2,1)S(1)}, bf16[384,512]{1,0:T(8,128)(2,1)S(1)}, u32[]{:S(2)}, u32[]{:S(2)}) collective-permute-start(bf16[384,512]{1,0:T(8,128)(2,1)S(1)} %get-tuple-element.62), channel_id=1, source_target_pairs={{0,2},{2,0},{4,6},{6,4},{8,10},{10,8},{12,14},{14,12},{16,18},{18,... | collective-permute-start | bytes 1179656 | tf_op jit(solution)/shard_map/ppermute | solution.py:457
  45.5 10.5 %collective-permute-start.13 = (bf16[384,512]{1,0:T(8,128)(2,1)S(1)}, bf16[384,512]{1,0:T(8,128)(2,1)S(1)}, u32[]{:S(2)}, u32[]{:S(2)}) collective-permute-start(bf16[384,512]{1,0:T(8,128)(2,1)S(1)} %get-tuple-element.61), channel_id=1, source_target_pairs={{0,2},{2,0},{4,6},{6,4},{8,10},{10,8},{12,14},{14,12},{16,18},{18,... | collective-permute-start | bytes 1179656 | tf_op jit(solution)/shard_map/ppermute | solution.py:457
  52.8 8.0 %collective-permute-start.17 = (bf16[384,512]{1,0:T(8,128)(2,1)S(1)}, bf16[384,512]{1,0:T(8,128)(2,1)S(1)}, u32[]{:S(2)}, u32[]{:S(2)}) collective-permute-start(bf16[384,512]{1,0:T(8,128)(2,1)S(1)} %slice.40), channel_id=1, source_target_pairs={{0,4},{2,6},{4,0},{6,2},{8,12},{10,14},{12,8},{14,10},{16,20},{18,... | collective-permute-start | bytes 1179656 | tf_op jit(solution)/shard_map/ppermute | solution.py:457
  53.4 7.8 %collective-permute-start.18 = (bf16[384,512]{1,0:T(8,128)(2,1)S(1)}, bf16[384,512]{1,0:T(8,128)(2,1)S(1)}, u32[]{:S(2)}, u32[]{:S(2)}) collective-permute-start(bf16[384,512]{1,0:T(8,128)(2,1)S(1)} %slice.41), channel_id=1, source_target_pairs={{0,8},{2,10},{4,12},{6,14},{8,0},{10,2},{12,4},{14,6},{16,24},{18,... | collective-permute-start | bytes 1179656 | tf_op jit(solution)/shard_map/ppermute | solution.py:457
  55.3 15.8 %collective-permute-start.16 = (bf16[512,768]{1,0:T(8,128)(2,1)S(1)}, bf16[512,768]{1,0:T(8,128)(2,1)S(1)}, u32[]{:S(2)}, u32[]{:S(2)}) collective-permute-start(bf16[512,768]{1,0:T(8,128)(2,1)S(1)} %shard_map.77.refs_2_), channel_id=1, source_target_pairs={{0,1},{1,0},{2,3},{3,2},{4,5},{5,4},{6,7},{7,6},{8,9},{9,8},{10,11... | collective-permute-start | bytes 2359304 | tf_op jit(solution)/shard_map/ppermute | solution.py:463
  55.9 5.4 %collective-permute-start.14 = (bf16[384,512]{1,0:T(8,128)(2,1)S(1)}, bf16[384,512]{1,0:T(8,128)(2,1)S(1)}, u32[]{:S(2)}, u32[]{:S(2)}) collective-permute-start(bf16[384,512]{1,0:T(8,128)(2,1)S(1)} %get-tuple-element.60), channel_id=1, source_target_pairs={{0,2},{2,0},{4,6},{6,4},{8,10},{10,8},{12,14},{14,12},{16,18},{18,... | collective-permute-start | bytes 1179656 | tf_op jit(solution)/shard_map/ppermute | solution.py:457
  56.0 5.9 %collective-permute-start.15 = (bf16[384,512]{1,0:T(8,128)(2,1)S(1)}, bf16[384,512]{1,0:T(8,128)(2,1)S(1)}, u32[]{:S(2)}, u32[]{:S(2)}) collective-permute-start(bf16[384,512]{1,0:T(8,128)(2,1)S(1)} %get-tuple-element.59), channel_id=1, source_target_pairs={{0,2},{2,0},{4,6},{6,4},{8,10},{10,8},{12,14},{14,12},{16,18},{18,... | collective-permute-start | bytes 1179656 | tf_op jit(solution)/shard_map/ppermute | solution.py:457
  60.7 1.7 %collective-permute-start.19 = (bf16[384,512]{1,0:T(8,128)(2,1)S(1)}, bf16[384,512]{1,0:T(8,128)(2,1)S(1)}, u32[]{:S(2)}, u32[]{:S(2)}) collective-permute-start(bf16[384,512]{1,0:T(8,128)(2,1)S(1)} %get-tuple-element.58), channel_id=1, source_target_pairs={{0,2},{2,0},{4,6},{6,4},{8,10},{10,8},{12,14},{14,12},{16,18},{18,... | collective-permute-start | bytes 1179656 | tf_op jit(solution)/shard_map/ppermute | solution.py:457
  61.2 1.8 %collective-permute-start.20 = (bf16[384,512]{1,0:T(8,128)(2,1)S(1)}, bf16[384,512]{1,0:T(8,128)(2,1)S(1)}, u32[]{:S(2)}, u32[]{:S(2)}) collective-permute-start(bf16[384,512]{1,0:T(8,128)(2,1)S(1)} %get-tuple-element.57), channel_id=1, source_target_pairs={{0,2},{2,0},{4,6},{6,4},{8,10},{10,8},{12,14},{14,12},{16,18},{18,... | collective-permute-start | bytes 1179656 | tf_op jit(solution)/shard_map/ppermute | solution.py:457
  61.3 9.4 %collective-permute-start.21 = (bf16[384,256]{1,0:T(8,128)(2,1)S(1)}, bf16[384,256]{1,0:T(8,128)(2,1)S(1)}, u32[]{:S(2)}, u32[]{:S(2)}) collective-permute-start(bf16[384,256]{1,0:T(8,128)(2,1)S(1)} %get-tuple-element.66), channel_id=1, source_target_pairs={{0,2},{2,0},{4,6},{6,4},{8,10},{10,8},{12,14},{14,12},{16,18},{18,... | collective-permute-start | bytes 589832 | tf_op jit(solution)/shard_map/ppermute | solution.py:457
  61.9 8.9 %collective-permute-start.22 = (bf16[384,256]{1,0:T(8,128)(2,1)S(1)}, bf16[384,256]{1,0:T(8,128)(2,1)S(1)}, u32[]{:S(2)}, u32[]{:S(2)}) collective-permute-start(bf16[384,256]{1,0:T(8,128)(2,1)S(1)} %get-tuple-element.65), channel_id=1, source_target_pairs={{0,2},{2,0},{4,6},{6,4},{8,10},{10,8},{12,14},{14,12},{16,18},{18,... | collective-permute-start | bytes 589832 | tf_op jit(solution)/shard_map/ppermute | solution.py:457
  62.5 8.3 %collective-permute-start.23 = (bf16[384,256]{1,0:T(8,128)(2,1)S(1)}, bf16[384,256]{1,0:T(8,128)(2,1)S(1)}, u32[]{:S(2)}, u32[]{:S(2)}) collective-permute-start(bf16[384,256]{1,0:T(8,128)(2,1)S(1)} %get-tuple-element.64), channel_id=1, source_target_pairs={{0,2},{2,0},{4,6},{6,4},{8,10},{10,8},{12,14},{14,12},{16,18},{18,... | collective-permute-start | bytes 589832 | tf_op jit(solution)/shard_map/ppermute | solution.py:457
  63.0 7.8 %collective-permute-start.24 = (bf16[384,256]{1,0:T(8,128)(2,1)S(1)}, bf16[384,256]{1,0:T(8,128)(2,1)S(1)}, u32[]{:S(2)}, u32[]{:S(2)}) collective-permute-start(bf16[384,256]{1,0:T(8,128)(2,1)S(1)} %get-tuple-element.63), channel_id=1, source_target_pairs={{0,2},{2,0},{4,6},{6,4},{8,10},{10,8},{12,14},{14,12},{16,18},{18,... | collective-permute-start | bytes 589832 | tf_op jit(solution)/shard_map/ppermute | solution.py:457
  (8 other events, 90.2 us)

commit v13 on v12

--- a/solution.py
+++ b/solution.py
@@ -500,7 +500,7 @@
     normed2 = norm((2, 3), [within2, within3], [carry2, carry3])
     far2 = flip(normed2)
 
-    total = project_own(after(meta, far0), [normed0, normed1, normed2], weight, columns)
+    total = project_own(meta, [normed0, normed1, normed2], weight, columns)
     w0.append(swap(behind(w0[0], normed0), plane))
     w2.append(swap(behind(w0[1], normed2)[:, :quarter], 2))
     w2.append(swap(behind(w2[0], normed2)[:, quarter:], plane))

time: 74.6 us -> 74.6 us (level)
  no operation moved by 1% of the time
where the time goes in v13:
time: 74.6 us; the launch traced here: 74.3 us
  Pallas kernels  28.2 us (38%)
  starting transfers between devices  24.8 us (33%)
  waiting for transfers between devices  19.8 us (27%)
  local copies, waits for them, and re-layouts  1.04 us (1%)
    pallas_call x13, Pallas kernels, local(): call(kernel, (1,), specs or [whole(a.shape) for a in arrays], [whole(s.sh...  15.5 us
    ppermute x19, waiting for transfers between devices, swap(): return lax.ppermute(x, 'seq', [(i, i ^ bit) for i in range(n_seq)])  15.2 us
    ppermute x19, starting transfers between devices, swap(): return lax.ppermute(x, 'seq', [(i, i ^ bit) for i in range(n_seq)])  10.9 us
    ppermute x2, starting transfers between devices, shift(): lax.ppermute(x, 'seq', [(i, i + count) for i in range(n_seq - count)])  8.15 us
    pallas_call x2, Pallas kernels, project_more(): call(kernel, (1,), [vmem] * (1 + count + len(flat)), pl.BlockSpec(memory_...  5.76 us
    ppermute x4, starting transfers between devices, flip(): return lax.ppermute(x, 'head', [(0, 1), (1, 0)])  5.76 us
    pallas_call x1, Pallas kernels, project_own(): call(kernel, (OWN_TILES,), [whole(p.shape) for p in pieces] + [pl.BlockSp...  4.97 us
    ppermute x2, waiting for transfers between devices, shift(): lax.ppermute(x, 'seq', [(i, i + count) for i in range(n_seq - count)])  2.37 us
  transfers between devices with their start and end apart: 25, of which 14 were waited for; matrix products, arithmetic and copies ran while one was open for 0% of the time, Pallas kernels for 31%

profile of v13, /device:TPU:0, one launch (start us, length us, event | category | flops | bytes accessed | tf_op | source)
XLA Modules:
  0.0 74.3 jit_solution(3282266724831055916)
XLA Ops:
  0.7 2.0 %shard_map.64 = bf16[384,1024]{1,0:T(8,128)(2,1)S(1)} custom-call(s32[24]{0:T(128)S(1)} %concatenate.3.meta_ref, bf16[1536,4096]{1,0:T(8,128)(2,1)} %refs_6_.3), custom_call_target="tpu_custom_call" | custom-call | flops 6000000000 | bytes 1024 | tf_op jit(solution)/shard_map/pallas_call | solution.py:159
  2.7 3.0 %collective-permute-start.6 = (bf16[384,1024]{1,0:T(8,128)(2,1)S(1)}, bf16[384,1024]{1,0:T(8,128)(2,1)S(1)}, u32[]{:S(2)}, u32[]{:S(2)}) collective-permute-start(bf16[384,1024]{1,0:T(8,128)(2,1)S(1)} %shard_map.64), channel_id=1, source_target_pairs={{0,1},{1,0},{2,3},{3,2},{4,5},{5,4},{6,7},{7,6},{8,9},{9,8},{10,11... | collective-permute-start | bytes 2359304 | tf_op jit(solution)/shard_map/ppermute | solution.py:463
  5.8 1.7 %shard_map.65 = (bf16[2,384,128]{2,1,0:T(8,128)(2,1)S(1)}, bf16[2,384,128]{2,1,0:T(8,128)(2,1)S(1)}) custom-call(s32[24]{0:T(128)S(1)} %concatenate.3.meta_ref, bf16[512,1536]{1,0:T(8,128)(2,1)S(1)} %copy-done, bf16[512,1536]{1,0:T(8,128)(2,1)S(1)} %copy-done, bf16[512,1536]{1,0:T(8,128)(2,1)S(1)} %copy-done, bf16[512,1536]{1,0:T(8,128)(2,1)S(1)} %copy-done, ...), custom_call_target="tpu_custom_call" | custom-call | flops 2000000000 | bytes 1024 | tf_op jit(solution)/shard_map/pallas_call | solution.py:123
  7.5 1.9 %shard_map.66 = (f32[512,384]{1,0:T(8,128)S(1)}, bf16[512,512]{1,0:T(8,128)(2,1)S(1)}) custom-call(s32[24]{0:T(128)S(1)} %concatenate.3.meta_ref, bf16[512,1536]{1,0:T(8,128)(2,1)S(1)} %copy-done.2, bf16[512,1536]{1,0:T(8,128)(2,1)S(1)} %copy-done, bf16[512,1536]{1,0:T(8,128)(2,1)S(1)} %copy-done.1), custom_call_target="tpu_custom_call" | custom-call | flops 2000000000 | bytes 1024 | tf_op jit(solution)/shard_map/pallas_call | solution.py:123
  10.1 1.6 %collective-permute-start.1 = (bf16[384,128]{1,0:T(8,128)(2,1)S(1)}, bf16[384,128]{1,0:T(8,128)(2,1)S(1)}, u32[]{:S(2)}, u32[]{:S(2)}) collective-permute-start(bf16[384,128]{1,0:T(8,128)(2,1)S(1)} %get-tuple-element.41), channel_id=1, source_target_pairs={{0,4},{2,6},{4,0},{6,2},{8,12},{10,14},{12,8},{14,10},{16,20},{18,... | collective-permute-start | bytes 294920 | tf_op jit(solution)/shard_map/ppermute | solution.py:457
  11.7 1.8 %shard_map.68.refs_1_ = f32[512,384]{1,0:T(8,128)S(1)} custom-call(s32[24]{0:T(128)S(1)} %concatenate.3.meta_ref, bf16[512,1536]{1,0:T(8,128)(2,1)S(1)} %copy-done.2, bf16[512,1536]{1,0:T(8,128)(2,1)S(1)} %copy-done, bf16[512,1536]{1,0:T(8,128)(2,1)S(1)} %copy-done.1, bf16[512,512]{1,0:T(8,128)(2,1)S(1)} %get-tuple-element.39.rest_0_), custom_call_target="tpu_custom_call" | custom-call | flops 2000000000 | bytes 1024 | tf_op jit(solution)/shard_map/pallas_call | solution.py:123
  13.5 1.9 %collective-permute-done.1.b_ref = bf16[384,128]{1,0:T(8,128)(2,1)S(1)} collective-permute-done((bf16[384,128]{1,0:T(8,128)(2,1)S(1)}, bf16[384,128]{1,0:T(8,128)(2,1)S(1)}, u32[]{:S(2)}, u32[]{:S(2)}) %collective-permute-start.1) | collective-permute-done | bytes 98336 | tf_op jit(solution)/shard_map/ppermute | solution.py:457
  16.0 3.5 %collective-permute-start.2 = (bf16[384,128]{1,0:T(8,128)(2,1)S(1)}, bf16[384,128]{1,0:T(8,128)(2,1)S(1)}, u32[]{:S(2)}, u32[]{:S(2)}) collective-permute-start(bf16[384,128]{1,0:T(8,128)(2,1)S(1)} %shard_map.69.a_ref), channel_id=1, source_target_pairs={{0,8},{2,10},{4,12},{6,14},{8,16},{10,18},{12,20},{14,22},{16,24},... | collective-permute-start | bytes 294920 | tf_op jit(solution)/shard_map/ppermute | solution.py:460
  19.5 1.8 %shard_map.70.refs_1_ = f32[512,384]{1,0:T(8,128)S(1)} custom-call(s32[24]{0:T(128)S(1)} %concatenate.3.meta_ref, bf16[512,1536]{1,0:T(8,128)(2,1)S(1)} %copy-done.2, bf16[512,1536]{1,0:T(8,128)(2,1)S(1)} %copy-done, bf16[512,1536]{1,0:T(8,128)(2,1)S(1)} %copy-done.1, bf16[512,512]{1,0:T(8,128)(2,1)S(1)} %get-tuple-element.39.rest_0_), custom_call_target="tpu_custom_call" | custom-call | flops 2000000000 | bytes 1024 | tf_op jit(solution)/shard_map/pallas_call | solution.py:123
  22.3 1.0 %collective-permute-done.6.refs_2_ = bf16[384,1024]{1,0:T(8,128)(2,1)S(1)} collective-permute-done((bf16[384,1024]{1,0:T(8,128)(2,1)S(1)}, bf16[384,1024]{1,0:T(8,128)(2,1)S(1)}, u32[]{:S(2)}, u32[]{:S(2)}) %collective-permute-start.6) | collective-permute-done | bytes 786464 | tf_op jit(solution)/shard_map/ppermute | solution.py:463
  23.3 1.7 %collective-permute-start.7 = (bf16[384,1024]{1,0:T(8,128)(2,1)S(1)}, bf16[384,1024]{1,0:T(8,128)(2,1)S(1)}, u32[]{:S(2)}, u32[]{:S(2)}) collective-permute-start(bf16[384,1024]{1,0:T(8,128)(2,1)S(1)} %collective-permute-done.6.refs_2_), channel_id=1, source_target_pairs={{0,4},{2,6},{4,0},{6,2},{8,12},{10,14},{12,8},{14,10},{16,20},{18,... | collective-permute-start | bytes 2359304 | tf_op jit(solution)/shard_map/ppermute | solution.py:457
  25.0 4.7 %collective-permute-start.3 = (bf16[384,128]{1,0:T(8,128)(2,1)S(1)}, bf16[384,128]{1,0:T(8,128)(2,1)S(1)}, u32[]{:S(2)}, u32[]{:S(2)}) collective-permute-start(bf16[384,128]{1,0:T(8,128)(2,1)S(1)} %shard_map.71), channel_id=1, source_target_pairs={{0,16},{2,18},{4,20},{6,22},{8,24},{10,26},{12,28},{14,30},{1,17},... | collective-permute-start | bytes 294920 | tf_op jit(solution)/shard_map/ppermute | solution.py:460
  29.7 2.0 %collective-permute-done.3.far_ref = bf16[384,128]{1,0:T(8,128)(2,1)S(1)} collective-permute-done((bf16[384,128]{1,0:T(8,128)(2,1)S(1)}, bf16[384,128]{1,0:T(8,128)(2,1)S(1)}, u32[]{:S(2)}, u32[]{:S(2)}) %collective-permute-start.3) | collective-permute-done | bytes 98336 | tf_op jit(solution)/shard_map/ppermute | solution.py:460
  33.4 1.6 %collective-permute-start.5 = (bf16[512,384]{1,0:T(8,128)(2,1)S(1)}, bf16[512,384]{1,0:T(8,128)(2,1)S(1)}, u32[]{:S(2)}, u32[]{:S(2)}) collective-permute-start(bf16[512,384]{1,0:T(8,128)(2,1)S(1)} %shard_map.73.refs_0_), channel_id=1, source_target_pairs={{0,1},{1,0},{2,3},{3,2},{4,5},{5,4},{6,7},{7,6},{8,9},{9,8},{10,11... | collective-permute-start | bytes 1179656 | tf_op jit(solution)/shard_map/ppermute | solution.py:463
  35.0 2.4 %collective-permute-start.11 = (bf16[384,1024]{1,0:T(8,128)(2,1)S(1)}, bf16[384,1024]{1,0:T(8,128)(2,1)S(1)}, u32[]{:S(2)}, u32[]{:S(2)}) collective-permute-start(bf16[384,1024]{1,0:T(8,128)(2,1)S(1)} %collective-permute-done.6.refs_2_), channel_id=1, source_target_pairs={{0,8},{2,10},{4,12},{6,14},{8,0},{10,2},{12,4},{14,6},{16,24},{18,... | collective-permute-start | bytes 2359304 | tf_op jit(solution)/shard_map/ppermute | solution.py:457
  38.0 1.8 %shard_map.76.refs_5_ = f32[512,384]{1,0:T(8,128)S(1)} custom-call(s32[24]{0:T(128)S(1)} %concatenate.3.meta_ref, bf16[512,1536]{1,0:T(8,128)(2,1)S(1)} %copy-done.2, bf16[512,1536]{1,0:T(8,128)(2,1)S(1)} %copy-done, bf16[512,1536]{1,0:T(8,128)(2,1)S(1)} %copy-done.1, bf16[512,512]{1,0:T(8,128)(2,1)S(1)} %get-tuple-element.39.rest_0_), custom_call_target="tpu_custom_call" | custom-call | flops 2000000000 | bytes 1024 | tf_op jit(solution)/shard_map/pallas_call | solution.py:123
  43.1 1.1 %collective-permute-done.8.chip_ref = bf16[384,128]{1,0:T(8,128)(2,1)S(1)} collective-permute-done((bf16[384,128]{1,0:T(8,128)(2,1)S(1)}, bf16[384,128]{1,0:T(8,128)(2,1)S(1)}, u32[]{:S(2)}, u32[]{:S(2)}) %collective-permute-start.8) | collective-permute-done | bytes 98336 | tf_op jit(solution)/shard_map/ppermute | solution.py:457
  46.1 1.3 %shard_map.77.refs_2_ = bf16[512,768]{1,0:T(8,128)(2,1)S(1)} custom-call(s32[24]{0:T(128)S(1)} %concatenate.3.meta_ref, bf16[512,1536]{1,0:T(8,128)(2,1)S(1)} %copy-done.2, f32[512,384]{1,0:T(8,128)S(1)} %shard_map.70.refs_1_, bf16[384,128]{1,0:T(8,128)(2,1)S(1)} %get-tuple-element.49.refs_2_, f32[1,1536]{1,0:T(1,128)S(1)} %reshape.2.refs_3_.refs_7_, ...), custom_call_target="tpu_custom_call" | custom-call | flops 2000000000 | bytes 1024 | tf_op jit(solution)/shard_map/pallas_call | solution.py:123
  47.5 5.3 %collective-permute-done.11.refs_3_ = bf16[384,1024]{1,0:T(8,128)(2,1)S(1)} collective-permute-done((bf16[384,1024]{1,0:T(8,128)(2,1)S(1)}, bf16[384,1024]{1,0:T(8,128)(2,1)S(1)}, u32[]{:S(2)}, u32[]{:S(2)}) %collective-permute-start.11) | collective-permute-done | bytes 786464 | tf_op jit(solution)/shard_map/ppermute | solution.py:457
  53.4 1.8 %collective-permute-start.18 = (bf16[384,512]{1,0:T(8,128)(2,1)S(1)}, bf16[384,512]{1,0:T(8,128)(2,1)S(1)}, u32[]{:S(2)}, u32[]{:S(2)}) collective-permute-start(bf16[384,512]{1,0:T(8,128)(2,1)S(1)} %slice.41), channel_id=1, source_target_pairs={{0,8},{2,10},{4,12},{6,14},{8,0},{10,2},{12,4},{14,6},{16,24},{18,... | collective-permute-start | bytes 1179656 | tf_op jit(solution)/shard_map/ppermute | solution.py:457
  56.5 4.3 %collective-permute-done.17.refs_2_ = bf16[384,512]{1,0:T(8,128)(2,1)S(1)} collective-permute-done((bf16[384,512]{1,0:T(8,128)(2,1)S(1)}, bf16[384,512]{1,0:T(8,128)(2,1)S(1)}, u32[]{:S(2)}, u32[]{:S(2)}) %collective-permute-start.17) | collective-permute-done | bytes 393248 | tf_op jit(solution)/shard_map/ppermute | solution.py:457
  63.2 5.0 %shard_map.78.t_ref = f32[512,2048]{1,0:T(8,128)S(1)} custom-call(s32[24]{0:T(128)S(1)} %concatenate.3.meta_ref, bf16[512,384]{1,0:T(8,128)(2,1)S(1)} %shard_map.73.refs_0_, bf16[512,384]{1,0:T(8,128)(2,1)S(1)} %shard_map.74.refs_1_, bf16[512,768]{1,0:T(8,128)(2,1)S(1)} %shard_map.77.refs_2_, bf16[1536,4096]{1,0:T(8,128)(2,1)S(1)} %bitcast.5, ...), custom_call_target="tpu_custom_call" | custom-call | flops 1000000 | bytes 1024 | tf_op jit(solution)/shard_map/pallas_call | solution.py:374
  68.2 2.6 %shard_map.79.t_ref = f32[512,2048]{1,0:T(8,128)S(1)} custom-call(s32[24]{0:T(128)S(1)} %concatenate.3.meta_ref, f32[512,2048]{1,0:T(8,128)S(1)} %shard_map.78.t_ref, bf16[512,384]{1,0:T(8,128)(2,1)S(1)} %collective-permute-done.5.refs_0_, bf16[512,384]{1,0:T(8,128)(2,1)S(1)} %collective-permute-done.10.refs_1_, ...), custom_call_target="tpu_custom_call", output_to_operand_aliasing={{}: (1, {})} | custom-call | flops 1000000 | bytes 1024 | tf_op jit(solution)/shard_map/pallas_call | solution.py:429
  71.0 3.2 %shard_map.80 = bf16[512,2048]{1,0:T(8,128)(2,1)} custom-call(s32[24]{0:T(128)S(1)} %concatenate.3.meta_ref, f32[512,2048]{1,0:T(8,128)S(1)} %shard_map.79.t_ref, bf16[512,768]{1,0:T(8,128)(2,1)S(1)} %collective-permute-done.16.refs_0_, bf16[384,1024]{1,0:T(8,128)(2,1)S(1)} %collective-permute-done.7.refs_1_, ...), custom_call_target="tpu_custom_call" | custom-call | flops 1000000 | bytes 1024 | tf_op jit(solution)/shard_map/pallas_call | solution.py:429
  (68 shorter events, 15.1 us)
Async XLA Ops:
  2.7 20.6 %collective-permute-start.6 = (bf16[384,1024]{1,0:T(8,128)(2,1)S(1)}, bf16[384,1024]{1,0:T(8,128)(2,1)S(1)}, u32[]{:S(2)}, u32[]{:S(2)}) collective-permute-start(bf16[384,1024]{1,0:T(8,128)(2,1)S(1)} %shard_map.64), channel_id=1, source_target_pairs={{0,1},{1,0},{2,3},{3,2},{4,5},{5,4},{6,7},{7,6},{8,9},{9,8},{10,11... | collective-permute-start | bytes 2359304 | tf_op jit(solution)/shard_map/ppermute | solution.py:463
  7.4 2.0 %collective-permute-start = (bf16[2,384,128]{2,1,0:T(8,128)(2,1)S(1)}, bf16[2,384,128]{2,1,0:T(8,128)(2,1)S(1)}, u32[]{:S(2)}, u32[]{:S(2)}) collective-permute-start(bf16[2,384,128]{2,1,0:T(8,128)(2,1)S(1)} %get-tuple-element.31), channel_id=1, source_target_pairs={{0,2},{2,0},{4,6},{6,4},{8,10},{10,8},{12,14},{14,12},{16,18},{18,... | collective-permute-start | bytes 589832 | tf_op jit(solution)/shard_map/ppermute | solution.py:457
  10.1 5.3 %collective-permute-start.1 = (bf16[384,128]{1,0:T(8,128)(2,1)S(1)}, bf16[384,128]{1,0:T(8,128)(2,1)S(1)}, u32[]{:S(2)}, u32[]{:S(2)}) collective-permute-start(bf16[384,128]{1,0:T(8,128)(2,1)S(1)} %get-tuple-element.41), channel_id=1, source_target_pairs={{0,4},{2,6},{4,0},{6,2},{8,12},{10,14},{12,8},{14,10},{16,20},{18,... | collective-permute-start | bytes 294920 | tf_op jit(solution)/shard_map/ppermute | solution.py:457
  16.0 5.7 %collective-permute-start.2 = (bf16[384,128]{1,0:T(8,128)(2,1)S(1)}, bf16[384,128]{1,0:T(8,128)(2,1)S(1)}, u32[]{:S(2)}, u32[]{:S(2)}) collective-permute-start(bf16[384,128]{1,0:T(8,128)(2,1)S(1)} %shard_map.69.a_ref), channel_id=1, source_target_pairs={{0,8},{2,10},{4,12},{6,14},{8,16},{10,18},{12,20},{14,22},{16,24},... | collective-permute-start | bytes 294920 | tf_op jit(solution)/shard_map/ppermute | solution.py:460
  23.3 19.8 %collective-permute-start.7 = (bf16[384,1024]{1,0:T(8,128)(2,1)S(1)}, bf16[384,1024]{1,0:T(8,128)(2,1)S(1)}, u32[]{:S(2)}, u32[]{:S(2)}) collective-permute-start(bf16[384,1024]{1,0:T(8,128)(2,1)S(1)} %collective-permute-done.6.refs_2_), channel_id=1, source_target_pairs={{0,4},{2,6},{4,0},{6,2},{8,12},{10,14},{12,8},{14,10},{16,20},{18,... | collective-permute-start | bytes 2359304 | tf_op jit(solution)/shard_map/ppermute | solution.py:457
  25.0 6.7 %collective-permute-start.3 = (bf16[384,128]{1,0:T(8,128)(2,1)S(1)}, bf16[384,128]{1,0:T(8,128)(2,1)S(1)}, u32[]{:S(2)}, u32[]{:S(2)}) collective-permute-start(bf16[384,128]{1,0:T(8,128)(2,1)S(1)} %shard_map.71), channel_id=1, source_target_pairs={{0,16},{2,18},{4,20},{6,22},{8,24},{10,26},{12,28},{14,30},{1,17},... | collective-permute-start | bytes 294920 | tf_op jit(solution)/shard_map/ppermute | solution.py:460
  33.4 8.9 %collective-permute-start.5 = (bf16[512,384]{1,0:T(8,128)(2,1)S(1)}, bf16[512,384]{1,0:T(8,128)(2,1)S(1)}, u32[]{:S(2)}, u32[]{:S(2)}) collective-permute-start(bf16[512,384]{1,0:T(8,128)(2,1)S(1)} %shard_map.73.refs_0_), channel_id=1, source_target_pairs={{0,1},{1,0},{2,3},{3,2},{4,5},{5,4},{6,7},{7,6},{8,9},{9,8},{10,11... | collective-permute-start | bytes 1179656 | tf_op jit(solution)/shard_map/ppermute | solution.py:463
  35.0 17.7 %collective-permute-start.11 = (bf16[384,1024]{1,0:T(8,128)(2,1)S(1)}, bf16[384,1024]{1,0:T(8,128)(2,1)S(1)}, u32[]{:S(2)}, u32[]{:S(2)}) collective-permute-start(bf16[384,1024]{1,0:T(8,128)(2,1)S(1)} %collective-permute-done.6.refs_2_), channel_id=1, source_target_pairs={{0,8},{2,10},{4,12},{6,14},{8,0},{10,2},{12,4},{14,6},{16,24},{18,... | collective-permute-start | bytes 2359304 | tf_op jit(solution)/shard_map/ppermute | solution.py:457
  37.5 2.4 %collective-permute-start.4 = (bf16[384,128]{1,0:T(8,128)(2,1)S(1)}, bf16[384,128]{1,0:T(8,128)(2,1)S(1)}, u32[]{:S(2)}, u32[]{:S(2)}) collective-permute-start(bf16[384,128]{1,0:T(8,128)(2,1)S(1)} %get-tuple-element.45), channel_id=1, source_target_pairs={{0,2},{2,0},{4,6},{6,4},{8,10},{10,8},{12,14},{14,12},{16,18},{18,... | collective-permute-start | bytes 294920 | tf_op jit(solution)/shard_map/ppermute | solution.py:457
  37.5 6.7 %collective-permute-start.8 = (bf16[384,128]{1,0:T(8,128)(2,1)S(1)}, bf16[384,128]{1,0:T(8,128)(2,1)S(1)}, u32[]{:S(2)}, u32[]{:S(2)}) collective-permute-start(bf16[384,128]{1,0:T(8,128)(2,1)S(1)} %get-tuple-element.48), channel_id=1, source_target_pairs={{0,4},{2,6},{4,0},{6,2},{8,12},{10,14},{12,8},{14,10},{16,20},{18,... | collective-permute-start | bytes 294920 | tf_op jit(solution)/shard_map/ppermute | solution.py:457
  40.9 14.4 %collective-permute-start.10 = (bf16[512,384]{1,0:T(8,128)(2,1)S(1)}, bf16[512,384]{1,0:T(8,128)(2,1)S(1)}, u32[]{:S(2)}, u32[]{:S(2)}) collective-permute-start(bf16[512,384]{1,0:T(8,128)(2,1)S(1)} %shard_map.74.refs_1_), channel_id=1, source_target_pairs={{0,1},{1,0},{2,3},{3,2},{4,5},{5,4},{6,7},{7,6},{8,9},{9,8},{10,11... | collective-permute-start | bytes 1179656 | tf_op jit(solution)/shard_map/ppermute | solution.py:463
  44.9 11.0 %collective-permute-start.12 = (bf16[384,512]{1,0:T(8,128)(2,1)S(1)}, bf16[384,512]{1,0:T(8,128)(2,1)S(1)}, u32[]{:S(2)}, u32[]{:S(2)}) collective-permute-start(bf16[384,512]{1,0:T(8,128)(2,1)S(1)} %get-tuple-element.60), channel_id=1, source_target_pairs={{0,2},{2,0},{4,6},{6,4},{8,10},{10,8},{12,14},{14,12},{16,18},{18,... | collective-permute-start | bytes 1179656 | tf_op jit(solution)/shard_map/ppermute | solution.py:457
  45.5 10.5 %collective-permute-start.13 = (bf16[384,512]{1,0:T(8,128)(2,1)S(1)}, bf16[384,512]{1,0:T(8,128)(2,1)S(1)}, u32[]{:S(2)}, u32[]{:S(2)}) collective-permute-start(bf16[384,512]{1,0:T(8,128)(2,1)S(1)} %get-tuple-element.59), channel_id=1, source_target_pairs={{0,2},{2,0},{4,6},{6,4},{8,10},{10,8},{12,14},{14,12},{16,18},{18,... | collective-permute-start | bytes 1179656 | tf_op jit(solution)/shard_map/ppermute | solution.py:457
  52.8 8.0 %collective-permute-start.17 = (bf16[384,512]{1,0:T(8,128)(2,1)S(1)}, bf16[384,512]{1,0:T(8,128)(2,1)S(1)}, u32[]{:S(2)}, u32[]{:S(2)}) collective-permute-start(bf16[384,512]{1,0:T(8,128)(2,1)S(1)} %slice.40), channel_id=1, source_target_pairs={{0,4},{2,6},{4,0},{6,2},{8,12},{10,14},{12,8},{14,10},{16,20},{18,... | collective-permute-start | bytes 1179656 | tf_op jit(solution)/shard_map/ppermute | solution.py:457
  53.4 7.8 %collective-permute-start.18 = (bf16[384,512]{1,0:T(8,128)(2,1)S(1)}, bf16[384,512]{1,0:T(8,128)(2,1)S(1)}, u32[]{:S(2)}, u32[]{:S(2)}) collective-permute-start(bf16[384,512]{1,0:T(8,128)(2,1)S(1)} %slice.41), channel_id=1, source_target_pairs={{0,8},{2,10},{4,12},{6,14},{8,0},{10,2},{12,4},{14,6},{16,24},{18,... | collective-permute-start | bytes 1179656 | tf_op jit(solution)/shard_map/ppermute | solution.py:457
  55.3 15.8 %collective-permute-start.16 = (bf16[512,768]{1,0:T(8,128)(2,1)S(1)}, bf16[512,768]{1,0:T(8,128)(2,1)S(1)}, u32[]{:S(2)}, u32[]{:S(2)}) collective-permute-start(bf16[512,768]{1,0:T(8,128)(2,1)S(1)} %shard_map.77.refs_2_), channel_id=1, source_target_pairs={{0,1},{1,0},{2,3},{3,2},{4,5},{5,4},{6,7},{7,6},{8,9},{9,8},{10,11... | collective-permute-start | bytes 2359304 | tf_op jit(solution)/shard_map/ppermute | solution.py:463
  55.9 5.4 %collective-permute-start.14 = (bf16[384,512]{1,0:T(8,128)(2,1)S(1)}, bf16[384,512]{1,0:T(8,128)(2,1)S(1)}, u32[]{:S(2)}, u32[]{:S(2)}) collective-permute-start(bf16[384,512]{1,0:T(8,128)(2,1)S(1)} %get-tuple-element.58), channel_id=1, source_target_pairs={{0,2},{2,0},{4,6},{6,4},{8,10},{10,8},{12,14},{14,12},{16,18},{18,... | collective-permute-start | bytes 1179656 | tf_op jit(solution)/shard_map/ppermute | solution.py:457
  56.0 5.9 %collective-permute-start.15 = (bf16[384,512]{1,0:T(8,128)(2,1)S(1)}, bf16[384,512]{1,0:T(8,128)(2,1)S(1)}, u32[]{:S(2)}, u32[]{:S(2)}) collective-permute-start(bf16[384,512]{1,0:T(8,128)(2,1)S(1)} %get-tuple-element.57), channel_id=1, source_target_pairs={{0,2},{2,0},{4,6},{6,4},{8,10},{10,8},{12,14},{14,12},{16,18},{18,... | collective-permute-start | bytes 1179656 | tf_op jit(solution)/shard_map/ppermute | solution.py:457
  60.7 1.7 %collective-permute-start.19 = (bf16[384,512]{1,0:T(8,128)(2,1)S(1)}, bf16[384,512]{1,0:T(8,128)(2,1)S(1)}, u32[]{:S(2)}, u32[]{:S(2)}) collective-permute-start(bf16[384,512]{1,0:T(8,128)(2,1)S(1)} %get-tuple-element.56), channel_id=1, source_target_pairs={{0,2},{2,0},{4,6},{6,4},{8,10},{10,8},{12,14},{14,12},{16,18},{18,... | collective-permute-start | bytes 1179656 | tf_op jit(solution)/shard_map/ppermute | solution.py:457
  61.2 1.8 %collective-permute-start.20 = (bf16[384,512]{1,0:T(8,128)(2,1)S(1)}, bf16[384,512]{1,0:T(8,128)(2,1)S(1)}, u32[]{:S(2)}, u32[]{:S(2)}) collective-permute-start(bf16[384,512]{1,0:T(8,128)(2,1)S(1)} %get-tuple-element.55), channel_id=1, source_target_pairs={{0,2},{2,0},{4,6},{6,4},{8,10},{10,8},{12,14},{14,12},{16,18},{18,... | collective-permute-start | bytes 1179656 | tf_op jit(solution)/shard_map/ppermute | solution.py:457
  61.3 9.4 %collective-permute-start.21 = (bf16[384,256]{1,0:T(8,128)(2,1)S(1)}, bf16[384,256]{1,0:T(8,128)(2,1)S(1)}, u32[]{:S(2)}, u32[]{:S(2)}) collective-permute-start(bf16[384,256]{1,0:T(8,128)(2,1)S(1)} %get-tuple-element.64), channel_id=1, source_target_pairs={{0,2},{2,0},{4,6},{6,4},{8,10},{10,8},{12,14},{14,12},{16,18},{18,... | collective-permute-start | bytes 589832 | tf_op jit(solution)/shard_map/ppermute | solution.py:457
  61.9 8.9 %collective-permute-start.22 = (bf16[384,256]{1,0:T(8,128)(2,1)S(1)}, bf16[384,256]{1,0:T(8,128)(2,1)S(1)}, u32[]{:S(2)}, u32[]{:S(2)}) collective-permute-start(bf16[384,256]{1,0:T(8,128)(2,1)S(1)} %get-tuple-element.63), channel_id=1, source_target_pairs={{0,2},{2,0},{4,6},{6,4},{8,10},{10,8},{12,14},{14,12},{16,18},{18,... | collective-permute-start | bytes 589832 | tf_op jit(solution)/shard_map/ppermute | solution.py:457
  62.5 8.3 %collective-permute-start.23 = (bf16[384,256]{1,0:T(8,128)(2,1)S(1)}, bf16[384,256]{1,0:T(8,128)(2,1)S(1)}, u32[]{:S(2)}, u32[]{:S(2)}) collective-permute-start(bf16[384,256]{1,0:T(8,128)(2,1)S(1)} %get-tuple-element.62), channel_id=1, source_target_pairs={{0,2},{2,0},{4,6},{6,4},{8,10},{10,8},{12,14},{14,12},{16,18},{18,... | collective-permute-start | bytes 589832 | tf_op jit(solution)/shard_map/ppermute | solution.py:457
  63.0 7.8 %collective-permute-start.24 = (bf16[384,256]{1,0:T(8,128)(2,1)S(1)}, bf16[384,256]{1,0:T(8,128)(2,1)S(1)}, u32[]{:S(2)}, u32[]{:S(2)}) collective-permute-start(bf16[384,256]{1,0:T(8,128)(2,1)S(1)} %get-tuple-element.61), channel_id=1, source_target_pairs={{0,2},{2,0},{4,6},{6,4},{8,10},{10,8},{12,14},{14,12},{16,18},{18,... | collective-permute-start | bytes 589832 | tf_op jit(solution)/shard_map/ppermute | solution.py:457
  (8 other events, 90.2 us)
